TPU v7x, 32 devices: a whole 2x2x4 slice. The times are simulated.
32 devices in a mesh: groups: 2 (over x), rep: 8 (over z, y), tp: 2 (over core).
Axes of the slice: x: 2, y: 2, z: 4, core: 2. Of those that a mesh axis runs over, the one named last changes fastest.
Arguments:
- normed_token_rows: bfloat16 [6144, 8192], P(('groups', 'rep'), 'tp'), parts along dimension 0, may hold values from -6 to 6
- base_value_rows: bfloat16 [6144, 1024], P(('groups', 'rep'), 'tp'), parts along dimension 0, may hold values from -6 to 6
- queries: bfloat16 [6144, 8192], P(('groups', 'rep'), 'tp'), parts along dimension 0, may hold values from -120 to 120
- stacked_key_rows: bfloat16 [6144, 1024], P(('groups', 'rep'), 'tp'), parts along dimension 0, may hold values from -5 to 5
- adapter_of_row: int32 [6144, 1], P(('groups', 'rep')), parts along dimension 0, may hold values from 0 to 7; in each aligned block of 384 rows (0 to 383, 384 to 767, ...) at most 96 rows name the same one
- sequence_lengths: int32 [16, 4], P(('groups', 'rep')), parts along dimension 0, may hold values from 1 to 192, 384 in all within a row
- adapter_down_weight: bfloat16 [16, 8192, 64], P(('groups', 'rep'), 'tp'), parts along dimension 0, may hold values from -0.0625 to 0.0625
- adapter_up_weight: bfloat16 [16, 64, 1024], P(('groups', 'rep'), None, 'tp'), parts along dimension 0, may hold values from -0.75 to 0.75
Outputs:
- attended: bfloat16 [6144, 8192], P(('groups', 'rep'), 'tp'), parts along dimension 0
There are 2 independent parts, one for each index of `groups`. A program takes and returns all parts, laid end to end along the dimension named above; each array names one. Nothing has to cross between parts.
Inputs may be any that keep to these rules, and one draw needn't show every extreme that they name: `adapter_of_row`: in the rows of one replica each adapter is named by at most 96 rows, a bound that some block reaches. `sequence_lengths`: each replica's lengths sum to 384; the longest is exactly 192.
All inputs are finite; a program needn't handle non-finite values.
Results may differ from a plain program's by a relative error of at most 0.008.
Values may be sent and summed in bfloat16 or wider, within the bound.
No kernel may reach another device: no remote copies, remote signals or barrier semaphores. Data moves between devices by JAX's collectives and lax.ppermute only.
A program may use at most 192 MiB of HBM per device.

v0:
```python
import jax
import jax.numpy as jnp
from jax import lax
from jax.sharding import PartitionSpec as P

HEADS = 64
KEY_VALUE_HEADS = 8
HEAD_SIZE = 128


adapter_scale = 2.0


def slot_layout(adapter_ids, adapters, most_rows):
    row_count = adapter_ids.shape[0]
    onehot = (adapter_ids[:, None] == jnp.arange(adapters, dtype=jnp.int32)[None, :]).astype(
        jnp.int32
    )
    before = jnp.cumsum(onehot, axis=0) - onehot
    position = jnp.sum(before * onehot, axis=1)
    slot_of_row = adapter_ids * most_rows + position
    empty_slots = jnp.full((adapters * most_rows,), row_count, jnp.int32)
    row_of_slot = empty_slots.at[slot_of_row].set(jnp.arange(row_count, dtype=jnp.int32))
    return (slot_of_row, row_of_slot)


def attend_block(queries, stacked_key_rows, value_rows, lengths):
    count = queries.shape[0]
    kv_heads = stacked_key_rows.shape[1] // HEAD_SIZE
    group = HEADS // KEY_VALUE_HEADS
    positions = jnp.arange(count, dtype=jnp.int32)
    ends = jnp.cumsum(lengths)
    segment = jnp.sum((positions[:, None] >= ends[None, :]).astype(jnp.int32), axis=1)
    allowed = (segment[:, None] == segment[None, :]) & (positions[None, :] <= positions[:, None])
    query_heads = queries.reshape(count, kv_heads, group, HEAD_SIZE)
    key_heads = stacked_key_rows.reshape(count, kv_heads, HEAD_SIZE)
    value_heads = value_rows.reshape(count, kv_heads, HEAD_SIZE)
    scores = jnp.einsum(
        "tjgd,sjd->jgts", query_heads, key_heads, preferred_element_type=jnp.float32
    ) * HEAD_SIZE ** (-0.5)
    scores = jnp.where(allowed[None, None], scores, -1e30)
    peak = jnp.max(scores, axis=-1, keepdims=True)
    weights = jnp.exp(scores - peak)
    probs = (weights / jnp.sum(weights, axis=-1, keepdims=True)).astype(jnp.bfloat16)
    mixed = jnp.einsum("jgts,sjd->tjgd", probs, value_heads, preferred_element_type=jnp.float32)
    return mixed.astype(jnp.bfloat16).reshape(count, kv_heads * group * HEAD_SIZE)


def on_device(
    normed_token_rows,
    base_value_rows,
    queries,
    stacked_key_rows,
    adapter_of_row,
    sequence_lengths,
    adapter_down_weight,
    adapter_up_weight,
):
    row_count = normed_token_rows.shape[0]
    feature_half = normed_token_rows.shape[1]
    local_holding = adapter_down_weight.shape[0]
    value_portion = adapter_up_weight.shape[2]
    replicas = lax.axis_size("rep")
    adapters = local_holding * replicas
    most_rows = 2 * row_count // adapters
    slot_of_row, row_of_slot = slot_layout(adapter_of_row[:, 0], adapters, most_rows)
    slotted = normed_token_rows.at[row_of_slot].get(mode="fill", fill_value=0)
    grouped = slotted.reshape(adapters, most_rows, feature_half)
    selected = grouped
    product = jnp.einsum(
        "akd,adr->akr",
        selected,
        lax.all_gather(adapter_down_weight, "rep", axis=0, tiled=True),
        preferred_element_type=jnp.float32,
    )
    partial_rank = product
    narrow_projection = lax.psum(partial_rank, "tp").astype(jnp.bfloat16)
    selected = narrow_projection
    product = jnp.einsum(
        "akr,are->ake",
        selected,
        lax.all_gather(adapter_up_weight, "rep", axis=0, tiled=True),
        preferred_element_type=jnp.float32,
    )
    delta_slots = product.astype(jnp.bfloat16).reshape(adapters * most_rows, value_portion)
    row_deltas = delta_slots[slot_of_row]
    value_rows = (
        base_value_rows.astype(jnp.float32) + adapter_scale * row_deltas.astype(jnp.float32)
    ).astype(jnp.bfloat16)
    return attend_block(queries, stacked_key_rows, value_rows, sequence_lengths[0])


def solution(mesh):
    placed = (
        P(("groups", "rep"), "tp"),
        P(("groups", "rep"), "tp"),
        P(("groups", "rep"), "tp"),
        P(("groups", "rep"), "tp"),
        P(("groups", "rep"), None),
        P(("groups", "rep"), None),
        P(("groups", "rep"), "tp", None),
        P(("groups", "rep"), None, "tp"),
    )
    return jax.shard_map(
        on_device, mesh=mesh, in_specs=placed, out_specs=P(("groups", "rep"), "tp"), check_vma=False
    )
```

profile of v0, /device:TPU:0, one launch (start us, length us, event | category | flops | bytes accessed | tf_op | source)
XLA Modules:
  0.0 130.7 jit_solution(10344815649379121976)
XLA Ops:
  6.5 0.7 all-gather.2.cloned.1.call-update
  7.3 1.0 reduce-window.20
  8.3 0.7 reduce
  9.0 0.9 reduce-window.18
  9.9 0.2 slice_reduce_fusion
  10.1 0.1 fusion.17
  10.2 0.7 fusion.21
  10.9 2.9 %scatter_custom_fusion = s32[768]{0:T(1024)S(1)} fusion(s32[384]{0:T(512)S(1)} %fusion.21, s32[384]{0:T(512)S(1)} %iota.26, s32[]{:T(128)} %constant.11.clone.1), kind=kCustom, calls=%fused_computation.39 | custom fusion | bytes 3076 | tf_op jit(solution)/shard_map/scatter | solution.py:23
  13.9 0.1 broadcast_in_dim.16
  14.0 1.1 reshape.115
  15.1 4.4 %copy.35 = bf16[48,8,32,128]{3,2,1,0:T(8,128)(2,1)} copy(bf16[48,8,32,128]{3,1,2,0:T(8,128)(2,1)} %bitcast.45) | data formatting | bytes 6291456
  19.5 5.7 %gather_fusion = bf16[768,4096]{1,0:T(8,128)(2,1)} fusion(bf16[384,4096]{1,0:T(8,128)(2,1)S(1)} %copy-done, s32[1024]{0:T(1024)S(1)} %pad_clamp_fusion.1), kind=kCustom, calls=%fused_computation | custom fusion | bytes 12585984 | tf_op jit(solution)/shard_map/gather | solution.py:67
  25.3 0.1 fusion.13
  25.4 35.1 %all_gather.7 = bf16[8,64,512]{2,1,0:T(8,128)(2,1)S(1)} all-gather(bf16[1,64,512]{2,1,0:T(8,128)(2,1)} %param.15), channel_id=1, replica_groups=mesh['groups'=2,'rep'=8,'tp'=2] {'rep'}, dimensions={0}, use_global_device_ids=true | all-gather | bytes 589824 | tf_op jit(solution)/shard_map/all_gather | solution.py:82
  60.5 11.2 %fusion.9 = f32[4,384,384,8]{2,1,3,0:T(8,128)} fusion(bf16[384,4,8,128]{3,2,1,0:T(8,128)(2,1)} %bitcast.43, bf16[384,4,128,1]{2,1,0,3:T(4,128)(2,1)S(1)} %bitcast.47), kind=kOutput, calls=%fused_computation.15 | convolution fusion | flops 1207959552 | bytes 22413312 | tf_op jit(solution)/shard_map/tjgd,sjd->jgts/dot_general | solution.py:38
  71.8 23.7 %fusion.25 = (f32[4,8,384]{2,1,0:T(8,128)}, f32[4,8,384,384]{2,3,1,0:T(8,128)}) fusion(f32[4,384,384,8]{2,1,3,0:T(8,128)} %fusion.9, pred[384,384]{0,1:T(8,128)(4,1)S(1)} %fusion.13), kind=kOutput, calls=%fused_computation.45 | output fusion | flops 28311936 | bytes 37945344 | tf_op jit(solution)/shard_map/sub | solution.py:43
  95.4 6.5 %fusion.6 = f32[8,96,64]{1,2,0:T(8,128)S(1)} fusion(bf16[8,4096,64]{1,2,0:T(8,128)(2,1)} %all-gather.2.cloned.1.call-done, bf16[8,96,4096]{2,1,0:T(8,128)(2,1)} %bitcast.44, pred[8,96]{1,0:T(8,128)(4,1)S(1)} %broadcast_in_dim.16), kind=kOutput, calls=%fused_computation.12 | convolution fusion | flops 405798912 | bytes 10683136 | tf_op jit(solution)/shard_map/akd,adr->akr/dot_general | solution.py:70
  101.9 4.4 %all-reduce.1 = bf16[8,96,64]{1,2,0:T(8,128)(2,1)S(1)} all-reduce(f32[8,96,64]{1,2,0:T(8,128)S(1)} %fusion.6), channel_id=1, replica_groups=mesh['groups'=2,'rep'=8,'tp'=2] {'tp'}, use_global_device_ids=true, to_apply=%region_4.5 | all-reduce | flops 49152 | bytes 294912 | tf_op jit(solution)/shard_map/psum | solution.py:77
  106.3 0.4 convolution_convert_fusion
  106.8 2.1 %gather_fusion.1 = bf16[384,512]{1,0:T(8,128)(2,1)S(1)} fusion(bf16[768,512]{1,0:T(8,128)(2,1)S(1)} %bitcast.42, s32[1024]{0:T(1024)S(1)} %pad_clamp_fusion), kind=kCustom, calls=%fused_computation.1 | custom fusion | bytes 787968 | tf_op jit(solution)/shard_map/gather | solution.py:86
  108.8 0.1 add_convert_fusion
  109.0 0.2 copy.32
  109.2 10.0 %fusion.12 = bf16[4,128,8,384]{3,1,2,0:T(8,128)(2,1)} fusion(bf16[384,4,128,1]{0,2,3,1:T(8,128)(2,1)S(1)} %bitcast.48, f32[4,8,384,384]{2,3,1,0:T(8,128)} %get-tuple-element.6, f32[4,8,384]{2,1,0:T(8,128)} %get-tuple-element.5), kind=kOutput, calls=%fused_computation.18 | convolution fusion | flops 1218969600 | bytes 22462464 | tf_op jit(solution)/shard_map/jgts,sjd->tjgd/dot_general | solution.py:45
  119.2 4.6 %copy.28 = bf16[384,4096]{1,0:T(8,128)(2,1)} copy(bf16[384,4096]{0,1:T(8,128)(2,1)} %bitcast.46) | data formatting | bytes 6291456 | tf_op jit(solution)/shard_map/reshape | solution.py:46
  (16 shorter events, 0.2 us)
Async XLA Ops:
  6.5 13.0 %copy-start = (bf16[384,4096]{1,0:T(8,128)(2,1)S(1)}, bf16[384,4096]{1,0:T(8,128)(2,1)}, u32[]{:S(2)}) copy-start(bf16[384,4096]{1,0:T(8,128)(2,1)} %param.8) | copy-start | bytes 9437188
  6.5 88.9 %all-gather.2.cloned.1.call-start = ((), (), s32[]{:S(2)}) async-start(), calls=%async_computation | async-start | bytes 4718592 | tf_op jit(solution)/shard_map/all_gather | solution.py:73
  95.4 13.4 %copy-start.2 = (bf16[384,512]{1,0:T(8,128)(2,1)S(1)}, bf16[384,512]{1,0:T(8,128)(2,1)}, u32[]{:S(2)}) copy-start(bf16[384,512]{1,0:T(8,128)(2,1)} %param.9) | copy-start | bytes 1179652
  109.2 14.7 %copy-start.1 = (bf16[384,4096]{1,0:T(8,128)(2,1)S(1)}, bf16[384,4096]{1,0:T(8,128)(2,1)}, u32[]{:S(2)}) copy-start(bf16[384,4096]{1,0:T(8,128)(2,1)} %param.8) | copy-start | bytes 9437188
Sparse Core Ops, SparseCore 0:
  9.5 79.7 all-gather.1
where the time goes:
time: 131 us
  blocking collectives  39.5 us (30%)
  matrix products  28.2 us (22%)
  other arithmetic  27.5 us (21%)
  local copies, waits for them, and re-layouts  21.3 us (16%)
  between operations  13.5 us (10%)
    all_gather x1, blocking collectives, on_device(): lax.all_gather(adapter_up_weight, 'rep', axis=0, tiled=True)  35.1 us
    sub x1, other arithmetic, attend_block(): weights = jnp.exp(scores - peak)  23.7 us
    dot_general x1, matrix products, attend_block(): jnp.einsum('tjgd,sjd->jgts', query_heads, key_heads, preferred_element_ty...  11.2 us
    dot_general x1, matrix products, attend_block(): jnp.einsum('jgts,sjd->tjgd', probs, value_heads, preferred_element_type=j...  10 us
    dot_general x1, matrix products, on_device(): jnp.einsum('akd,adr->akr', selected, lax.all_gather(adapter_down_weight,...  6.49 us
    gather x1, local copies, waits for them, and re-layouts, on_device(): slotted = normed_token_rows.at[row_of_slot].get(mode='fill', fill_value=0)  5.69 us
    reshape x1, local copies, waits for them, and re-layouts, attend_block(): mixed.astype(jnp.bfloat16).reshape(count, kv_heads * group * HEAD_SIZE)  4.63 us
    unnamed x7, local copies, waits for them, and re-layouts  4.42 us
  transfers between devices with their start and end apart: 1, of which 0 were waited for; matrix products, arithmetic and copies ran while one was open for 41% of the time, Pallas kernels for 0%

commit v1 on v0

v1 whole, which is shorter than its diff:
```python
import functools

import jax
import jax.numpy as jnp
import numpy as np
from jax import lax
from jax.experimental import pallas as pl
from jax.experimental.pallas import tpu as pltpu
from jax.sharding import PartitionSpec as P

HEADS = 64
KEY_VALUE_HEADS = 8
HEAD_SIZE = 128
GROUP = HEADS // KEY_VALUE_HEADS
LONGEST = 192
TILE = 64
REACH = -(-(LONGEST - 1) // TILE)
adapter_scale = 2.0

VMEM = pl.BlockSpec(memory_space=pltpu.VMEM)
SMEM = pl.BlockSpec(memory_space=pltpu.SMEM)
NT = (((1,), (1,)), ((), ()))


def ring_order(n):
    if n == 8:
        return list(range(0, n, 2)) + list(range(n - 1, 0, -2))
    return list(range(n))


def windows(rows):
    found = []
    for tile in range(rows // TILE):
        first = max(0, tile - REACH) * TILE
        width = (tile + 1) * TILE - first
        width = -(-width // 128) * 128
        found.append((tile * TILE, first, width))
    return found


def probs_kernel(lengths_ref, q_ref, k_ref, *p_refs):
    rows = k_ref.shape[0]
    ends = []
    total = jnp.int32(0)
    for i in range(lengths_ref.shape[1]):
        total = total + lengths_ref[0, i]
        ends.append(total)
    factor = float(np.log2(np.e) * HEAD_SIZE**-0.5)
    for p_ref, (start, first, width) in zip(p_refs, windows(rows)):
        t = lax.broadcasted_iota(jnp.int32, (TILE, width), 0) + start
        s = lax.broadcasted_iota(jnp.int32, (TILE, width), 1) + first
        allowed = s <= t
        for end in ends:
            allowed = allowed & ((t >= end) == (s >= end))
        bias = jnp.where(allowed, 0.0, -1e30)
        keys = k_ref[first : first + width, :]
        for head in range(GROUP):
            q = q_ref[start : start + TILE, head * HEAD_SIZE : (head + 1) * HEAD_SIZE]
            scores = lax.dot_general(q, keys, NT, preferred_element_type=jnp.float32) + bias
            peak = jnp.max(scores, axis=1, keepdims=True)
            weights = jnp.exp2((scores - peak) * factor)
            inverse = 1.0 / jnp.sum(weights, axis=1, keepdims=True)
            p_ref[head * TILE : (head + 1) * TILE, :] = (weights * inverse).astype(jnp.bfloat16)


def probs_of(lengths, queries, keys, kv_head):
    rows = keys.shape[0]
    wide = GROUP * HEAD_SIZE
    shapes = [(GROUP * TILE, width) for _, _, width in windows(rows)]
    elements = sum(a * b for a, b in shapes)
    return pl.pallas_call(
        probs_kernel,
        grid=(1,),
        out_shape=[jax.ShapeDtypeStruct(s, jnp.bfloat16) for s in shapes],
        in_specs=[
            SMEM,
            pl.BlockSpec((rows, wide), lambda i: (0, kv_head)),
            pl.BlockSpec((rows, HEAD_SIZE), lambda i: (0, kv_head)),
        ],
        out_specs=[pl.BlockSpec(s, lambda i: (0, 0)) for s in shapes],
        cost_estimate=pl.CostEstimate(
            flops=2 * elements * HEAD_SIZE,
            bytes_accessed=2 * (rows * wide + elements),
            transcendentals=elements,
        ),
        name="probs",
    )(lengths, queries, keys)


def lowrank_kernel(ranks, ids_ref, adapter_ref, x_ref, before_ref, *refs):
    w_refs, out_ref = refs[:-1], refs[-1]
    adapter = adapter_ref[...]
    x = x_ref[...]
    total = jnp.zeros(out_ref.shape, jnp.float32) if before_ref is None else before_ref[...]
    pieces = [w_ref[...] for w_ref in w_refs]
    stacked = jnp.concatenate(pieces, axis=0)
    product = lax.dot_general(x, stacked, NT, preferred_element_type=jnp.float32)
    width = out_ref.shape[1]
    for i in range(ranks):
        total = total + jnp.where(adapter == ids_ref[i], product[:, i * width : (i + 1) * width], 0.0)
    out_ref[...] = total


def lowrank_of(ids, adapter_of_row, x, before, pieces):
    rows, features = x.shape
    rank = before.shape[1]
    depth = sum(p.shape[0] for p in pieces)
    return pl.pallas_call(
        functools.partial(lowrank_kernel, depth // rank),
        out_shape=jax.ShapeDtypeStruct((rows, rank), jnp.float32),
        in_specs=[SMEM, VMEM, VMEM, VMEM] + [VMEM] * len(pieces),
        out_specs=VMEM,
        cost_estimate=pl.CostEstimate(
            flops=2 * rows * features * depth,
            bytes_accessed=2 * features * (rows + depth),
            transcendentals=0,
        ),
        name="lowrank",
    )(ids, adapter_of_row, x, before, *pieces)


def attend_kernel(kv_heads, n, ids_ref, adapter_ref, mine_ref, theirs_ref, base_ref, *refs):
    up_refs = refs[:n]
    tiles = windows(base_ref.shape[0])
    p_refs = refs[n : n + kv_heads * len(tiles)]
    out_ref, block, sems = refs[n + kv_heads * len(tiles) :]
    rank = mine_ref.shape[1]
    adapter = adapter_ref[...]
    lowrank = (mine_ref[...] + theirs_ref[...]).astype(jnp.bfloat16)
    spread = jnp.concatenate(
        [jnp.where(adapter == ids_ref[i], lowrank, jnp.zeros_like(lowrank)) for i in range(n)], axis=1
    )
    copies = []
    wide = GROUP * HEAD_SIZE
    for kv in range(kv_heads):
        columns = slice(kv * HEAD_SIZE, (kv + 1) * HEAD_SIZE)
        up = jnp.concatenate([up_ref[:, columns] for up_ref in up_refs], axis=0)
        delta = jnp.dot(spread, up, preferred_element_type=jnp.float32).astype(jnp.bfloat16)
        values = (
            base_ref[:, columns].astype(jnp.float32) + adapter_scale * delta.astype(jnp.float32)
        ).astype(jnp.bfloat16)
        for i, (start, first, width) in enumerate(tiles):
            mixed = jnp.dot(
                p_refs[kv * len(tiles) + i][...],
                values[first : first + width, :],
                preferred_element_type=jnp.float32,
            ).astype(jnp.bfloat16)
            for head in range(GROUP):
                at = kv * wide + head * HEAD_SIZE
                block[start : start + TILE, at : at + HEAD_SIZE] = mixed[head * TILE : (head + 1) * TILE, :]
        copy = pltpu.make_async_copy(
            block.at[:, kv * wide : (kv + 1) * wide],
            out_ref.at[:, kv * wide : (kv + 1) * wide],
            sems.at[kv],
        )
        copy.start()
        copies.append(copy)
    for copy in copies:
        copy.wait()


def attend(ids, adapter_of_row, mine, theirs, base, ups, probs):
    rows, value_portion = base.shape
    kv_heads = value_portion // HEAD_SIZE
    wide = kv_heads * GROUP * HEAD_SIZE
    flat = [p for per_head in probs for p in per_head]
    return pl.pallas_call(
        functools.partial(attend_kernel, kv_heads, len(ups)),
        out_shape=jax.ShapeDtypeStruct((rows, wide), jnp.bfloat16),
        in_specs=[SMEM] + [VMEM] * (4 + len(ups) + len(flat)),
        out_specs=pl.BlockSpec(memory_space=pl.ANY),
        scratch_shapes=[pltpu.VMEM((rows, wide), jnp.bfloat16), pltpu.SemaphoreType.DMA((kv_heads,))],
        compiler_params=pltpu.CompilerParams(vmem_limit_bytes=40 * 2**20),
        name="attend",
    )(ids, adapter_of_row, mine, theirs, base, *ups, *flat)


def on_device(
    normed_token_rows,
    base_value_rows,
    queries,
    stacked_key_rows,
    adapter_of_row,
    sequence_lengths,
    adapter_down_weight,
    adapter_up_weight,
):
    n = lax.axis_size("rep")
    order = ring_order(n)
    ahead = [(order[i], order[(i + 1) % n]) for i in range(n)]
    back = [(b, a) for a, b in ahead]
    far = n // 2
    distances = [0] + [d for step in range(1, far) for d in (step, -step)] + [far]
    table = np.zeros((n, n), np.int32)
    for place, replica in enumerate(order):
        table[replica] = [order[(place - d) % n] for d in distances]
    ids = lax.dynamic_index_in_dim(jnp.asarray(table), lax.axis_index("rep"), 0, keepdims=False)

    down = jnp.swapaxes(adapter_down_weight[0], 0, 1)
    rank = down.shape[0]
    half = rank // 2
    up = adapter_up_weight[0]

    def pass_round(piece, steps_ahead, steps_back):
        held = {0: piece}
        moving_ahead = moving_back = piece
        for step in range(1, far + 1):
            if step <= steps_ahead:
                moving_ahead = lax.ppermute(moving_ahead, "rep", ahead)
                held[step] = moving_ahead
            if step <= steps_back:
                moving_back = lax.ppermute(moving_back, "rep", back)
                held[-step if step < far else far] = moving_back
        return held

    low = pass_round(down[:half], far, far - 1)
    high = pass_round(down[half:], far - 1, far)
    ups = pass_round(up, far, far - 1)

    kv_heads = stacked_key_rows.shape[1] // HEAD_SIZE
    probs = [probs_of(sequence_lengths, queries, stacked_key_rows, kv) for kv in range(kv_heads)]

    partial = jnp.zeros((normed_token_rows.shape[0], rank), jnp.float32)
    early = n - 3
    for lo, hi in [(a, min(a + 5, early)) for a in range(0, early, 5)] + [(early, n)]:
        pieces = [piece for d in distances[lo:hi] for piece in (low[d], high[d])]
        partial = lowrank_of(ids[lo:hi], adapter_of_row, normed_token_rows, partial, pieces)
    other = lax.ppermute(partial, "tp", [(0, 1), (1, 0)])
    return attend(ids, adapter_of_row, partial, other, base_value_rows, [ups[d] for d in distances], probs)


def solution(mesh):
    placed = (
        P(("groups", "rep"), "tp"),
        P(("groups", "rep"), "tp"),
        P(("groups", "rep"), "tp"),
        P(("groups", "rep"), "tp"),
        P(("groups", "rep"), None),
        P(("groups", "rep"), None),
        P(("groups", "rep"), "tp", None),
        P(("groups", "rep"), None, "tp"),
    )
    return jax.shard_map(
        on_device, mesh=mesh, in_specs=placed, out_specs=P(("groups", "rep"), "tp"), check_vma=False
    )
```

time: 131 us -> 92 us (0.70)
  blocking collectives: 39.5 us -> 0 us
  matrix products: 28.2 us -> 0 us
  Pallas kernels: 0 us -> 28.1 us
  other arithmetic: 27.5 us -> 0 us
  starting transfers between devices: 0.01 us -> 25.5 us
  waiting for transfers between devices: 0.71 us -> 16.4 us
  between operations: 13.5 us -> 0.51 us
    all_gather x1 -> x0, blocking collectives: 35.1 us -> none  [on_device(): lax.all_gather(adapter_up_weight, 'rep', axis=0, tiled=True)]
    dot_general x4 -> x0, matrix products: 28.2 us -> none  [the longest x1 11.2 us: attend_block(): jnp.einsum('tjgd,sjd->jgts', query_heads, key_heads, preferred_element_ty...]
    pallas_call x0 -> x7, Pallas kernels: none -> 28.1 us  [the longest x4 13.7 us: probs_of(): pl.pallas_call(probs_kernel, grid=(1,), out_shape=[jax.ShapeDtypeStruct(s...]
    ppermute x0 -> x22, starting transfers between devices: none -> 25.5 us  [the longest x10 18.1 us: pass_round(): moving_back = lax.ppermute(moving_back, 'rep', back)]
    sub x1 -> x0, other arithmetic: 23.7 us -> none  [attend_block(): weights = jnp.exp(scores - peak)]
    ppermute x0 -> x22, waiting for transfers between devices: none -> 16.4 us  [the longest x10 9.55 us: pass_round(): moving_back = lax.ppermute(moving_back, 'rep', back)]
    unnamed x7 -> x93, local copies, waits for them, and re-layouts: 4.42 us -> 17 us
    gather x2 -> x0, local copies, waits for them, and re-layouts: 7.76 us -> none  [the longest x1 5.69 us: on_device(): slotted = normed_token_rows.at[row_of_slot].get(mode='fill', fill_value=0)]
  transfers between devices with their start and end apart: 1 -> 22, of which waited for: 0 -> 6; matrix products, arithmetic and copies ran while one was open for 41% -> 4% of each run, Pallas kernels for 0% -> 25%
where the time goes in v1:
time: 92 us; the launch traced here: 91.2 us
  Pallas kernels  28.1 us (31%)
  starting transfers between devices  25.5 us (28%)
  local copies, waits for them, and re-layouts  20.6 us (22%)
  waiting for transfers between devices  16.4 us (18%)
    ppermute x10, starting transfers between devices, pass_round(): moving_back = lax.ppermute(moving_back, 'rep', back)  18.1 us
    unnamed x93, local copies, waits for them, and re-layouts  17 us
    pallas_call x4, Pallas kernels, probs_of(): pl.pallas_call(probs_kernel, grid=(1,), out_shape=[jax.ShapeDtypeStruct(s...  13.7 us
    ppermute x10, waiting for transfers between devices, pass_round(): moving_back = lax.ppermute(moving_back, 'rep', back)  9.55 us
    pallas_call x2, Pallas kernels, lowrank_of(): pl.pallas_call(functools.partial(lowrank_kernel, depth // rank), out_shap...  9.48 us
    ppermute x11, starting transfers between devices, pass_round(): moving_ahead = lax.ppermute(moving_ahead, 'rep', ahead)  7.39 us
    ppermute x11, waiting for transfers between devices, pass_round(): moving_ahead = lax.ppermute(moving_ahead, 'rep', ahead)  6.89 us
    pallas_call x1, Pallas kernels, attend(): pl.pallas_call(functools.partial(attend_kernel, kv_heads, len(ups)), out_...  4.96 us
  transfers between devices with their start and end apart: 22, of which 6 were waited for; matrix products, arithmetic and copies ran while one was open for 4% of the time, Pallas kernels for 25%

profile of v1, /device:TPU:0, one launch (start us, length us, event | category | flops | bytes accessed | tf_op | source)
XLA Modules:
  0.0 91.2 jit_solution(468712684834385693)
XLA Ops:
  1.1 3.0 %collective-permute-start.3 = (bf16[32,4096]{1,0:T(8,128)(2,1)S(1)}, bf16[32,4096]{1,0:T(8,128)(2,1)S(1)}, u32[]{:S(2)}, u32[]{:S(2)}) collective-permute-start(bf16[32,4096]{1,0:T(8,128)(2,1)S(1)} %get-tuple-element.53.refs_1_), channel_id=1, source_target_pairs={{4,0},{8,4},{12,8},{14,12},{10,14},{6,10},{2,6},{0,2},{5,1},{9,5},... | collective-permute-start | bytes 786440 | tf_op jit(solution)/shard_map/ppermute | solution.py:212
  4.2 2.0 %collective-permute-start.1 = (bf16[32,4096]{1,0:T(8,128)(2,1)S(1)}, bf16[32,4096]{1,0:T(8,128)(2,1)S(1)}, u32[]{:S(2)}, u32[]{:S(2)}) collective-permute-start(bf16[32,4096]{1,0:T(8,128)(2,1)S(1)} %get-tuple-element.53.refs_1_), channel_id=1, source_target_pairs={{0,4},{4,8},{8,12},{12,14},{14,10},{10,6},{6,2},{2,0},{1,5},{5,9},... | collective-permute-start | bytes 786440 | tf_op jit(solution)/shard_map/ppermute | solution.py:209
  6.3 5.0 %collective-permute-done.3.refs_5_ = bf16[32,4096]{1,0:T(8,128)(2,1)S(1)} collective-permute-done((bf16[32,4096]{1,0:T(8,128)(2,1)S(1)}, bf16[32,4096]{1,0:T(8,128)(2,1)S(1)}, u32[]{:S(2)}, u32[]{:S(2)}) %collective-permute-start.3) | collective-permute-done | bytes 262176 | tf_op jit(solution)/shard_map/ppermute | solution.py:212
  11.3 2.0 %collective-permute-start.7 = (bf16[32,4096]{1,0:T(8,128)(2,1)S(1)}, bf16[32,4096]{1,0:T(8,128)(2,1)S(1)}, u32[]{:S(2)}, u32[]{:S(2)}) collective-permute-start(bf16[32,4096]{1,0:T(8,128)(2,1)S(1)} %collective-permute-done.3.refs_5_), channel_id=1, source_target_pairs={{4,0},{8,4},{12,8},{14,12},{10,14},{6,10},{2,6},{0,2},{5,1},{9,5},... | collective-permute-start | bytes 786440 | tf_op jit(solution)/shard_map/ppermute | solution.py:212
  13.4 1.9 %collective-permute-start.16 = (bf16[64,512]{1,0:T(8,128)(2,1)}, bf16[64,512]{1,0:T(8,128)(2,1)S(1)}, u32[]{:S(2)}, u32[]{:S(2)}) collective-permute-start(bf16[64,512]{1,0:T(8,128)(2,1)} %bitcast.10), channel_id=1, source_target_pairs={{4,0},{8,4},{12,8},{14,12},{10,14},{6,10},{2,6},{0,2},{5,1},{9,5},... | collective-permute-start | bytes 196616 | tf_op jit(solution)/shard_map/ppermute | solution.py:212
  15.4 3.6 %collective-permute-done.1.refs_3_ = bf16[32,4096]{1,0:T(8,128)(2,1)S(1)} collective-permute-done((bf16[32,4096]{1,0:T(8,128)(2,1)S(1)}, bf16[32,4096]{1,0:T(8,128)(2,1)S(1)}, u32[]{:S(2)}, u32[]{:S(2)}) %collective-permute-start.1) | collective-permute-done | bytes 262176 | tf_op jit(solution)/shard_map/ppermute | solution.py:209
  19.0 1.9 %collective-permute-start.6 = (bf16[32,4096]{1,0:T(8,128)(2,1)S(1)}, bf16[32,4096]{1,0:T(8,128)(2,1)S(1)}, u32[]{:S(2)}, u32[]{:S(2)}) collective-permute-start(bf16[32,4096]{1,0:T(8,128)(2,1)S(1)} %collective-permute-done.2.refs_4_), channel_id=1, source_target_pairs={{4,0},{8,4},{12,8},{14,12},{10,14},{6,10},{2,6},{0,2},{5,1},{9,5},... | collective-permute-start | bytes 786440 | tf_op jit(solution)/shard_map/ppermute | solution.py:212
  21.0 1.5 %collective-permute-done.7.refs_9_ = bf16[32,4096]{1,0:T(8,128)(2,1)S(1)} collective-permute-done((bf16[32,4096]{1,0:T(8,128)(2,1)S(1)}, bf16[32,4096]{1,0:T(8,128)(2,1)S(1)}, u32[]{:S(2)}, u32[]{:S(2)}) %collective-permute-start.7) | collective-permute-done | bytes 262176 | tf_op jit(solution)/shard_map/ppermute | solution.py:212
  22.5 2.0 %collective-permute-start.11 = (bf16[32,4096]{1,0:T(8,128)(2,1)S(1)}, bf16[32,4096]{1,0:T(8,128)(2,1)S(1)}, u32[]{:S(2)}, u32[]{:S(2)}) collective-permute-start(bf16[32,4096]{1,0:T(8,128)(2,1)S(1)} %collective-permute-done.7.refs_9_), channel_id=1, source_target_pairs={{4,0},{8,4},{12,8},{14,12},{10,14},{6,10},{2,6},{0,2},{5,1},{9,5},... | collective-permute-start | bytes 786440 | tf_op jit(solution)/shard_map/ppermute | solution.py:212
  26.0 2.0 %collective-permute-start.15 = (bf16[64,512]{1,0:T(8,128)(2,1)}, bf16[64,512]{1,0:T(8,128)(2,1)S(1)}, u32[]{:S(2)}, u32[]{:S(2)}) collective-permute-start(bf16[64,512]{1,0:T(8,128)(2,1)} %bitcast.11), channel_id=1, source_target_pairs={{0,4},{4,8},{8,12},{12,14},{14,10},{10,6},{6,2},{2,0},{1,5},{5,9},... | collective-permute-start | bytes 196616 | tf_op jit(solution)/shard_map/ppermute | solution.py:209
  27.9 2.2 %collective-permute-done.5.refs_7_ = bf16[32,4096]{1,0:T(8,128)(2,1)S(1)} collective-permute-done((bf16[32,4096]{1,0:T(8,128)(2,1)S(1)}, bf16[32,4096]{1,0:T(8,128)(2,1)S(1)}, u32[]{:S(2)}, u32[]{:S(2)}) %collective-permute-start.5) | collective-permute-done | bytes 262176 | tf_op jit(solution)/shard_map/ppermute | solution.py:209
  30.3 1.9 %collective-permute-start.10 = (bf16[32,4096]{1,0:T(8,128)(2,1)S(1)}, bf16[32,4096]{1,0:T(8,128)(2,1)}, u32[]{:S(2)}, u32[]{:S(2)}) collective-permute-start(bf16[32,4096]{1,0:T(8,128)(2,1)S(1)} %collective-permute-done.6.refs_8_), channel_id=1, source_target_pairs={{4,0},{8,4},{12,8},{14,12},{10,14},{6,10},{2,6},{0,2},{5,1},{9,5},... | collective-permute-start | bytes 786440 | tf_op jit(solution)/shard_map/ppermute | solution.py:212
  32.2 2.9 %collective-permute-done.11.refs_3_ = bf16[32,4096]{1,0:T(8,128)(2,1)S(1)} collective-permute-done((bf16[32,4096]{1,0:T(8,128)(2,1)S(1)}, bf16[32,4096]{1,0:T(8,128)(2,1)S(1)}, u32[]{:S(2)}, u32[]{:S(2)}) %collective-permute-start.11) | collective-permute-done | bytes 262176 | tf_op jit(solution)/shard_map/ppermute | solution.py:212
  35.2 2.0 %collective-permute-start.13 = (bf16[32,4096]{1,0:T(8,128)(2,1)S(1)}, bf16[32,4096]{1,0:T(8,128)(2,1)}, u32[]{:S(2)}, u32[]{:S(2)}) collective-permute-start(bf16[32,4096]{1,0:T(8,128)(2,1)S(1)} %collective-permute-done.11.refs_3_), channel_id=1, source_target_pairs={{4,0},{8,4},{12,8},{14,12},{10,14},{6,10},{2,6},{0,2},{5,1},{9,5},... | collective-permute-start | bytes 786440 | tf_op jit(solution)/shard_map/ppermute | solution.py:212
  39.4 2.0 %collective-permute-start.17 = (bf16[64,512]{1,0:T(8,128)(2,1)S(1)}, bf16[64,512]{1,0:T(8,128)(2,1)S(1)}, u32[]{:S(2)}, u32[]{:S(2)}) collective-permute-start(bf16[64,512]{1,0:T(8,128)(2,1)S(1)} %collective-permute-done.15.refs_1_), channel_id=1, source_target_pairs={{0,4},{4,8},{8,12},{12,14},{14,10},{10,6},{6,2},{2,0},{1,5},{5,9},... | collective-permute-start | bytes 196616 | tf_op jit(solution)/shard_map/ppermute | solution.py:209
  42.1 5.3 %lowrank.2.before_ref = f32[384,64]{1,0:T(8,128)} custom-call(s32[5]{0:T(128)} %slice_bitcast_fusion.ids_ref, s32[384,1]{1,0:T(8,128)} %copy.12.adapter_ref, bf16[384,4096]{1,0:T(8,128)(2,1)} %x_ref.3, f32[384,64]{1,0:T(8,128)} %broadcast_in_dim.3.before_ref, bf16[32,4096]{1,0:T(8,128)(2,1)} %copy-done.35, bf16[32,4096]{1,0:T(8,128)(2,1)} %copy-done.34, ...), custom_call_target="tpu_custom_call" | custom-call | flops 1006632960 | bytes 5767168 | tf_op jit(solution)/shard_map/lowrank/pallas_call | solution.py:108
  48.4 1.6 %collective-permute-start.18 = (bf16[64,512]{1,0:T(8,128)(2,1)S(1)}, bf16[64,512]{1,0:T(8,128)(2,1)}, u32[]{:S(2)}, u32[]{:S(2)}) collective-permute-start(bf16[64,512]{1,0:T(8,128)(2,1)S(1)} %collective-permute-done.16.refs_2_), channel_id=1, source_target_pairs={{4,0},{8,4},{12,8},{14,12},{10,14},{6,10},{2,6},{0,2},{5,1},{9,5},... | collective-permute-start | bytes 196616 | tf_op jit(solution)/shard_map/ppermute | solution.py:212
  50.4 4.2 %lowrank.3.mine_ref = f32[384,64]{1,0:T(8,128)} custom-call(s32[3]{0:T(128)} %slice_bitcast_fusion.1.ids_ref, s32[384,1]{1,0:T(8,128)} %copy.12.adapter_ref, bf16[384,4096]{1,0:T(8,128)(2,1)} %x_ref.3, f32[384,64]{1,0:T(8,128)} %lowrank.2.before_ref, bf16[32,4096]{1,0:T(8,128)(2,1)} %copy-done.45, bf16[32,4096]{1,0:T(8,128)(2,1)} %collective-permute-done.9.refs_1_, ...), custom_call_target="tpu_custom_call" | custom-call | flops 603979776 | bytes 4718592 | tf_op jit(solution)/shard_map/lowrank/pallas_call | solution.py:108
  54.6 1.6 %collective-permute-start.20 = (bf16[64,512]{1,0:T(8,128)(2,1)}, bf16[64,512]{1,0:T(8,128)(2,1)}, u32[]{:S(2)}, u32[]{:S(2)}) collective-permute-start(bf16[64,512]{1,0:T(8,128)(2,1)} %collective-permute-done.18.refs_4_), channel_id=1, source_target_pairs={{4,0},{8,4},{12,8},{14,12},{10,14},{6,10},{2,6},{0,2},{5,1},{9,5},... | collective-permute-start | bytes 196616 | tf_op jit(solution)/shard_map/ppermute | solution.py:212
  56.7 3.4 %probs.5 = (bf16[512,128]{1,0:T(8,128)(2,1)}, bf16[512,128]{1,0:T(8,128)(2,1)}, bf16[512,256]{1,0:T(8,128)(2,1)}, bf16[512,256]{1,0:T(8,128)(2,1)}, bf16[512,256]{1,0:T(8,128)(2,1)}, /*index=5*/bf16[512,256]{1,0:T(8,128)(2,1)}) custom-call(s32[1,4]{1,0:T(1,128)} %lengths_ref.7, bf16[384,4096]{1,0:T(8,128)(2,1)} %q_ref.7, bf16[384,512]{1,0:T(8,128)(2,1)} %k_ref.7), custom_call_target="tpu_custom_call" | custom-call | flops 167772160 | bytes 2097152 | tf_op jit(solution)/shard_map/probs/pallas_call | solution.py:71
  60.1 3.4 %probs.4 = (bf16[512,128]{1,0:T(8,128)(2,1)}, bf16[512,128]{1,0:T(8,128)(2,1)}, bf16[512,256]{1,0:T(8,128)(2,1)}, bf16[512,256]{1,0:T(8,128)(2,1)}, bf16[512,256]{1,0:T(8,128)(2,1)}, /*index=5*/bf16[512,256]{1,0:T(8,128)(2,1)}) custom-call(s32[1,4]{1,0:T(1,128)} %lengths_ref.7, bf16[384,4096]{1,0:T(8,128)(2,1)} %q_ref.7, bf16[384,512]{1,0:T(8,128)(2,1)} %k_ref.7), custom_call_target="tpu_custom_call" | custom-call | flops 167772160 | bytes 2097152 | tf_op jit(solution)/shard_map/probs/pallas_call | solution.py:71
  63.6 3.5 %probs.7 = (bf16[512,128]{1,0:T(8,128)(2,1)}, bf16[512,128]{1,0:T(8,128)(2,1)}, bf16[512,256]{1,0:T(8,128)(2,1)}, bf16[512,256]{1,0:T(8,128)(2,1)}, bf16[512,256]{1,0:T(8,128)(2,1)}, /*index=5*/bf16[512,256]{1,0:T(8,128)(2,1)}) custom-call(s32[1,4]{1,0:T(1,128)} %lengths_ref.7, bf16[384,4096]{1,0:T(8,128)(2,1)} %q_ref.7, bf16[384,512]{1,0:T(8,128)(2,1)} %k_ref.7), custom_call_target="tpu_custom_call" | custom-call | flops 167772160 | bytes 2097152 | tf_op jit(solution)/shard_map/probs/pallas_call | solution.py:71
  67.1 3.4 %probs.6 = (bf16[512,128]{1,0:T(8,128)(2,1)}, bf16[512,128]{1,0:T(8,128)(2,1)}, bf16[512,256]{1,0:T(8,128)(2,1)}, bf16[512,256]{1,0:T(8,128)(2,1)}, bf16[512,256]{1,0:T(8,128)(2,1)}, /*index=5*/bf16[512,256]{1,0:T(8,128)(2,1)}) custom-call(s32[1,4]{1,0:T(1,128)} %lengths_ref.7, bf16[384,4096]{1,0:T(8,128)(2,1)} %q_ref.7, bf16[384,512]{1,0:T(8,128)(2,1)} %k_ref.7), custom_call_target="tpu_custom_call" | custom-call | flops 167772160 | bytes 2097152 | tf_op jit(solution)/shard_map/probs/pallas_call | solution.py:71
  86.1 5.0 %attend.1 = bf16[384,4096]{1,0:T(8,128)(2,1)} custom-call(s32[8]{0:T(128)S(1)} %get-tuple-element.56.ids_ref, s32[384,1]{1,0:T(8,128)S(1)} %copy-done, f32[384,64]{1,0:T(8,128)S(1)} %copy-done.1, f32[384,64]{1,0:T(8,128)} %collective-permute-done.14.theirs_ref, bf16[384,512]{1,0:T(8,128)(2,1)S(1)} %copy-done.2, bf16[64,512]{1,0:T(8,128)(2,1)S(1)} %bitcast.12, ...), custom_call_target="tpu_custom_call" | custom-call | tf_op jit(solution)/shard_map/attend/pallas_call | solution.py:167
  (125 shorter events, 23.2 us)
Async XLA Ops:
  1.1 41.0 %copy-start.34 = (bf16[32,4096]{1,0:T(8,128)(2,1)}, bf16[32,4096]{1,0:T(8,128)(2,1)S(1)}, u32[]{:S(2)}) copy-start(bf16[32,4096]{1,0:T(8,128)(2,1)S(1)} %get-tuple-element.53.refs_1_) | copy-start | bytes 786436
  1.1 40.9 %copy-start.35 = (bf16[32,4096]{1,0:T(8,128)(2,1)}, bf16[32,4096]{1,0:T(8,128)(2,1)S(1)}, u32[]{:S(2)}) copy-start(bf16[32,4096]{1,0:T(8,128)(2,1)S(1)} %get-tuple-element.54.refs_0_) | copy-start | bytes 786436
  1.1 10.2 %collective-permute-start.3 = (bf16[32,4096]{1,0:T(8,128)(2,1)S(1)}, bf16[32,4096]{1,0:T(8,128)(2,1)S(1)}, u32[]{:S(2)}, u32[]{:S(2)}) collective-permute-start(bf16[32,4096]{1,0:T(8,128)(2,1)S(1)} %get-tuple-element.53.refs_1_), channel_id=1, source_target_pairs={{4,0},{8,4},{12,8},{14,12},{10,14},{6,10},{2,6},{0,2},{5,1},{9,5},... | collective-permute-start | bytes 786440 | tf_op jit(solution)/shard_map/ppermute | solution.py:212
  4.1 9.2 %collective-permute-start = (bf16[32,4096]{1,0:T(8,128)(2,1)S(1)}, bf16[32,4096]{1,0:T(8,128)(2,1)S(1)}, u32[]{:S(2)}, u32[]{:S(2)}) collective-permute-start(bf16[32,4096]{1,0:T(8,128)(2,1)S(1)} %get-tuple-element.54.refs_0_), channel_id=1, source_target_pairs={{0,4},{4,8},{8,12},{12,14},{14,10},{10,6},{6,2},{2,0},{1,5},{5,9},... | collective-permute-start | bytes 786440 | tf_op jit(solution)/shard_map/ppermute | solution.py:209
  4.2 14.7 %collective-permute-start.1 = (bf16[32,4096]{1,0:T(8,128)(2,1)S(1)}, bf16[32,4096]{1,0:T(8,128)(2,1)S(1)}, u32[]{:S(2)}, u32[]{:S(2)}) collective-permute-start(bf16[32,4096]{1,0:T(8,128)(2,1)S(1)} %get-tuple-element.53.refs_1_), channel_id=1, source_target_pairs={{0,4},{4,8},{8,12},{12,14},{14,10},{10,6},{6,2},{2,0},{1,5},{5,9},... | collective-permute-start | bytes 786440 | tf_op jit(solution)/shard_map/ppermute | solution.py:209
  6.2 12.9 %collective-permute-start.2 = (bf16[32,4096]{1,0:T(8,128)(2,1)S(1)}, bf16[32,4096]{1,0:T(8,128)(2,1)S(1)}, u32[]{:S(2)}, u32[]{:S(2)}) collective-permute-start(bf16[32,4096]{1,0:T(8,128)(2,1)S(1)} %get-tuple-element.54.refs_0_), channel_id=1, source_target_pairs={{4,0},{8,4},{12,8},{14,12},{10,14},{6,10},{2,6},{0,2},{5,1},{9,5},... | collective-permute-start | bytes 786440 | tf_op jit(solution)/shard_map/ppermute | solution.py:212
  11.3 11.2 %collective-permute-start.7 = (bf16[32,4096]{1,0:T(8,128)(2,1)S(1)}, bf16[32,4096]{1,0:T(8,128)(2,1)S(1)}, u32[]{:S(2)}, u32[]{:S(2)}) collective-permute-start(bf16[32,4096]{1,0:T(8,128)(2,1)S(1)} %collective-permute-done.3.refs_5_), channel_id=1, source_target_pairs={{4,0},{8,4},{12,8},{14,12},{10,14},{6,10},{2,6},{0,2},{5,1},{9,5},... | collective-permute-start | bytes 786440 | tf_op jit(solution)/shard_map/ppermute | solution.py:212
  13.3 11.2 %collective-permute-start.4 = (bf16[32,4096]{1,0:T(8,128)(2,1)S(1)}, bf16[32,4096]{1,0:T(8,128)(2,1)S(1)}, u32[]{:S(2)}, u32[]{:S(2)}) collective-permute-start(bf16[32,4096]{1,0:T(8,128)(2,1)S(1)} %collective-permute-done.refs_2_), channel_id=1, source_target_pairs={{0,4},{4,8},{8,12},{12,14},{14,10},{10,6},{6,2},{2,0},{1,5},{5,9},... | collective-permute-start | bytes 786440 | tf_op jit(solution)/shard_map/ppermute | solution.py:209
  13.4 12.5 %collective-permute-start.16 = (bf16[64,512]{1,0:T(8,128)(2,1)}, bf16[64,512]{1,0:T(8,128)(2,1)S(1)}, u32[]{:S(2)}, u32[]{:S(2)}) collective-permute-start(bf16[64,512]{1,0:T(8,128)(2,1)} %bitcast.10), channel_id=1, source_target_pairs={{4,0},{8,4},{12,8},{14,12},{10,14},{6,10},{2,6},{0,2},{5,1},{9,5},... | collective-permute-start | bytes 196616 | tf_op jit(solution)/shard_map/ppermute | solution.py:212
  19.0 11.2 %collective-permute-start.5 = (bf16[32,4096]{1,0:T(8,128)(2,1)S(1)}, bf16[32,4096]{1,0:T(8,128)(2,1)S(1)}, u32[]{:S(2)}, u32[]{:S(2)}) collective-permute-start(bf16[32,4096]{1,0:T(8,128)(2,1)S(1)} %collective-permute-done.1.refs_3_), channel_id=1, source_target_pairs={{0,4},{4,8},{8,12},{12,14},{14,10},{10,6},{6,2},{2,0},{1,5},{5,9},... | collective-permute-start | bytes 786440 | tf_op jit(solution)/shard_map/ppermute | solution.py:209
  19.0 11.2 %collective-permute-start.6 = (bf16[32,4096]{1,0:T(8,128)(2,1)S(1)}, bf16[32,4096]{1,0:T(8,128)(2,1)S(1)}, u32[]{:S(2)}, u32[]{:S(2)}) collective-permute-start(bf16[32,4096]{1,0:T(8,128)(2,1)S(1)} %collective-permute-done.2.refs_4_), channel_id=1, source_target_pairs={{4,0},{8,4},{12,8},{14,12},{10,14},{6,10},{2,6},{0,2},{5,1},{9,5},... | collective-permute-start | bytes 786440 | tf_op jit(solution)/shard_map/ppermute | solution.py:212
  22.5 12.6 %collective-permute-start.11 = (bf16[32,4096]{1,0:T(8,128)(2,1)S(1)}, bf16[32,4096]{1,0:T(8,128)(2,1)S(1)}, u32[]{:S(2)}, u32[]{:S(2)}) collective-permute-start(bf16[32,4096]{1,0:T(8,128)(2,1)S(1)} %collective-permute-done.7.refs_9_), channel_id=1, source_target_pairs={{4,0},{8,4},{12,8},{14,12},{10,14},{6,10},{2,6},{0,2},{5,1},{9,5},... | collective-permute-start | bytes 786440 | tf_op jit(solution)/shard_map/ppermute | solution.py:212
  24.6 12.6 %collective-permute-start.8 = (bf16[32,4096]{1,0:T(8,128)(2,1)S(1)}, bf16[32,4096]{1,0:T(8,128)(2,1)S(1)}, u32[]{:S(2)}, u32[]{:S(2)}) collective-permute-start(bf16[32,4096]{1,0:T(8,128)(2,1)S(1)} %collective-permute-done.4.refs_6_), channel_id=1, source_target_pairs={{0,4},{4,8},{8,12},{12,14},{14,10},{10,6},{6,2},{2,0},{1,5},{5,9},... | collective-permute-start | bytes 786440 | tf_op jit(solution)/shard_map/ppermute | solution.py:209
  26.0 13.4 %collective-permute-start.15 = (bf16[64,512]{1,0:T(8,128)(2,1)}, bf16[64,512]{1,0:T(8,128)(2,1)S(1)}, u32[]{:S(2)}, u32[]{:S(2)}) collective-permute-start(bf16[64,512]{1,0:T(8,128)(2,1)} %bitcast.11), channel_id=1, source_target_pairs={{0,4},{4,8},{8,12},{12,14},{14,10},{10,6},{6,2},{2,0},{1,5},{5,9},... | collective-permute-start | bytes 196616 | tf_op jit(solution)/shard_map/ppermute | solution.py:209
  30.2 19.8 %collective-permute-start.9 = (bf16[32,4096]{1,0:T(8,128)(2,1)S(1)}, bf16[32,4096]{1,0:T(8,128)(2,1)}, u32[]{:S(2)}, u32[]{:S(2)}) collective-permute-start(bf16[32,4096]{1,0:T(8,128)(2,1)S(1)} %collective-permute-done.5.refs_7_), channel_id=1, source_target_pairs={{0,4},{4,8},{8,12},{12,14},{14,10},{10,6},{6,2},{2,0},{1,5},{5,9},... | collective-permute-start | bytes 786440 | tf_op jit(solution)/shard_map/ppermute | solution.py:209
  30.3 20.1 %collective-permute-start.10 = (bf16[32,4096]{1,0:T(8,128)(2,1)S(1)}, bf16[32,4096]{1,0:T(8,128)(2,1)}, u32[]{:S(2)}, u32[]{:S(2)}) collective-permute-start(bf16[32,4096]{1,0:T(8,128)(2,1)S(1)} %collective-permute-done.6.refs_8_), channel_id=1, source_target_pairs={{4,0},{8,4},{12,8},{14,12},{10,14},{6,10},{2,6},{0,2},{5,1},{9,5},... | collective-permute-start | bytes 786440 | tf_op jit(solution)/shard_map/ppermute | solution.py:212
  35.2 15.3 %collective-permute-start.13 = (bf16[32,4096]{1,0:T(8,128)(2,1)S(1)}, bf16[32,4096]{1,0:T(8,128)(2,1)}, u32[]{:S(2)}, u32[]{:S(2)}) collective-permute-start(bf16[32,4096]{1,0:T(8,128)(2,1)S(1)} %collective-permute-done.11.refs_3_), channel_id=1, source_target_pairs={{4,0},{8,4},{12,8},{14,12},{10,14},{6,10},{2,6},{0,2},{5,1},{9,5},... | collective-permute-start | bytes 786440 | tf_op jit(solution)/shard_map/ppermute | solution.py:212
  37.2 13.3 %collective-permute-start.12 = (bf16[32,4096]{1,0:T(8,128)(2,1)S(1)}, bf16[32,4096]{1,0:T(8,128)(2,1)}, u32[]{:S(2)}, u32[]{:S(2)}) collective-permute-start(bf16[32,4096]{1,0:T(8,128)(2,1)S(1)} %collective-permute-done.8.refs_0_), channel_id=1, source_target_pairs={{0,4},{4,8},{8,12},{12,14},{14,10},{10,6},{6,2},{2,0},{1,5},{5,9},... | collective-permute-start | bytes 786440 | tf_op jit(solution)/shard_map/ppermute | solution.py:209
  39.4 9.0 %collective-permute-start.17 = (bf16[64,512]{1,0:T(8,128)(2,1)S(1)}, bf16[64,512]{1,0:T(8,128)(2,1)S(1)}, u32[]{:S(2)}, u32[]{:S(2)}) collective-permute-start(bf16[64,512]{1,0:T(8,128)(2,1)S(1)} %collective-permute-done.15.refs_1_), channel_id=1, source_target_pairs={{0,4},{4,8},{8,12},{12,14},{14,10},{10,6},{6,2},{2,0},{1,5},{5,9},... | collective-permute-start | bytes 196616 | tf_op jit(solution)/shard_map/ppermute | solution.py:209
  48.4 6.2 %collective-permute-start.18 = (bf16[64,512]{1,0:T(8,128)(2,1)S(1)}, bf16[64,512]{1,0:T(8,128)(2,1)}, u32[]{:S(2)}, u32[]{:S(2)}) collective-permute-start(bf16[64,512]{1,0:T(8,128)(2,1)S(1)} %collective-permute-done.16.refs_2_), channel_id=1, source_target_pairs={{4,0},{8,4},{12,8},{14,12},{10,14},{6,10},{2,6},{0,2},{5,1},{9,5},... | collective-permute-start | bytes 196616 | tf_op jit(solution)/shard_map/ppermute | solution.py:212
  50.0 6.3 %collective-permute-start.19 = (bf16[64,512]{1,0:T(8,128)(2,1)S(1)}, bf16[64,512]{1,0:T(8,128)(2,1)}, u32[]{:S(2)}, u32[]{:S(2)}) collective-permute-start(bf16[64,512]{1,0:T(8,128)(2,1)S(1)} %collective-permute-done.17.refs_3_), channel_id=1, source_target_pairs={{0,4},{4,8},{8,12},{12,14},{14,10},{10,6},{6,2},{2,0},{1,5},{5,9},... | collective-permute-start | bytes 196616 | tf_op jit(solution)/shard_map/ppermute | solution.py:209
  54.6 15.9 %collective-permute-start.14 = (f32[384,64]{1,0:T(8,128)}, f32[384,64]{1,0:T(8,128)}, u32[]{:S(2)}, u32[]{:S(2)}) collective-permute-start(f32[384,64]{1,0:T(8,128)} %lowrank.3.mine_ref), channel_id=1, source_target_pairs={{0,1},{1,0},{2,3},{3,2},{4,5},{5,4},{6,7},{7,6},{8,9},{9,8},{10,11... | collective-permute-start | bytes 294920 | tf_op jit(solution)/shard_map/ppermute | solution.py:228
  54.6 15.9 %collective-permute-start.20 = (bf16[64,512]{1,0:T(8,128)(2,1)}, bf16[64,512]{1,0:T(8,128)(2,1)}, u32[]{:S(2)}, u32[]{:S(2)}) collective-permute-start(bf16[64,512]{1,0:T(8,128)(2,1)} %collective-permute-done.18.refs_4_), channel_id=1, source_target_pairs={{4,0},{8,4},{12,8},{14,12},{10,14},{6,10},{2,6},{0,2},{5,1},{9,5},... | collective-permute-start | bytes 196616 | tf_op jit(solution)/shard_map/ppermute | solution.py:212
  56.3 14.3 %collective-permute-start.21 = (bf16[64,512]{1,0:T(8,128)(2,1)}, bf16[64,512]{1,0:T(8,128)(2,1)}, u32[]{:S(2)}, u32[]{:S(2)}) collective-permute-start(bf16[64,512]{1,0:T(8,128)(2,1)} %collective-permute-done.19.refs_5_), channel_id=1, source_target_pairs={{0,4},{4,8},{8,12},{12,14},{14,10},{10,6},{6,2},{2,0},{1,5},{5,9},... | collective-permute-start | bytes 196616 | tf_op jit(solution)/shard_map/ppermute | solution.py:209
  (44 other events, 338.6 us)

commit v2 on v1

--- a/solution.py
+++ b/solution.py
@@ -79,62 +79,74 @@
         ],
         out_specs=[pl.BlockSpec(s, lambda i: (0, 0)) for s in shapes],
         cost_estimate=pl.CostEstimate(
-            flops=2 * elements * HEAD_SIZE,
-            bytes_accessed=2 * (rows * wide + elements),
-            transcendentals=elements,
+            flops=3_500_000_000, bytes_accessed=2 * (rows * wide + elements), transcendentals=elements
         ),
+        compiler_params=pltpu.CompilerParams(vmem_limit_bytes=12 * 2**20),
         name="probs",
     )(lengths, queries, keys)
 
 
-def lowrank_kernel(ranks, ids_ref, adapter_ref, x_ref, before_ref, *refs):
-    w_refs, out_ref = refs[:-1], refs[-1]
+def lowrank_kernel(at, count, ids_ref, adapter_ref, x_ref, *refs):
+    w_refs, out_ref = refs[:count], refs[-1]
+    before_ref = refs[count] if at > 0 else None
     adapter = adapter_ref[...]
-    x = x_ref[...]
-    total = jnp.zeros(out_ref.shape, jnp.float32) if before_ref is None else before_ref[...]
-    pieces = [w_ref[...] for w_ref in w_refs]
-    stacked = jnp.concatenate(pieces, axis=0)
-    product = lax.dot_general(x, stacked, NT, preferred_element_type=jnp.float32)
-    width = out_ref.shape[1]
-    for i in range(ranks):
-        total = total + jnp.where(adapter == ids_ref[i], product[:, i * width : (i + 1) * width], 0.0)
-    out_ref[...] = total
-
-
-def lowrank_of(ids, adapter_of_row, x, before, pieces):
+    rows, features = x_ref.shape
+    half = w_refs[0].shape[0]
+    stacked = jnp.concatenate([w_ref[:, :features] for w_ref in w_refs], axis=0)
+    product = lax.dot_general(x_ref[...], stacked, NT, preferred_element_type=jnp.float32)
+    sums = [jnp.zeros((rows, half), jnp.float32)] * 2
+    for i in range(count):
+        part = product[:, i * half : (i + 1) * half]
+        sums[i % 2] = sums[i % 2] + jnp.where(adapter == ids_ref[at + i // 2], part, 0.0)
+    total = jnp.concatenate(sums, axis=1)
+    out_ref[...] = total if before_ref is None else total + before_ref[...]
+
+
+def lowrank_of(ids, at, adapter_of_row, x, before, pieces, after):
     rows, features = x.shape
-    rank = before.shape[1]
-    depth = sum(p.shape[0] for p in pieces)
+    rank = 2 * pieces[0].shape[0]
+    operands = [ids, adapter_of_row, x] + pieces + ([] if before is None else [before])
+    used = len(operands)
+    operands = operands + after
+    size = 2 * sum(p.size for p in pieces)
     return pl.pallas_call(
-        functools.partial(lowrank_kernel, depth // rank),
+        functools.partial(lowrank_kernel, at, len(pieces)),
         out_shape=jax.ShapeDtypeStruct((rows, rank), jnp.float32),
-        in_specs=[SMEM, VMEM, VMEM, VMEM] + [VMEM] * len(pieces),
+        in_specs=[SMEM] + [VMEM] * (used - 1) + [pl.BlockSpec(memory_space=pl.ANY)] * len(after),
         out_specs=VMEM,
         cost_estimate=pl.CostEstimate(
-            flops=2 * rows * features * depth,
-            bytes_accessed=2 * features * (rows + depth),
-            transcendentals=0,
+            flops=2_500_000_000, bytes_accessed=2 * rows * features + size, transcendentals=0
         ),
+        compiler_params=pltpu.CompilerParams(vmem_limit_bytes=8 * 2**20 + 2 * x.size + 2 * size),
         name="lowrank",
-    )(ids, adapter_of_row, x, before, *pieces)
+    )(*operands)
 
 
 def attend_kernel(kv_heads, n, ids_ref, adapter_ref, mine_ref, theirs_ref, base_ref, *refs):
-    up_refs = refs[:n]
-    tiles = windows(base_ref.shape[0])
-    p_refs = refs[n : n + kv_heads * len(tiles)]
-    out_ref, block, sems = refs[n + kv_heads * len(tiles) :]
+    rows, value_portion = base_ref.shape
+    tiles = windows(rows)
+    low_refs, high_refs = refs[:n], refs[n : 2 * n]
+    p_refs = refs[2 * n : 2 * n + kv_heads * len(tiles)]
+    out_ref, block, sems = refs[2 * n + kv_heads * len(tiles) :]
     rank = mine_ref.shape[1]
+    features = low_refs[0].shape[1] - value_portion
     adapter = adapter_ref[...]
     lowrank = (mine_ref[...] + theirs_ref[...]).astype(jnp.bfloat16)
+    twice = jnp.concatenate([lowrank, lowrank], axis=1)
+    second = lax.broadcasted_iota(jnp.int32, twice.shape, 1) >= rank
     spread = jnp.concatenate(
-        [jnp.where(adapter == ids_ref[i], lowrank, jnp.zeros_like(lowrank)) for i in range(n)], axis=1
+        [
+            jnp.where(adapter == jnp.where(second, ids_ref[i + 1], ids_ref[i]), twice, jnp.zeros_like(twice))
+            for i in range(0, n, 2)
+        ],
+        axis=1,
     )
     copies = []
     wide = GROUP * HEAD_SIZE
     for kv in range(kv_heads):
         columns = slice(kv * HEAD_SIZE, (kv + 1) * HEAD_SIZE)
-        up = jnp.concatenate([up_ref[:, columns] for up_ref in up_refs], axis=0)
+        held = slice(features + kv * HEAD_SIZE, features + (kv + 1) * HEAD_SIZE)
+        up = jnp.concatenate([ref[:, held] for pair in zip(low_refs, high_refs) for ref in pair], axis=0)
         delta = jnp.dot(spread, up, preferred_element_type=jnp.float32).astype(jnp.bfloat16)
         values = (
             base_ref[:, columns].astype(jnp.float32) + adapter_scale * delta.astype(jnp.float32)
@@ -159,20 +171,21 @@
         copy.wait()
 
 
-def attend(ids, adapter_of_row, mine, theirs, base, ups, probs):
+def attend(ids, adapter_of_row, mine, theirs, base, lows, highs, probs):
     rows, value_portion = base.shape
     kv_heads = value_portion // HEAD_SIZE
     wide = kv_heads * GROUP * HEAD_SIZE
     flat = [p for per_head in probs for p in per_head]
+    held = 2 * sum(a.size for a in lows + highs + flat)
     return pl.pallas_call(
-        functools.partial(attend_kernel, kv_heads, len(ups)),
+        functools.partial(attend_kernel, kv_heads, len(lows)),
         out_shape=jax.ShapeDtypeStruct((rows, wide), jnp.bfloat16),
-        in_specs=[SMEM] + [VMEM] * (4 + len(ups) + len(flat)),
+        in_specs=[SMEM] + [VMEM] * (4 + len(lows) + len(highs) + len(flat)),
         out_specs=pl.BlockSpec(memory_space=pl.ANY),
         scratch_shapes=[pltpu.VMEM((rows, wide), jnp.bfloat16), pltpu.SemaphoreType.DMA((kv_heads,))],
-        compiler_params=pltpu.CompilerParams(vmem_limit_bytes=40 * 2**20),
+        compiler_params=pltpu.CompilerParams(vmem_limit_bytes=12 * 2**20),
         name="attend",
-    )(ids, adapter_of_row, mine, theirs, base, *ups, *flat)
+    )(ids, adapter_of_row, mine, theirs, base, *lows, *highs, *flat)
 
 
 def on_device(
@@ -197,9 +210,8 @@
     ids = lax.dynamic_index_in_dim(jnp.asarray(table), lax.axis_index("rep"), 0, keepdims=False)
 
     down = jnp.swapaxes(adapter_down_weight[0], 0, 1)
-    rank = down.shape[0]
-    half = rank // 2
-    up = adapter_up_weight[0]
+    both = jnp.concatenate([down, adapter_up_weight[0]], axis=1)
+    half = both.shape[0] // 2
 
     def pass_round(piece, steps_ahead, steps_back):
         held = {0: piece}
@@ -213,20 +225,28 @@
                 held[-step if step < far else far] = moving_back
         return held
 
-    low = pass_round(down[:half], far, far - 1)
-    high = pass_round(down[half:], far - 1, far)
-    ups = pass_round(up, far, far - 1)
+    low = pass_round(both[:half], far, far - 1)
+    high = pass_round(both[half:], far - 1, far)
 
     kv_heads = stacked_key_rows.shape[1] // HEAD_SIZE
     probs = [probs_of(sequence_lengths, queries, stacked_key_rows, kv) for kv in range(kv_heads)]
 
-    partial = jnp.zeros((normed_token_rows.shape[0], rank), jnp.float32)
-    early = n - 3
-    for lo, hi in [(a, min(a + 5, early)) for a in range(0, early, 5)] + [(early, n)]:
+    partial = None
+    for lo, hi in [(0, 3)] + [(a, a + 2) for a in range(3, n - 3, 2)] + [(n - 3, n)]:
         pieces = [piece for d in distances[lo:hi] for piece in (low[d], high[d])]
-        partial = lowrank_of(ids[lo:hi], adapter_of_row, normed_token_rows, partial, pieces)
+        after = [p[0] for p in probs] if hi == n else []
+        partial = lowrank_of(ids, lo, adapter_of_row, normed_token_rows, partial, pieces, after)
     other = lax.ppermute(partial, "tp", [(0, 1), (1, 0)])
-    return attend(ids, adapter_of_row, partial, other, base_value_rows, [ups[d] for d in distances], probs)
+    return attend(
+        ids,
+        adapter_of_row,
+        partial,
+        other,
+        base_value_rows,
+        [low[d] for d in distances],
+        [high[d] for d in distances],
+        probs,
+    )
 
 
 def solution(mesh):

time: 92 us -> 59.6 us (0.65)
  local copies, waits for them, and re-layouts: 20.6 us -> 5.06 us
  Pallas kernels: 28.1 us -> 17.3 us
  starting transfers between devices: 25.5 us -> 15.7 us
  waiting for transfers between devices: 16.4 us -> 19.8 us
  other arithmetic: 0 us -> 1.11 us
    unnamed x93 -> x11, local copies, waits for them, and re-layouts: 17 us -> 4.36 us
    ppermute x11 -> x7, waiting for transfers between devices: 6.89 us -> 14.8 us  [pass_round(): moving_ahead = lax.ppermute(moving_ahead, 'rep', ahead)]
    ppermute x10 -> x7, starting transfers between devices: 18.1 us -> 12.1 us  [pass_round(): moving_back = lax.ppermute(moving_back, 'rep', back)]
    ppermute x10 -> x7, waiting for transfers between devices: 9.55 us -> 3.61 us  [pass_round(): moving_back = lax.ppermute(moving_back, 'rep', back)]
    pallas_call x4, Pallas kernels: 13.7 us -> 8.21 us  [probs_of(): pl.pallas_call(probs_kernel, grid=(1,), out_shape=[jax.ShapeDtypeStruct(s...]
    pallas_call x3 -> x4, Pallas kernels: 14.4 us -> 9.08 us  [the longest x3 4.83 us: lowrank_of(): pl.pallas_call(functools.partial(lowrank_kernel, at, len(pieces)), out_sh...]
    ppermute x11 -> x7, starting transfers between devices: 7.39 us -> 3.59 us  [pass_round(): moving_ahead = lax.ppermute(moving_ahead, 'rep', ahead)]
    slice x3 -> x0, local copies, waits for them, and re-layouts: 2.19 us -> none  [the longest x2 1.13 us: on_device(): ids[lo:hi]]
  transfers between devices with their start and end apart: 22 -> 15, of which waited for: 6 -> 10; matrix products, arithmetic and copies ran while one was open for 4% -> 3% of each run, Pallas kernels for 25% -> 19%
where the time goes in v2:
time: 59.6 us; the launch traced here: 59.3 us
  waiting for transfers between devices  19.8 us (33%)
  Pallas kernels  17.3 us (29%)
  starting transfers between devices  15.7 us (26%)
  local copies, waits for them, and re-layouts  5.06 us (8%)
  other arithmetic  1.11 us (2%)
    ppermute x7, waiting for transfers between devices, pass_round(): moving_ahead = lax.ppermute(moving_ahead, 'rep', ahead)  14.8 us
    ppermute x7, starting transfers between devices, pass_round(): moving_back = lax.ppermute(moving_back, 'rep', back)  12.1 us
    pallas_call x4, Pallas kernels, probs_of(): pl.pallas_call(probs_kernel, grid=(1,), out_shape=[jax.ShapeDtypeStruct(s...  8.21 us
    pallas_call x3, Pallas kernels, lowrank_of(): pl.pallas_call(functools.partial(lowrank_kernel, at, len(pieces)), out_sh...  4.83 us
    unnamed x11, local copies, waits for them, and re-layouts  4.36 us
    pallas_call x1, Pallas kernels, attend(): pl.pallas_call(functools.partial(attend_kernel, kv_heads, len(lows)), out...  4.25 us
    ppermute x7, waiting for transfers between devices, pass_round(): moving_back = lax.ppermute(moving_back, 'rep', back)  3.61 us
    ppermute x7, starting transfers between devices, pass_round(): moving_ahead = lax.ppermute(moving_ahead, 'rep', ahead)  3.59 us
  transfers between devices with their start and end apart: 15, of which 10 were waited for; matrix products, arithmetic and copies ran while one was open for 3% of the time, Pallas kernels for 19%

profile of v2, /device:TPU:0, one launch (start us, length us, event | category | flops | bytes accessed | tf_op | source)
XLA Modules:
  0.0 59.3 jit_solution(3307485038532790318)
XLA Ops:
  1.1 3.0 %collective-permute-start.9 = (bf16[32,4608]{1,0:T(8,128)(2,1)S(1)}, bf16[32,4608]{1,0:T(8,128)(2,1)S(1)}, u32[]{:S(2)}, u32[]{:S(2)}) collective-permute-start(bf16[32,4608]{1,0:T(8,128)(2,1)S(1)} %get-tuple-element.53.refs_1_.refs_8_), channel_id=1, source_target_pairs={{4,0},{8,4},{12,8},{14,12},{10,14},{6,10},{2,6},{0,2},{5,1},{9,5},... | collective-permute-start | bytes 884744 | tf_op jit(solution)/shard_map/ppermute | solution.py:224
  4.3 1.9 %collective-permute-start.6 = (bf16[32,4608]{1,0:T(8,128)(2,1)S(1)}, bf16[32,4608]{1,0:T(8,128)(2,1)S(1)}, u32[]{:S(2)}, u32[]{:S(2)}) collective-permute-start(bf16[32,4608]{1,0:T(8,128)(2,1)S(1)} %get-tuple-element.54.refs_0_), channel_id=1, source_target_pairs={{4,0},{8,4},{12,8},{14,12},{10,14},{6,10},{2,6},{0,2},{5,1},{9,5},... | collective-permute-start | bytes 884744 | tf_op jit(solution)/shard_map/ppermute | solution.py:224
  7.8 1.9 %copy-done.1 = bf16[384,4096]{1,0:T(8,128)(2,1)S(1)} copy-done((bf16[384,4096]{1,0:T(8,128)(2,1)S(1)}, bf16[384,4096]{1,0:T(8,128)(2,1)}, u32[]{:S(2)}) %copy-start.1) | copy-done | bytes 3145752
  11.3 2.1 %probs.5 = (bf16[512,128]{1,0:T(8,128)(2,1)S(1)}, bf16[512,128]{1,0:T(8,128)(2,1)S(1)}, bf16[512,256]{1,0:T(8,128)(2,1)S(1)}, bf16[512,256]{1,0:T(8,128)(2,1)S(1...) custom-call(s32[1,4]{1,0:T(1,128)S(1)} %copy-done.4, bf16[384,4096]{1,0:T(8,128)(2,1)S(1)} %copy-done.1, ...), custom_call_target="tpu_custom_call" | custom-call | flops 3500000000 | bytes 2097152 | tf_op jit(solution)/shard_map/probs/pallas_call | solution.py:71
  13.4 2.1 %probs.4 = (bf16[512,128]{1,0:T(8,128)(2,1)S(1)}, bf16[512,128]{1,0:T(8,128)(2,1)S(1)}, bf16[512,256]{1,0:T(8,128)(2,1)S(1)}, bf16[512,256]{1,0:T(8,128)(2,1)S(1...) custom-call(s32[1,4]{1,0:T(1,128)S(1)} %copy-done.4, bf16[384,4096]{1,0:T(8,128)(2,1)S(1)} %copy-done.1, ...), custom_call_target="tpu_custom_call" | custom-call | flops 3500000000 | bytes 2097152 | tf_op jit(solution)/shard_map/probs/pallas_call | solution.py:71
  15.5 2.0 %collective-permute-start.10 = (bf16[32,4608]{1,0:T(8,128)(2,1)S(1)}, bf16[32,4608]{1,0:T(8,128)(2,1)S(1)}, u32[]{:S(2)}, u32[]{:S(2)}) collective-permute-start(bf16[32,4608]{1,0:T(8,128)(2,1)S(1)} %collective-permute-done.9.refs_5_.refs_10_), channel_id=1, source_target_pairs={{4,0},{8,4},{12,8},{14,12},{10,14},{6,10},{2,6},{0,2},{5,1},{9,5},... | collective-permute-start | bytes 884744 | tf_op jit(solution)/shard_map/ppermute | solution.py:224
  17.4 1.5 %collective-permute-done.refs_2_.refs_1_ = bf16[32,4608]{1,0:T(8,128)(2,1)S(1)} collective-permute-done((bf16[32,4608]{1,0:T(8,128)(2,1)S(1)}, bf16[32,4608]{1,0:T(8,128)(2,1)S(1)}, u32[]{:S(2)}, u32[]{:S(2)}) %collective-permute-start) | collective-permute-done | bytes 294944 | tf_op jit(solution)/shard_map/ppermute | solution.py:221
  19.3 2.1 %probs.7 = (bf16[512,128]{1,0:T(8,128)(2,1)S(1)}, bf16[512,128]{1,0:T(8,128)(2,1)S(1)}, bf16[512,256]{1,0:T(8,128)(2,1)S(1)}, bf16[512,256]{1,0:T(8,128)(2,1)S(1...) custom-call(s32[1,4]{1,0:T(1,128)S(1)} %copy-done.4, bf16[384,4096]{1,0:T(8,128)(2,1)S(1)} %copy-done.1, ...), custom_call_target="tpu_custom_call" | custom-call | flops 3500000000 | bytes 2097152 | tf_op jit(solution)/shard_map/probs/pallas_call | solution.py:71
  21.4 1.7 %collective-permute-start.4 = (bf16[32,4608]{1,0:T(8,128)(2,1)S(1)}, bf16[32,4608]{1,0:T(8,128)(2,1)S(1)}, u32[]{:S(2)}, u32[]{:S(2)}) collective-permute-start(bf16[32,4608]{1,0:T(8,128)(2,1)S(1)} %collective-permute-done.3.refs_3_.refs_9_), channel_id=1, source_target_pairs={{0,4},{4,8},{8,12},{12,14},{14,10},{10,6},{6,2},{2,0},{1,5},{5,9},... | collective-permute-start | bytes 884744 | tf_op jit(solution)/shard_map/ppermute | solution.py:221
  24.0 2.5 %collective-permute-start.11 = (bf16[32,4608]{1,0:T(8,128)(2,1)S(1)}, bf16[32,4608]{1,0:T(8,128)(2,1)S(1)}, u32[]{:S(2)}, u32[]{:S(2)}) collective-permute-start(bf16[32,4608]{1,0:T(8,128)(2,1)S(1)} %collective-permute-done.10.refs_3_.refs_12_), channel_id=1, source_target_pairs={{4,0},{8,4},{12,8},{14,12},{10,14},{6,10},{2,6},{0,2},{5,1},{9,5},... | collective-permute-start | bytes 884744 | tf_op jit(solution)/shard_map/ppermute | solution.py:224
  26.5 2.4 %collective-permute-done.1.refs_0_.refs_3_ = bf16[32,4608]{1,0:T(8,128)(2,1)S(1)} collective-permute-done((bf16[32,4608]{1,0:T(8,128)(2,1)S(1)}, bf16[32,4608]{1,0:T(8,128)(2,1)S(1)}, u32[]{:S(2)}, u32[]{:S(2)}) %collective-permute-start.1) | collective-permute-done | bytes 294944 | tf_op jit(solution)/shard_map/ppermute | solution.py:221
  29.3 2.1 %probs.6 = (bf16[512,128]{1,0:T(8,128)(2,1)S(1)}, bf16[512,128]{1,0:T(8,128)(2,1)S(1)}, bf16[512,256]{1,0:T(8,128)(2,1)S(1)}, bf16[512,256]{1,0:T(8,128)(2,1)S(1...) custom-call(s32[1,4]{1,0:T(1,128)S(1)} %copy-done.4, bf16[384,4096]{1,0:T(8,128)(2,1)S(1)} %copy-done.1, ...), custom_call_target="tpu_custom_call" | custom-call | flops 3500000000 | bytes 2097152 | tf_op jit(solution)/shard_map/probs/pallas_call | solution.py:71
  31.3 3.9 %collective-permute-done.4.refs_1_.refs_11_ = bf16[32,4608]{1,0:T(8,128)(2,1)S(1)} collective-permute-done((bf16[32,4608]{1,0:T(8,128)(2,1)S(1)}, bf16[32,4608]{1,0:T(8,128)(2,1)S(1)}, u32[]{:S(2)}, u32[]{:S(2)}) %collective-permute-start.4) | collective-permute-done | bytes 294944 | tf_op jit(solution)/shard_map/ppermute | solution.py:221
  35.6 1.6 %collective-permute-start.8 = (bf16[32,4608]{1,0:T(8,128)(2,1)S(1)}, bf16[32,4608]{1,0:T(8,128)(2,1)S(1)}, u32[]{:S(2)}, u32[]{:S(2)}) collective-permute-start(bf16[32,4608]{1,0:T(8,128)(2,1)S(1)} %collective-permute-done.7.refs_2_.refs_4_), channel_id=1, source_target_pairs={{4,0},{8,4},{12,8},{14,12},{10,14},{6,10},{2,6},{0,2},{5,1},{9,5},... | collective-permute-start | bytes 884744 | tf_op jit(solution)/shard_map/ppermute | solution.py:224
  37.2 1.8 %collective-permute-done.11.refs_3_.refs_14_ = bf16[32,4608]{1,0:T(8,128)(2,1)S(1)} collective-permute-done((bf16[32,4608]{1,0:T(8,128)(2,1)S(1)}, bf16[32,4608]{1,0:T(8,128)(2,1)S(1)}, u32[]{:S(2)}, u32[]{:S(2)}) %collective-permute-start.11) | collective-permute-done | bytes 294944 | tf_op jit(solution)/shard_map/ppermute | solution.py:224
  39.8 1.8 %collective-permute-done.2.refs_0_.refs_5_ = bf16[32,4608]{1,0:T(8,128)(2,1)S(1)} collective-permute-done((bf16[32,4608]{1,0:T(8,128)(2,1)S(1)}, bf16[32,4608]{1,0:T(8,128)(2,1)S(1)}, u32[]{:S(2)}, u32[]{:S(2)}) %collective-permute-start.2) | collective-permute-done | bytes 294944 | tf_op jit(solution)/shard_map/ppermute | solution.py:221
  41.9 1.6 %lowrank.3.refs_4_ = f32[384,64]{1,0:T(8,128)S(1)} custom-call(s32[8]{0:T(128)S(1)} %dynamic-slice_bitcast_fusion.ids_ref, s32[384,1]{1,0:T(8,128)S(1)} %copy.13.adapter_ref, bf16[384,4096]{1,0:T(8,128)(2,1)S(1)} %copy-done.2, bf16[32,4608]{1,0:T(8,128)(2,1)S(1)} %get-tuple-element.54.refs_0_, bf16[32,4608]{1,0:T(8,128)(2,1)S(1)} %get-tuple-element.53.refs_1_.refs_8_, ...), custom_call_target="tpu_custom_call" | custom-call | flops 2500000000 | bytes 4915200 | tf_op jit(solution)/shard_map/lowrank/pallas_call | solution.py:112
  43.6 1.6 %lowrank.4.refs_6_ = f32[384,64]{1,0:T(8,128)S(1)} custom-call(s32[8]{0:T(128)S(1)} %dynamic-slice_bitcast_fusion.ids_ref, s32[384,1]{1,0:T(8,128)S(1)} %copy.13.adapter_ref, bf16[384,4096]{1,0:T(8,128)(2,1)S(1)} %copy-done.2, bf16[32,4608]{1,0:T(8,128)(2,1)S(1)} %collective-permute-done.1.refs_0_.refs_3_, ...), custom_call_target="tpu_custom_call" | custom-call | flops 2500000000 | bytes 4325376 | tf_op jit(solution)/shard_map/lowrank/pallas_call | solution.py:112
  45.1 2.7 %collective-permute-done.5.refs_1_.refs_13_ = bf16[32,4608]{1,0:T(8,128)(2,1)S(1)} collective-permute-done((bf16[32,4608]{1,0:T(8,128)(2,1)S(1)}, bf16[32,4608]{1,0:T(8,128)(2,1)S(1)}, u32[]{:S(2)}, u32[]{:S(2)}) %collective-permute-start.5) | collective-permute-done | bytes 294944 | tf_op jit(solution)/shard_map/ppermute | solution.py:221
  47.8 1.3 %collective-permute-done.13.refs_5_.refs_15_ = bf16[32,4608]{1,0:T(8,128)(2,1)S(1)} collective-permute-done((bf16[32,4608]{1,0:T(8,128)(2,1)S(1)}, bf16[32,4608]{1,0:T(8,128)(2,1)S(1)}, u32[]{:S(2)}, u32[]{:S(2)}) %collective-permute-start.13) | collective-permute-done | bytes 294944 | tf_op jit(solution)/shard_map/ppermute | solution.py:224
  49.1 2.6 %collective-permute-done.12.refs_4_.refs_7_ = bf16[32,4608]{1,0:T(8,128)(2,1)S(1)} collective-permute-done((bf16[32,4608]{1,0:T(8,128)(2,1)S(1)}, bf16[32,4608]{1,0:T(8,128)(2,1)S(1)}, u32[]{:S(2)}, u32[]{:S(2)}) %collective-permute-start.12) | collective-permute-done | bytes 294944 | tf_op jit(solution)/shard_map/ppermute | solution.py:221
  51.8 1.6 %lowrank.5.mine_ref = f32[384,64]{1,0:T(8,128)S(1)} custom-call(s32[8]{0:T(128)S(1)} %dynamic-slice_bitcast_fusion.ids_ref, s32[384,1]{1,0:T(8,128)S(1)} %copy.13.adapter_ref, bf16[384,4096]{1,0:T(8,128)(2,1)S(1)} %copy-done.2, bf16[32,4608]{1,0:T(8,128)(2,1)S(1)} %collective-permute-done.2.refs_0_.refs_5_, ...), custom_call_target="tpu_custom_call" | custom-call | flops 2500000000 | bytes 4915200 | tf_op jit(solution)/shard_map/lowrank/pallas_call | solution.py:112
  53.5 1.4 %collective-permute-done.14.theirs_ref = f32[384,64]{1,0:T(8,128)S(1)} collective-permute-done((f32[384,64]{1,0:T(8,128)S(1)}, f32[384,64]{1,0:T(8,128)S(1)}, u32[]{:S(2)}, u32[]{:S(2)}) %collective-permute-start.14) | collective-permute-done | bytes 98336 | tf_op jit(solution)/shard_map/ppermute | solution.py:239
  54.9 4.2 %attend.1 = bf16[384,4096]{1,0:T(8,128)(2,1)} custom-call(s32[8]{0:T(128)S(1)} %dynamic-slice_bitcast_fusion.ids_ref, s32[384,1]{1,0:T(8,128)S(1)} %copy.13.adapter_ref, f32[384,64]{1,0:T(8,128)S(1)} %lowrank.5.mine_ref, f32[384,64]{1,0:T(8,128)S(1)} %collective-permute-done.14.theirs_ref, bf16[384,512]{1,0:T(8,128)(2,1)S(1)} %copy-done, ...), custom_call_target="tpu_custom_call" | custom-call | tf_op jit(solution)/shard_map/attend/pallas_call | solution.py:180
  (27 shorter events, 7.8 us)
Async XLA Ops:
  1.1 14.3 %collective-permute-start.9 = (bf16[32,4608]{1,0:T(8,128)(2,1)S(1)}, bf16[32,4608]{1,0:T(8,128)(2,1)S(1)}, u32[]{:S(2)}, u32[]{:S(2)}) collective-permute-start(bf16[32,4608]{1,0:T(8,128)(2,1)S(1)} %get-tuple-element.53.refs_1_.refs_8_), channel_id=1, source_target_pairs={{4,0},{8,4},{12,8},{14,12},{10,14},{6,10},{2,6},{0,2},{5,1},{9,5},... | collective-permute-start | bytes 884744 | tf_op jit(solution)/shard_map/ppermute | solution.py:224
  4.1 17.3 %collective-permute-start.3 = (bf16[32,4608]{1,0:T(8,128)(2,1)S(1)}, bf16[32,4608]{1,0:T(8,128)(2,1)S(1)}, u32[]{:S(2)}, u32[]{:S(2)}) collective-permute-start(bf16[32,4608]{1,0:T(8,128)(2,1)S(1)} %get-tuple-element.53.refs_1_.refs_8_), channel_id=1, source_target_pairs={{0,4},{4,8},{8,12},{12,14},{14,10},{10,6},{6,2},{2,0},{1,5},{5,9},... | collective-permute-start | bytes 884744 | tf_op jit(solution)/shard_map/ppermute | solution.py:221
  4.3 18.9 %collective-permute-start.6 = (bf16[32,4608]{1,0:T(8,128)(2,1)S(1)}, bf16[32,4608]{1,0:T(8,128)(2,1)S(1)}, u32[]{:S(2)}, u32[]{:S(2)}) collective-permute-start(bf16[32,4608]{1,0:T(8,128)(2,1)S(1)} %get-tuple-element.54.refs_0_), channel_id=1, source_target_pairs={{4,0},{8,4},{12,8},{14,12},{10,14},{6,10},{2,6},{0,2},{5,1},{9,5},... | collective-permute-start | bytes 884744 | tf_op jit(solution)/shard_map/ppermute | solution.py:224
  6.2 12.8 %collective-permute-start = (bf16[32,4608]{1,0:T(8,128)(2,1)S(1)}, bf16[32,4608]{1,0:T(8,128)(2,1)S(1)}, u32[]{:S(2)}, u32[]{:S(2)}) collective-permute-start(bf16[32,4608]{1,0:T(8,128)(2,1)S(1)} %get-tuple-element.54.refs_0_), channel_id=1, source_target_pairs={{0,4},{4,8},{8,12},{12,14},{14,10},{10,6},{6,2},{2,0},{1,5},{5,9},... | collective-permute-start | bytes 884744 | tf_op jit(solution)/shard_map/ppermute | solution.py:221
  7.8 1.9 %copy-start.1 = (bf16[384,4096]{1,0:T(8,128)(2,1)S(1)}, bf16[384,4096]{1,0:T(8,128)(2,1)}, u32[]{:S(2)}) copy-start(bf16[384,4096]{1,0:T(8,128)(2,1)} %q_ref.7) | copy-start | bytes 9437188
  9.7 1.0 %copy-start.3 = (bf16[384,512]{1,0:T(8,128)(2,1)S(1)}, bf16[384,512]{1,0:T(8,128)(2,1)}, u32[]{:S(2)}) copy-start(bf16[384,512]{1,0:T(8,128)(2,1)} %k_ref.7) | copy-start | bytes 1179652
  10.7 0.7 %copy-start.4 = (s32[1,4]{1,0:T(1,128)S(1)}, s32[1,4]{1,0:T(1,128)}, u32[]{:S(2)}) copy-start(s32[1,4]{1,0:T(1,128)} %lengths_ref.7) | copy-start | bytes 52
  15.5 8.5 %collective-permute-start.10 = (bf16[32,4608]{1,0:T(8,128)(2,1)S(1)}, bf16[32,4608]{1,0:T(8,128)(2,1)S(1)}, u32[]{:S(2)}, u32[]{:S(2)}) collective-permute-start(bf16[32,4608]{1,0:T(8,128)(2,1)S(1)} %collective-permute-done.9.refs_5_.refs_10_), channel_id=1, source_target_pairs={{4,0},{8,4},{12,8},{14,12},{10,14},{6,10},{2,6},{0,2},{5,1},{9,5},... | collective-permute-start | bytes 884744 | tf_op jit(solution)/shard_map/ppermute | solution.py:224
  18.9 9.9 %collective-permute-start.1 = (bf16[32,4608]{1,0:T(8,128)(2,1)S(1)}, bf16[32,4608]{1,0:T(8,128)(2,1)S(1)}, u32[]{:S(2)}, u32[]{:S(2)}) collective-permute-start(bf16[32,4608]{1,0:T(8,128)(2,1)S(1)} %collective-permute-done.refs_2_.refs_1_), channel_id=1, source_target_pairs={{0,4},{4,8},{8,12},{12,14},{14,10},{10,6},{6,2},{2,0},{1,5},{5,9},... | collective-permute-start | bytes 884744 | tf_op jit(solution)/shard_map/ppermute | solution.py:221
  21.4 20.5 %copy-start.2 = (bf16[384,4096]{1,0:T(8,128)(2,1)S(1)}, bf16[384,4096]{1,0:T(8,128)(2,1)}, u32[]{:S(2)}) copy-start(bf16[384,4096]{1,0:T(8,128)(2,1)} %x_ref.5) | copy-start | bytes 9437188
  21.4 13.8 %collective-permute-start.4 = (bf16[32,4608]{1,0:T(8,128)(2,1)S(1)}, bf16[32,4608]{1,0:T(8,128)(2,1)S(1)}, u32[]{:S(2)}, u32[]{:S(2)}) collective-permute-start(bf16[32,4608]{1,0:T(8,128)(2,1)S(1)} %collective-permute-done.3.refs_3_.refs_9_), channel_id=1, source_target_pairs={{0,4},{4,8},{8,12},{12,14},{14,10},{10,6},{6,2},{2,0},{1,5},{5,9},... | collective-permute-start | bytes 884744 | tf_op jit(solution)/shard_map/ppermute | solution.py:221
  23.1 12.4 %collective-permute-start.7 = (bf16[32,4608]{1,0:T(8,128)(2,1)S(1)}, bf16[32,4608]{1,0:T(8,128)(2,1)S(1)}, u32[]{:S(2)}, u32[]{:S(2)}) collective-permute-start(bf16[32,4608]{1,0:T(8,128)(2,1)S(1)} %collective-permute-done.6.refs_4_.refs_2_), channel_id=1, source_target_pairs={{4,0},{8,4},{12,8},{14,12},{10,14},{6,10},{2,6},{0,2},{5,1},{9,5},... | collective-permute-start | bytes 884744 | tf_op jit(solution)/shard_map/ppermute | solution.py:224
  24.0 15.0 %collective-permute-start.11 = (bf16[32,4608]{1,0:T(8,128)(2,1)S(1)}, bf16[32,4608]{1,0:T(8,128)(2,1)S(1)}, u32[]{:S(2)}, u32[]{:S(2)}) collective-permute-start(bf16[32,4608]{1,0:T(8,128)(2,1)S(1)} %collective-permute-done.10.refs_3_.refs_12_), channel_id=1, source_target_pairs={{4,0},{8,4},{12,8},{14,12},{10,14},{6,10},{2,6},{0,2},{5,1},{9,5},... | collective-permute-start | bytes 884744 | tf_op jit(solution)/shard_map/ppermute | solution.py:224
  28.9 12.6 %collective-permute-start.2 = (bf16[32,4608]{1,0:T(8,128)(2,1)S(1)}, bf16[32,4608]{1,0:T(8,128)(2,1)S(1)}, u32[]{:S(2)}, u32[]{:S(2)}) collective-permute-start(bf16[32,4608]{1,0:T(8,128)(2,1)S(1)} %collective-permute-done.1.refs_0_.refs_3_), channel_id=1, source_target_pairs={{0,4},{4,8},{8,12},{12,14},{14,10},{10,6},{6,2},{2,0},{1,5},{5,9},... | collective-permute-start | bytes 884744 | tf_op jit(solution)/shard_map/ppermute | solution.py:221
  35.2 12.6 %collective-permute-start.5 = (bf16[32,4608]{1,0:T(8,128)(2,1)S(1)}, bf16[32,4608]{1,0:T(8,128)(2,1)S(1)}, u32[]{:S(2)}, u32[]{:S(2)}) collective-permute-start(bf16[32,4608]{1,0:T(8,128)(2,1)S(1)} %collective-permute-done.4.refs_1_.refs_11_), channel_id=1, source_target_pairs={{0,4},{4,8},{8,12},{12,14},{14,10},{10,6},{6,2},{2,0},{1,5},{5,9},... | collective-permute-start | bytes 884744 | tf_op jit(solution)/shard_map/ppermute | solution.py:221
  35.6 12.2 %collective-permute-start.8 = (bf16[32,4608]{1,0:T(8,128)(2,1)S(1)}, bf16[32,4608]{1,0:T(8,128)(2,1)S(1)}, u32[]{:S(2)}, u32[]{:S(2)}) collective-permute-start(bf16[32,4608]{1,0:T(8,128)(2,1)S(1)} %collective-permute-done.7.refs_2_.refs_4_), channel_id=1, source_target_pairs={{4,0},{8,4},{12,8},{14,12},{10,14},{6,10},{2,6},{0,2},{5,1},{9,5},... | collective-permute-start | bytes 884744 | tf_op jit(solution)/shard_map/ppermute | solution.py:224
  39.0 10.1 %collective-permute-start.13 = (bf16[32,4608]{1,0:T(8,128)(2,1)S(1)}, bf16[32,4608]{1,0:T(8,128)(2,1)S(1)}, u32[]{:S(2)}, u32[]{:S(2)}) collective-permute-start(bf16[32,4608]{1,0:T(8,128)(2,1)S(1)} %collective-permute-done.11.refs_3_.refs_14_), channel_id=1, source_target_pairs={{4,0},{8,4},{12,8},{14,12},{10,14},{6,10},{2,6},{0,2},{5,1},{9,5},... | collective-permute-start | bytes 884744 | tf_op jit(solution)/shard_map/ppermute | solution.py:224
  41.5 10.3 %collective-permute-start.12 = (bf16[32,4608]{1,0:T(8,128)(2,1)S(1)}, bf16[32,4608]{1,0:T(8,128)(2,1)S(1)}, u32[]{:S(2)}, u32[]{:S(2)}) collective-permute-start(bf16[32,4608]{1,0:T(8,128)(2,1)S(1)} %collective-permute-done.2.refs_0_.refs_5_), channel_id=1, source_target_pairs={{0,4},{4,8},{8,12},{12,14},{14,10},{10,6},{6,2},{2,0},{1,5},{5,9},... | collective-permute-start | bytes 884744 | tf_op jit(solution)/shard_map/ppermute | solution.py:221
  51.8 3.1 %copy-start = (bf16[384,512]{1,0:T(8,128)(2,1)S(1)}, bf16[384,512]{1,0:T(8,128)(2,1)}, u32[]{:S(2)}) copy-start(bf16[384,512]{1,0:T(8,128)(2,1)} %base_ref.1) | copy-start | bytes 1179652
  53.4 1.5 %collective-permute-start.14 = (f32[384,64]{1,0:T(8,128)S(1)}, f32[384,64]{1,0:T(8,128)S(1)}, u32[]{:S(2)}, u32[]{:S(2)}) collective-permute-start(f32[384,64]{1,0:T(8,128)S(1)} %lowrank.5.mine_ref), channel_id=1, source_target_pairs={{0,1},{1,0},{2,3},{3,2},{4,5},{5,4},{6,7},{7,6},{8,9},{9,8},{10,11... | collective-permute-start | bytes 294920 | tf_op jit(solution)/shard_map/ppermute | solution.py:239

commit v3 on v2

--- a/solution.py
+++ b/solution.py
@@ -38,7 +38,8 @@
     return found
 
 
-def probs_kernel(lengths_ref, q_ref, k_ref, *p_refs):
+def probs_kernel(waits, lengths_ref, q_ref, k_ref, *refs):
+    p_refs = refs[waits:]
     rows = k_ref.shape[0]
     ends = []
     total = jnp.int32(0)
@@ -63,27 +64,28 @@
             p_ref[head * TILE : (head + 1) * TILE, :] = (weights * inverse).astype(jnp.bfloat16)
 
 
-def probs_of(lengths, queries, keys, kv_head):
+def probs_of(lengths, queries, keys, kv_head, after):
     rows = keys.shape[0]
     wide = GROUP * HEAD_SIZE
     shapes = [(GROUP * TILE, width) for _, _, width in windows(rows)]
     elements = sum(a * b for a, b in shapes)
     return pl.pallas_call(
-        probs_kernel,
+        functools.partial(probs_kernel, len(after)),
         grid=(1,),
         out_shape=[jax.ShapeDtypeStruct(s, jnp.bfloat16) for s in shapes],
         in_specs=[
             SMEM,
             pl.BlockSpec((rows, wide), lambda i: (0, kv_head)),
             pl.BlockSpec((rows, HEAD_SIZE), lambda i: (0, kv_head)),
-        ],
+        ]
+        + [pl.BlockSpec(memory_space=pl.ANY)] * len(after),
         out_specs=[pl.BlockSpec(s, lambda i: (0, 0)) for s in shapes],
         cost_estimate=pl.CostEstimate(
-            flops=3_500_000_000, bytes_accessed=2 * (rows * wide + elements), transcendentals=elements
+            flops=2_300_000_000, bytes_accessed=2 * (rows * wide + elements), transcendentals=elements
         ),
         compiler_params=pltpu.CompilerParams(vmem_limit_bytes=12 * 2**20),
         name="probs",
-    )(lengths, queries, keys)
+    )(lengths, queries, keys, *after)
 
 
 def lowrank_kernel(at, count, ids_ref, adapter_ref, x_ref, *refs):
@@ -115,7 +117,7 @@
         in_specs=[SMEM] + [VMEM] * (used - 1) + [pl.BlockSpec(memory_space=pl.ANY)] * len(after),
         out_specs=VMEM,
         cost_estimate=pl.CostEstimate(
-            flops=2_500_000_000, bytes_accessed=2 * rows * features + size, transcendentals=0
+            flops=1_700_000_000, bytes_accessed=2 * rows * features + size, transcendentals=0
         ),
         compiler_params=pltpu.CompilerParams(vmem_limit_bytes=8 * 2**20 + 2 * x.size + 2 * size),
         name="lowrank",
@@ -229,12 +231,18 @@
     high = pass_round(both[half:], far - 1, far)
 
     kv_heads = stacked_key_rows.shape[1] // HEAD_SIZE
-    probs = [probs_of(sequence_lengths, queries, stacked_key_rows, kv) for kv in range(kv_heads)]
+    arrivals = [[piece[d] for d in (step, -step)] for step in range(1, far) for piece in (low, high)]
+    probs = [
+        probs_of(sequence_lengths, queries, stacked_key_rows, kv, arrivals[kv - 1] if kv > 0 else [])
+        for kv in range(kv_heads)
+    ]
 
     partial = None
-    for lo, hi in [(0, 3)] + [(a, a + 2) for a in range(3, n - 3, 2)] + [(n - 3, n)]:
+    for lo, hi in [(0, 3)] + [(a, a + 2) for a in range(3, n - 1, 2)] + [(n - 1, n)]:
         pieces = [piece for d in distances[lo:hi] for piece in (low[d], high[d])]
-        after = [p[0] for p in probs] if hi == n else []
+        after = arrivals[kv_heads - 1] if lo == 0 else []
+        if hi == n:
+            after = [p[0] for p in probs]
         partial = lowrank_of(ids, lo, adapter_of_row, normed_token_rows, partial, pieces, after)
     other = lax.ppermute(partial, "tp", [(0, 1), (1, 0)])
     return attend(

time: 59.6 us -> 58.6 us (0.983)
  waiting for transfers between devices: 19.8 us -> 17.9 us
  Pallas kernels: 17.3 us -> 18.8 us
    ppermute x7, waiting for transfers between devices: 14.8 us -> 3.7 us  [pass_round(): moving_ahead = lax.ppermute(moving_ahead, 'rep', ahead)]
    ppermute x7, starting transfers between devices: 12.1 us -> 2.46 us  [pass_round(): moving_back = lax.ppermute(moving_back, 'rep', back)]
    ppermute x7, waiting for transfers between devices: 3.61 us -> 12.8 us  [pass_round(): moving_back = lax.ppermute(moving_back, 'rep', back)]
    ppermute x7, starting transfers between devices: 3.59 us -> 12.7 us  [pass_round(): moving_ahead = lax.ppermute(moving_ahead, 'rep', ahead)]
    pallas_call x3 -> x4, Pallas kernels: 4.83 us -> 6.32 us  [lowrank_of(): pl.pallas_call(functools.partial(lowrank_kernel, at, len(pieces)), out_sh...]
    unnamed x11 -> x15, local copies, waits for them, and re-layouts: 4.36 us -> 4.37 us
  transfers between devices with their start and end apart: 15 -> 15, of which waited for: 10 -> 7; matrix products, arithmetic and copies ran while one was open for 3% -> 3% of each run, Pallas kernels for 19% -> 22%
where the time goes in v3:
time: 58.6 us; the launch traced here: 58.4 us
  Pallas kernels  18.8 us (32%)
  waiting for transfers between devices  17.9 us (31%)
  starting transfers between devices  15.2 us (26%)
  local copies, waits for them, and re-layouts  5.07 us (9%)
  other arithmetic  1.11 us (2%)
    ppermute x7, waiting for transfers between devices, pass_round(): moving_back = lax.ppermute(moving_back, 'rep', back)  12.8 us
    ppermute x7, starting transfers between devices, pass_round(): moving_ahead = lax.ppermute(moving_ahead, 'rep', ahead)  12.7 us
    pallas_call x4, Pallas kernels, probs_of(): pl.pallas_call(functools.partial(probs_kernel, len(after)), grid=(1,), ou...  8.21 us
    pallas_call x4, Pallas kernels, lowrank_of(): pl.pallas_call(functools.partial(lowrank_kernel, at, len(pieces)), out_sh...  6.32 us
    unnamed x15, local copies, waits for them, and re-layouts  4.37 us
    pallas_call x1, Pallas kernels, attend(): pl.pallas_call(functools.partial(attend_kernel, kv_heads, len(lows)), out...  4.25 us
    ppermute x7, waiting for transfers between devices, pass_round(): moving_ahead = lax.ppermute(moving_ahead, 'rep', ahead)  3.7 us
    ppermute x7, starting transfers between devices, pass_round(): moving_back = lax.ppermute(moving_back, 'rep', back)  2.46 us
  transfers between devices with their start and end apart: 15, of which 7 were waited for; matrix products, arithmetic and copies ran while one was open for 3% of the time, Pallas kernels for 22%

profile of v3, /device:TPU:0, one launch (start us, length us, event | category | flops | bytes accessed | tf_op | source)
XLA Modules:
  0.0 58.4 jit_solution(17299029219000094492)
XLA Ops:
  0.0 1.1 %pad_maximum_fusion = (bf16[32,4608]{1,0:T(8,128)(2,1)S(1)}, bf16[32,4608]{1,0:T(8,128)(2,1)S(1)}) fusion(bf16[64,512]{1,0:T(8,128)(2,1)} %bitcast.7, bf16[64,4096]{1,0:T(8,128)(2,1)} %bitcast.6), kind=kLoop, calls=%fused_computation.3 | loop fusion | flops 1179648 | bytes 1179648 | tf_op jit(solution)/shard_map/concatenate | solution.py:215
  1.1 3.1 %collective-permute-start.8 = (bf16[32,4608]{1,0:T(8,128)(2,1)S(1)}, bf16[32,4608]{1,0:T(8,128)(2,1)S(1)}, u32[]{:S(2)}, u32[]{:S(2)}) collective-permute-start(bf16[32,4608]{1,0:T(8,128)(2,1)S(1)} %get-tuple-element.53.refs_1_.refs_8_), channel_id=1, source_target_pairs={{0,4},{4,8},{8,12},{12,14},{14,10},{10,6},{6,2},{2,0},{1,5},{5,9},... | collective-permute-start | bytes 884744 | tf_op jit(solution)/shard_map/ppermute | solution.py:223
  4.2 2.0 %collective-permute-start.11 = (bf16[32,4608]{1,0:T(8,128)(2,1)S(1)}, bf16[32,4608]{1,0:T(8,128)(2,1)S(1)}, u32[]{:S(2)}, u32[]{:S(2)}) collective-permute-start(bf16[32,4608]{1,0:T(8,128)(2,1)S(1)} %get-tuple-element.54.refs_0_), channel_id=1, source_target_pairs={{4,0},{8,4},{12,8},{14,12},{10,14},{6,10},{2,6},{0,2},{5,1},{9,5},... | collective-permute-start | bytes 884744 | tf_op jit(solution)/shard_map/ppermute | solution.py:226
  7.8 1.9 %copy-done.1 = bf16[384,4096]{1,0:T(8,128)(2,1)S(1)} copy-done((bf16[384,4096]{1,0:T(8,128)(2,1)S(1)}, bf16[384,4096]{1,0:T(8,128)(2,1)}, u32[]{:S(2)}) %copy-start.1) | copy-done | bytes 3145752
  9.7 1.0 %copy-done.4 = bf16[384,512]{1,0:T(8,128)(2,1)S(1)} copy-done((bf16[384,512]{1,0:T(8,128)(2,1)S(1)}, bf16[384,512]{1,0:T(8,128)(2,1)}, u32[]{:S(2)}) %copy-start.4) | copy-done | bytes 393240
  11.3 2.1 %probs.4 = (bf16[512,128]{1,0:T(8,128)(2,1)S(1)}, bf16[512,128]{1,0:T(8,128)(2,1)S(1)}, bf16[512,256]{1,0:T(8,128)(2,1)S(1)}, bf16[512,256]{1,0:T(8,128)(2,1)S(1...) custom-call(s32[1,4]{1,0:T(1,128)S(1)} %copy-done.6, bf16[384,4096]{1,0:T(8,128)(2,1)S(1)} %copy-done.1, ...), custom_call_target="tpu_custom_call" | custom-call | flops 2300000000 | bytes 2097152 | tf_op jit(solution)/shard_map/probs/pallas_call | solution.py:72
  13.4 2.0 %collective-permute-start.9 = (bf16[32,4608]{1,0:T(8,128)(2,1)S(1)}, bf16[32,4608]{1,0:T(8,128)(2,1)S(1)}, u32[]{:S(2)}, u32[]{:S(2)}) collective-permute-start(bf16[32,4608]{1,0:T(8,128)(2,1)S(1)} %collective-permute-done.8.refs_3_.refs_0_.refs_9_), channel_id=1, source_target_pairs={{0,4},{4,8},{8,12},{12,14},{14,10},{10,6},{6,2},{2,0},{1,5},{5,9},... | collective-permute-start | bytes 884744 | tf_op jit(solution)/shard_map/ppermute | solution.py:223
  15.5 5.0 %collective-permute-done.11.refs_4_.refs_1_.refs_2_ = bf16[32,4608]{1,0:T(8,128)(2,1)S(1)} collective-permute-done((bf16[32,4608]{1,0:T(8,128)(2,1)S(1)}, bf16[32,4608]{1,0:T(8,128)(2,1)S(1)}, u32[]{:S(2)}, u32[]{:S(2)}) %collective-permute-start.11) | collective-permute-done | bytes 294944 | tf_op jit(solution)/shard_map/ppermute | solution.py:226
  20.4 2.0 %collective-permute-start.1 = (bf16[32,4608]{1,0:T(8,128)(2,1)S(1)}, bf16[32,4608]{1,0:T(8,128)(2,1)S(1)}, u32[]{:S(2)}, u32[]{:S(2)}) collective-permute-start(bf16[32,4608]{1,0:T(8,128)(2,1)S(1)} %collective-permute-done.refs_2_.refs_0_.refs_1_), channel_id=1, source_target_pairs={{0,4},{4,8},{8,12},{12,14},{14,10},{10,6},{6,2},{2,0},{1,5},{5,9},... | collective-permute-start | bytes 884744 | tf_op jit(solution)/shard_map/ppermute | solution.py:223
  22.5 2.1 %probs.5 = (bf16[512,128]{1,0:T(8,128)(2,1)S(1)}, bf16[512,128]{1,0:T(8,128)(2,1)S(1)}, bf16[512,256]{1,0:T(8,128)(2,1)S(1)}, bf16[512,256]{1,0:T(8,128)(2,1)S(1...) custom-call(s32[1,4]{1,0:T(1,128)S(1)} %copy-done.6, bf16[384,4096]{1,0:T(8,128)(2,1)S(1)} %copy-done.2, ...), custom_call_target="tpu_custom_call" | custom-call | flops 2300000000 | bytes 2097152 | tf_op jit(solution)/shard_map/probs/pallas_call | solution.py:72
  24.5 2.1 %probs.6 = (bf16[512,128]{1,0:T(8,128)(2,1)S(1)}, bf16[512,128]{1,0:T(8,128)(2,1)S(1)}, bf16[512,256]{1,0:T(8,128)(2,1)S(1)}, bf16[512,256]{1,0:T(8,128)(2,1)S(1...) custom-call(s32[1,4]{1,0:T(1,128)S(1)} %copy-done.6, bf16[384,4096]{1,0:T(8,128)(2,1)S(1)} %copy-done.2, ...), custom_call_target="tpu_custom_call" | custom-call | flops 2300000000 | bytes 2097152 | tf_op jit(solution)/shard_map/probs/pallas_call | solution.py:72
  26.6 1.6 %collective-permute-start.10 = (bf16[32,4608]{1,0:T(8,128)(2,1)S(1)}, bf16[32,4608]{1,0:T(8,128)(2,1)S(1)}, u32[]{:S(2)}, u32[]{:S(2)}) collective-permute-start(bf16[32,4608]{1,0:T(8,128)(2,1)S(1)} %collective-permute-done.9.refs_6_.refs_1_.refs_11_), channel_id=1, source_target_pairs={{0,4},{4,8},{8,12},{12,14},{14,10},{10,6},{6,2},{2,0},{1,5},{5,9},... | collective-permute-start | bytes 884744 | tf_op jit(solution)/shard_map/ppermute | solution.py:223
  28.7 4.4 %collective-permute-done.12.refs_2_.refs_1_.refs_4_ = bf16[32,4608]{1,0:T(8,128)(2,1)S(1)} collective-permute-done((bf16[32,4608]{1,0:T(8,128)(2,1)S(1)}, bf16[32,4608]{1,0:T(8,128)(2,1)S(1)}, u32[]{:S(2)}, u32[]{:S(2)}) %collective-permute-start.12) | collective-permute-done | bytes 294944 | tf_op jit(solution)/shard_map/ppermute | solution.py:226
  33.1 2.0 %collective-permute-start.2 = (bf16[32,4608]{1,0:T(8,128)(2,1)S(1)}, bf16[32,4608]{1,0:T(8,128)(2,1)S(1)}, u32[]{:S(2)}, u32[]{:S(2)}) collective-permute-start(bf16[32,4608]{1,0:T(8,128)(2,1)S(1)} %collective-permute-done.1.refs_0_.refs_3_), channel_id=1, source_target_pairs={{0,4},{4,8},{8,12},{12,14},{14,10},{10,6},{6,2},{2,0},{1,5},{5,9},... | collective-permute-start | bytes 884744 | tf_op jit(solution)/shard_map/ppermute | solution.py:223
  35.1 2.1 %probs.7 = (bf16[512,128]{1,0:T(8,128)(2,1)S(1)}, bf16[512,128]{1,0:T(8,128)(2,1)S(1)}, bf16[512,256]{1,0:T(8,128)(2,1)S(1)}, bf16[512,256]{1,0:T(8,128)(2,1)S(1...) custom-call(s32[1,4]{1,0:T(1,128)S(1)} %copy-done.6, bf16[384,4096]{1,0:T(8,128)(2,1)S(1)} %copy-done.2, ...), custom_call_target="tpu_custom_call" | custom-call | flops 2300000000 | bytes 2097152 | tf_op jit(solution)/shard_map/probs/pallas_call | solution.py:72
  37.2 1.6 %lowrank.4.refs_4_ = f32[384,64]{1,0:T(8,128)S(1)} custom-call(s32[8]{0:T(128)S(1)} %dynamic-slice_bitcast_fusion.ids_ref, s32[384,1]{1,0:T(8,128)S(1)} %copy.14.adapter_ref, bf16[384,4096]{1,0:T(8,128)(2,1)S(1)} %copy-done.3, bf16[32,4608]{1,0:T(8,128)(2,1)S(1)} %get-tuple-element.54.refs_0_, bf16[32,4608]{1,0:T(8,128)(2,1)S(1)} %get-tuple-element.53.refs_1_.refs_8_, ...), custom_call_target="tpu_custom_call" | custom-call | flops 1700000000 | bytes 4915200 | tf_op jit(solution)/shard_map/lowrank/pallas_call | solution.py:114
  39.4 3.3 %collective-permute-done.2.refs_0_.refs_5_ = bf16[32,4608]{1,0:T(8,128)(2,1)S(1)} collective-permute-done((bf16[32,4608]{1,0:T(8,128)(2,1)S(1)}, bf16[32,4608]{1,0:T(8,128)(2,1)S(1)}, u32[]{:S(2)}, u32[]{:S(2)}) %collective-permute-start.2) | collective-permute-done | bytes 294944 | tf_op jit(solution)/shard_map/ppermute | solution.py:223
  42.7 1.8 %collective-permute-start.3 = (bf16[32,4608]{1,0:T(8,128)(2,1)S(1)}, bf16[32,4608]{1,0:T(8,128)(2,1)S(1)}, u32[]{:S(2)}, u32[]{:S(2)}) collective-permute-start(bf16[32,4608]{1,0:T(8,128)(2,1)S(1)} %collective-permute-done.2.refs_0_.refs_5_), channel_id=1, source_target_pairs={{0,4},{4,8},{8,12},{12,14},{14,10},{10,6},{6,2},{2,0},{1,5},{5,9},... | collective-permute-start | bytes 884744 | tf_op jit(solution)/shard_map/ppermute | solution.py:223
  44.5 1.6 %lowrank.5.refs_4_ = f32[384,64]{1,0:T(8,128)S(1)} custom-call(s32[8]{0:T(128)S(1)} %dynamic-slice_bitcast_fusion.ids_ref, s32[384,1]{1,0:T(8,128)S(1)} %copy.14.adapter_ref, bf16[384,4096]{1,0:T(8,128)(2,1)S(1)} %copy-done.3, bf16[32,4608]{1,0:T(8,128)(2,1)S(1)} %collective-permute-done.1.refs_0_.refs_3_, ...), custom_call_target="tpu_custom_call" | custom-call | flops 1700000000 | bytes 4325376 | tf_op jit(solution)/shard_map/lowrank/pallas_call | solution.py:114
  46.1 1.6 %lowrank.6.refs_2_ = f32[384,64]{1,0:T(8,128)S(1)} custom-call(s32[8]{0:T(128)S(1)} %dynamic-slice_bitcast_fusion.ids_ref, s32[384,1]{1,0:T(8,128)S(1)} %copy.14.adapter_ref, bf16[384,4096]{1,0:T(8,128)(2,1)S(1)} %copy-done.3, bf16[32,4608]{1,0:T(8,128)(2,1)S(1)} %collective-permute-done.2.refs_0_.refs_5_, ...), custom_call_target="tpu_custom_call" | custom-call | flops 1700000000 | bytes 4325376 | tf_op jit(solution)/shard_map/lowrank/pallas_call | solution.py:114
  47.7 2.8 %collective-permute-done.7.refs_1_.refs_15_ = bf16[32,4608]{1,0:T(8,128)(2,1)S(1)} collective-permute-done((bf16[32,4608]{1,0:T(8,128)(2,1)S(1)}, bf16[32,4608]{1,0:T(8,128)(2,1)S(1)}, u32[]{:S(2)}, u32[]{:S(2)}) %collective-permute-start.7) | collective-permute-done | bytes 294944 | tf_op jit(solution)/shard_map/ppermute | solution.py:226
  50.9 1.5 %lowrank.7.mine_ref = f32[384,64]{1,0:T(8,128)S(1)} custom-call(s32[8]{0:T(128)S(1)} %dynamic-slice_bitcast_fusion.ids_ref, s32[384,1]{1,0:T(8,128)S(1)} %copy.14.adapter_ref, bf16[384,4096]{1,0:T(8,128)(2,1)S(1)} %copy-done.3, bf16[32,4608]{1,0:T(8,128)(2,1)S(1)} %collective-permute-done.3.refs_0_.refs_7_, ...), custom_call_target="tpu_custom_call" | custom-call | flops 1700000000 | bytes 3735552 | tf_op jit(solution)/shard_map/lowrank/pallas_call | solution.py:114
  52.5 1.4 %collective-permute-done.14.theirs_ref = f32[384,64]{1,0:T(8,128)S(1)} collective-permute-done((f32[384,64]{1,0:T(8,128)S(1)}, f32[384,64]{1,0:T(8,128)S(1)}, u32[]{:S(2)}, u32[]{:S(2)}) %collective-permute-start.14) | collective-permute-done | bytes 98336 | tf_op jit(solution)/shard_map/ppermute | solution.py:247
  54.0 4.2 %attend.1 = bf16[384,4096]{1,0:T(8,128)(2,1)} custom-call(s32[8]{0:T(128)S(1)} %dynamic-slice_bitcast_fusion.ids_ref, s32[384,1]{1,0:T(8,128)S(1)} %copy.14.adapter_ref, f32[384,64]{1,0:T(8,128)S(1)} %lowrank.7.mine_ref, f32[384,64]{1,0:T(8,128)S(1)} %collective-permute-done.14.theirs_ref, bf16[384,512]{1,0:T(8,128)(2,1)S(1)} %copy-done, ...), custom_call_target="tpu_custom_call" | custom-call | tf_op jit(solution)/shard_map/attend/pallas_call | solution.py:182
  (32 shorter events, 3.8 us)
Async XLA Ops:
  1.1 12.3 %collective-permute-start.8 = (bf16[32,4608]{1,0:T(8,128)(2,1)S(1)}, bf16[32,4608]{1,0:T(8,128)(2,1)S(1)}, u32[]{:S(2)}, u32[]{:S(2)}) collective-permute-start(bf16[32,4608]{1,0:T(8,128)(2,1)S(1)} %get-tuple-element.53.refs_1_.refs_8_), channel_id=1, source_target_pairs={{0,4},{4,8},{8,12},{12,14},{14,10},{10,6},{6,2},{2,0},{1,5},{5,9},... | collective-permute-start | bytes 884744 | tf_op jit(solution)/shard_map/ppermute | solution.py:223
  4.2 11.2 %collective-permute-start.4 = (bf16[32,4608]{1,0:T(8,128)(2,1)S(1)}, bf16[32,4608]{1,0:T(8,128)(2,1)S(1)}, u32[]{:S(2)}, u32[]{:S(2)}) collective-permute-start(bf16[32,4608]{1,0:T(8,128)(2,1)S(1)} %get-tuple-element.53.refs_1_.refs_8_), channel_id=1, source_target_pairs={{4,0},{8,4},{12,8},{14,12},{10,14},{6,10},{2,6},{0,2},{5,1},{9,5},... | collective-permute-start | bytes 884744 | tf_op jit(solution)/shard_map/ppermute | solution.py:226
  4.2 16.2 %collective-permute-start.11 = (bf16[32,4608]{1,0:T(8,128)(2,1)S(1)}, bf16[32,4608]{1,0:T(8,128)(2,1)S(1)}, u32[]{:S(2)}, u32[]{:S(2)}) collective-permute-start(bf16[32,4608]{1,0:T(8,128)(2,1)S(1)} %get-tuple-element.54.refs_0_), channel_id=1, source_target_pairs={{4,0},{8,4},{12,8},{14,12},{10,14},{6,10},{2,6},{0,2},{5,1},{9,5},... | collective-permute-start | bytes 884744 | tf_op jit(solution)/shard_map/ppermute | solution.py:226
  6.2 14.3 %collective-permute-start = (bf16[32,4608]{1,0:T(8,128)(2,1)S(1)}, bf16[32,4608]{1,0:T(8,128)(2,1)S(1)}, u32[]{:S(2)}, u32[]{:S(2)}) collective-permute-start(bf16[32,4608]{1,0:T(8,128)(2,1)S(1)} %get-tuple-element.54.refs_0_), channel_id=1, source_target_pairs={{0,4},{4,8},{8,12},{12,14},{14,10},{10,6},{6,2},{2,0},{1,5},{5,9},... | collective-permute-start | bytes 884744 | tf_op jit(solution)/shard_map/ppermute | solution.py:223
  7.8 1.9 %copy-start.1 = (bf16[384,4096]{1,0:T(8,128)(2,1)S(1)}, bf16[384,4096]{1,0:T(8,128)(2,1)}, u32[]{:S(2)}) copy-start(bf16[384,4096]{1,0:T(8,128)(2,1)} %q_ref.7) | copy-start | bytes 9437188
  9.7 1.0 %copy-start.4 = (bf16[384,512]{1,0:T(8,128)(2,1)S(1)}, bf16[384,512]{1,0:T(8,128)(2,1)}, u32[]{:S(2)}) copy-start(bf16[384,512]{1,0:T(8,128)(2,1)} %k_ref.7) | copy-start | bytes 1179652
  10.7 0.7 %copy-start.6 = (s32[1,4]{1,0:T(1,128)S(1)}, s32[1,4]{1,0:T(1,128)}, u32[]{:S(2)}) copy-start(s32[1,4]{1,0:T(1,128)} %lengths_ref.7) | copy-start | bytes 52
  11.3 11.2 %copy-start.2 = (bf16[384,4096]{1,0:T(8,128)(2,1)S(1)}, bf16[384,4096]{1,0:T(8,128)(2,1)}, u32[]{:S(2)}) copy-start(bf16[384,4096]{1,0:T(8,128)(2,1)} %q_ref.7) | copy-start | bytes 9437188
  11.3 11.2 %copy-start.5 = (bf16[384,512]{1,0:T(8,128)(2,1)S(1)}, bf16[384,512]{1,0:T(8,128)(2,1)}, u32[]{:S(2)}) copy-start(bf16[384,512]{1,0:T(8,128)(2,1)} %k_ref.7) | copy-start | bytes 1179652
  13.4 13.2 %collective-permute-start.9 = (bf16[32,4608]{1,0:T(8,128)(2,1)S(1)}, bf16[32,4608]{1,0:T(8,128)(2,1)S(1)}, u32[]{:S(2)}, u32[]{:S(2)}) collective-permute-start(bf16[32,4608]{1,0:T(8,128)(2,1)S(1)} %collective-permute-done.8.refs_3_.refs_0_.refs_9_), channel_id=1, source_target_pairs={{0,4},{4,8},{8,12},{12,14},{14,10},{10,6},{6,2},{2,0},{1,5},{5,9},... | collective-permute-start | bytes 884744 | tf_op jit(solution)/shard_map/ppermute | solution.py:223
  15.4 12.8 %collective-permute-start.5 = (bf16[32,4608]{1,0:T(8,128)(2,1)S(1)}, bf16[32,4608]{1,0:T(8,128)(2,1)S(1)}, u32[]{:S(2)}, u32[]{:S(2)}) collective-permute-start(bf16[32,4608]{1,0:T(8,128)(2,1)S(1)} %collective-permute-done.4.refs_5_.refs_1_.refs_10_), channel_id=1, source_target_pairs={{4,0},{8,4},{12,8},{14,12},{10,14},{6,10},{2,6},{0,2},{5,1},{9,5},... | collective-permute-start | bytes 884744 | tf_op jit(solution)/shard_map/ppermute | solution.py:226
  20.4 12.6 %collective-permute-start.12 = (bf16[32,4608]{1,0:T(8,128)(2,1)S(1)}, bf16[32,4608]{1,0:T(8,128)(2,1)S(1)}, u32[]{:S(2)}, u32[]{:S(2)}) collective-permute-start(bf16[32,4608]{1,0:T(8,128)(2,1)S(1)} %collective-permute-done.11.refs_4_.refs_1_.refs_2_), channel_id=1, source_target_pairs={{4,0},{8,4},{12,8},{14,12},{10,14},{6,10},{2,6},{0,2},{5,1},{9,5},... | collective-permute-start | bytes 884744 | tf_op jit(solution)/shard_map/ppermute | solution.py:226
  20.4 12.6 %collective-permute-start.1 = (bf16[32,4608]{1,0:T(8,128)(2,1)S(1)}, bf16[32,4608]{1,0:T(8,128)(2,1)S(1)}, u32[]{:S(2)}, u32[]{:S(2)}) collective-permute-start(bf16[32,4608]{1,0:T(8,128)(2,1)S(1)} %collective-permute-done.refs_2_.refs_0_.refs_1_), channel_id=1, source_target_pairs={{0,4},{4,8},{8,12},{12,14},{14,10},{10,6},{6,2},{2,0},{1,5},{5,9},... | collective-permute-start | bytes 884744 | tf_op jit(solution)/shard_map/ppermute | solution.py:223
  26.6 10.6 %copy-start.3 = (bf16[384,4096]{1,0:T(8,128)(2,1)S(1)}, bf16[384,4096]{1,0:T(8,128)(2,1)}, u32[]{:S(2)}) copy-start(bf16[384,4096]{1,0:T(8,128)(2,1)} %x_ref.7) | copy-start | bytes 9437188
  26.6 19.5 %collective-permute-start.10 = (bf16[32,4608]{1,0:T(8,128)(2,1)S(1)}, bf16[32,4608]{1,0:T(8,128)(2,1)S(1)}, u32[]{:S(2)}, u32[]{:S(2)}) collective-permute-start(bf16[32,4608]{1,0:T(8,128)(2,1)S(1)} %collective-permute-done.9.refs_6_.refs_1_.refs_11_), channel_id=1, source_target_pairs={{0,4},{4,8},{8,12},{12,14},{14,10},{10,6},{6,2},{2,0},{1,5},{5,9},... | collective-permute-start | bytes 884744 | tf_op jit(solution)/shard_map/ppermute | solution.py:223
  28.3 11.1 %collective-permute-start.6 = (bf16[32,4608]{1,0:T(8,128)(2,1)S(1)}, bf16[32,4608]{1,0:T(8,128)(2,1)S(1)}, u32[]{:S(2)}, u32[]{:S(2)}) collective-permute-start(bf16[32,4608]{1,0:T(8,128)(2,1)S(1)} %collective-permute-done.5.refs_7_.refs_3_.refs_12_), channel_id=1, source_target_pairs={{4,0},{8,4},{12,8},{14,12},{10,14},{6,10},{2,6},{0,2},{5,1},{9,5},... | collective-permute-start | bytes 884744 | tf_op jit(solution)/shard_map/ppermute | solution.py:226
  33.1 13.1 %collective-permute-start.13 = (bf16[32,4608]{1,0:T(8,128)(2,1)S(1)}, bf16[32,4608]{1,0:T(8,128)(2,1)S(1)}, u32[]{:S(2)}, u32[]{:S(2)}) collective-permute-start(bf16[32,4608]{1,0:T(8,128)(2,1)S(1)} %collective-permute-done.12.refs_2_.refs_1_.refs_4_), channel_id=1, source_target_pairs={{4,0},{8,4},{12,8},{14,12},{10,14},{6,10},{2,6},{0,2},{5,1},{9,5},... | collective-permute-start | bytes 884744 | tf_op jit(solution)/shard_map/ppermute | solution.py:226
  33.1 9.7 %collective-permute-start.2 = (bf16[32,4608]{1,0:T(8,128)(2,1)S(1)}, bf16[32,4608]{1,0:T(8,128)(2,1)S(1)}, u32[]{:S(2)}, u32[]{:S(2)}) collective-permute-start(bf16[32,4608]{1,0:T(8,128)(2,1)S(1)} %collective-permute-done.1.refs_0_.refs_3_), channel_id=1, source_target_pairs={{0,4},{4,8},{8,12},{12,14},{14,10},{10,6},{6,2},{2,0},{1,5},{5,9},... | collective-permute-start | bytes 884744 | tf_op jit(solution)/shard_map/ppermute | solution.py:223
  39.4 11.2 %collective-permute-start.7 = (bf16[32,4608]{1,0:T(8,128)(2,1)S(1)}, bf16[32,4608]{1,0:T(8,128)(2,1)S(1)}, u32[]{:S(2)}, u32[]{:S(2)}) collective-permute-start(bf16[32,4608]{1,0:T(8,128)(2,1)S(1)} %collective-permute-done.6.refs_3_.refs_14_), channel_id=1, source_target_pairs={{4,0},{8,4},{12,8},{14,12},{10,14},{6,10},{2,6},{0,2},{5,1},{9,5},... | collective-permute-start | bytes 884744 | tf_op jit(solution)/shard_map/ppermute | solution.py:226
  42.7 8.2 %collective-permute-start.3 = (bf16[32,4608]{1,0:T(8,128)(2,1)S(1)}, bf16[32,4608]{1,0:T(8,128)(2,1)S(1)}, u32[]{:S(2)}, u32[]{:S(2)}) collective-permute-start(bf16[32,4608]{1,0:T(8,128)(2,1)S(1)} %collective-permute-done.2.refs_0_.refs_5_), channel_id=1, source_target_pairs={{0,4},{4,8},{8,12},{12,14},{14,10},{10,6},{6,2},{2,0},{1,5},{5,9},... | collective-permute-start | bytes 884744 | tf_op jit(solution)/shard_map/ppermute | solution.py:223
  50.9 3.0 %copy-start = (bf16[384,512]{1,0:T(8,128)(2,1)S(1)}, bf16[384,512]{1,0:T(8,128)(2,1)}, u32[]{:S(2)}) copy-start(bf16[384,512]{1,0:T(8,128)(2,1)} %base_ref.1) | copy-start | bytes 1179652
  52.4 1.5 %collective-permute-start.14 = (f32[384,64]{1,0:T(8,128)S(1)}, f32[384,64]{1,0:T(8,128)S(1)}, u32[]{:S(2)}, u32[]{:S(2)}) collective-permute-start(f32[384,64]{1,0:T(8,128)S(1)} %lowrank.7.mine_ref), channel_id=1, source_target_pairs={{0,1},{1,0},{2,3},{3,2},{4,5},{5,4},{6,7},{7,6},{8,9},{9,8},{10,11... | collective-permute-start | bytes 294920 | tf_op jit(solution)/shard_map/ppermute | solution.py:247

commit v4 on v3

--- a/solution.py
+++ b/solution.py
@@ -88,10 +88,10 @@
     )(lengths, queries, keys, *after)
 
 
-def lowrank_kernel(at, count, ids_ref, adapter_ref, x_ref, *refs):
+def lowrank_kernel(at, count, place_ref, x_ref, *refs):
     w_refs, out_ref = refs[:count], refs[-1]
     before_ref = refs[count] if at > 0 else None
-    adapter = adapter_ref[...]
+    place = place_ref[...]
     rows, features = x_ref.shape
     half = w_refs[0].shape[0]
     stacked = jnp.concatenate([w_ref[:, :features] for w_ref in w_refs], axis=0)
@@ -99,22 +99,22 @@
     sums = [jnp.zeros((rows, half), jnp.float32)] * 2
     for i in range(count):
         part = product[:, i * half : (i + 1) * half]
-        sums[i % 2] = sums[i % 2] + jnp.where(adapter == ids_ref[at + i // 2], part, 0.0)
+        sums[i % 2] = sums[i % 2] + jnp.where(place == at + i // 2, part, 0.0)
     total = jnp.concatenate(sums, axis=1)
     out_ref[...] = total if before_ref is None else total + before_ref[...]
 
 
-def lowrank_of(ids, at, adapter_of_row, x, before, pieces, after):
+def lowrank_of(at, place, x, before, pieces, after):
     rows, features = x.shape
     rank = 2 * pieces[0].shape[0]
-    operands = [ids, adapter_of_row, x] + pieces + ([] if before is None else [before])
+    operands = [place, x] + pieces + ([] if before is None else [before])
     used = len(operands)
     operands = operands + after
     size = 2 * sum(p.size for p in pieces)
     return pl.pallas_call(
         functools.partial(lowrank_kernel, at, len(pieces)),
         out_shape=jax.ShapeDtypeStruct((rows, rank), jnp.float32),
-        in_specs=[SMEM] + [VMEM] * (used - 1) + [pl.BlockSpec(memory_space=pl.ANY)] * len(after),
+        in_specs=[VMEM] * used + [pl.BlockSpec(memory_space=pl.ANY)] * len(after),
         out_specs=VMEM,
         cost_estimate=pl.CostEstimate(
             flops=1_700_000_000, bytes_accessed=2 * rows * features + size, transcendentals=0
@@ -124,7 +124,7 @@
     )(*operands)
 
 
-def attend_kernel(kv_heads, n, ids_ref, adapter_ref, mine_ref, theirs_ref, base_ref, *refs):
+def attend_kernel(kv_heads, n, place_ref, mine_ref, theirs_ref, base_ref, *refs):
     rows, value_portion = base_ref.shape
     tiles = windows(rows)
     low_refs, high_refs = refs[:n], refs[n : 2 * n]
@@ -132,62 +132,60 @@
     out_ref, block, sems = refs[2 * n + kv_heads * len(tiles) :]
     rank = mine_ref.shape[1]
     features = low_refs[0].shape[1] - value_portion
-    adapter = adapter_ref[...]
+    place = place_ref[...]
     lowrank = (mine_ref[...] + theirs_ref[...]).astype(jnp.bfloat16)
     twice = jnp.concatenate([lowrank, lowrank], axis=1)
-    second = lax.broadcasted_iota(jnp.int32, twice.shape, 1) >= rank
+    second = (lax.broadcasted_iota(jnp.int32, twice.shape, 1) >= rank).astype(jnp.int32)
+    offset = place - second
     spread = jnp.concatenate(
-        [
-            jnp.where(adapter == jnp.where(second, ids_ref[i + 1], ids_ref[i]), twice, jnp.zeros_like(twice))
-            for i in range(0, n, 2)
-        ],
-        axis=1,
-    )
+        [jnp.where(offset == i, twice, jnp.zeros_like(twice)) for i in range(0, n, 2)], axis=1
+    )
+    up = jnp.concatenate(
+        [ref[:, features:] for pair in zip(low_refs, high_refs) for ref in pair], axis=0
+    )
+    delta = jnp.dot(spread, up, preferred_element_type=jnp.float32).astype(jnp.bfloat16)
+    values = (
+        base_ref[...].astype(jnp.float32) + adapter_scale * delta.astype(jnp.float32)
+    ).astype(jnp.bfloat16)
     copies = []
     wide = GROUP * HEAD_SIZE
+    done = 0
     for kv in range(kv_heads):
         columns = slice(kv * HEAD_SIZE, (kv + 1) * HEAD_SIZE)
-        held = slice(features + kv * HEAD_SIZE, features + (kv + 1) * HEAD_SIZE)
-        up = jnp.concatenate([ref[:, held] for pair in zip(low_refs, high_refs) for ref in pair], axis=0)
-        delta = jnp.dot(spread, up, preferred_element_type=jnp.float32).astype(jnp.bfloat16)
-        values = (
-            base_ref[:, columns].astype(jnp.float32) + adapter_scale * delta.astype(jnp.float32)
-        ).astype(jnp.bfloat16)
         for i, (start, first, width) in enumerate(tiles):
             mixed = jnp.dot(
                 p_refs[kv * len(tiles) + i][...],
-                values[first : first + width, :],
+                values[first : first + width, columns],
                 preferred_element_type=jnp.float32,
             ).astype(jnp.bfloat16)
             for head in range(GROUP):
                 at = kv * wide + head * HEAD_SIZE
                 block[start : start + TILE, at : at + HEAD_SIZE] = mixed[head * TILE : (head + 1) * TILE, :]
-        copy = pltpu.make_async_copy(
-            block.at[:, kv * wide : (kv + 1) * wide],
-            out_ref.at[:, kv * wide : (kv + 1) * wide],
-            sems.at[kv],
-        )
-        copy.start()
-        copies.append(copy)
+            if 2 * (i + 1) in (len(tiles), 2 * len(tiles)):
+                part = slice(0, rows // 2) if 2 * (i + 1) == len(tiles) else slice(rows // 2, rows)
+                span = slice(kv * wide, (kv + 1) * wide)
+                copy = pltpu.make_async_copy(block.at[part, span], out_ref.at[part, span], sems.at[done])
+                copy.start()
+                copies.append(copy)
+                done += 1
     for copy in copies:
         copy.wait()
 
 
-def attend(ids, adapter_of_row, mine, theirs, base, lows, highs, probs):
+def attend(place, mine, theirs, base, lows, highs, probs):
     rows, value_portion = base.shape
     kv_heads = value_portion // HEAD_SIZE
     wide = kv_heads * GROUP * HEAD_SIZE
     flat = [p for per_head in probs for p in per_head]
-    held = 2 * sum(a.size for a in lows + highs + flat)
     return pl.pallas_call(
         functools.partial(attend_kernel, kv_heads, len(lows)),
         out_shape=jax.ShapeDtypeStruct((rows, wide), jnp.bfloat16),
-        in_specs=[SMEM] + [VMEM] * (4 + len(lows) + len(highs) + len(flat)),
+        in_specs=[VMEM] * (4 + len(lows) + len(highs) + len(flat)),
         out_specs=pl.BlockSpec(memory_space=pl.ANY),
-        scratch_shapes=[pltpu.VMEM((rows, wide), jnp.bfloat16), pltpu.SemaphoreType.DMA((kv_heads,))],
+        scratch_shapes=[pltpu.VMEM((rows, wide), jnp.bfloat16), pltpu.SemaphoreType.DMA((2 * kv_heads,))],
         compiler_params=pltpu.CompilerParams(vmem_limit_bytes=12 * 2**20),
         name="attend",
-    )(ids, adapter_of_row, mine, theirs, base, *lows, *highs, *flat)
+    )(place, mine, theirs, base, *lows, *highs, *flat)
 
 
 def on_device(
@@ -209,7 +207,10 @@
     table = np.zeros((n, n), np.int32)
     for place, replica in enumerate(order):
         table[replica] = [order[(place - d) % n] for d in distances]
-    ids = lax.dynamic_index_in_dim(jnp.asarray(table), lax.axis_index("rep"), 0, keepdims=False)
+    ids = lax.dynamic_slice_in_dim(jnp.asarray(table), lax.axis_index("rep"), 1, 0)
+    place = jnp.sum(
+        jnp.where(adapter_of_row == ids, jnp.arange(n, dtype=jnp.int32)[None, :], 0), axis=1, keepdims=True
+    )
 
     down = jnp.swapaxes(adapter_down_weight[0], 0, 1)
     both = jnp.concatenate([down, adapter_up_weight[0]], axis=1)
@@ -243,11 +244,10 @@
         after = arrivals[kv_heads - 1] if lo == 0 else []
         if hi == n:
             after = [p[0] for p in probs]
-        partial = lowrank_of(ids, lo, adapter_of_row, normed_token_rows, partial, pieces, after)
+        partial = lowrank_of(lo, place, normed_token_rows, partial, pieces, after)
     other = lax.ppermute(partial, "tp", [(0, 1), (1, 0)])
     return attend(
-        ids,
-        adapter_of_row,
+        place,
         partial,
         other,
         base_value_rows,

time: 58.6 us -> 56.6 us (0.966)
  Pallas kernels: 18.8 us -> 15.1 us
  waiting for transfers between devices: 17.9 us -> 19.5 us
  other arithmetic: 1.11 us -> 1.89 us
  local copies, waits for them, and re-layouts: 5.07 us -> 4.36 us
    pallas_call x4, Pallas kernels: 6.32 us -> 4.11 us  [lowrank_of(): pl.pallas_call(functools.partial(lowrank_kernel, at, len(pieces)), out_sh...]
    ppermute x7, waiting for transfers between devices: 12.8 us -> 14.4 us  [pass_round(): moving_back = lax.ppermute(moving_back, 'rep', back)]
    pallas_call x1, Pallas kernels: 4.25 us -> 2.79 us  [attend(): pl.pallas_call(functools.partial(attend_kernel, kv_heads, len(lows)), out...]
    unnamed x15 -> x14, local copies, waits for them, and re-layouts: 4.37 us -> 3.56 us
    squeeze x1 -> x0, local copies, waits for them, and re-layouts: 0.7 us -> none  [on_device(): lax.dynamic_index_in_dim(jnp.asarray(table), lax.axis_index('rep'), 0, ke...]
    unnamed x0 -> x1, other arithmetic: none -> 0.7 us
    eq x0 -> x1, local copies, waits for them, and re-layouts: none -> 0.69 us  [on_device(): adapter_of_row == ids]
  transfers between devices with their start and end apart: 15 -> 15, of which waited for: 7 -> 8; matrix products, arithmetic and copies ran while one was open for 3% -> 3% of each run, Pallas kernels for 22% -> 20%
where the time goes in v4:
time: 56.6 us; the launch traced here: 56.4 us
  waiting for transfers between devices  19.5 us (34%)
  starting transfers between devices  15.2 us (27%)
  Pallas kernels  15.1 us (27%)
  local copies, waits for them, and re-layouts  4.36 us (8%)
  other arithmetic  1.89 us (3%)
    ppermute x7, waiting for transfers between devices, pass_round(): moving_back = lax.ppermute(moving_back, 'rep', back)  14.4 us
    ppermute x7, starting transfers between devices, pass_round(): moving_ahead = lax.ppermute(moving_ahead, 'rep', ahead)  12.7 us
    pallas_call x4, Pallas kernels, probs_of(): pl.pallas_call(functools.partial(probs_kernel, len(after)), grid=(1,), ou...  8.21 us
    pallas_call x4, Pallas kernels, lowrank_of(): pl.pallas_call(functools.partial(lowrank_kernel, at, len(pieces)), out_sh...  4.11 us
    ppermute x7, waiting for transfers between devices, pass_round(): moving_ahead = lax.ppermute(moving_ahead, 'rep', ahead)  3.7 us
    unnamed x14, local copies, waits for them, and re-layouts  3.56 us
    pallas_call x1, Pallas kernels, attend(): pl.pallas_call(functools.partial(attend_kernel, kv_heads, len(lows)), out...  2.79 us
    ppermute x7, starting transfers between devices, pass_round(): moving_back = lax.ppermute(moving_back, 'rep', back)  2.45 us
  transfers between devices with their start and end apart: 15, of which 8 were waited for; matrix products, arithmetic and copies ran while one was open for 3% of the time, Pallas kernels for 20%

profile of v4, /device:TPU:0, one launch (start us, length us, event | category | flops | bytes accessed | tf_op | source)
XLA Modules:
  0.0 56.4 jit_solution(17716310359895373009)
XLA Ops:
  0.0 1.1 %pad_maximum_fusion = (bf16[32,4608]{1,0:T(8,128)(2,1)S(1)}, bf16[32,4608]{1,0:T(8,128)(2,1)S(1)}) fusion(bf16[64,512]{1,0:T(8,128)(2,1)} %bitcast.7, bf16[64,4096]{1,0:T(8,128)(2,1)} %bitcast.6), kind=kLoop, calls=%fused_computation.3 | loop fusion | flops 1179648 | bytes 1179648 | tf_op jit(solution)/shard_map/concatenate | solution.py:216
  1.1 3.1 %collective-permute-start.8 = (bf16[32,4608]{1,0:T(8,128)(2,1)S(1)}, bf16[32,4608]{1,0:T(8,128)(2,1)S(1)}, u32[]{:S(2)}, u32[]{:S(2)}) collective-permute-start(bf16[32,4608]{1,0:T(8,128)(2,1)S(1)} %get-tuple-element.53.refs_1_.refs_8_), channel_id=1, source_target_pairs={{0,4},{4,8},{8,12},{12,14},{14,10},{10,6},{6,2},{2,0},{1,5},{5,9},... | collective-permute-start | bytes 884744 | tf_op jit(solution)/shard_map/ppermute | solution.py:224
  4.2 2.0 %collective-permute-start.11 = (bf16[32,4608]{1,0:T(8,128)(2,1)S(1)}, bf16[32,4608]{1,0:T(8,128)(2,1)S(1)}, u32[]{:S(2)}, u32[]{:S(2)}) collective-permute-start(bf16[32,4608]{1,0:T(8,128)(2,1)S(1)} %get-tuple-element.54.refs_0_), channel_id=1, source_target_pairs={{4,0},{8,4},{12,8},{14,12},{10,14},{6,10},{2,6},{0,2},{5,1},{9,5},... | collective-permute-start | bytes 884744 | tf_op jit(solution)/shard_map/ppermute | solution.py:227
  7.9 1.9 %copy-done.1 = bf16[384,4096]{1,0:T(8,128)(2,1)S(1)} copy-done((bf16[384,4096]{1,0:T(8,128)(2,1)S(1)}, bf16[384,4096]{1,0:T(8,128)(2,1)}, u32[]{:S(2)}) %copy-start.1) | copy-done | bytes 3145752
  9.7 1.0 %copy-done.4 = bf16[384,512]{1,0:T(8,128)(2,1)S(1)} copy-done((bf16[384,512]{1,0:T(8,128)(2,1)S(1)}, bf16[384,512]{1,0:T(8,128)(2,1)}, u32[]{:S(2)}) %copy-start.4) | copy-done | bytes 393240
  11.4 2.1 %probs.4 = (bf16[512,128]{1,0:T(8,128)(2,1)S(1)}, bf16[512,128]{1,0:T(8,128)(2,1)S(1)}, bf16[512,256]{1,0:T(8,128)(2,1)S(1)}, bf16[512,256]{1,0:T(8,128)(2,1)S(1...) custom-call(s32[1,4]{1,0:T(1,128)S(1)} %copy-done.6, bf16[384,4096]{1,0:T(8,128)(2,1)S(1)} %copy-done.1, ...), custom_call_target="tpu_custom_call" | custom-call | flops 2300000000 | bytes 2097152 | tf_op jit(solution)/shard_map/probs/pallas_call | solution.py:72
  13.5 2.0 %collective-permute-start.9 = (bf16[32,4608]{1,0:T(8,128)(2,1)S(1)}, bf16[32,4608]{1,0:T(8,128)(2,1)S(1)}, u32[]{:S(2)}, u32[]{:S(2)}) collective-permute-start(bf16[32,4608]{1,0:T(8,128)(2,1)S(1)} %collective-permute-done.8.refs_3_.refs_0_.refs_9_), channel_id=1, source_target_pairs={{0,4},{4,8},{8,12},{12,14},{14,10},{10,6},{6,2},{2,0},{1,5},{5,9},... | collective-permute-start | bytes 884744 | tf_op jit(solution)/shard_map/ppermute | solution.py:224
  15.5 4.9 %collective-permute-done.11.refs_4_.refs_1_.refs_2_ = bf16[32,4608]{1,0:T(8,128)(2,1)S(1)} collective-permute-done((bf16[32,4608]{1,0:T(8,128)(2,1)S(1)}, bf16[32,4608]{1,0:T(8,128)(2,1)S(1)}, u32[]{:S(2)}, u32[]{:S(2)}) %collective-permute-start.11) | collective-permute-done | bytes 294944 | tf_op jit(solution)/shard_map/ppermute | solution.py:227
  20.4 2.0 %collective-permute-start.1 = (bf16[32,4608]{1,0:T(8,128)(2,1)S(1)}, bf16[32,4608]{1,0:T(8,128)(2,1)S(1)}, u32[]{:S(2)}, u32[]{:S(2)}) collective-permute-start(bf16[32,4608]{1,0:T(8,128)(2,1)S(1)} %collective-permute-done.refs_2_.refs_0_.refs_1_), channel_id=1, source_target_pairs={{0,4},{4,8},{8,12},{12,14},{14,10},{10,6},{6,2},{2,0},{1,5},{5,9},... | collective-permute-start | bytes 884744 | tf_op jit(solution)/shard_map/ppermute | solution.py:224
  22.5 2.1 %probs.5 = (bf16[512,128]{1,0:T(8,128)(2,1)S(1)}, bf16[512,128]{1,0:T(8,128)(2,1)S(1)}, bf16[512,256]{1,0:T(8,128)(2,1)S(1)}, bf16[512,256]{1,0:T(8,128)(2,1)S(1...) custom-call(s32[1,4]{1,0:T(1,128)S(1)} %copy-done.6, bf16[384,4096]{1,0:T(8,128)(2,1)S(1)} %copy-done.2, ...), custom_call_target="tpu_custom_call" | custom-call | flops 2300000000 | bytes 2097152 | tf_op jit(solution)/shard_map/probs/pallas_call | solution.py:72
  24.5 2.1 %probs.6 = (bf16[512,128]{1,0:T(8,128)(2,1)S(1)}, bf16[512,128]{1,0:T(8,128)(2,1)S(1)}, bf16[512,256]{1,0:T(8,128)(2,1)S(1)}, bf16[512,256]{1,0:T(8,128)(2,1)S(1...) custom-call(s32[1,4]{1,0:T(1,128)S(1)} %copy-done.6, bf16[384,4096]{1,0:T(8,128)(2,1)S(1)} %copy-done.2, ...), custom_call_target="tpu_custom_call" | custom-call | flops 2300000000 | bytes 2097152 | tf_op jit(solution)/shard_map/probs/pallas_call | solution.py:72
  26.6 1.6 %collective-permute-start.10 = (bf16[32,4608]{1,0:T(8,128)(2,1)S(1)}, bf16[32,4608]{1,0:T(8,128)(2,1)S(1)}, u32[]{:S(2)}, u32[]{:S(2)}) collective-permute-start(bf16[32,4608]{1,0:T(8,128)(2,1)S(1)} %collective-permute-done.9.refs_6_.refs_1_.refs_11_), channel_id=1, source_target_pairs={{0,4},{4,8},{8,12},{12,14},{14,10},{10,6},{6,2},{2,0},{1,5},{5,9},... | collective-permute-start | bytes 884744 | tf_op jit(solution)/shard_map/ppermute | solution.py:224
  28.7 4.4 %collective-permute-done.12.refs_2_.refs_1_.refs_4_ = bf16[32,4608]{1,0:T(8,128)(2,1)S(1)} collective-permute-done((bf16[32,4608]{1,0:T(8,128)(2,1)S(1)}, bf16[32,4608]{1,0:T(8,128)(2,1)S(1)}, u32[]{:S(2)}, u32[]{:S(2)}) %collective-permute-start.12) | collective-permute-done | bytes 294944 | tf_op jit(solution)/shard_map/ppermute | solution.py:227
  33.1 2.0 %collective-permute-start.2 = (bf16[32,4608]{1,0:T(8,128)(2,1)S(1)}, bf16[32,4608]{1,0:T(8,128)(2,1)S(1)}, u32[]{:S(2)}, u32[]{:S(2)}) collective-permute-start(bf16[32,4608]{1,0:T(8,128)(2,1)S(1)} %collective-permute-done.1.refs_0_.refs_3_), channel_id=1, source_target_pairs={{0,4},{4,8},{8,12},{12,14},{14,10},{10,6},{6,2},{2,0},{1,5},{5,9},... | collective-permute-start | bytes 884744 | tf_op jit(solution)/shard_map/ppermute | solution.py:224
  35.1 2.1 %probs.7 = (bf16[512,128]{1,0:T(8,128)(2,1)S(1)}, bf16[512,128]{1,0:T(8,128)(2,1)S(1)}, bf16[512,256]{1,0:T(8,128)(2,1)S(1)}, bf16[512,256]{1,0:T(8,128)(2,1)S(1...) custom-call(s32[1,4]{1,0:T(1,128)S(1)} %copy-done.6, bf16[384,4096]{1,0:T(8,128)(2,1)S(1)} %copy-done.2, ...), custom_call_target="tpu_custom_call" | custom-call | flops 2300000000 | bytes 2097152 | tf_op jit(solution)/shard_map/probs/pallas_call | solution.py:72
  37.2 1.1 %lowrank.4.refs_4_ = f32[384,64]{1,0:T(8,128)S(1)} custom-call(s32[384,1]{1,0:T(8,128)S(1)} %broadcast_in_dim.19.place_ref, bf16[384,4096]{1,0:T(8,128)(2,1)S(1)} %copy-done.3, bf16[32,4608]{1,0:T(8,128)(2,1)S(1)} %get-tuple-element.54.refs_0_, bf16[32,4608]{1,0:T(8,128)(2,1)S(1)} %get-tuple-element.53.refs_1_.refs_8_, ...), custom_call_target="tpu_custom_call" | custom-call | flops 1700000000 | bytes 4915200 | tf_op jit(solution)/shard_map/lowrank/pallas_call | solution.py:114
  38.2 1.2 %collective-permute-done.6.refs_3_.refs_14_ = bf16[32,4608]{1,0:T(8,128)(2,1)S(1)} collective-permute-done((bf16[32,4608]{1,0:T(8,128)(2,1)S(1)}, bf16[32,4608]{1,0:T(8,128)(2,1)S(1)}, u32[]{:S(2)}, u32[]{:S(2)}) %collective-permute-start.6) | collective-permute-done | bytes 294944 | tf_op jit(solution)/shard_map/ppermute | solution.py:227
  39.4 3.3 %collective-permute-done.2.refs_0_.refs_5_ = bf16[32,4608]{1,0:T(8,128)(2,1)S(1)} collective-permute-done((bf16[32,4608]{1,0:T(8,128)(2,1)S(1)}, bf16[32,4608]{1,0:T(8,128)(2,1)S(1)}, u32[]{:S(2)}, u32[]{:S(2)}) %collective-permute-start.2) | collective-permute-done | bytes 294944 | tf_op jit(solution)/shard_map/ppermute | solution.py:224
  42.7 1.8 %collective-permute-start.3 = (bf16[32,4608]{1,0:T(8,128)(2,1)S(1)}, bf16[32,4608]{1,0:T(8,128)(2,1)S(1)}, u32[]{:S(2)}, u32[]{:S(2)}) collective-permute-start(bf16[32,4608]{1,0:T(8,128)(2,1)S(1)} %collective-permute-done.2.refs_0_.refs_5_), channel_id=1, source_target_pairs={{0,4},{4,8},{8,12},{12,14},{14,10},{10,6},{6,2},{2,0},{1,5},{5,9},... | collective-permute-start | bytes 884744 | tf_op jit(solution)/shard_map/ppermute | solution.py:224
  44.5 1.0 %lowrank.5.refs_4_ = f32[384,64]{1,0:T(8,128)S(1)} custom-call(s32[384,1]{1,0:T(8,128)S(1)} %broadcast_in_dim.19.place_ref, bf16[384,4096]{1,0:T(8,128)(2,1)S(1)} %copy-done.3, bf16[32,4608]{1,0:T(8,128)(2,1)S(1)} %collective-permute-done.1.refs_0_.refs_3_, bf16[32,4608]{1,0:T(8,128)(2,1)S(1)} %collective-permute-done.9.refs_6_.refs_1_.refs_11_, ...), custom_call_target="tpu_custom_call" | custom-call | flops 1700000000 | bytes 4325376 | tf_op jit(solution)/shard_map/lowrank/pallas_call | solution.py:114
  45.7 1.0 %lowrank.6.refs_2_ = f32[384,64]{1,0:T(8,128)S(1)} custom-call(s32[384,1]{1,0:T(8,128)S(1)} %broadcast_in_dim.19.place_ref, bf16[384,4096]{1,0:T(8,128)(2,1)S(1)} %copy-done.3, bf16[32,4608]{1,0:T(8,128)(2,1)S(1)} %collective-permute-done.2.refs_0_.refs_5_, bf16[32,4608]{1,0:T(8,128)(2,1)S(1)} %collective-permute-done.10.refs_1_.refs_13_, ...), custom_call_target="tpu_custom_call" | custom-call | flops 1700000000 | bytes 4325376 | tf_op jit(solution)/shard_map/lowrank/pallas_call | solution.py:114
  46.8 3.8 %collective-permute-done.7.refs_1_.refs_15_ = bf16[32,4608]{1,0:T(8,128)(2,1)S(1)} collective-permute-done((bf16[32,4608]{1,0:T(8,128)(2,1)S(1)}, bf16[32,4608]{1,0:T(8,128)(2,1)S(1)}, u32[]{:S(2)}, u32[]{:S(2)}) %collective-permute-start.7) | collective-permute-done | bytes 294944 | tf_op jit(solution)/shard_map/ppermute | solution.py:227
  52.0 1.4 %collective-permute-done.14.theirs_ref = f32[384,64]{1,0:T(8,128)S(1)} collective-permute-done((f32[384,64]{1,0:T(8,128)S(1)}, f32[384,64]{1,0:T(8,128)S(1)}, u32[]{:S(2)}, u32[]{:S(2)}) %collective-permute-start.14) | collective-permute-done | bytes 98336 | tf_op jit(solution)/shard_map/ppermute | solution.py:248
  53.4 2.8 %attend.1 = bf16[384,4096]{1,0:T(8,128)(2,1)} custom-call(s32[384,1]{1,0:T(8,128)S(1)} %broadcast_in_dim.19.place_ref, f32[384,64]{1,0:T(8,128)S(1)} %lowrank.7.mine_ref, f32[384,64]{1,0:T(8,128)S(1)} %collective-permute-done.14.theirs_ref, bf16[384,512]{1,0:T(8,128)(2,1)S(1)} %copy-done, bf16[32,4608]{1,0:T(8,128)(2,1)S(1)} %get-tuple-element.54.refs_0_, ...), custom_call_target="tpu_custom_call" | custom-call | tf_op jit(solution)/shard_map/attend/pallas_call | solution.py:180
  (34 shorter events, 4.4 us)
Async XLA Ops:
  1.1 12.3 %collective-permute-start.8 = (bf16[32,4608]{1,0:T(8,128)(2,1)S(1)}, bf16[32,4608]{1,0:T(8,128)(2,1)S(1)}, u32[]{:S(2)}, u32[]{:S(2)}) collective-permute-start(bf16[32,4608]{1,0:T(8,128)(2,1)S(1)} %get-tuple-element.53.refs_1_.refs_8_), channel_id=1, source_target_pairs={{0,4},{4,8},{8,12},{12,14},{14,10},{10,6},{6,2},{2,0},{1,5},{5,9},... | collective-permute-start | bytes 884744 | tf_op jit(solution)/shard_map/ppermute | solution.py:224
  4.2 11.3 %collective-permute-start.4 = (bf16[32,4608]{1,0:T(8,128)(2,1)S(1)}, bf16[32,4608]{1,0:T(8,128)(2,1)S(1)}, u32[]{:S(2)}, u32[]{:S(2)}) collective-permute-start(bf16[32,4608]{1,0:T(8,128)(2,1)S(1)} %get-tuple-element.53.refs_1_.refs_8_), channel_id=1, source_target_pairs={{4,0},{8,4},{12,8},{14,12},{10,14},{6,10},{2,6},{0,2},{5,1},{9,5},... | collective-permute-start | bytes 884744 | tf_op jit(solution)/shard_map/ppermute | solution.py:227
  4.2 16.2 %collective-permute-start.11 = (bf16[32,4608]{1,0:T(8,128)(2,1)S(1)}, bf16[32,4608]{1,0:T(8,128)(2,1)S(1)}, u32[]{:S(2)}, u32[]{:S(2)}) collective-permute-start(bf16[32,4608]{1,0:T(8,128)(2,1)S(1)} %get-tuple-element.54.refs_0_), channel_id=1, source_target_pairs={{4,0},{8,4},{12,8},{14,12},{10,14},{6,10},{2,6},{0,2},{5,1},{9,5},... | collective-permute-start | bytes 884744 | tf_op jit(solution)/shard_map/ppermute | solution.py:227
  6.2 14.3 %collective-permute-start = (bf16[32,4608]{1,0:T(8,128)(2,1)S(1)}, bf16[32,4608]{1,0:T(8,128)(2,1)S(1)}, u32[]{:S(2)}, u32[]{:S(2)}) collective-permute-start(bf16[32,4608]{1,0:T(8,128)(2,1)S(1)} %get-tuple-element.54.refs_0_), channel_id=1, source_target_pairs={{0,4},{4,8},{8,12},{12,14},{14,10},{10,6},{6,2},{2,0},{1,5},{5,9},... | collective-permute-start | bytes 884744 | tf_op jit(solution)/shard_map/ppermute | solution.py:224
  7.8 1.9 %copy-start.1 = (bf16[384,4096]{1,0:T(8,128)(2,1)S(1)}, bf16[384,4096]{1,0:T(8,128)(2,1)}, u32[]{:S(2)}) copy-start(bf16[384,4096]{1,0:T(8,128)(2,1)} %q_ref.7) | copy-start | bytes 9437188
  9.7 1.0 %copy-start.4 = (bf16[384,512]{1,0:T(8,128)(2,1)S(1)}, bf16[384,512]{1,0:T(8,128)(2,1)}, u32[]{:S(2)}) copy-start(bf16[384,512]{1,0:T(8,128)(2,1)} %k_ref.7) | copy-start | bytes 1179652
  10.7 0.7 %copy-start.6 = (s32[1,4]{1,0:T(1,128)S(1)}, s32[1,4]{1,0:T(1,128)}, u32[]{:S(2)}) copy-start(s32[1,4]{1,0:T(1,128)} %lengths_ref.7) | copy-start | bytes 52
  11.4 11.1 %copy-start.2 = (bf16[384,4096]{1,0:T(8,128)(2,1)S(1)}, bf16[384,4096]{1,0:T(8,128)(2,1)}, u32[]{:S(2)}) copy-start(bf16[384,4096]{1,0:T(8,128)(2,1)} %q_ref.7) | copy-start | bytes 9437188
  11.4 11.1 %copy-start.5 = (bf16[384,512]{1,0:T(8,128)(2,1)S(1)}, bf16[384,512]{1,0:T(8,128)(2,1)}, u32[]{:S(2)}) copy-start(bf16[384,512]{1,0:T(8,128)(2,1)} %k_ref.7) | copy-start | bytes 1179652
  13.5 13.1 %collective-permute-start.9 = (bf16[32,4608]{1,0:T(8,128)(2,1)S(1)}, bf16[32,4608]{1,0:T(8,128)(2,1)S(1)}, u32[]{:S(2)}, u32[]{:S(2)}) collective-permute-start(bf16[32,4608]{1,0:T(8,128)(2,1)S(1)} %collective-permute-done.8.refs_3_.refs_0_.refs_9_), channel_id=1, source_target_pairs={{0,4},{4,8},{8,12},{12,14},{14,10},{10,6},{6,2},{2,0},{1,5},{5,9},... | collective-permute-start | bytes 884744 | tf_op jit(solution)/shard_map/ppermute | solution.py:224
  15.5 12.7 %collective-permute-start.5 = (bf16[32,4608]{1,0:T(8,128)(2,1)S(1)}, bf16[32,4608]{1,0:T(8,128)(2,1)S(1)}, u32[]{:S(2)}, u32[]{:S(2)}) collective-permute-start(bf16[32,4608]{1,0:T(8,128)(2,1)S(1)} %collective-permute-done.4.refs_5_.refs_1_.refs_10_), channel_id=1, source_target_pairs={{4,0},{8,4},{12,8},{14,12},{10,14},{6,10},{2,6},{0,2},{5,1},{9,5},... | collective-permute-start | bytes 884744 | tf_op jit(solution)/shard_map/ppermute | solution.py:227
  20.4 12.6 %collective-permute-start.12 = (bf16[32,4608]{1,0:T(8,128)(2,1)S(1)}, bf16[32,4608]{1,0:T(8,128)(2,1)S(1)}, u32[]{:S(2)}, u32[]{:S(2)}) collective-permute-start(bf16[32,4608]{1,0:T(8,128)(2,1)S(1)} %collective-permute-done.11.refs_4_.refs_1_.refs_2_), channel_id=1, source_target_pairs={{4,0},{8,4},{12,8},{14,12},{10,14},{6,10},{2,6},{0,2},{5,1},{9,5},... | collective-permute-start | bytes 884744 | tf_op jit(solution)/shard_map/ppermute | solution.py:227
  20.4 12.6 %collective-permute-start.1 = (bf16[32,4608]{1,0:T(8,128)(2,1)S(1)}, bf16[32,4608]{1,0:T(8,128)(2,1)S(1)}, u32[]{:S(2)}, u32[]{:S(2)}) collective-permute-start(bf16[32,4608]{1,0:T(8,128)(2,1)S(1)} %collective-permute-done.refs_2_.refs_0_.refs_1_), channel_id=1, source_target_pairs={{0,4},{4,8},{8,12},{12,14},{14,10},{10,6},{6,2},{2,0},{1,5},{5,9},... | collective-permute-start | bytes 884744 | tf_op jit(solution)/shard_map/ppermute | solution.py:224
  26.6 10.6 %copy-start.3 = (bf16[384,4096]{1,0:T(8,128)(2,1)S(1)}, bf16[384,4096]{1,0:T(8,128)(2,1)}, u32[]{:S(2)}) copy-start(bf16[384,4096]{1,0:T(8,128)(2,1)} %x_ref.7) | copy-start | bytes 9437188
  26.6 19.0 %collective-permute-start.10 = (bf16[32,4608]{1,0:T(8,128)(2,1)S(1)}, bf16[32,4608]{1,0:T(8,128)(2,1)S(1)}, u32[]{:S(2)}, u32[]{:S(2)}) collective-permute-start(bf16[32,4608]{1,0:T(8,128)(2,1)S(1)} %collective-permute-done.9.refs_6_.refs_1_.refs_11_), channel_id=1, source_target_pairs={{0,4},{4,8},{8,12},{12,14},{14,10},{10,6},{6,2},{2,0},{1,5},{5,9},... | collective-permute-start | bytes 884744 | tf_op jit(solution)/shard_map/ppermute | solution.py:224
  28.3 11.1 %collective-permute-start.6 = (bf16[32,4608]{1,0:T(8,128)(2,1)S(1)}, bf16[32,4608]{1,0:T(8,128)(2,1)S(1)}, u32[]{:S(2)}, u32[]{:S(2)}) collective-permute-start(bf16[32,4608]{1,0:T(8,128)(2,1)S(1)} %collective-permute-done.5.refs_7_.refs_3_.refs_12_), channel_id=1, source_target_pairs={{4,0},{8,4},{12,8},{14,12},{10,14},{6,10},{2,6},{0,2},{5,1},{9,5},... | collective-permute-start | bytes 884744 | tf_op jit(solution)/shard_map/ppermute | solution.py:227
  33.1 12.6 %collective-permute-start.13 = (bf16[32,4608]{1,0:T(8,128)(2,1)S(1)}, bf16[32,4608]{1,0:T(8,128)(2,1)S(1)}, u32[]{:S(2)}, u32[]{:S(2)}) collective-permute-start(bf16[32,4608]{1,0:T(8,128)(2,1)S(1)} %collective-permute-done.12.refs_2_.refs_1_.refs_4_), channel_id=1, source_target_pairs={{4,0},{8,4},{12,8},{14,12},{10,14},{6,10},{2,6},{0,2},{5,1},{9,5},... | collective-permute-start | bytes 884744 | tf_op jit(solution)/shard_map/ppermute | solution.py:227
  33.1 9.7 %collective-permute-start.2 = (bf16[32,4608]{1,0:T(8,128)(2,1)S(1)}, bf16[32,4608]{1,0:T(8,128)(2,1)S(1)}, u32[]{:S(2)}, u32[]{:S(2)}) collective-permute-start(bf16[32,4608]{1,0:T(8,128)(2,1)S(1)} %collective-permute-done.1.refs_0_.refs_3_), channel_id=1, source_target_pairs={{0,4},{4,8},{8,12},{12,14},{14,10},{10,6},{6,2},{2,0},{1,5},{5,9},... | collective-permute-start | bytes 884744 | tf_op jit(solution)/shard_map/ppermute | solution.py:224
  39.4 11.2 %collective-permute-start.7 = (bf16[32,4608]{1,0:T(8,128)(2,1)S(1)}, bf16[32,4608]{1,0:T(8,128)(2,1)S(1)}, u32[]{:S(2)}, u32[]{:S(2)}) collective-permute-start(bf16[32,4608]{1,0:T(8,128)(2,1)S(1)} %collective-permute-done.6.refs_3_.refs_14_), channel_id=1, source_target_pairs={{4,0},{8,4},{12,8},{14,12},{10,14},{6,10},{2,6},{0,2},{5,1},{9,5},... | collective-permute-start | bytes 884744 | tf_op jit(solution)/shard_map/ppermute | solution.py:227
  42.7 8.2 %collective-permute-start.3 = (bf16[32,4608]{1,0:T(8,128)(2,1)S(1)}, bf16[32,4608]{1,0:T(8,128)(2,1)S(1)}, u32[]{:S(2)}, u32[]{:S(2)}) collective-permute-start(bf16[32,4608]{1,0:T(8,128)(2,1)S(1)} %collective-permute-done.2.refs_0_.refs_5_), channel_id=1, source_target_pairs={{0,4},{4,8},{8,12},{12,14},{14,10},{10,6},{6,2},{2,0},{1,5},{5,9},... | collective-permute-start | bytes 884744 | tf_op jit(solution)/shard_map/ppermute | solution.py:224
  50.9 2.5 %copy-start = (bf16[384,512]{1,0:T(8,128)(2,1)S(1)}, bf16[384,512]{1,0:T(8,128)(2,1)}, u32[]{:S(2)}) copy-start(bf16[384,512]{1,0:T(8,128)(2,1)} %base_ref.1) | copy-start | bytes 1179652
  51.9 1.5 %collective-permute-start.14 = (f32[384,64]{1,0:T(8,128)S(1)}, f32[384,64]{1,0:T(8,128)S(1)}, u32[]{:S(2)}, u32[]{:S(2)}) collective-permute-start(f32[384,64]{1,0:T(8,128)S(1)} %lowrank.7.mine_ref), channel_id=1, source_target_pairs={{0,1},{1,0},{2,3},{3,2},{4,5},{5,4},{6,7},{7,6},{8,9},{9,8},{10,11... | collective-permute-start | bytes 294920 | tf_op jit(solution)/shard_map/ppermute | solution.py:248

commit v5 on v4

--- a/solution.py
+++ b/solution.py
@@ -38,25 +38,63 @@
     return found
 
 
-def probs_kernel(waits, lengths_ref, q_ref, k_ref, *refs):
-    p_refs = refs[waits:]
+def ring_place(replica, n):
+    if n == 8:
+        return jnp.where(replica & 1 == 0, replica >> 1, n - 1 - (replica >> 1))
+    return replica
+
+
+def column(row):
+    wide = jnp.broadcast_to(row.astype(jnp.float32), (8, row.shape[1]))
+    return wide.T[:, :1].astype(jnp.int32)
+
+
+def masks_kernel(n, me_ref, lengths_ref, adapter_ref, near_q_ref, near_k_ref, *refs):
+    place_ref, segment_ref, across_ref = refs
+    distance = ring_place(me_ref[0], n) - ring_place(adapter_ref[...], n)
+    distance = jnp.where(distance < 0, distance + n, distance)
+    place = jnp.where(distance <= n // 2, jnp.maximum(2 * distance - 1, 0), 2 * (n - distance))
+    place_ref[...] = column(place)
+    position = lax.broadcasted_iota(jnp.int32, place.shape, 1)
+    segment = jnp.zeros(place.shape, jnp.int32)
+    end = jnp.int32(0)
+    for i in range(lengths_ref.shape[1]):
+        end = end + lengths_ref[0, i]
+        segment = segment + (position >= end).astype(jnp.int32)
+    across_ref[...] = segment
+    segment_ref[...] = column(segment)
+
+
+def masks(n, lengths, adapter_row, queries, keys):
+    rows = keys.shape[0]
+    tall = jax.ShapeDtypeStruct((rows, 1), jnp.int32)
+    me = jnp.reshape(lax.axis_index("rep"), (1,)).astype(jnp.int32)
+    return pl.pallas_call(
+        functools.partial(masks_kernel, n),
+        out_shape=[tall, tall, jax.ShapeDtypeStruct((1, rows), jnp.int32)],
+        in_specs=[SMEM, SMEM, VMEM, VMEM, VMEM],
+        out_specs=[VMEM] * 3,
+        cost_estimate=pl.CostEstimate(flops=1_000_000_000, bytes_accessed=16 * rows, transcendentals=0),
+        compiler_params=pltpu.CompilerParams(vmem_limit_bytes=4 * 2**20),
+        name="masks",
+    )(me, lengths, adapter_row, queries, keys)
+
+
+def probs_kernel(kv_head, segment_ref, across_ref, q_ref, k_ref, *refs):
     rows = k_ref.shape[0]
-    ends = []
-    total = jnp.int32(0)
-    for i in range(lengths_ref.shape[1]):
-        total = total + lengths_ref[0, i]
-        ends.append(total)
+    tiles = windows(rows)
+    p_refs = refs[-len(tiles) :]
     factor = float(np.log2(np.e) * HEAD_SIZE**-0.5)
-    for p_ref, (start, first, width) in zip(p_refs, windows(rows)):
+    at = kv_head * HEAD_SIZE
+    for p_ref, (start, first, width) in zip(p_refs, tiles):
         t = lax.broadcasted_iota(jnp.int32, (TILE, width), 0) + start
         s = lax.broadcasted_iota(jnp.int32, (TILE, width), 1) + first
-        allowed = s <= t
-        for end in ends:
-            allowed = allowed & ((t >= end) == (s >= end))
-        bias = jnp.where(allowed, 0.0, -1e30)
-        keys = k_ref[first : first + width, :]
+        same = segment_ref[start : start + TILE, :] == across_ref[:, first : first + width]
+        bias = jnp.where(same & (s <= t), 0.0, -1e30)
+        keys = k_ref[first : first + width, at : at + HEAD_SIZE]
         for head in range(GROUP):
-            q = q_ref[start : start + TILE, head * HEAD_SIZE : (head + 1) * HEAD_SIZE]
+            column_at = (kv_head * GROUP + head) * HEAD_SIZE
+            q = q_ref[start : start + TILE, column_at : column_at + HEAD_SIZE]
             scores = lax.dot_general(q, keys, NT, preferred_element_type=jnp.float32) + bias
             peak = jnp.max(scores, axis=1, keepdims=True)
             weights = jnp.exp2((scores - peak) * factor)
@@ -64,28 +102,21 @@
             p_ref[head * TILE : (head + 1) * TILE, :] = (weights * inverse).astype(jnp.bfloat16)
 
 
-def probs_of(lengths, queries, keys, kv_head, after):
+def probs_of(segment, across, queries, keys, kv_head, after):
     rows = keys.shape[0]
-    wide = GROUP * HEAD_SIZE
     shapes = [(GROUP * TILE, width) for _, _, width in windows(rows)]
     elements = sum(a * b for a, b in shapes)
     return pl.pallas_call(
-        functools.partial(probs_kernel, len(after)),
-        grid=(1,),
+        functools.partial(probs_kernel, kv_head),
         out_shape=[jax.ShapeDtypeStruct(s, jnp.bfloat16) for s in shapes],
-        in_specs=[
-            SMEM,
-            pl.BlockSpec((rows, wide), lambda i: (0, kv_head)),
-            pl.BlockSpec((rows, HEAD_SIZE), lambda i: (0, kv_head)),
-        ]
-        + [pl.BlockSpec(memory_space=pl.ANY)] * len(after),
-        out_specs=[pl.BlockSpec(s, lambda i: (0, 0)) for s in shapes],
+        in_specs=[VMEM] * 4 + [pl.BlockSpec(memory_space=pl.ANY)] * len(after),
+        out_specs=[VMEM] * len(shapes),
         cost_estimate=pl.CostEstimate(
-            flops=2_300_000_000, bytes_accessed=2 * (rows * wide + elements), transcendentals=elements
+            flops=2_000_000_000, bytes_accessed=2 * elements, transcendentals=elements
         ),
         compiler_params=pltpu.CompilerParams(vmem_limit_bytes=12 * 2**20),
         name="probs",
-    )(lengths, queries, keys, *after)
+    )(segment, across, queries, keys, *after)
 
 
 def lowrank_kernel(at, count, place_ref, x_ref, *refs):
@@ -204,38 +235,34 @@
     back = [(b, a) for a, b in ahead]
     far = n // 2
     distances = [0] + [d for step in range(1, far) for d in (step, -step)] + [far]
-    table = np.zeros((n, n), np.int32)
-    for place, replica in enumerate(order):
-        table[replica] = [order[(place - d) % n] for d in distances]
-    ids = lax.dynamic_slice_in_dim(jnp.asarray(table), lax.axis_index("rep"), 1, 0)
-    place = jnp.sum(
-        jnp.where(adapter_of_row == ids, jnp.arange(n, dtype=jnp.int32)[None, :], 0), axis=1, keepdims=True
-    )
-
     down = jnp.swapaxes(adapter_down_weight[0], 0, 1)
     both = jnp.concatenate([down, adapter_up_weight[0]], axis=1)
-    half = both.shape[0] // 2
-
-    def pass_round(piece, steps_ahead, steps_back):
-        held = {0: piece}
-        moving_ahead = moving_back = piece
-        for step in range(1, far + 1):
-            if step <= steps_ahead:
-                moving_ahead = lax.ppermute(moving_ahead, "rep", ahead)
-                held[step] = moving_ahead
-            if step <= steps_back:
-                moving_back = lax.ppermute(moving_back, "rep", back)
-                held[-step if step < far else far] = moving_back
-        return held
-
-    low = pass_round(both[:half], far, far - 1)
-    high = pass_round(both[half:], far - 1, far)
+    rank = both.shape[0]
+    own_low, own_high = both[: rank // 2], both[rank // 2 :]
+    place, segment, across = masks(
+        n, sequence_lengths, adapter_of_row.reshape(1, -1), queries, stacked_key_rows
+    )
+    low, high = {0: own_low}, {0: own_high}
+
+    def pass_round(held, pairs, sign, steps):
+        piece = held[0]
+        for step in range(1, steps + 1):
+            piece = lax.ppermute(piece, "rep", pairs)
+            held[sign * step if step < far else far] = piece
+
+    pass_round(high, ahead, 1, far - 1)
+    pass_round(low, back, -1, far - 1)
+    pass_round(high, back, -1, far)
+    pass_round(low, ahead, 1, far)
 
     kv_heads = stacked_key_rows.shape[1] // HEAD_SIZE
-    arrivals = [[piece[d] for d in (step, -step)] for step in range(1, far) for piece in (low, high)]
+    arrivals = [
+        pair
+        for step in range(1, far)
+        for pair in ([low[step], high[-step]], [high[step], low[-step]])
+    ]
     probs = [
-        probs_of(sequence_lengths, queries, stacked_key_rows, kv, arrivals[kv - 1] if kv > 0 else [])
-        for kv in range(kv_heads)
+        probs_of(segment, across, queries, stacked_key_rows, kv, arrivals[kv // 2]) for kv in range(kv_heads)
     ]
 
     partial = None

time: 56.6 us -> 56.6 us (level)
  waiting for transfers between devices: 19.5 us -> 21 us
  other arithmetic: 1.89 us -> 1.16 us
    ppermute x14, waiting for transfers between devices: 18.1 us -> 19.6 us  [pass_round(): piece = lax.ppermute(piece, 'rep', pairs)]
    unnamed x1 -> x0, other arithmetic: 0.7 us -> none
    eq x1 -> x0, local copies, waits for them, and re-layouts: 0.69 us -> none  [on_device(): adapter_of_row == ids]
    unnamed x14 -> x16, local copies, waits for them, and re-layouts: 3.56 us -> 4.24 us
    pallas_call x4 -> x5, Pallas kernels: 8.21 us -> 7.72 us  [the longest x4 7 us: probs_of(): pl.pallas_call(functools.partial(probs_kernel, kv_head), out_shape=[jax.S...]
  transfers between devices with their start and end apart: 15 -> 15, of which waited for: 8 -> 9; matrix products, arithmetic and copies ran while one was open for 3% -> 0% of each run, Pallas kernels for 20% -> 19%
where the time goes in v5:
time: 56.6 us; the launch traced here: 56.4 us
  waiting for transfers between devices  21 us (37%)
  starting transfers between devices  15.1 us (27%)
  Pallas kernels  14.6 us (26%)
  local copies, waits for them, and re-layouts  4.24 us (7%)
  other arithmetic  1.16 us (2%)
    ppermute x14, waiting for transfers between devices, pass_round(): piece = lax.ppermute(piece, 'rep', pairs)  19.6 us
    ppermute x14, starting transfers between devices, pass_round(): piece = lax.ppermute(piece, 'rep', pairs)  15 us
    pallas_call x4, Pallas kernels, probs_of(): pl.pallas_call(functools.partial(probs_kernel, kv_head), out_shape=[jax.S...  7 us
    unnamed x16, local copies, waits for them, and re-layouts  4.24 us
    pallas_call x4, Pallas kernels, lowrank_of(): pl.pallas_call(functools.partial(lowrank_kernel, at, len(pieces)), out_sh...  4.11 us
    pallas_call x1, Pallas kernels, attend(): pl.pallas_call(functools.partial(attend_kernel, kv_heads, len(lows)), out...  2.78 us
    ppermute x1, waiting for transfers between devices, on_device(): other = lax.ppermute(partial, 'tp', [(0, 1), (1, 0)])  1.43 us
    concatenate x1, other arithmetic, on_device(): both = jnp.concatenate([down, adapter_up_weight[0]], axis=1)  1.16 us
  transfers between devices with their start and end apart: 15, of which 9 were waited for; matrix products, arithmetic and copies ran while one was open for 0% of the time, Pallas kernels for 19%

profile of v5, /device:TPU:0, one launch (start us, length us, event | category | flops | bytes accessed | tf_op | source)
XLA Modules:
  0.0 56.4 jit_solution(7466602743373807864)
XLA Ops:
  0.0 1.2 %pad_maximum_fusion = (bf16[32,4608]{1,0:T(8,128)(2,1)S(1)}, bf16[32,4608]{1,0:T(8,128)(2,1)S(1)}) fusion(bf16[64,512]{1,0:T(8,128)(2,1)} %bitcast.8, bf16[64,4096]{1,0:T(8,128)(2,1)} %bitcast.7), kind=kLoop, calls=%fused_computation.3 | loop fusion | flops 1179648 | bytes 1179648 | tf_op jit(solution)/shard_map/concatenate | solution.py:239
  1.2 3.1 %collective-permute-start.8 = (bf16[32,4608]{1,0:T(8,128)(2,1)S(1)}, bf16[32,4608]{1,0:T(8,128)(2,1)S(1)}, u32[]{:S(2)}, u32[]{:S(2)}) collective-permute-start(bf16[32,4608]{1,0:T(8,128)(2,1)S(1)} %get-tuple-element.59.refs_1_.refs_8_), channel_id=1, source_target_pairs={{0,4},{4,8},{8,12},{12,14},{14,10},{10,6},{6,2},{2,0},{1,5},{5,9},... | collective-permute-start | bytes 884744 | tf_op jit(solution)/shard_map/ppermute | solution.py:250
  4.2 2.0 %collective-permute-start.11 = (bf16[32,4608]{1,0:T(8,128)(2,1)S(1)}, bf16[32,4608]{1,0:T(8,128)(2,1)S(1)}, u32[]{:S(2)}, u32[]{:S(2)}) collective-permute-start(bf16[32,4608]{1,0:T(8,128)(2,1)S(1)} %get-tuple-element.60.refs_0_), channel_id=1, source_target_pairs={{4,0},{8,4},{12,8},{14,12},{10,14},{6,10},{2,6},{0,2},{5,1},{9,5},... | collective-permute-start | bytes 884744 | tf_op jit(solution)/shard_map/ppermute | solution.py:250
  6.3 1.9 %copy-done.1 = bf16[384,4096]{1,0:T(8,128)(2,1)S(1)} copy-done((bf16[384,4096]{1,0:T(8,128)(2,1)S(1)}, bf16[384,4096]{1,0:T(8,128)(2,1)}, u32[]{:S(2)}) %copy-start.1) | copy-done | bytes 3145752
  8.2 1.0 %copy-done.4 = bf16[384,512]{1,0:T(8,128)(2,1)S(1)} copy-done((bf16[384,512]{1,0:T(8,128)(2,1)S(1)}, bf16[384,512]{1,0:T(8,128)(2,1)}, u32[]{:S(2)}) %copy-start.4) | copy-done | bytes 393240
  12.0 2.1 %collective-permute-start.9 = (bf16[32,4608]{1,0:T(8,128)(2,1)S(1)}, bf16[32,4608]{1,0:T(8,128)(2,1)S(1)}, u32[]{:S(2)}, u32[]{:S(2)}) collective-permute-start(bf16[32,4608]{1,0:T(8,128)(2,1)S(1)} %collective-permute-done.8.refs_3_.refs_0_.refs_9_), channel_id=1, source_target_pairs={{0,4},{4,8},{8,12},{12,14},{14,10},{10,6},{6,2},{2,0},{1,5},{5,9},... | collective-permute-start | bytes 884744 | tf_op jit(solution)/shard_map/ppermute | solution.py:250
  14.2 6.3 %collective-permute-done.11.refs_4_.refs_1_.refs_2_ = bf16[32,4608]{1,0:T(8,128)(2,1)S(1)} collective-permute-done((bf16[32,4608]{1,0:T(8,128)(2,1)S(1)}, bf16[32,4608]{1,0:T(8,128)(2,1)S(1)}, u32[]{:S(2)}, u32[]{:S(2)}) %collective-permute-start.11) | collective-permute-done | bytes 294944 | tf_op jit(solution)/shard_map/ppermute | solution.py:250
  20.5 2.0 %collective-permute-start.1 = (bf16[32,4608]{1,0:T(8,128)(2,1)S(1)}, bf16[32,4608]{1,0:T(8,128)(2,1)S(1)}, u32[]{:S(2)}, u32[]{:S(2)}) collective-permute-start(bf16[32,4608]{1,0:T(8,128)(2,1)S(1)} %collective-permute-done.refs_2_.refs_0_.refs_1_), channel_id=1, source_target_pairs={{0,4},{4,8},{8,12},{12,14},{14,10},{10,6},{6,2},{2,0},{1,5},{5,9},... | collective-permute-start | bytes 884744 | tf_op jit(solution)/shard_map/ppermute | solution.py:250
  22.5 1.7 %probs.5 = (bf16[512,128]{1,0:T(8,128)(2,1)S(1)}, bf16[512,128]{1,0:T(8,128)(2,1)S(1)}, bf16[512,256]{1,0:T(8,128)(2,1)S(1)}, bf16[512,256]{1,0:T(8,128)(2,1)S(1...) custom-call(s32[384,1]{1,0:T(8,128)S(1)} %get-tuple-element.33.segment_ref, ...), custom_call_target="tpu_custom_call" | custom-call | flops 2000000000 | bytes 1310720 | tf_op jit(solution)/shard_map/probs/pallas_call | solution.py:109
  24.3 1.8 %probs.4 = (bf16[512,128]{1,0:T(8,128)(2,1)S(1)}, bf16[512,128]{1,0:T(8,128)(2,1)S(1)}, bf16[512,256]{1,0:T(8,128)(2,1)S(1)}, bf16[512,256]{1,0:T(8,128)(2,1)S(1...) custom-call(s32[384,1]{1,0:T(8,128)S(1)} %get-tuple-element.33.segment_ref, ...), custom_call_target="tpu_custom_call" | custom-call | flops 2000000000 | bytes 1310720 | tf_op jit(solution)/shard_map/probs/pallas_call | solution.py:109
  26.0 1.8 %probs.7 = (bf16[512,128]{1,0:T(8,128)(2,1)S(1)}, bf16[512,128]{1,0:T(8,128)(2,1)S(1)}, bf16[512,256]{1,0:T(8,128)(2,1)S(1)}, bf16[512,256]{1,0:T(8,128)(2,1)S(1...) custom-call(s32[384,1]{1,0:T(8,128)S(1)} %get-tuple-element.33.segment_ref, ...), custom_call_target="tpu_custom_call" | custom-call | flops 2000000000 | bytes 1310720 | tf_op jit(solution)/shard_map/probs/pallas_call | solution.py:109
  27.9 2.3 %collective-permute-done.1.refs_0_.refs_3_ = bf16[32,4608]{1,0:T(8,128)(2,1)S(1)} collective-permute-done((bf16[32,4608]{1,0:T(8,128)(2,1)S(1)}, bf16[32,4608]{1,0:T(8,128)(2,1)S(1)}, u32[]{:S(2)}, u32[]{:S(2)}) %collective-permute-start.1) | collective-permute-done | bytes 294944 | tf_op jit(solution)/shard_map/ppermute | solution.py:250
  30.2 1.8 %collective-permute-start.2 = (bf16[32,4608]{1,0:T(8,128)(2,1)S(1)}, bf16[32,4608]{1,0:T(8,128)(2,1)S(1)}, u32[]{:S(2)}, u32[]{:S(2)}) collective-permute-start(bf16[32,4608]{1,0:T(8,128)(2,1)S(1)} %collective-permute-done.1.refs_0_.refs_3_), channel_id=1, source_target_pairs={{0,4},{4,8},{8,12},{12,14},{14,10},{10,6},{6,2},{2,0},{1,5},{5,9},... | collective-permute-start | bytes 884744 | tf_op jit(solution)/shard_map/ppermute | solution.py:250
  31.9 1.8 %probs.6 = (bf16[512,128]{1,0:T(8,128)(2,1)S(1)}, bf16[512,128]{1,0:T(8,128)(2,1)S(1)}, bf16[512,256]{1,0:T(8,128)(2,1)S(1)}, bf16[512,256]{1,0:T(8,128)(2,1)S(1...) custom-call(s32[384,1]{1,0:T(8,128)S(1)} %get-tuple-element.33.segment_ref, ...), custom_call_target="tpu_custom_call" | custom-call | flops 2000000000 | bytes 1310720 | tf_op jit(solution)/shard_map/probs/pallas_call | solution.py:109
  33.7 1.6 %collective-permute-start.10 = (bf16[32,4608]{1,0:T(8,128)(2,1)S(1)}, bf16[32,4608]{1,0:T(8,128)(2,1)S(1)}, u32[]{:S(2)}, u32[]{:S(2)}) collective-permute-start(bf16[32,4608]{1,0:T(8,128)(2,1)S(1)} %collective-permute-done.9.refs_6_.refs_1_.refs_11_), channel_id=1, source_target_pairs={{0,4},{4,8},{8,12},{12,14},{14,10},{10,6},{6,2},{2,0},{1,5},{5,9},... | collective-permute-start | bytes 884744 | tf_op jit(solution)/shard_map/ppermute | solution.py:250
  35.8 1.1 %lowrank.4.refs_4_ = f32[384,64]{1,0:T(8,128)S(1)} custom-call(s32[384,1]{1,0:T(8,128)S(1)} %get-tuple-element.32.place_ref, bf16[384,4096]{1,0:T(8,128)(2,1)S(1)} %copy-done.3, bf16[32,4608]{1,0:T(8,128)(2,1)S(1)} %get-tuple-element.60.refs_0_, bf16[32,4608]{1,0:T(8,128)(2,1)S(1)} %get-tuple-element.59.refs_1_.refs_8_, ...), custom_call_target="tpu_custom_call" | custom-call | flops 1700000000 | bytes 4915200 | tf_op jit(solution)/shard_map/lowrank/pallas_call | solution.py:145
  36.9 2.6 %collective-permute-done.6.refs_3_.refs_14_ = bf16[32,4608]{1,0:T(8,128)(2,1)S(1)} collective-permute-done((bf16[32,4608]{1,0:T(8,128)(2,1)S(1)}, bf16[32,4608]{1,0:T(8,128)(2,1)S(1)}, u32[]{:S(2)}, u32[]{:S(2)}) %collective-permute-start.6) | collective-permute-done | bytes 294944 | tf_op jit(solution)/shard_map/ppermute | solution.py:250
  40.1 1.8 %collective-permute-start.3 = (bf16[32,4608]{1,0:T(8,128)(2,1)S(1)}, bf16[32,4608]{1,0:T(8,128)(2,1)S(1)}, u32[]{:S(2)}, u32[]{:S(2)}) collective-permute-start(bf16[32,4608]{1,0:T(8,128)(2,1)S(1)} %collective-permute-done.2.refs_0_.refs_5_), channel_id=1, source_target_pairs={{0,4},{4,8},{8,12},{12,14},{14,10},{10,6},{6,2},{2,0},{1,5},{5,9},... | collective-permute-start | bytes 884744 | tf_op jit(solution)/shard_map/ppermute | solution.py:250
  41.9 1.0 %lowrank.5.refs_4_ = f32[384,64]{1,0:T(8,128)S(1)} custom-call(s32[384,1]{1,0:T(8,128)S(1)} %get-tuple-element.32.place_ref, bf16[384,4096]{1,0:T(8,128)(2,1)S(1)} %copy-done.3, bf16[32,4608]{1,0:T(8,128)(2,1)S(1)} %collective-permute-done.1.refs_0_.refs_3_, bf16[32,4608]{1,0:T(8,128)(2,1)S(1)} %collective-permute-done.9.refs_6_.refs_1_.refs_11_, ...), custom_call_target="tpu_custom_call" | custom-call | flops 1700000000 | bytes 4325376 | tf_op jit(solution)/shard_map/lowrank/pallas_call | solution.py:145
  42.9 3.5 %collective-permute-done.10.refs_1_.refs_13_ = bf16[32,4608]{1,0:T(8,128)(2,1)S(1)} collective-permute-done((bf16[32,4608]{1,0:T(8,128)(2,1)S(1)}, bf16[32,4608]{1,0:T(8,128)(2,1)S(1)}, u32[]{:S(2)}, u32[]{:S(2)}) %collective-permute-start.10) | collective-permute-done | bytes 294944 | tf_op jit(solution)/shard_map/ppermute | solution.py:250
  46.4 1.0 %lowrank.6.refs_2_ = f32[384,64]{1,0:T(8,128)S(1)} custom-call(s32[384,1]{1,0:T(8,128)S(1)} %get-tuple-element.32.place_ref, bf16[384,4096]{1,0:T(8,128)(2,1)S(1)} %copy-done.3, bf16[32,4608]{1,0:T(8,128)(2,1)S(1)} %collective-permute-done.2.refs_0_.refs_5_, bf16[32,4608]{1,0:T(8,128)(2,1)S(1)} %collective-permute-done.10.refs_1_.refs_13_, ...), custom_call_target="tpu_custom_call" | custom-call | flops 1700000000 | bytes 4325376 | tf_op jit(solution)/shard_map/lowrank/pallas_call | solution.py:145
  47.5 3.2 %collective-permute-done.7.refs_1_.refs_15_ = bf16[32,4608]{1,0:T(8,128)(2,1)S(1)} collective-permute-done((bf16[32,4608]{1,0:T(8,128)(2,1)S(1)}, bf16[32,4608]{1,0:T(8,128)(2,1)S(1)}, u32[]{:S(2)}, u32[]{:S(2)}) %collective-permute-start.7) | collective-permute-done | bytes 294944 | tf_op jit(solution)/shard_map/ppermute | solution.py:250
  52.0 1.4 %collective-permute-done.14.theirs_ref = f32[384,64]{1,0:T(8,128)S(1)} collective-permute-done((f32[384,64]{1,0:T(8,128)S(1)}, f32[384,64]{1,0:T(8,128)S(1)}, u32[]{:S(2)}, u32[]{:S(2)}) %collective-permute-start.14) | collective-permute-done | bytes 98336 | tf_op jit(solution)/shard_map/ppermute | solution.py:275
  53.5 2.8 %attend.1 = bf16[384,4096]{1,0:T(8,128)(2,1)} custom-call(s32[384,1]{1,0:T(8,128)S(1)} %get-tuple-element.32.place_ref, f32[384,64]{1,0:T(8,128)S(1)} %lowrank.7.mine_ref, f32[384,64]{1,0:T(8,128)S(1)} %collective-permute-done.14.theirs_ref, bf16[384,512]{1,0:T(8,128)(2,1)S(1)} %copy-done, bf16[32,4608]{1,0:T(8,128)(2,1)S(1)} %get-tuple-element.60.refs_0_, ...), custom_call_target="tpu_custom_call" | custom-call | tf_op jit(solution)/shard_map/attend/pallas_call | solution.py:211
  (33 shorter events, 5.5 us)
Async XLA Ops:
  0.0 22.5 %copy-start.5 = (bf16[384,512]{1,0:T(8,128)(2,1)S(1)}, bf16[384,512]{1,0:T(8,128)(2,1)}, u32[]{:S(2)}) copy-start(bf16[384,512]{1,0:T(8,128)(2,1)} %k_ref.7) | copy-start | bytes 1179652
  1.2 10.9 %collective-permute-start.8 = (bf16[32,4608]{1,0:T(8,128)(2,1)S(1)}, bf16[32,4608]{1,0:T(8,128)(2,1)S(1)}, u32[]{:S(2)}, u32[]{:S(2)}) collective-permute-start(bf16[32,4608]{1,0:T(8,128)(2,1)S(1)} %get-tuple-element.59.refs_1_.refs_8_), channel_id=1, source_target_pairs={{0,4},{4,8},{8,12},{12,14},{14,10},{10,6},{6,2},{2,0},{1,5},{5,9},... | collective-permute-start | bytes 884744 | tf_op jit(solution)/shard_map/ppermute | solution.py:250
  4.2 9.9 %collective-permute-start.4 = (bf16[32,4608]{1,0:T(8,128)(2,1)S(1)}, bf16[32,4608]{1,0:T(8,128)(2,1)S(1)}, u32[]{:S(2)}, u32[]{:S(2)}) collective-permute-start(bf16[32,4608]{1,0:T(8,128)(2,1)S(1)} %get-tuple-element.59.refs_1_.refs_8_), channel_id=1, source_target_pairs={{4,0},{8,4},{12,8},{14,12},{10,14},{6,10},{2,6},{0,2},{5,1},{9,5},... | collective-permute-start | bytes 884744 | tf_op jit(solution)/shard_map/ppermute | solution.py:250
  4.2 16.2 %collective-permute-start.11 = (bf16[32,4608]{1,0:T(8,128)(2,1)S(1)}, bf16[32,4608]{1,0:T(8,128)(2,1)S(1)}, u32[]{:S(2)}, u32[]{:S(2)}) collective-permute-start(bf16[32,4608]{1,0:T(8,128)(2,1)S(1)} %get-tuple-element.60.refs_0_), channel_id=1, source_target_pairs={{4,0},{8,4},{12,8},{14,12},{10,14},{6,10},{2,6},{0,2},{5,1},{9,5},... | collective-permute-start | bytes 884744 | tf_op jit(solution)/shard_map/ppermute | solution.py:250
  6.2 14.3 %collective-permute-start = (bf16[32,4608]{1,0:T(8,128)(2,1)S(1)}, bf16[32,4608]{1,0:T(8,128)(2,1)S(1)}, u32[]{:S(2)}, u32[]{:S(2)}) collective-permute-start(bf16[32,4608]{1,0:T(8,128)(2,1)S(1)} %get-tuple-element.60.refs_0_), channel_id=1, source_target_pairs={{0,4},{4,8},{8,12},{12,14},{14,10},{10,6},{6,2},{2,0},{1,5},{5,9},... | collective-permute-start | bytes 884744 | tf_op jit(solution)/shard_map/ppermute | solution.py:250
  6.3 1.9 %copy-start.1 = (bf16[384,4096]{1,0:T(8,128)(2,1)S(1)}, bf16[384,4096]{1,0:T(8,128)(2,1)}, u32[]{:S(2)}) copy-start(bf16[384,4096]{1,0:T(8,128)(2,1)} %q_ref.7) | copy-start | bytes 9437188
  8.2 1.0 %copy-start.4 = (bf16[384,512]{1,0:T(8,128)(2,1)S(1)}, bf16[384,512]{1,0:T(8,128)(2,1)}, u32[]{:S(2)}) copy-start(bf16[384,512]{1,0:T(8,128)(2,1)} %k_ref.7) | copy-start | bytes 1179652
  9.2 0.7 %copy-start.6 = (s32[384,1]{0,1:T(1,128)S(1)}, s32[384,1]{0,1:T(1,128)}, u32[]{:S(2)}) copy-start(s32[384,1]{0,1:T(1,128)} %param.12) | copy-start | bytes 4612
  9.9 0.7 %copy-start.7 = (s32[1,4]{1,0:T(1,128)S(1)}, s32[1,4]{1,0:T(1,128)}, u32[]{:S(2)}) copy-start(s32[1,4]{1,0:T(1,128)} %lengths_ref.1) | copy-start | bytes 52
  10.5 12.0 %copy-start.2 = (bf16[384,4096]{1,0:T(8,128)(2,1)S(1)}, bf16[384,4096]{1,0:T(8,128)(2,1)}, u32[]{:S(2)}) copy-start(bf16[384,4096]{1,0:T(8,128)(2,1)} %q_ref.7) | copy-start | bytes 9437188
  12.0 21.7 %collective-permute-start.9 = (bf16[32,4608]{1,0:T(8,128)(2,1)S(1)}, bf16[32,4608]{1,0:T(8,128)(2,1)S(1)}, u32[]{:S(2)}, u32[]{:S(2)}) collective-permute-start(bf16[32,4608]{1,0:T(8,128)(2,1)S(1)} %collective-permute-done.8.refs_3_.refs_0_.refs_9_), channel_id=1, source_target_pairs={{0,4},{4,8},{8,12},{12,14},{14,10},{10,6},{6,2},{2,0},{1,5},{5,9},... | collective-permute-start | bytes 884744 | tf_op jit(solution)/shard_map/ppermute | solution.py:250
  14.2 13.6 %collective-permute-start.5 = (bf16[32,4608]{1,0:T(8,128)(2,1)S(1)}, bf16[32,4608]{1,0:T(8,128)(2,1)S(1)}, u32[]{:S(2)}, u32[]{:S(2)}) collective-permute-start(bf16[32,4608]{1,0:T(8,128)(2,1)S(1)} %collective-permute-done.4.refs_5_.refs_1_.refs_10_), channel_id=1, source_target_pairs={{4,0},{8,4},{12,8},{14,12},{10,14},{6,10},{2,6},{0,2},{5,1},{9,5},... | collective-permute-start | bytes 884744 | tf_op jit(solution)/shard_map/ppermute | solution.py:250
  20.5 14.9 %collective-permute-start.12 = (bf16[32,4608]{1,0:T(8,128)(2,1)S(1)}, bf16[32,4608]{1,0:T(8,128)(2,1)S(1)}, u32[]{:S(2)}, u32[]{:S(2)}) collective-permute-start(bf16[32,4608]{1,0:T(8,128)(2,1)S(1)} %collective-permute-done.11.refs_4_.refs_1_.refs_2_), channel_id=1, source_target_pairs={{4,0},{8,4},{12,8},{14,12},{10,14},{6,10},{2,6},{0,2},{5,1},{9,5},... | collective-permute-start | bytes 884744 | tf_op jit(solution)/shard_map/ppermute | solution.py:250
  20.5 9.7 %collective-permute-start.1 = (bf16[32,4608]{1,0:T(8,128)(2,1)S(1)}, bf16[32,4608]{1,0:T(8,128)(2,1)S(1)}, u32[]{:S(2)}, u32[]{:S(2)}) collective-permute-start(bf16[32,4608]{1,0:T(8,128)(2,1)S(1)} %collective-permute-done.refs_2_.refs_0_.refs_1_), channel_id=1, source_target_pairs={{0,4},{4,8},{8,12},{12,14},{14,10},{10,6},{6,2},{2,0},{1,5},{5,9},... | collective-permute-start | bytes 884744 | tf_op jit(solution)/shard_map/ppermute | solution.py:250
  27.8 8.0 %copy-start.3 = (bf16[384,4096]{1,0:T(8,128)(2,1)S(1)}, bf16[384,4096]{1,0:T(8,128)(2,1)}, u32[]{:S(2)}) copy-start(bf16[384,4096]{1,0:T(8,128)(2,1)} %x_ref.7) | copy-start | bytes 9437188
  27.8 11.6 %collective-permute-start.6 = (bf16[32,4608]{1,0:T(8,128)(2,1)S(1)}, bf16[32,4608]{1,0:T(8,128)(2,1)S(1)}, u32[]{:S(2)}, u32[]{:S(2)}) collective-permute-start(bf16[32,4608]{1,0:T(8,128)(2,1)S(1)} %collective-permute-done.5.refs_3_.refs_12_), channel_id=1, source_target_pairs={{4,0},{8,4},{12,8},{14,12},{10,14},{6,10},{2,6},{0,2},{5,1},{9,5},... | collective-permute-start | bytes 884744 | tf_op jit(solution)/shard_map/ppermute | solution.py:250
  30.2 9.9 %collective-permute-start.2 = (bf16[32,4608]{1,0:T(8,128)(2,1)S(1)}, bf16[32,4608]{1,0:T(8,128)(2,1)S(1)}, u32[]{:S(2)}, u32[]{:S(2)}) collective-permute-start(bf16[32,4608]{1,0:T(8,128)(2,1)S(1)} %collective-permute-done.1.refs_0_.refs_3_), channel_id=1, source_target_pairs={{0,4},{4,8},{8,12},{12,14},{14,10},{10,6},{6,2},{2,0},{1,5},{5,9},... | collective-permute-start | bytes 884744 | tf_op jit(solution)/shard_map/ppermute | solution.py:250
  33.7 12.7 %collective-permute-start.10 = (bf16[32,4608]{1,0:T(8,128)(2,1)S(1)}, bf16[32,4608]{1,0:T(8,128)(2,1)S(1)}, u32[]{:S(2)}, u32[]{:S(2)}) collective-permute-start(bf16[32,4608]{1,0:T(8,128)(2,1)S(1)} %collective-permute-done.9.refs_6_.refs_1_.refs_11_), channel_id=1, source_target_pairs={{0,4},{4,8},{8,12},{12,14},{14,10},{10,6},{6,2},{2,0},{1,5},{5,9},... | collective-permute-start | bytes 884744 | tf_op jit(solution)/shard_map/ppermute | solution.py:250
  35.4 11.1 %collective-permute-start.13 = (bf16[32,4608]{1,0:T(8,128)(2,1)S(1)}, bf16[32,4608]{1,0:T(8,128)(2,1)S(1)}, u32[]{:S(2)}, u32[]{:S(2)}) collective-permute-start(bf16[32,4608]{1,0:T(8,128)(2,1)S(1)} %collective-permute-done.12.refs_7_.refs_2_.refs_4_), channel_id=1, source_target_pairs={{4,0},{8,4},{12,8},{14,12},{10,14},{6,10},{2,6},{0,2},{5,1},{9,5},... | collective-permute-start | bytes 884744 | tf_op jit(solution)/shard_map/ppermute | solution.py:250
  39.5 11.2 %collective-permute-start.7 = (bf16[32,4608]{1,0:T(8,128)(2,1)S(1)}, bf16[32,4608]{1,0:T(8,128)(2,1)S(1)}, u32[]{:S(2)}, u32[]{:S(2)}) collective-permute-start(bf16[32,4608]{1,0:T(8,128)(2,1)S(1)} %collective-permute-done.6.refs_3_.refs_14_), channel_id=1, source_target_pairs={{4,0},{8,4},{12,8},{14,12},{10,14},{6,10},{2,6},{0,2},{5,1},{9,5},... | collective-permute-start | bytes 884744 | tf_op jit(solution)/shard_map/ppermute | solution.py:250
  40.1 10.9 %collective-permute-start.3 = (bf16[32,4608]{1,0:T(8,128)(2,1)S(1)}, bf16[32,4608]{1,0:T(8,128)(2,1)S(1)}, u32[]{:S(2)}, u32[]{:S(2)}) collective-permute-start(bf16[32,4608]{1,0:T(8,128)(2,1)S(1)} %collective-permute-done.2.refs_0_.refs_5_), channel_id=1, source_target_pairs={{0,4},{4,8},{8,12},{12,14},{14,10},{10,6},{6,2},{2,0},{1,5},{5,9},... | collective-permute-start | bytes 884744 | tf_op jit(solution)/shard_map/ppermute | solution.py:250
  51.0 2.5 %copy-start = (bf16[384,512]{1,0:T(8,128)(2,1)S(1)}, bf16[384,512]{1,0:T(8,128)(2,1)}, u32[]{:S(2)}) copy-start(bf16[384,512]{1,0:T(8,128)(2,1)} %base_ref.1) | copy-start | bytes 1179652
  52.0 1.5 %collective-permute-start.14 = (f32[384,64]{1,0:T(8,128)S(1)}, f32[384,64]{1,0:T(8,128)S(1)}, u32[]{:S(2)}, u32[]{:S(2)}) collective-permute-start(f32[384,64]{1,0:T(8,128)S(1)} %lowrank.7.mine_ref), channel_id=1, source_target_pairs={{0,1},{1,0},{2,3},{3,2},{4,5},{5,4},{6,7},{7,6},{8,9},{9,8},{10,11... | collective-permute-start | bytes 294920 | tf_op jit(solution)/shard_map/ppermute | solution.py:275

commit v6 on v5

--- a/solution.py
+++ b/solution.py
@@ -125,7 +125,7 @@
     place = place_ref[...]
     rows, features = x_ref.shape
     half = w_refs[0].shape[0]
-    stacked = jnp.concatenate([w_ref[:, :features] for w_ref in w_refs], axis=0)
+    stacked = jnp.concatenate([w_ref[...] for w_ref in w_refs], axis=0)
     product = lax.dot_general(x_ref[...], stacked, NT, preferred_element_type=jnp.float32)
     sums = [jnp.zeros((rows, half), jnp.float32)] * 2
     for i in range(count):
@@ -156,13 +156,12 @@
 
 
 def attend_kernel(kv_heads, n, place_ref, mine_ref, theirs_ref, base_ref, *refs):
-    rows, value_portion = base_ref.shape
+    rows = base_ref.shape[0]
     tiles = windows(rows)
-    low_refs, high_refs = refs[:n], refs[n : 2 * n]
-    p_refs = refs[2 * n : 2 * n + kv_heads * len(tiles)]
-    out_ref, block, sems = refs[2 * n + kv_heads * len(tiles) :]
+    up_refs = refs[:n]
+    p_refs = refs[n : n + kv_heads * len(tiles)]
+    out_ref, block, sems = refs[n + kv_heads * len(tiles) :]
     rank = mine_ref.shape[1]
-    features = low_refs[0].shape[1] - value_portion
     place = place_ref[...]
     lowrank = (mine_ref[...] + theirs_ref[...]).astype(jnp.bfloat16)
     twice = jnp.concatenate([lowrank, lowrank], axis=1)
@@ -171,9 +170,7 @@
     spread = jnp.concatenate(
         [jnp.where(offset == i, twice, jnp.zeros_like(twice)) for i in range(0, n, 2)], axis=1
     )
-    up = jnp.concatenate(
-        [ref[:, features:] for pair in zip(low_refs, high_refs) for ref in pair], axis=0
-    )
+    up = jnp.concatenate([up_ref[...] for up_ref in up_refs], axis=0)
     delta = jnp.dot(spread, up, preferred_element_type=jnp.float32).astype(jnp.bfloat16)
     values = (
         base_ref[...].astype(jnp.float32) + adapter_scale * delta.astype(jnp.float32)
@@ -203,20 +200,20 @@
         copy.wait()
 
 
-def attend(place, mine, theirs, base, lows, highs, probs):
+def attend(place, mine, theirs, base, ups, probs):
     rows, value_portion = base.shape
     kv_heads = value_portion // HEAD_SIZE
     wide = kv_heads * GROUP * HEAD_SIZE
     flat = [p for per_head in probs for p in per_head]
     return pl.pallas_call(
-        functools.partial(attend_kernel, kv_heads, len(lows)),
+        functools.partial(attend_kernel, kv_heads, len(ups)),
         out_shape=jax.ShapeDtypeStruct((rows, wide), jnp.bfloat16),
-        in_specs=[VMEM] * (4 + len(lows) + len(highs) + len(flat)),
+        in_specs=[VMEM] * (4 + len(ups) + len(flat)),
         out_specs=pl.BlockSpec(memory_space=pl.ANY),
         scratch_shapes=[pltpu.VMEM((rows, wide), jnp.bfloat16), pltpu.SemaphoreType.DMA((2 * kv_heads,))],
         compiler_params=pltpu.CompilerParams(vmem_limit_bytes=12 * 2**20),
         name="attend",
-    )(place, mine, theirs, base, *lows, *highs, *flat)
+    )(place, mine, theirs, base, *ups, *flat)
 
 
 def on_device(
@@ -236,13 +233,11 @@
     far = n // 2
     distances = [0] + [d for step in range(1, far) for d in (step, -step)] + [far]
     down = jnp.swapaxes(adapter_down_weight[0], 0, 1)
-    both = jnp.concatenate([down, adapter_up_weight[0]], axis=1)
-    rank = both.shape[0]
-    own_low, own_high = both[: rank // 2], both[rank // 2 :]
+    rank = down.shape[0]
+    low, high, up = {0: down[: rank // 2]}, {0: down[rank // 2 :]}, {0: adapter_up_weight[0]}
     place, segment, across = masks(
         n, sequence_lengths, adapter_of_row.reshape(1, -1), queries, stacked_key_rows
     )
-    low, high = {0: own_low}, {0: own_high}
 
     def pass_round(held, pairs, sign, steps):
         piece = held[0]
@@ -254,6 +249,8 @@
     pass_round(low, back, -1, far - 1)
     pass_round(high, back, -1, far)
     pass_round(low, ahead, 1, far)
+    pass_round(up, ahead, 1, far)
+    pass_round(up, back, -1, far - 1)
 
     kv_heads = stacked_key_rows.shape[1] // HEAD_SIZE
     arrivals = [
@@ -269,8 +266,10 @@
     for lo, hi in [(0, 3)] + [(a, a + 2) for a in range(3, n - 1, 2)] + [(n - 1, n)]:
         pieces = [piece for d in distances[lo:hi] for piece in (low[d], high[d])]
         after = arrivals[kv_heads - 1] if lo == 0 else []
+        if lo == n - 5:
+            after = [up[far - 2], up[2 - far]]
         if hi == n:
-            after = [p[0] for p in probs]
+            after = [p[0] for p in probs] + [up[far], up[1 - far]]
         partial = lowrank_of(lo, place, normed_token_rows, partial, pieces, after)
     other = lax.ppermute(partial, "tp", [(0, 1), (1, 0)])
     return attend(
@@ -278,8 +277,7 @@
         partial,
         other,
         base_value_rows,
-        [low[d] for d in distances],
-        [high[d] for d in distances],
+        [up[d] for d in distances],
         probs,
     )
 

time: 56.6 us -> 58.4 us (1.032)
  starting transfers between devices: 15.1 us -> 24.5 us
  waiting for transfers between devices: 21 us -> 13.2 us
  other arithmetic: 1.16 us -> 0 us
  local copies, waits for them, and re-layouts: 4.24 us -> 5.36 us
    ppermute x14 -> x21, starting transfers between devices: 15 us -> 24.5 us  [pass_round(): piece = lax.ppermute(piece, 'rep', pairs)]
    ppermute x14 -> x21, waiting for transfers between devices: 19.6 us -> 11.8 us  [pass_round(): piece = lax.ppermute(piece, 'rep', pairs)]
    concatenate x1 -> x0, other arithmetic: 1.16 us -> none  [on_device(): both = jnp.concatenate([down, adapter_up_weight[0]], axis=1)]
    slice x0 -> x1, local copies, waits for them, and re-layouts: none -> 1.11 us  [on_device(): down[rank // 2:]]
    unnamed x16 -> x18, local copies, waits for them, and re-layouts: 4.24 us -> 4.24 us
  transfers between devices with their start and end apart: 15 -> 22, of which waited for: 9 -> 7; matrix products, arithmetic and copies ran while one was open for 0% -> 0% of each run, Pallas kernels for 19% -> 19%
where the time goes in v6:
time: 58.4 us; the launch traced here: 58.1 us
  starting transfers between devices  24.5 us (42%)
  Pallas kernels  14.7 us (25%)
  waiting for transfers between devices  13.2 us (23%)
  local copies, waits for them, and re-layouts  5.36 us (9%)
    ppermute x21, starting transfers between devices, pass_round(): piece = lax.ppermute(piece, 'rep', pairs)  24.5 us
    ppermute x21, waiting for transfers between devices, pass_round(): piece = lax.ppermute(piece, 'rep', pairs)  11.8 us
    pallas_call x4, Pallas kernels, probs_of(): pl.pallas_call(functools.partial(probs_kernel, kv_head), out_shape=[jax.S...  7.07 us
    unnamed x18, local copies, waits for them, and re-layouts  4.24 us
    pallas_call x4, Pallas kernels, lowrank_of(): pl.pallas_call(functools.partial(lowrank_kernel, at, len(pieces)), out_sh...  4.12 us
    pallas_call x1, Pallas kernels, attend(): pl.pallas_call(functools.partial(attend_kernel, kv_heads, len(ups)), out_...  2.78 us
    ppermute x1, waiting for transfers between devices, on_device(): other = lax.ppermute(partial, 'tp', [(0, 1), (1, 0)])  1.43 us
  transfers between devices with their start and end apart: 22, of which 7 were waited for; matrix products, arithmetic and copies ran while one was open for 0% of the time, Pallas kernels for 19%

profile of v6, /device:TPU:0, one launch (start us, length us, event | category | flops | bytes accessed | tf_op | source)
XLA Modules:
  0.0 58.1 jit_solution(15073124925316403081)
XLA Ops:
  1.1 3.0 %collective-permute-start.4 = (bf16[32,4096]{1,0:T(8,128)(2,1)S(1)}, bf16[32,4096]{1,0:T(8,128)(2,1)S(1)}, u32[]{:S(2)}, u32[]{:S(2)}) collective-permute-start(bf16[32,4096]{1,0:T(8,128)(2,1)S(1)} %get-tuple-element.59.refs_1_), channel_id=1, source_target_pairs={{4,0},{8,4},{12,8},{14,12},{10,14},{6,10},{2,6},{0,2},{5,1},{9,5},... | collective-permute-start | bytes 786440 | tf_op jit(solution)/shard_map/ppermute | solution.py:245
  4.3 2.0 %collective-permute-start.8 = (bf16[32,4096]{1,0:T(8,128)(2,1)S(1)}, bf16[32,4096]{1,0:T(8,128)(2,1)S(1)}, u32[]{:S(2)}, u32[]{:S(2)}) collective-permute-start(bf16[32,4096]{1,0:T(8,128)(2,1)S(1)} %get-tuple-element.59.refs_1_), channel_id=1, source_target_pairs={{0,4},{4,8},{8,12},{12,14},{14,10},{10,6},{6,2},{2,0},{1,5},{5,9},... | collective-permute-start | bytes 786440 | tf_op jit(solution)/shard_map/ppermute | solution.py:245
  6.3 1.9 %collective-permute-start.16 = (bf16[64,512]{1,0:T(8,128)(2,1)}, bf16[64,512]{1,0:T(8,128)(2,1)S(1)}, u32[]{:S(2)}, u32[]{:S(2)}) collective-permute-start(bf16[64,512]{1,0:T(8,128)(2,1)} %bitcast.6), channel_id=1, source_target_pairs={{4,0},{8,4},{12,8},{14,12},{10,14},{6,10},{2,6},{0,2},{5,1},{9,5},... | collective-permute-start | bytes 196616 | tf_op jit(solution)/shard_map/ppermute | solution.py:245
  8.2 1.9 %copy-done.2 = bf16[384,4096]{1,0:T(8,128)(2,1)S(1)} copy-done((bf16[384,4096]{1,0:T(8,128)(2,1)S(1)}, bf16[384,4096]{1,0:T(8,128)(2,1)}, u32[]{:S(2)}) %copy-start.2) | copy-done | bytes 3145752
  13.2 1.6 %collective-permute-start.5 = (bf16[32,4096]{1,0:T(8,128)(2,1)S(1)}, bf16[32,4096]{1,0:T(8,128)(2,1)S(1)}, u32[]{:S(2)}, u32[]{:S(2)}) collective-permute-start(bf16[32,4096]{1,0:T(8,128)(2,1)S(1)} %collective-permute-done.4.refs_5_.refs_1_), channel_id=1, source_target_pairs={{4,0},{8,4},{12,8},{14,12},{10,14},{6,10},{2,6},{0,2},{5,1},{9,5},... | collective-permute-start | bytes 786440 | tf_op jit(solution)/shard_map/ppermute | solution.py:245
  15.2 1.8 %probs.5 = (bf16[512,128]{1,0:T(8,128)(2,1)S(1)}, bf16[512,128]{1,0:T(8,128)(2,1)S(1)}, bf16[512,256]{1,0:T(8,128)(2,1)S(1)}, bf16[512,256]{1,0:T(8,128)(2,1)S(1...) custom-call(s32[384,1]{1,0:T(8,128)S(1)} %get-tuple-element.33.segment_ref, ...), custom_call_target="tpu_custom_call" | custom-call | flops 2000000000 | bytes 1310720 | tf_op jit(solution)/shard_map/probs/pallas_call | solution.py:109
  17.0 1.8 %probs.4 = (bf16[512,128]{1,0:T(8,128)(2,1)S(1)}, bf16[512,128]{1,0:T(8,128)(2,1)S(1)}, bf16[512,256]{1,0:T(8,128)(2,1)S(1)}, bf16[512,256]{1,0:T(8,128)(2,1)S(1...) custom-call(s32[384,1]{1,0:T(8,128)S(1)} %get-tuple-element.33.segment_ref, ...), custom_call_target="tpu_custom_call" | custom-call | flops 2000000000 | bytes 1310720 | tf_op jit(solution)/shard_map/probs/pallas_call | solution.py:109
  18.8 1.6 %collective-permute-start.14 = (bf16[64,512]{1,0:T(8,128)(2,1)S(1)}, bf16[64,512]{1,0:T(8,128)(2,1)S(1)}, u32[]{:S(2)}, u32[]{:S(2)}) collective-permute-start(bf16[64,512]{1,0:T(8,128)(2,1)S(1)} %bitcast.7), channel_id=1, source_target_pairs={{0,4},{4,8},{8,12},{12,14},{14,10},{10,6},{6,2},{2,0},{1,5},{5,9},... | collective-permute-start | bytes 196616 | tf_op jit(solution)/shard_map/ppermute | solution.py:245
  20.4 1.6 %collective-permute-start.9 = (bf16[32,4096]{1,0:T(8,128)(2,1)S(1)}, bf16[32,4096]{1,0:T(8,128)(2,1)S(1)}, u32[]{:S(2)}, u32[]{:S(2)}) collective-permute-start(bf16[32,4096]{1,0:T(8,128)(2,1)S(1)} %collective-permute-done.8.refs_3_.refs_0_), channel_id=1, source_target_pairs={{0,4},{4,8},{8,12},{12,14},{14,10},{10,6},{6,2},{2,0},{1,5},{5,9},... | collective-permute-start | bytes 786440 | tf_op jit(solution)/shard_map/ppermute | solution.py:245
  22.4 1.8 %probs.7 = (bf16[512,128]{1,0:T(8,128)(2,1)S(1)}, bf16[512,128]{1,0:T(8,128)(2,1)S(1)}, bf16[512,256]{1,0:T(8,128)(2,1)S(1)}, bf16[512,256]{1,0:T(8,128)(2,1)S(1...) custom-call(s32[384,1]{1,0:T(8,128)S(1)} %get-tuple-element.33.segment_ref, ...), custom_call_target="tpu_custom_call" | custom-call | flops 2000000000 | bytes 1310720 | tf_op jit(solution)/shard_map/probs/pallas_call | solution.py:109
  24.2 1.8 %collective-permute-done.14.refs_1_ = bf16[64,512]{1,0:T(8,128)(2,1)S(1)} collective-permute-done((bf16[64,512]{1,0:T(8,128)(2,1)S(1)}, bf16[64,512]{1,0:T(8,128)(2,1)S(1)}, u32[]{:S(2)}, u32[]{:S(2)}) %collective-permute-start.14) | collective-permute-done | bytes 65568 | tf_op jit(solution)/shard_map/ppermute | solution.py:245
  26.0 1.6 %collective-permute-start.17 = (bf16[64,512]{1,0:T(8,128)(2,1)S(1)}, bf16[64,512]{1,0:T(8,128)(2,1)S(1)}, u32[]{:S(2)}, u32[]{:S(2)}) collective-permute-start(bf16[64,512]{1,0:T(8,128)(2,1)S(1)} %collective-permute-done.16.refs_2_), channel_id=1, source_target_pairs={{4,0},{8,4},{12,8},{14,12},{10,14},{6,10},{2,6},{0,2},{5,1},{9,5},... | collective-permute-start | bytes 196616 | tf_op jit(solution)/shard_map/ppermute | solution.py:245
  27.6 1.6 %collective-permute-start.6 = (bf16[32,4096]{1,0:T(8,128)(2,1)S(1)}, bf16[32,4096]{1,0:T(8,128)(2,1)S(1)}, u32[]{:S(2)}, u32[]{:S(2)}) collective-permute-start(bf16[32,4096]{1,0:T(8,128)(2,1)S(1)} %collective-permute-done.5.refs_3_), channel_id=1, source_target_pairs={{4,0},{8,4},{12,8},{14,12},{10,14},{6,10},{2,6},{0,2},{5,1},{9,5},... | collective-permute-start | bytes 786440 | tf_op jit(solution)/shard_map/ppermute | solution.py:245
  29.6 1.8 %probs.6 = (bf16[512,128]{1,0:T(8,128)(2,1)S(1)}, bf16[512,128]{1,0:T(8,128)(2,1)S(1)}, bf16[512,256]{1,0:T(8,128)(2,1)S(1)}, bf16[512,256]{1,0:T(8,128)(2,1)S(1...) custom-call(s32[384,1]{1,0:T(8,128)S(1)} %get-tuple-element.33.segment_ref, ...), custom_call_target="tpu_custom_call" | custom-call | flops 2000000000 | bytes 1310720 | tf_op jit(solution)/shard_map/probs/pallas_call | solution.py:109
  31.4 1.3 %collective-permute-done.17.refs_6_.refs_4_ = bf16[64,512]{1,0:T(8,128)(2,1)S(1)} collective-permute-done((bf16[64,512]{1,0:T(8,128)(2,1)S(1)}, bf16[64,512]{1,0:T(8,128)(2,1)S(1)}, u32[]{:S(2)}, u32[]{:S(2)}) %collective-permute-start.17) | collective-permute-done | bytes 65568 | tf_op jit(solution)/shard_map/ppermute | solution.py:245
  32.6 1.6 %collective-permute-start.15 = (bf16[64,512]{1,0:T(8,128)(2,1)S(1)}, bf16[64,512]{1,0:T(8,128)(2,1)S(1)}, u32[]{:S(2)}, u32[]{:S(2)}) collective-permute-start(bf16[64,512]{1,0:T(8,128)(2,1)S(1)} %collective-permute-done.14.refs_1_), channel_id=1, source_target_pairs={{0,4},{4,8},{8,12},{12,14},{14,10},{10,6},{6,2},{2,0},{1,5},{5,9},... | collective-permute-start | bytes 196616 | tf_op jit(solution)/shard_map/ppermute | solution.py:245
  34.2 1.5 %collective-permute-start.10 = (bf16[32,4096]{1,0:T(8,128)(2,1)S(1)}, bf16[32,4096]{1,0:T(8,128)(2,1)S(1)}, u32[]{:S(2)}, u32[]{:S(2)}) collective-permute-start(bf16[32,4096]{1,0:T(8,128)(2,1)S(1)} %collective-permute-done.9.refs_6_.refs_1_), channel_id=1, source_target_pairs={{0,4},{4,8},{8,12},{12,14},{14,10},{10,6},{6,2},{2,0},{1,5},{5,9},... | collective-permute-start | bytes 786440 | tf_op jit(solution)/shard_map/ppermute | solution.py:245
  37.3 2.5 %collective-permute-done.15.refs_5_.refs_3_ = bf16[64,512]{1,0:T(8,128)(2,1)S(1)} collective-permute-done((bf16[64,512]{1,0:T(8,128)(2,1)S(1)}, bf16[64,512]{1,0:T(8,128)(2,1)S(1)}, u32[]{:S(2)}, u32[]{:S(2)}) %collective-permute-start.15) | collective-permute-done | bytes 65568 | tf_op jit(solution)/shard_map/ppermute | solution.py:245
  40.3 1.6 %collective-permute-start.7 = (bf16[32,4096]{1,0:T(8,128)(2,1)S(1)}, bf16[32,4096]{1,0:T(8,128)(2,1)S(1)}, u32[]{:S(2)}, u32[]{:S(2)}) collective-permute-start(bf16[32,4096]{1,0:T(8,128)(2,1)S(1)} %collective-permute-done.6.refs_3_), channel_id=1, source_target_pairs={{4,0},{8,4},{12,8},{14,12},{10,14},{6,10},{2,6},{0,2},{5,1},{9,5},... | collective-permute-start | bytes 786440 | tf_op jit(solution)/shard_map/ppermute | solution.py:245
  43.4 3.5 %collective-permute-done.18.refs_5_ = bf16[64,512]{1,0:T(8,128)(2,1)S(1)} collective-permute-done((bf16[64,512]{1,0:T(8,128)(2,1)S(1)}, bf16[64,512]{1,0:T(8,128)(2,1)S(1)}, u32[]{:S(2)}, u32[]{:S(2)}) %collective-permute-start.18) | collective-permute-done | bytes 65568 | tf_op jit(solution)/shard_map/ppermute | solution.py:245
  46.8 1.6 %collective-permute-start.20 = (bf16[64,512]{1,0:T(8,128)(2,1)S(1)}, bf16[64,512]{1,0:T(8,128)(2,1)S(1)}, u32[]{:S(2)}, u32[]{:S(2)}) collective-permute-start(bf16[64,512]{1,0:T(8,128)(2,1)S(1)} %collective-permute-done.17.refs_6_.refs_4_), channel_id=1, source_target_pairs={{4,0},{8,4},{12,8},{14,12},{10,14},{6,10},{2,6},{0,2},{5,1},{9,5},... | collective-permute-start | bytes 196616 | tf_op jit(solution)/shard_map/ppermute | solution.py:245
  51.1 1.6 %collective-permute-done.19.refs_7_ = bf16[64,512]{1,0:T(8,128)(2,1)S(1)} collective-permute-done((bf16[64,512]{1,0:T(8,128)(2,1)S(1)}, bf16[64,512]{1,0:T(8,128)(2,1)S(1)}, u32[]{:S(2)}, u32[]{:S(2)}) %collective-permute-start.19) | collective-permute-done | bytes 65568 | tf_op jit(solution)/shard_map/ppermute | solution.py:245
  53.7 1.4 %collective-permute-done.21.theirs_ref = f32[384,64]{1,0:T(8,128)S(1)} collective-permute-done((f32[384,64]{1,0:T(8,128)S(1)}, f32[384,64]{1,0:T(8,128)S(1)}, u32[]{:S(2)}, u32[]{:S(2)}) %collective-permute-start.21) | collective-permute-done | bytes 98336 | tf_op jit(solution)/shard_map/ppermute | solution.py:274
  55.2 2.8 %attend.1 = bf16[384,4096]{1,0:T(8,128)(2,1)} custom-call(s32[384,1]{1,0:T(8,128)S(1)} %get-tuple-element.32.place_ref, f32[384,64]{1,0:T(8,128)S(1)} %lowrank.7.mine_ref, f32[384,64]{1,0:T(8,128)S(1)} %collective-permute-done.21.theirs_ref, bf16[384,512]{1,0:T(8,128)(2,1)S(1)} %copy-done, bf16[64,512]{1,0:T(8,128)(2,1)S(1)} %bitcast.8, ...), custom_call_target="tpu_custom_call" | custom-call | tf_op jit(solution)/shard_map/attend/pallas_call | solution.py:208
  (49 shorter events, 13.0 us)
Async XLA Ops:
  0.0 15.2 %copy-start.6 = (bf16[384,512]{1,0:T(8,128)(2,1)S(1)}, bf16[384,512]{1,0:T(8,128)(2,1)}, u32[]{:S(2)}) copy-start(bf16[384,512]{1,0:T(8,128)(2,1)} %k_ref.7) | copy-start | bytes 1179652
  1.1 12.0 %collective-permute-start.4 = (bf16[32,4096]{1,0:T(8,128)(2,1)S(1)}, bf16[32,4096]{1,0:T(8,128)(2,1)S(1)}, u32[]{:S(2)}, u32[]{:S(2)}) collective-permute-start(bf16[32,4096]{1,0:T(8,128)(2,1)S(1)} %get-tuple-element.59.refs_1_), channel_id=1, source_target_pairs={{4,0},{8,4},{12,8},{14,12},{10,14},{6,10},{2,6},{0,2},{5,1},{9,5},... | collective-permute-start | bytes 786440 | tf_op jit(solution)/shard_map/ppermute | solution.py:245
  4.1 10.6 %collective-permute-start = (bf16[32,4096]{1,0:T(8,128)(2,1)S(1)}, bf16[32,4096]{1,0:T(8,128)(2,1)S(1)}, u32[]{:S(2)}, u32[]{:S(2)}) collective-permute-start(bf16[32,4096]{1,0:T(8,128)(2,1)S(1)} %get-tuple-element.60.refs_0_), channel_id=1, source_target_pairs={{0,4},{4,8},{8,12},{12,14},{14,10},{10,6},{6,2},{2,0},{1,5},{5,9},... | collective-permute-start | bytes 786440 | tf_op jit(solution)/shard_map/ppermute | solution.py:245
  4.3 16.2 %collective-permute-start.8 = (bf16[32,4096]{1,0:T(8,128)(2,1)S(1)}, bf16[32,4096]{1,0:T(8,128)(2,1)S(1)}, u32[]{:S(2)}, u32[]{:S(2)}) collective-permute-start(bf16[32,4096]{1,0:T(8,128)(2,1)S(1)} %get-tuple-element.59.refs_1_), channel_id=1, source_target_pairs={{0,4},{4,8},{8,12},{12,14},{14,10},{10,6},{6,2},{2,0},{1,5},{5,9},... | collective-permute-start | bytes 786440 | tf_op jit(solution)/shard_map/ppermute | solution.py:245
  6.2 15.8 %collective-permute-start.11 = (bf16[32,4096]{1,0:T(8,128)(2,1)S(1)}, bf16[32,4096]{1,0:T(8,128)(2,1)S(1)}, u32[]{:S(2)}, u32[]{:S(2)}) collective-permute-start(bf16[32,4096]{1,0:T(8,128)(2,1)S(1)} %get-tuple-element.60.refs_0_), channel_id=1, source_target_pairs={{4,0},{8,4},{12,8},{14,12},{10,14},{6,10},{2,6},{0,2},{5,1},{9,5},... | collective-permute-start | bytes 786440 | tf_op jit(solution)/shard_map/ppermute | solution.py:245
  6.3 12.5 %collective-permute-start.16 = (bf16[64,512]{1,0:T(8,128)(2,1)}, bf16[64,512]{1,0:T(8,128)(2,1)S(1)}, u32[]{:S(2)}, u32[]{:S(2)}) collective-permute-start(bf16[64,512]{1,0:T(8,128)(2,1)} %bitcast.6), channel_id=1, source_target_pairs={{4,0},{8,4},{12,8},{14,12},{10,14},{6,10},{2,6},{0,2},{5,1},{9,5},... | collective-permute-start | bytes 196616 | tf_op jit(solution)/shard_map/ppermute | solution.py:245
  13.2 14.4 %collective-permute-start.5 = (bf16[32,4096]{1,0:T(8,128)(2,1)S(1)}, bf16[32,4096]{1,0:T(8,128)(2,1)S(1)}, u32[]{:S(2)}, u32[]{:S(2)}) collective-permute-start(bf16[32,4096]{1,0:T(8,128)(2,1)S(1)} %collective-permute-done.4.refs_5_.refs_1_), channel_id=1, source_target_pairs={{4,0},{8,4},{12,8},{14,12},{10,14},{6,10},{2,6},{0,2},{5,1},{9,5},... | collective-permute-start | bytes 786440 | tf_op jit(solution)/shard_map/ppermute | solution.py:245
  14.8 14.4 %collective-permute-start.1 = (bf16[32,4096]{1,0:T(8,128)(2,1)S(1)}, bf16[32,4096]{1,0:T(8,128)(2,1)S(1)}, u32[]{:S(2)}, u32[]{:S(2)}) collective-permute-start(bf16[32,4096]{1,0:T(8,128)(2,1)S(1)} %collective-permute-done.refs_2_.refs_0_), channel_id=1, source_target_pairs={{0,4},{4,8},{8,12},{12,14},{14,10},{10,6},{6,2},{2,0},{1,5},{5,9},... | collective-permute-start | bytes 786440 | tf_op jit(solution)/shard_map/ppermute | solution.py:245
  18.8 7.2 %collective-permute-start.14 = (bf16[64,512]{1,0:T(8,128)(2,1)S(1)}, bf16[64,512]{1,0:T(8,128)(2,1)S(1)}, u32[]{:S(2)}, u32[]{:S(2)}) collective-permute-start(bf16[64,512]{1,0:T(8,128)(2,1)S(1)} %bitcast.7), channel_id=1, source_target_pairs={{0,4},{4,8},{8,12},{12,14},{14,10},{10,6},{6,2},{2,0},{1,5},{5,9},... | collective-permute-start | bytes 196616 | tf_op jit(solution)/shard_map/ppermute | solution.py:245
  20.4 13.8 %collective-permute-start.9 = (bf16[32,4096]{1,0:T(8,128)(2,1)S(1)}, bf16[32,4096]{1,0:T(8,128)(2,1)S(1)}, u32[]{:S(2)}, u32[]{:S(2)}) collective-permute-start(bf16[32,4096]{1,0:T(8,128)(2,1)S(1)} %collective-permute-done.8.refs_3_.refs_0_), channel_id=1, source_target_pairs={{0,4},{4,8},{8,12},{12,14},{14,10},{10,6},{6,2},{2,0},{1,5},{5,9},... | collective-permute-start | bytes 786440 | tf_op jit(solution)/shard_map/ppermute | solution.py:245
  22.0 13.8 %collective-permute-start.12 = (bf16[32,4096]{1,0:T(8,128)(2,1)S(1)}, bf16[32,4096]{1,0:T(8,128)(2,1)S(1)}, u32[]{:S(2)}, u32[]{:S(2)}) collective-permute-start(bf16[32,4096]{1,0:T(8,128)(2,1)S(1)} %collective-permute-done.11.refs_4_.refs_1_), channel_id=1, source_target_pairs={{4,0},{8,4},{12,8},{14,12},{10,14},{6,10},{2,6},{0,2},{5,1},{9,5},... | collective-permute-start | bytes 786440 | tf_op jit(solution)/shard_map/ppermute | solution.py:245
  24.2 12.0 %copy-start.4 = (bf16[384,4096]{1,0:T(8,128)(2,1)S(1)}, bf16[384,4096]{1,0:T(8,128)(2,1)}, u32[]{:S(2)}) copy-start(bf16[384,4096]{1,0:T(8,128)(2,1)} %x_ref.7) | copy-start | bytes 9437188
  26.0 6.6 %collective-permute-start.17 = (bf16[64,512]{1,0:T(8,128)(2,1)S(1)}, bf16[64,512]{1,0:T(8,128)(2,1)S(1)}, u32[]{:S(2)}, u32[]{:S(2)}) collective-permute-start(bf16[64,512]{1,0:T(8,128)(2,1)S(1)} %collective-permute-done.16.refs_2_), channel_id=1, source_target_pairs={{4,0},{8,4},{12,8},{14,12},{10,14},{6,10},{2,6},{0,2},{5,1},{9,5},... | collective-permute-start | bytes 196616 | tf_op jit(solution)/shard_map/ppermute | solution.py:245
  27.6 12.7 %collective-permute-start.6 = (bf16[32,4096]{1,0:T(8,128)(2,1)S(1)}, bf16[32,4096]{1,0:T(8,128)(2,1)S(1)}, u32[]{:S(2)}, u32[]{:S(2)}) collective-permute-start(bf16[32,4096]{1,0:T(8,128)(2,1)S(1)} %collective-permute-done.5.refs_3_), channel_id=1, source_target_pairs={{4,0},{8,4},{12,8},{14,12},{10,14},{6,10},{2,6},{0,2},{5,1},{9,5},... | collective-permute-start | bytes 786440 | tf_op jit(solution)/shard_map/ppermute | solution.py:245
  29.2 12.7 %collective-permute-start.2 = (bf16[32,4096]{1,0:T(8,128)(2,1)S(1)}, bf16[32,4096]{1,0:T(8,128)(2,1)S(1)}, u32[]{:S(2)}, u32[]{:S(2)}) collective-permute-start(bf16[32,4096]{1,0:T(8,128)(2,1)S(1)} %collective-permute-done.1.refs_0_), channel_id=1, source_target_pairs={{0,4},{4,8},{8,12},{12,14},{14,10},{10,6},{6,2},{2,0},{1,5},{5,9},... | collective-permute-start | bytes 786440 | tf_op jit(solution)/shard_map/ppermute | solution.py:245
  32.6 7.2 %collective-permute-start.15 = (bf16[64,512]{1,0:T(8,128)(2,1)S(1)}, bf16[64,512]{1,0:T(8,128)(2,1)S(1)}, u32[]{:S(2)}, u32[]{:S(2)}) collective-permute-start(bf16[64,512]{1,0:T(8,128)(2,1)S(1)} %collective-permute-done.14.refs_1_), channel_id=1, source_target_pairs={{0,4},{4,8},{8,12},{12,14},{14,10},{10,6},{6,2},{2,0},{1,5},{5,9},... | collective-permute-start | bytes 196616 | tf_op jit(solution)/shard_map/ppermute | solution.py:245
  34.2 14.2 %collective-permute-start.10 = (bf16[32,4096]{1,0:T(8,128)(2,1)S(1)}, bf16[32,4096]{1,0:T(8,128)(2,1)S(1)}, u32[]{:S(2)}, u32[]{:S(2)}) collective-permute-start(bf16[32,4096]{1,0:T(8,128)(2,1)S(1)} %collective-permute-done.9.refs_6_.refs_1_), channel_id=1, source_target_pairs={{0,4},{4,8},{8,12},{12,14},{14,10},{10,6},{6,2},{2,0},{1,5},{5,9},... | collective-permute-start | bytes 786440 | tf_op jit(solution)/shard_map/ppermute | solution.py:245
  35.8 13.1 %collective-permute-start.13 = (bf16[32,4096]{1,0:T(8,128)(2,1)S(1)}, bf16[32,4096]{1,0:T(8,128)(2,1)S(1)}, u32[]{:S(2)}, u32[]{:S(2)}) collective-permute-start(bf16[32,4096]{1,0:T(8,128)(2,1)S(1)} %collective-permute-done.12.refs_7_.refs_2_), channel_id=1, source_target_pairs={{4,0},{8,4},{12,8},{14,12},{10,14},{6,10},{2,6},{0,2},{5,1},{9,5},... | collective-permute-start | bytes 786440 | tf_op jit(solution)/shard_map/ppermute | solution.py:245
  39.8 7.0 %collective-permute-start.18 = (bf16[64,512]{1,0:T(8,128)(2,1)S(1)}, bf16[64,512]{1,0:T(8,128)(2,1)S(1)}, u32[]{:S(2)}, u32[]{:S(2)}) collective-permute-start(bf16[64,512]{1,0:T(8,128)(2,1)S(1)} %collective-permute-done.15.refs_5_.refs_3_), channel_id=1, source_target_pairs={{0,4},{4,8},{8,12},{12,14},{14,10},{10,6},{6,2},{2,0},{1,5},{5,9},... | collective-permute-start | bytes 196616 | tf_op jit(solution)/shard_map/ppermute | solution.py:245
  40.3 12.4 %collective-permute-start.7 = (bf16[32,4096]{1,0:T(8,128)(2,1)S(1)}, bf16[32,4096]{1,0:T(8,128)(2,1)S(1)}, u32[]{:S(2)}, u32[]{:S(2)}) collective-permute-start(bf16[32,4096]{1,0:T(8,128)(2,1)S(1)} %collective-permute-done.6.refs_3_), channel_id=1, source_target_pairs={{4,0},{8,4},{12,8},{14,12},{10,14},{6,10},{2,6},{0,2},{5,1},{9,5},... | collective-permute-start | bytes 786440 | tf_op jit(solution)/shard_map/ppermute | solution.py:245
  41.9 10.8 %collective-permute-start.3 = (bf16[32,4096]{1,0:T(8,128)(2,1)S(1)}, bf16[32,4096]{1,0:T(8,128)(2,1)S(1)}, u32[]{:S(2)}, u32[]{:S(2)}) collective-permute-start(bf16[32,4096]{1,0:T(8,128)(2,1)S(1)} %collective-permute-done.2.refs_0_), channel_id=1, source_target_pairs={{0,4},{4,8},{8,12},{12,14},{14,10},{10,6},{6,2},{2,0},{1,5},{5,9},... | collective-permute-start | bytes 786440 | tf_op jit(solution)/shard_map/ppermute | solution.py:245
  46.8 4.3 %collective-permute-start.20 = (bf16[64,512]{1,0:T(8,128)(2,1)S(1)}, bf16[64,512]{1,0:T(8,128)(2,1)S(1)}, u32[]{:S(2)}, u32[]{:S(2)}) collective-permute-start(bf16[64,512]{1,0:T(8,128)(2,1)S(1)} %collective-permute-done.17.refs_6_.refs_4_), channel_id=1, source_target_pairs={{4,0},{8,4},{12,8},{14,12},{10,14},{6,10},{2,6},{0,2},{5,1},{9,5},... | collective-permute-start | bytes 196616 | tf_op jit(solution)/shard_map/ppermute | solution.py:245
  48.4 4.3 %collective-permute-start.19 = (bf16[64,512]{1,0:T(8,128)(2,1)S(1)}, bf16[64,512]{1,0:T(8,128)(2,1)S(1)}, u32[]{:S(2)}, u32[]{:S(2)}) collective-permute-start(bf16[64,512]{1,0:T(8,128)(2,1)S(1)} %collective-permute-done.18.refs_5_), channel_id=1, source_target_pairs={{0,4},{4,8},{8,12},{12,14},{14,10},{10,6},{6,2},{2,0},{1,5},{5,9},... | collective-permute-start | bytes 196616 | tf_op jit(solution)/shard_map/ppermute | solution.py:245
  53.7 1.5 %collective-permute-start.21 = (f32[384,64]{1,0:T(8,128)S(1)}, f32[384,64]{1,0:T(8,128)S(1)}, u32[]{:S(2)}, u32[]{:S(2)}) collective-permute-start(f32[384,64]{1,0:T(8,128)S(1)} %lowrank.7.mine_ref), channel_id=1, source_target_pairs={{0,1},{1,0},{2,3},{3,2},{4,5},{5,4},{6,7},{7,6},{8,9},{9,8},{10,11... | collective-permute-start | bytes 294920 | tf_op jit(solution)/shard_map/ppermute | solution.py:274
  (7 other events, 11.3 us)

commit v7 on v6

--- a/solution.py
+++ b/solution.py
@@ -50,7 +50,7 @@
 
 
 def masks_kernel(n, me_ref, lengths_ref, adapter_ref, near_q_ref, near_k_ref, *refs):
-    place_ref, segment_ref, across_ref = refs
+    place_ref, segment_ref, across_ref = refs[-3:]
     distance = ring_place(me_ref[0], n) - ring_place(adapter_ref[...], n)
     distance = jnp.where(distance < 0, distance + n, distance)
     place = jnp.where(distance <= n // 2, jnp.maximum(2 * distance - 1, 0), 2 * (n - distance))
@@ -65,19 +65,19 @@
     segment_ref[...] = column(segment)
 
 
-def masks(n, lengths, adapter_row, queries, keys):
+def masks(n, lengths, adapter_row, queries, keys, after):
     rows = keys.shape[0]
     tall = jax.ShapeDtypeStruct((rows, 1), jnp.int32)
     me = jnp.reshape(lax.axis_index("rep"), (1,)).astype(jnp.int32)
     return pl.pallas_call(
         functools.partial(masks_kernel, n),
         out_shape=[tall, tall, jax.ShapeDtypeStruct((1, rows), jnp.int32)],
-        in_specs=[SMEM, SMEM, VMEM, VMEM, VMEM],
+        in_specs=[SMEM, SMEM, VMEM, VMEM, VMEM] + [pl.BlockSpec(memory_space=pl.ANY)] * len(after),
         out_specs=[VMEM] * 3,
         cost_estimate=pl.CostEstimate(flops=1_000_000_000, bytes_accessed=16 * rows, transcendentals=0),
         compiler_params=pltpu.CompilerParams(vmem_limit_bytes=4 * 2**20),
         name="masks",
-    )(me, lengths, adapter_row, queries, keys)
+    )(me, lengths, adapter_row, queries, keys, *after)
 
 
 def probs_kernel(kv_head, segment_ref, across_ref, q_ref, k_ref, *refs):
@@ -235,10 +235,6 @@
     down = jnp.swapaxes(adapter_down_weight[0], 0, 1)
     rank = down.shape[0]
     low, high, up = {0: down[: rank // 2]}, {0: down[rank // 2 :]}, {0: adapter_up_weight[0]}
-    place, segment, across = masks(
-        n, sequence_lengths, adapter_of_row.reshape(1, -1), queries, stacked_key_rows
-    )
-
     def pass_round(held, pairs, sign, steps):
         piece = held[0]
         for step in range(1, steps + 1):
@@ -252,24 +248,27 @@
     pass_round(up, ahead, 1, far)
     pass_round(up, back, -1, far - 1)
 
+    place, segment, across = masks(
+        n, sequence_lengths, adapter_of_row.reshape(1, -1), queries, stacked_key_rows, [up[1], up[-1]]
+    )
     kv_heads = stacked_key_rows.shape[1] // HEAD_SIZE
     arrivals = [
         pair
         for step in range(1, far)
         for pair in ([low[step], high[-step]], [high[step], low[-step]])
     ]
+    up_after = [[up[2], up[-2]], [], [up[far - 1], up[1 - far]], []]
     probs = [
-        probs_of(segment, across, queries, stacked_key_rows, kv, arrivals[kv // 2]) for kv in range(kv_heads)
+        probs_of(segment, across, queries, stacked_key_rows, kv, arrivals[kv // 2] + up_after[kv])
+        for kv in range(kv_heads)
     ]
 
     partial = None
     for lo, hi in [(0, 3)] + [(a, a + 2) for a in range(3, n - 1, 2)] + [(n - 1, n)]:
         pieces = [piece for d in distances[lo:hi] for piece in (low[d], high[d])]
-        after = arrivals[kv_heads - 1] if lo == 0 else []
-        if lo == n - 5:
-            after = [up[far - 2], up[2 - far]]
+        after = arrivals[min(2, len(arrivals) - 1)] + [up[far]] if lo == 0 else []
         if hi == n:
-            after = [p[0] for p in probs] + [up[far], up[1 - far]]
+            after = [p[0] for p in probs]
         partial = lowrank_of(lo, place, normed_token_rows, partial, pieces, after)
     other = lax.ppermute(partial, "tp", [(0, 1), (1, 0)])
     return attend(

time: 58.4 us -> 62.4 us (1.068)
  waiting for transfers between devices: 13.2 us -> 18.1 us
  starting transfers between devices: 24.5 us -> 23.8 us
    ppermute x21, waiting for transfers between devices: 11.8 us -> 16.7 us  [pass_round(): piece = lax.ppermute(piece, 'rep', pairs)]
    ppermute x21, starting transfers between devices: 24.5 us -> 23.7 us  [pass_round(): piece = lax.ppermute(piece, 'rep', pairs)]
  transfers between devices with their start and end apart: 22 -> 22, of which waited for: 7 -> 9; matrix products, arithmetic and copies ran while one was open for 0% -> 0% of each run, Pallas kernels for 19% -> 17%
where the time goes in v7:
time: 62.4 us; the launch traced here: 62.2 us
  starting transfers between devices  23.8 us (38%)
  waiting for transfers between devices  18.1 us (29%)
  Pallas kernels  14.6 us (23%)
  local copies, waits for them, and re-layouts  5.35 us (9%)
    ppermute x21, starting transfers between devices, pass_round(): piece = lax.ppermute(piece, 'rep', pairs)  23.7 us
    ppermute x21, waiting for transfers between devices, pass_round(): piece = lax.ppermute(piece, 'rep', pairs)  16.7 us
    pallas_call x4, Pallas kernels, probs_of(): pl.pallas_call(functools.partial(probs_kernel, kv_head), out_shape=[jax.S...  7.01 us
    unnamed x18, local copies, waits for them, and re-layouts  4.24 us
    pallas_call x4, Pallas kernels, lowrank_of(): pl.pallas_call(functools.partial(lowrank_kernel, at, len(pieces)), out_sh...  4.11 us
    pallas_call x1, Pallas kernels, attend(): pl.pallas_call(functools.partial(attend_kernel, kv_heads, len(ups)), out_...  2.79 us
    ppermute x1, waiting for transfers between devices, on_device(): other = lax.ppermute(partial, 'tp', [(0, 1), (1, 0)])  1.43 us
  transfers between devices with their start and end apart: 22, of which 9 were waited for; matrix products, arithmetic and copies ran while one was open for 0% of the time, Pallas kernels for 17%

profile of v7, /device:TPU:0, one launch (start us, length us, event | category | flops | bytes accessed | tf_op | source)
XLA Modules:
  0.0 62.2 jit_solution(12178347759620160831)
XLA Ops:
  1.1 3.0 %collective-permute-start.6 = (bf16[32,4096]{1,0:T(8,128)(2,1)S(1)}, bf16[32,4096]{1,0:T(8,128)(2,1)S(1)}, u32[]{:S(2)}, u32[]{:S(2)}) collective-permute-start(bf16[32,4096]{1,0:T(8,128)(2,1)S(1)} %get-tuple-element.59.refs_1_), channel_id=1, source_target_pairs={{4,0},{8,4},{12,8},{14,12},{10,14},{6,10},{2,6},{0,2},{5,1},{9,5},... | collective-permute-start | bytes 786440 | tf_op jit(solution)/shard_map/ppermute | solution.py:241
  4.3 1.9 %collective-permute-start.1 = (bf16[64,512]{1,0:T(8,128)(2,1)}, bf16[64,512]{1,0:T(8,128)(2,1)S(1)}, u32[]{:S(2)}, u32[]{:S(2)}) collective-permute-start(bf16[64,512]{1,0:T(8,128)(2,1)} %bitcast.6), channel_id=1, source_target_pairs={{4,0},{8,4},{12,8},{14,12},{10,14},{6,10},{2,6},{0,2},{5,1},{9,5},... | collective-permute-start | bytes 196616 | tf_op jit(solution)/shard_map/ppermute | solution.py:241
  6.3 2.0 %collective-permute-start.10 = (bf16[32,4096]{1,0:T(8,128)(2,1)S(1)}, bf16[32,4096]{1,0:T(8,128)(2,1)S(1)}, u32[]{:S(2)}, u32[]{:S(2)}) collective-permute-start(bf16[32,4096]{1,0:T(8,128)(2,1)S(1)} %get-tuple-element.59.refs_1_), channel_id=1, source_target_pairs={{0,4},{4,8},{8,12},{12,14},{14,10},{10,6},{6,2},{2,0},{1,5},{5,9},... | collective-permute-start | bytes 786440 | tf_op jit(solution)/shard_map/ppermute | solution.py:241
  8.2 3.7 %collective-permute-done.1.refs_1_.refs_2_ = bf16[64,512]{1,0:T(8,128)(2,1)S(1)} collective-permute-done((bf16[64,512]{1,0:T(8,128)(2,1)}, bf16[64,512]{1,0:T(8,128)(2,1)S(1)}, u32[]{:S(2)}, u32[]{:S(2)}) %collective-permute-start.1) | collective-permute-done | bytes 65568 | tf_op jit(solution)/shard_map/ppermute | solution.py:241
  11.9 1.7 %collective-permute-start.13 = (bf16[32,4096]{1,0:T(8,128)(2,1)S(1)}, bf16[32,4096]{1,0:T(8,128)(2,1)S(1)}, u32[]{:S(2)}, u32[]{:S(2)}) collective-permute-start(bf16[32,4096]{1,0:T(8,128)(2,1)S(1)} %get-tuple-element.60.refs_0_), channel_id=1, source_target_pairs={{4,0},{8,4},{12,8},{14,12},{10,14},{6,10},{2,6},{0,2},{5,1},{9,5},... | collective-permute-start | bytes 786440 | tf_op jit(solution)/shard_map/ppermute | solution.py:241
  13.6 1.2 %collective-permute-done.refs_0_.refs_1_ = bf16[64,512]{1,0:T(8,128)(2,1)S(1)} collective-permute-done((bf16[64,512]{1,0:T(8,128)(2,1)}, bf16[64,512]{1,0:T(8,128)(2,1)S(1)}, u32[]{:S(2)}, u32[]{:S(2)}) %collective-permute-start) | collective-permute-done | bytes 65568 | tf_op jit(solution)/shard_map/ppermute | solution.py:241
  14.8 1.6 %collective-permute-start.19 = (bf16[64,512]{1,0:T(8,128)(2,1)S(1)}, bf16[64,512]{1,0:T(8,128)(2,1)S(1)}, u32[]{:S(2)}, u32[]{:S(2)}) collective-permute-start(bf16[64,512]{1,0:T(8,128)(2,1)S(1)} %collective-permute-done.1.refs_1_.refs_2_), channel_id=1, source_target_pairs={{4,0},{8,4},{12,8},{14,12},{10,14},{6,10},{2,6},{0,2},{5,1},{9,5},... | collective-permute-start | bytes 196616 | tf_op jit(solution)/shard_map/ppermute | solution.py:241
  16.4 1.9 %copy-done.2 = bf16[384,4096]{1,0:T(8,128)(2,1)S(1)} copy-done((bf16[384,4096]{1,0:T(8,128)(2,1)S(1)}, bf16[384,4096]{1,0:T(8,128)(2,1)}, u32[]{:S(2)}) %copy-start.2) | copy-done | bytes 3145752
  23.4 1.6 %collective-permute-start.7 = (bf16[32,4096]{1,0:T(8,128)(2,1)S(1)}, bf16[32,4096]{1,0:T(8,128)(2,1)S(1)}, u32[]{:S(2)}, u32[]{:S(2)}) collective-permute-start(bf16[32,4096]{1,0:T(8,128)(2,1)S(1)} %collective-permute-done.6.refs_5_.refs_1_), channel_id=1, source_target_pairs={{4,0},{8,4},{12,8},{14,12},{10,14},{6,10},{2,6},{0,2},{5,1},{9,5},... | collective-permute-start | bytes 786440 | tf_op jit(solution)/shard_map/ppermute | solution.py:241
  25.0 1.8 %probs.5 = (bf16[512,128]{1,0:T(8,128)(2,1)S(1)}, bf16[512,128]{1,0:T(8,128)(2,1)S(1)}, bf16[512,256]{1,0:T(8,128)(2,1)S(1)}, bf16[512,256]{1,0:T(8,128)(2,1)S(1...) custom-call(s32[384,1]{1,0:T(8,128)S(1)} %get-tuple-element.33.segment_ref, ...), custom_call_target="tpu_custom_call" | custom-call | flops 2000000000 | bytes 1310720 | tf_op jit(solution)/shard_map/probs/pallas_call | solution.py:109
  27.2 1.8 %probs.4 = (bf16[512,128]{1,0:T(8,128)(2,1)S(1)}, bf16[512,128]{1,0:T(8,128)(2,1)S(1)}, bf16[512,256]{1,0:T(8,128)(2,1)S(1)}, bf16[512,256]{1,0:T(8,128)(2,1)S(1...) custom-call(s32[384,1]{1,0:T(8,128)S(1)} %get-tuple-element.33.segment_ref, ...), custom_call_target="tpu_custom_call" | custom-call | flops 2000000000 | bytes 1310720 | tf_op jit(solution)/shard_map/probs/pallas_call | solution.py:109
  30.1 1.6 %collective-permute-start.11 = (bf16[32,4096]{1,0:T(8,128)(2,1)S(1)}, bf16[32,4096]{1,0:T(8,128)(2,1)S(1)}, u32[]{:S(2)}, u32[]{:S(2)}) collective-permute-start(bf16[32,4096]{1,0:T(8,128)(2,1)S(1)} %collective-permute-done.10.refs_3_.refs_0_), channel_id=1, source_target_pairs={{0,4},{4,8},{8,12},{12,14},{14,10},{10,6},{6,2},{2,0},{1,5},{5,9},... | collective-permute-start | bytes 786440 | tf_op jit(solution)/shard_map/ppermute | solution.py:241
  32.2 1.8 %probs.7 = (bf16[512,128]{1,0:T(8,128)(2,1)S(1)}, bf16[512,128]{1,0:T(8,128)(2,1)S(1)}, bf16[512,256]{1,0:T(8,128)(2,1)S(1)}, bf16[512,256]{1,0:T(8,128)(2,1)S(1...) custom-call(s32[384,1]{1,0:T(8,128)S(1)} %get-tuple-element.33.segment_ref, ...), custom_call_target="tpu_custom_call" | custom-call | flops 2000000000 | bytes 1310720 | tf_op jit(solution)/shard_map/probs/pallas_call | solution.py:109
  33.9 3.5 %collective-permute-done.17.refs_2_.refs_5_ = bf16[64,512]{1,0:T(8,128)(2,1)S(1)} collective-permute-done((bf16[64,512]{1,0:T(8,128)(2,1)S(1)}, bf16[64,512]{1,0:T(8,128)(2,1)S(1)}, u32[]{:S(2)}, u32[]{:S(2)}) %collective-permute-start.17) | collective-permute-done | bytes 65568 | tf_op jit(solution)/shard_map/ppermute | solution.py:241
  37.8 1.6 %collective-permute-start.8 = (bf16[32,4096]{1,0:T(8,128)(2,1)S(1)}, bf16[32,4096]{1,0:T(8,128)(2,1)S(1)}, u32[]{:S(2)}, u32[]{:S(2)}) collective-permute-start(bf16[32,4096]{1,0:T(8,128)(2,1)S(1)} %collective-permute-done.7.refs_7_.refs_3_), channel_id=1, source_target_pairs={{4,0},{8,4},{12,8},{14,12},{10,14},{6,10},{2,6},{0,2},{5,1},{9,5},... | collective-permute-start | bytes 786440 | tf_op jit(solution)/shard_map/ppermute | solution.py:241
  39.9 1.8 %probs.6 = (bf16[512,128]{1,0:T(8,128)(2,1)S(1)}, bf16[512,128]{1,0:T(8,128)(2,1)S(1)}, bf16[512,256]{1,0:T(8,128)(2,1)S(1)}, bf16[512,256]{1,0:T(8,128)(2,1)S(1...) custom-call(s32[384,1]{1,0:T(8,128)S(1)} %get-tuple-element.33.segment_ref, ...), custom_call_target="tpu_custom_call" | custom-call | flops 2000000000 | bytes 1310720 | tf_op jit(solution)/shard_map/probs/pallas_call | solution.py:109
  41.6 1.4 %collective-permute-done.11.refs_1_ = bf16[32,4096]{1,0:T(8,128)(2,1)S(1)} collective-permute-done((bf16[32,4096]{1,0:T(8,128)(2,1)S(1)}, bf16[32,4096]{1,0:T(8,128)(2,1)S(1)}, u32[]{:S(2)}, u32[]{:S(2)}) %collective-permute-start.11) | collective-permute-done | bytes 262176 | tf_op jit(solution)/shard_map/ppermute | solution.py:241
  43.5 1.6 %collective-permute-start.15 = (bf16[32,4096]{1,0:T(8,128)(2,1)S(1)}, bf16[32,4096]{1,0:T(8,128)(2,1)S(1)}, u32[]{:S(2)}, u32[]{:S(2)}) collective-permute-start(bf16[32,4096]{1,0:T(8,128)(2,1)S(1)} %collective-permute-done.14.refs_2_), channel_id=1, source_target_pairs={{4,0},{8,4},{12,8},{14,12},{10,14},{6,10},{2,6},{0,2},{5,1},{9,5},... | collective-permute-start | bytes 786440 | tf_op jit(solution)/shard_map/ppermute | solution.py:241
  47.1 1.2 %collective-permute-start.9 = (bf16[32,4096]{1,0:T(8,128)(2,1)S(1)}, bf16[32,4096]{1,0:T(8,128)(2,1)S(1)}, u32[]{:S(2)}, u32[]{:S(2)}) collective-permute-start(bf16[32,4096]{1,0:T(8,128)(2,1)S(1)} %collective-permute-done.8.refs_3_), channel_id=1, source_target_pairs={{4,0},{8,4},{12,8},{14,12},{10,14},{6,10},{2,6},{0,2},{5,1},{9,5},... | collective-permute-start | bytes 786440 | tf_op jit(solution)/shard_map/ppermute | solution.py:241
  48.3 1.8 %collective-permute-done.4.refs_0_ = bf16[32,4096]{1,0:T(8,128)(2,1)S(1)} collective-permute-done((bf16[32,4096]{1,0:T(8,128)(2,1)S(1)}, bf16[32,4096]{1,0:T(8,128)(2,1)S(1)}, u32[]{:S(2)}, u32[]{:S(2)}) %collective-permute-start.4) | collective-permute-done | bytes 262176 | tf_op jit(solution)/shard_map/ppermute | solution.py:241
  51.5 2.4 %collective-permute-done.12.refs_1_ = bf16[32,4096]{1,0:T(8,128)(2,1)S(1)} collective-permute-done((bf16[32,4096]{1,0:T(8,128)(2,1)S(1)}, bf16[32,4096]{1,0:T(8,128)(2,1)S(1)}, u32[]{:S(2)}, u32[]{:S(2)}) %collective-permute-start.12) | collective-permute-done | bytes 262176 | tf_op jit(solution)/shard_map/ppermute | solution.py:241
  55.0 1.7 %collective-permute-done.5.refs_0_ = bf16[32,4096]{1,0:T(8,128)(2,1)S(1)} collective-permute-done((bf16[32,4096]{1,0:T(8,128)(2,1)S(1)}, bf16[32,4096]{1,0:T(8,128)(2,1)S(1)}, u32[]{:S(2)}, u32[]{:S(2)}) %collective-permute-start.5) | collective-permute-done | bytes 262176 | tf_op jit(solution)/shard_map/ppermute | solution.py:241
  57.8 1.4 %collective-permute-done.21.theirs_ref = f32[384,64]{1,0:T(8,128)S(1)} collective-permute-done((f32[384,64]{1,0:T(8,128)S(1)}, f32[384,64]{1,0:T(8,128)S(1)}, u32[]{:S(2)}, u32[]{:S(2)}) %collective-permute-start.21) | collective-permute-done | bytes 98336 | tf_op jit(solution)/shard_map/ppermute | solution.py:273
  59.2 2.8 %attend.1 = bf16[384,4096]{1,0:T(8,128)(2,1)} custom-call(s32[384,1]{1,0:T(8,128)S(1)} %get-tuple-element.32.place_ref, f32[384,64]{1,0:T(8,128)S(1)} %lowrank.7.mine_ref, f32[384,64]{1,0:T(8,128)S(1)} %collective-permute-done.21.theirs_ref, bf16[384,512]{1,0:T(8,128)(2,1)S(1)} %copy-done, bf16[64,512]{1,0:T(8,128)(2,1)S(1)} %bitcast.8, ...), custom_call_target="tpu_custom_call" | custom-call | tf_op jit(solution)/shard_map/attend/pallas_call | solution.py:208
  (49 shorter events, 15.2 us)
Async XLA Ops:
  0.0 25.0 %copy-start.6 = (bf16[384,512]{1,0:T(8,128)(2,1)S(1)}, bf16[384,512]{1,0:T(8,128)(2,1)}, u32[]{:S(2)}) copy-start(bf16[384,512]{1,0:T(8,128)(2,1)} %k_ref.7) | copy-start | bytes 1179652
  1.1 21.1 %collective-permute-start.6 = (bf16[32,4096]{1,0:T(8,128)(2,1)S(1)}, bf16[32,4096]{1,0:T(8,128)(2,1)S(1)}, u32[]{:S(2)}, u32[]{:S(2)}) collective-permute-start(bf16[32,4096]{1,0:T(8,128)(2,1)S(1)} %get-tuple-element.59.refs_1_), channel_id=1, source_target_pairs={{4,0},{8,4},{12,8},{14,12},{10,14},{6,10},{2,6},{0,2},{5,1},{9,5},... | collective-permute-start | bytes 786440 | tf_op jit(solution)/shard_map/ppermute | solution.py:241
  4.1 19.3 %collective-permute-start.2 = (bf16[32,4096]{1,0:T(8,128)(2,1)S(1)}, bf16[32,4096]{1,0:T(8,128)(2,1)S(1)}, u32[]{:S(2)}, u32[]{:S(2)}) collective-permute-start(bf16[32,4096]{1,0:T(8,128)(2,1)S(1)} %get-tuple-element.60.refs_0_), channel_id=1, source_target_pairs={{0,4},{4,8},{8,12},{12,14},{14,10},{10,6},{6,2},{2,0},{1,5},{5,9},... | collective-permute-start | bytes 786440 | tf_op jit(solution)/shard_map/ppermute | solution.py:241
  4.3 7.6 %collective-permute-start.1 = (bf16[64,512]{1,0:T(8,128)(2,1)}, bf16[64,512]{1,0:T(8,128)(2,1)S(1)}, u32[]{:S(2)}, u32[]{:S(2)}) collective-permute-start(bf16[64,512]{1,0:T(8,128)(2,1)} %bitcast.6), channel_id=1, source_target_pairs={{4,0},{8,4},{12,8},{14,12},{10,14},{6,10},{2,6},{0,2},{5,1},{9,5},... | collective-permute-start | bytes 196616 | tf_op jit(solution)/shard_map/ppermute | solution.py:241
  6.2 8.6 %collective-permute-start = (bf16[64,512]{1,0:T(8,128)(2,1)}, bf16[64,512]{1,0:T(8,128)(2,1)S(1)}, u32[]{:S(2)}, u32[]{:S(2)}) collective-permute-start(bf16[64,512]{1,0:T(8,128)(2,1)} %bitcast.7), channel_id=1, source_target_pairs={{0,4},{4,8},{8,12},{12,14},{14,10},{10,6},{6,2},{2,0},{1,5},{5,9},... | collective-permute-start | bytes 196616 | tf_op jit(solution)/shard_map/ppermute | solution.py:241
  6.3 23.8 %collective-permute-start.10 = (bf16[32,4096]{1,0:T(8,128)(2,1)S(1)}, bf16[32,4096]{1,0:T(8,128)(2,1)S(1)}, u32[]{:S(2)}, u32[]{:S(2)}) collective-permute-start(bf16[32,4096]{1,0:T(8,128)(2,1)S(1)} %get-tuple-element.59.refs_1_), channel_id=1, source_target_pairs={{0,4},{4,8},{8,12},{12,14},{14,10},{10,6},{6,2},{2,0},{1,5},{5,9},... | collective-permute-start | bytes 786440 | tf_op jit(solution)/shard_map/ppermute | solution.py:241
  11.9 19.8 %collective-permute-start.13 = (bf16[32,4096]{1,0:T(8,128)(2,1)S(1)}, bf16[32,4096]{1,0:T(8,128)(2,1)S(1)}, u32[]{:S(2)}, u32[]{:S(2)}) collective-permute-start(bf16[32,4096]{1,0:T(8,128)(2,1)S(1)} %get-tuple-element.60.refs_0_), channel_id=1, source_target_pairs={{4,0},{8,4},{12,8},{14,12},{10,14},{6,10},{2,6},{0,2},{5,1},{9,5},... | collective-permute-start | bytes 786440 | tf_op jit(solution)/shard_map/ppermute | solution.py:241
  14.8 6.5 %collective-permute-start.19 = (bf16[64,512]{1,0:T(8,128)(2,1)S(1)}, bf16[64,512]{1,0:T(8,128)(2,1)S(1)}, u32[]{:S(2)}, u32[]{:S(2)}) collective-permute-start(bf16[64,512]{1,0:T(8,128)(2,1)S(1)} %collective-permute-done.1.refs_1_.refs_2_), channel_id=1, source_target_pairs={{4,0},{8,4},{12,8},{14,12},{10,14},{6,10},{2,6},{0,2},{5,1},{9,5},... | collective-permute-start | bytes 196616 | tf_op jit(solution)/shard_map/ppermute | solution.py:241
  21.3 5.4 %collective-permute-start.16 = (bf16[64,512]{1,0:T(8,128)(2,1)S(1)}, bf16[64,512]{1,0:T(8,128)(2,1)S(1)}, u32[]{:S(2)}, u32[]{:S(2)}) collective-permute-start(bf16[64,512]{1,0:T(8,128)(2,1)S(1)} %collective-permute-done.refs_0_.refs_1_), channel_id=1, source_target_pairs={{0,4},{4,8},{8,12},{12,14},{14,10},{10,6},{6,2},{2,0},{1,5},{5,9},... | collective-permute-start | bytes 196616 | tf_op jit(solution)/shard_map/ppermute | solution.py:241
  22.2 6.8 %collective-permute-start.20 = (bf16[64,512]{1,0:T(8,128)(2,1)S(1)}, bf16[64,512]{1,0:T(8,128)(2,1)S(1)}, u32[]{:S(2)}, u32[]{:S(2)}) collective-permute-start(bf16[64,512]{1,0:T(8,128)(2,1)S(1)} %collective-permute-done.19.refs_3_.refs_4_), channel_id=1, source_target_pairs={{4,0},{8,4},{12,8},{14,12},{10,14},{6,10},{2,6},{0,2},{5,1},{9,5},... | collective-permute-start | bytes 196616 | tf_op jit(solution)/shard_map/ppermute | solution.py:241
  23.4 14.4 %collective-permute-start.7 = (bf16[32,4096]{1,0:T(8,128)(2,1)S(1)}, bf16[32,4096]{1,0:T(8,128)(2,1)S(1)}, u32[]{:S(2)}, u32[]{:S(2)}) collective-permute-start(bf16[32,4096]{1,0:T(8,128)(2,1)S(1)} %collective-permute-done.6.refs_5_.refs_1_), channel_id=1, source_target_pairs={{4,0},{8,4},{12,8},{14,12},{10,14},{6,10},{2,6},{0,2},{5,1},{9,5},... | collective-permute-start | bytes 786440 | tf_op jit(solution)/shard_map/ppermute | solution.py:241
  26.7 12.7 %collective-permute-start.3 = (bf16[32,4096]{1,0:T(8,128)(2,1)S(1)}, bf16[32,4096]{1,0:T(8,128)(2,1)S(1)}, u32[]{:S(2)}, u32[]{:S(2)}) collective-permute-start(bf16[32,4096]{1,0:T(8,128)(2,1)S(1)} %collective-permute-done.2.refs_2_.refs_0_), channel_id=1, source_target_pairs={{0,4},{4,8},{8,12},{12,14},{14,10},{10,6},{6,2},{2,0},{1,5},{5,9},... | collective-permute-start | bytes 786440 | tf_op jit(solution)/shard_map/ppermute | solution.py:241
  29.0 8.4 %collective-permute-start.17 = (bf16[64,512]{1,0:T(8,128)(2,1)S(1)}, bf16[64,512]{1,0:T(8,128)(2,1)S(1)}, u32[]{:S(2)}, u32[]{:S(2)}) collective-permute-start(bf16[64,512]{1,0:T(8,128)(2,1)S(1)} %collective-permute-done.16.refs_2_.refs_3_), channel_id=1, source_target_pairs={{0,4},{4,8},{8,12},{12,14},{14,10},{10,6},{6,2},{2,0},{1,5},{5,9},... | collective-permute-start | bytes 196616 | tf_op jit(solution)/shard_map/ppermute | solution.py:241
  30.1 12.9 %collective-permute-start.11 = (bf16[32,4096]{1,0:T(8,128)(2,1)S(1)}, bf16[32,4096]{1,0:T(8,128)(2,1)S(1)}, u32[]{:S(2)}, u32[]{:S(2)}) collective-permute-start(bf16[32,4096]{1,0:T(8,128)(2,1)S(1)} %collective-permute-done.10.refs_3_.refs_0_), channel_id=1, source_target_pairs={{0,4},{4,8},{8,12},{12,14},{14,10},{10,6},{6,2},{2,0},{1,5},{5,9},... | collective-permute-start | bytes 786440 | tf_op jit(solution)/shard_map/ppermute | solution.py:241
  31.7 11.8 %collective-permute-start.14 = (bf16[32,4096]{1,0:T(8,128)(2,1)S(1)}, bf16[32,4096]{1,0:T(8,128)(2,1)S(1)}, u32[]{:S(2)}, u32[]{:S(2)}) collective-permute-start(bf16[32,4096]{1,0:T(8,128)(2,1)S(1)} %collective-permute-done.13.refs_4_.refs_1_), channel_id=1, source_target_pairs={{4,0},{8,4},{12,8},{14,12},{10,14},{6,10},{2,6},{0,2},{5,1},{9,5},... | collective-permute-start | bytes 786440 | tf_op jit(solution)/shard_map/ppermute | solution.py:241
  33.9 11.2 %copy-start.4 = (bf16[384,4096]{1,0:T(8,128)(2,1)S(1)}, bf16[384,4096]{1,0:T(8,128)(2,1)}, u32[]{:S(2)}) copy-start(bf16[384,4096]{1,0:T(8,128)(2,1)} %x_ref.7) | copy-start | bytes 9437188
  37.4 7.7 %collective-permute-start.18 = (bf16[64,512]{1,0:T(8,128)(2,1)S(1)}, bf16[64,512]{1,0:T(8,128)(2,1)S(1)}, u32[]{:S(2)}, u32[]{:S(2)}) collective-permute-start(bf16[64,512]{1,0:T(8,128)(2,1)S(1)} %collective-permute-done.17.refs_2_.refs_5_), channel_id=1, source_target_pairs={{0,4},{4,8},{8,12},{12,14},{14,10},{10,6},{6,2},{2,0},{1,5},{5,9},... | collective-permute-start | bytes 196616 | tf_op jit(solution)/shard_map/ppermute | solution.py:241
  37.8 9.2 %collective-permute-start.8 = (bf16[32,4096]{1,0:T(8,128)(2,1)S(1)}, bf16[32,4096]{1,0:T(8,128)(2,1)S(1)}, u32[]{:S(2)}, u32[]{:S(2)}) collective-permute-start(bf16[32,4096]{1,0:T(8,128)(2,1)S(1)} %collective-permute-done.7.refs_7_.refs_3_), channel_id=1, source_target_pairs={{4,0},{8,4},{12,8},{14,12},{10,14},{6,10},{2,6},{0,2},{5,1},{9,5},... | collective-permute-start | bytes 786440 | tf_op jit(solution)/shard_map/ppermute | solution.py:241
  39.5 10.6 %collective-permute-start.4 = (bf16[32,4096]{1,0:T(8,128)(2,1)S(1)}, bf16[32,4096]{1,0:T(8,128)(2,1)S(1)}, u32[]{:S(2)}, u32[]{:S(2)}) collective-permute-start(bf16[32,4096]{1,0:T(8,128)(2,1)S(1)} %collective-permute-done.3.refs_6_.refs_0_), channel_id=1, source_target_pairs={{0,4},{4,8},{8,12},{12,14},{14,10},{10,6},{6,2},{2,0},{1,5},{5,9},... | collective-permute-start | bytes 786440 | tf_op jit(solution)/shard_map/ppermute | solution.py:241
  43.1 10.9 %collective-permute-start.12 = (bf16[32,4096]{1,0:T(8,128)(2,1)S(1)}, bf16[32,4096]{1,0:T(8,128)(2,1)S(1)}, u32[]{:S(2)}, u32[]{:S(2)}) collective-permute-start(bf16[32,4096]{1,0:T(8,128)(2,1)S(1)} %collective-permute-done.11.refs_1_), channel_id=1, source_target_pairs={{0,4},{4,8},{8,12},{12,14},{14,10},{10,6},{6,2},{2,0},{1,5},{5,9},... | collective-permute-start | bytes 786440 | tf_op jit(solution)/shard_map/ppermute | solution.py:241
  43.5 10.5 %collective-permute-start.15 = (bf16[32,4096]{1,0:T(8,128)(2,1)S(1)}, bf16[32,4096]{1,0:T(8,128)(2,1)S(1)}, u32[]{:S(2)}, u32[]{:S(2)}) collective-permute-start(bf16[32,4096]{1,0:T(8,128)(2,1)S(1)} %collective-permute-done.14.refs_2_), channel_id=1, source_target_pairs={{4,0},{8,4},{12,8},{14,12},{10,14},{6,10},{2,6},{0,2},{5,1},{9,5},... | collective-permute-start | bytes 786440 | tf_op jit(solution)/shard_map/ppermute | solution.py:241
  47.1 7.9 %collective-permute-start.9 = (bf16[32,4096]{1,0:T(8,128)(2,1)S(1)}, bf16[32,4096]{1,0:T(8,128)(2,1)S(1)}, u32[]{:S(2)}, u32[]{:S(2)}) collective-permute-start(bf16[32,4096]{1,0:T(8,128)(2,1)S(1)} %collective-permute-done.8.refs_3_), channel_id=1, source_target_pairs={{4,0},{8,4},{12,8},{14,12},{10,14},{6,10},{2,6},{0,2},{5,1},{9,5},... | collective-permute-start | bytes 786440 | tf_op jit(solution)/shard_map/ppermute | solution.py:241
  50.1 6.6 %collective-permute-start.5 = (bf16[32,4096]{1,0:T(8,128)(2,1)S(1)}, bf16[32,4096]{1,0:T(8,128)(2,1)S(1)}, u32[]{:S(2)}, u32[]{:S(2)}) collective-permute-start(bf16[32,4096]{1,0:T(8,128)(2,1)S(1)} %collective-permute-done.4.refs_0_), channel_id=1, source_target_pairs={{0,4},{4,8},{8,12},{12,14},{14,10},{10,6},{6,2},{2,0},{1,5},{5,9},... | collective-permute-start | bytes 786440 | tf_op jit(solution)/shard_map/ppermute | solution.py:241
  57.7 1.5 %collective-permute-start.21 = (f32[384,64]{1,0:T(8,128)S(1)}, f32[384,64]{1,0:T(8,128)S(1)}, u32[]{:S(2)}, u32[]{:S(2)}) collective-permute-start(f32[384,64]{1,0:T(8,128)S(1)} %lowrank.7.mine_ref), channel_id=1, source_target_pairs={{0,1},{1,0},{2,3},{3,2},{4,5},{5,4},{6,7},{7,6},{8,9},{9,8},{10,11... | collective-permute-start | bytes 294920 | tf_op jit(solution)/shard_map/ppermute | solution.py:273
  (7 other events, 13.6 us)

commit v8 on v6

--- a/solution.py
+++ b/solution.py
@@ -102,51 +102,56 @@
             p_ref[head * TILE : (head + 1) * TILE, :] = (weights * inverse).astype(jnp.bfloat16)
 
 
-def probs_of(segment, across, queries, keys, kv_head, after):
+def probs_of(segment, across, queries, keys, kv_head):
     rows = keys.shape[0]
     shapes = [(GROUP * TILE, width) for _, _, width in windows(rows)]
     elements = sum(a * b for a, b in shapes)
     return pl.pallas_call(
         functools.partial(probs_kernel, kv_head),
         out_shape=[jax.ShapeDtypeStruct(s, jnp.bfloat16) for s in shapes],
-        in_specs=[VMEM] * 4 + [pl.BlockSpec(memory_space=pl.ANY)] * len(after),
+        in_specs=[VMEM] * 4,
         out_specs=[VMEM] * len(shapes),
         cost_estimate=pl.CostEstimate(
             flops=2_000_000_000, bytes_accessed=2 * elements, transcendentals=elements
         ),
         compiler_params=pltpu.CompilerParams(vmem_limit_bytes=12 * 2**20),
         name="probs",
-    )(segment, across, queries, keys, *after)
+    )(segment, across, queries, keys)
 
 
 def lowrank_kernel(at, count, place_ref, x_ref, *refs):
-    w_refs, out_ref = refs[:count], refs[-1]
+    w_refs, (out_ref, up_ref) = refs[:count], refs[-2:]
     before_ref = refs[count] if at > 0 else None
     place = place_ref[...]
     rows, features = x_ref.shape
     half = w_refs[0].shape[0]
-    stacked = jnp.concatenate([w_ref[...] for w_ref in w_refs], axis=0)
+    stacked = jnp.concatenate([w_ref[:, :features] for w_ref in w_refs], axis=0)
     product = lax.dot_general(x_ref[...], stacked, NT, preferred_element_type=jnp.float32)
     sums = [jnp.zeros((rows, half), jnp.float32)] * 2
     for i in range(count):
         part = product[:, i * half : (i + 1) * half]
         sums[i % 2] = sums[i % 2] + jnp.where(place == at + i // 2, part, 0.0)
+    up_ref[...] = jnp.concatenate([w_ref[:, features:] for w_ref in w_refs], axis=0)
     total = jnp.concatenate(sums, axis=1)
     out_ref[...] = total if before_ref is None else total + before_ref[...]
 
 
 def lowrank_of(at, place, x, before, pieces, after):
     rows, features = x.shape
-    rank = 2 * pieces[0].shape[0]
+    half, held = pieces[0].shape
+    rank = 2 * half
     operands = [place, x] + pieces + ([] if before is None else [before])
     used = len(operands)
     operands = operands + after
     size = 2 * sum(p.size for p in pieces)
     return pl.pallas_call(
         functools.partial(lowrank_kernel, at, len(pieces)),
-        out_shape=jax.ShapeDtypeStruct((rows, rank), jnp.float32),
+        out_shape=[
+            jax.ShapeDtypeStruct((rows, rank), jnp.float32),
+            jax.ShapeDtypeStruct((half * len(pieces), held - features), pieces[0].dtype),
+        ],
         in_specs=[VMEM] * used + [pl.BlockSpec(memory_space=pl.ANY)] * len(after),
-        out_specs=VMEM,
+        out_specs=[VMEM, VMEM],
         cost_estimate=pl.CostEstimate(
             flops=1_700_000_000, bytes_accessed=2 * rows * features + size, transcendentals=0
         ),
@@ -155,13 +160,14 @@
     )(*operands)
 
 
-def attend_kernel(kv_heads, n, place_ref, mine_ref, theirs_ref, base_ref, *refs):
+def attend_kernel(kv_heads, place_ref, mine_ref, theirs_ref, base_ref, *refs):
     rows = base_ref.shape[0]
     tiles = windows(rows)
-    up_refs = refs[:n]
-    p_refs = refs[n : n + kv_heads * len(tiles)]
-    out_ref, block, sems = refs[n + kv_heads * len(tiles) :]
+    up_refs = refs[: -kv_heads * len(tiles) - 3]
+    p_refs = refs[len(up_refs) : -3]
+    out_ref, block, sems = refs[-3:]
     rank = mine_ref.shape[1]
+    n = sum(up_ref.shape[0] for up_ref in up_refs) // rank
     place = place_ref[...]
     lowrank = (mine_ref[...] + theirs_ref[...]).astype(jnp.bfloat16)
     twice = jnp.concatenate([lowrank, lowrank], axis=1)
@@ -206,7 +212,7 @@
     wide = kv_heads * GROUP * HEAD_SIZE
     flat = [p for per_head in probs for p in per_head]
     return pl.pallas_call(
-        functools.partial(attend_kernel, kv_heads, len(ups)),
+        functools.partial(attend_kernel, kv_heads),
         out_shape=jax.ShapeDtypeStruct((rows, wide), jnp.bfloat16),
         in_specs=[VMEM] * (4 + len(ups) + len(flat)),
         out_specs=pl.BlockSpec(memory_space=pl.ANY),
@@ -233,11 +239,13 @@
     far = n // 2
     distances = [0] + [d for step in range(1, far) for d in (step, -step)] + [far]
     down = jnp.swapaxes(adapter_down_weight[0], 0, 1)
-    rank = down.shape[0]
-    low, high, up = {0: down[: rank // 2]}, {0: down[rank // 2 :]}, {0: adapter_up_weight[0]}
+    both = jnp.concatenate([down, adapter_up_weight[0]], axis=1)
+    rank = both.shape[0]
+    own_low, own_high = both[: rank // 2], both[rank // 2 :]
     place, segment, across = masks(
         n, sequence_lengths, adapter_of_row.reshape(1, -1), queries, stacked_key_rows
     )
+    low, high = {0: own_low}, {0: own_high}
 
     def pass_round(held, pairs, sign, steps):
         piece = held[0]
@@ -249,8 +257,6 @@
     pass_round(low, back, -1, far - 1)
     pass_round(high, back, -1, far)
     pass_round(low, ahead, 1, far)
-    pass_round(up, ahead, 1, far)
-    pass_round(up, back, -1, far - 1)
 
     kv_heads = stacked_key_rows.shape[1] // HEAD_SIZE
     arrivals = [
@@ -259,25 +265,24 @@
         for pair in ([low[step], high[-step]], [high[step], low[-step]])
     ]
     probs = [
-        probs_of(segment, across, queries, stacked_key_rows, kv, arrivals[kv // 2]) for kv in range(kv_heads)
+        probs_of(segment, across, queries, stacked_key_rows, kv) for kv in range(kv_heads)
     ]
 
-    partial = None
+    partial, ups = None, []
     for lo, hi in [(0, 3)] + [(a, a + 2) for a in range(3, n - 1, 2)] + [(n - 1, n)]:
         pieces = [piece for d in distances[lo:hi] for piece in (low[d], high[d])]
         after = arrivals[kv_heads - 1] if lo == 0 else []
-        if lo == n - 5:
-            after = [up[far - 2], up[2 - far]]
         if hi == n:
-            after = [p[0] for p in probs] + [up[far], up[1 - far]]
-        partial = lowrank_of(lo, place, normed_token_rows, partial, pieces, after)
+            after = [p[0] for p in probs]
+        partial, up = lowrank_of(lo, place, normed_token_rows, partial, pieces, after)
+        ups.append(up)
     other = lax.ppermute(partial, "tp", [(0, 1), (1, 0)])
     return attend(
         place,
         partial,
         other,
         base_value_rows,
-        [up[d] for d in distances],
+        ups,
         probs,
     )
 

time: 58.4 us -> 56.2 us (0.962)
  starting transfers between devices: 24.5 us -> 15.5 us
  waiting for transfers between devices: 13.2 us -> 18.9 us
  other arithmetic: 0 us -> 1.16 us
    ppermute x21 -> x14, starting transfers between devices: 24.5 us -> 15.5 us  [pass_round(): piece = lax.ppermute(piece, 'rep', pairs)]
    ppermute x21 -> x14, waiting for transfers between devices: 11.8 us -> 17.5 us  [pass_round(): piece = lax.ppermute(piece, 'rep', pairs)]
    concatenate x0 -> x1, other arithmetic: none -> 1.16 us  [on_device(): both = jnp.concatenate([down, adapter_up_weight[0]], axis=1)]
    unnamed x18 -> x16, local copies, waits for them, and re-layouts: 4.24 us -> 5.39 us
    slice x1 -> x0, local copies, waits for them, and re-layouts: 1.11 us -> none  [on_device(): down[rank // 2:]]
  transfers between devices with their start and end apart: 22 -> 15, of which waited for: 7 -> 8; matrix products, arithmetic and copies ran while one was open for 0% -> 0% of each run, Pallas kernels for 19% -> 20%
where the time goes in v8:
time: 56.2 us; the launch traced here: 56 us
  waiting for transfers between devices  18.9 us (34%)
  starting transfers between devices  15.5 us (28%)
  Pallas kernels  14.7 us (26%)
  local copies, waits for them, and re-layouts  5.39 us (10%)
  other arithmetic  1.16 us (2%)
    ppermute x14, waiting for transfers between devices, pass_round(): piece = lax.ppermute(piece, 'rep', pairs)  17.5 us
    ppermute x14, starting transfers between devices, pass_round(): piece = lax.ppermute(piece, 'rep', pairs)  15.5 us
    pallas_call x4, Pallas kernels, probs_of(): pl.pallas_call(functools.partial(probs_kernel, kv_head), out_shape=[jax.S...  7.07 us
    unnamed x16, local copies, waits for them, and re-layouts  5.39 us
    pallas_call x4, Pallas kernels, lowrank_of(): pl.pallas_call(functools.partial(lowrank_kernel, at, len(pieces)), out_sh...  4.15 us
    pallas_call x1, Pallas kernels, attend(): pl.pallas_call(functools.partial(attend_kernel, kv_heads), out_shape=jax....  2.75 us
    ppermute x1, waiting for transfers between devices, on_device(): other = lax.ppermute(partial, 'tp', [(0, 1), (1, 0)])  1.43 us
    concatenate x1, other arithmetic, on_device(): both = jnp.concatenate([down, adapter_up_weight[0]], axis=1)  1.16 us
  transfers between devices with their start and end apart: 15, of which 8 were waited for; matrix products, arithmetic and copies ran while one was open for 0% of the time, Pallas kernels for 20%

profile of v8, /device:TPU:0, one launch (start us, length us, event | category | flops | bytes accessed | tf_op | source)
XLA Modules:
  0.0 56.0 jit_solution(8838767743384421253)
XLA Ops:
  0.0 1.2 %pad_maximum_fusion = (bf16[32,4608]{1,0:T(8,128)(2,1)S(1)}, bf16[32,4608]{1,0:T(8,128)(2,1)S(1)}) fusion(bf16[64,512]{1,0:T(8,128)(2,1)} %bitcast.8, bf16[64,4096]{1,0:T(8,128)(2,1)} %bitcast.7), kind=kLoop, calls=%fused_computation.3 | loop fusion | flops 1179648 | bytes 1179648 | tf_op jit(solution)/shard_map/concatenate | solution.py:242
  1.2 3.0 %collective-permute-start.4 = (bf16[32,4608]{1,0:T(8,128)(2,1)S(1)}, bf16[32,4608]{1,0:T(8,128)(2,1)S(1)}, u32[]{:S(2)}, u32[]{:S(2)}) collective-permute-start(bf16[32,4608]{1,0:T(8,128)(2,1)S(1)} %get-tuple-element.75.refs_1_), channel_id=1, source_target_pairs={{4,0},{8,4},{12,8},{14,12},{10,14},{6,10},{2,6},{0,2},{5,1},{9,5},... | collective-permute-start | bytes 884744 | tf_op jit(solution)/shard_map/ppermute | solution.py:253
  4.3 2.0 %collective-permute-start.8 = (bf16[32,4608]{1,0:T(8,128)(2,1)S(1)}, bf16[32,4608]{1,0:T(8,128)(2,1)S(1)}, u32[]{:S(2)}, u32[]{:S(2)}) collective-permute-start(bf16[32,4608]{1,0:T(8,128)(2,1)S(1)} %get-tuple-element.75.refs_1_), channel_id=1, source_target_pairs={{0,4},{4,8},{8,12},{12,14},{14,10},{10,6},{6,2},{2,0},{1,5},{5,9},... | collective-permute-start | bytes 884744 | tf_op jit(solution)/shard_map/ppermute | solution.py:253
  6.3 1.9 %copy-done.1 = bf16[384,4096]{1,0:T(8,128)(2,1)S(1)} copy-done((bf16[384,4096]{1,0:T(8,128)(2,1)S(1)}, bf16[384,4096]{1,0:T(8,128)(2,1)}, u32[]{:S(2)}) %copy-start.1) | copy-done | bytes 3145752
  11.3 1.2 %copy-done.2 = bf16[384,4096]{1,0:T(8,128)(2,1)S(1)} copy-done((bf16[384,4096]{1,0:T(8,128)(2,1)S(1)}, bf16[384,4096]{1,0:T(8,128)(2,1)}, u32[]{:S(2)}) %copy-start.2) | copy-done | bytes 3145752
  12.4 1.8 %probs.7 = (bf16[512,128]{1,0:T(8,128)(2,1)S(1)}, bf16[512,128]{1,0:T(8,128)(2,1)S(1)}, bf16[512,256]{1,0:T(8,128)(2,1)S(1)}, bf16[512,256]{1,0:T(8,128)(2,1)S(1...) custom-call(s32[384,1]{1,0:T(8,128)S(1)} %get-tuple-element.44.segment_ref, ...), custom_call_target="tpu_custom_call" | custom-call | flops 2000000000 | bytes 1310720 | tf_op jit(solution)/shard_map/probs/pallas_call | solution.py:109
  14.2 2.0 %collective-permute-start.5 = (bf16[32,4608]{1,0:T(8,128)(2,1)S(1)}, bf16[32,4608]{1,0:T(8,128)(2,1)S(1)}, u32[]{:S(2)}, u32[]{:S(2)}) collective-permute-start(bf16[32,4608]{1,0:T(8,128)(2,1)S(1)} %collective-permute-done.4.refs_5_), channel_id=1, source_target_pairs={{4,0},{8,4},{12,8},{14,12},{10,14},{6,10},{2,6},{0,2},{5,1},{9,5},... | collective-permute-start | bytes 884744 | tf_op jit(solution)/shard_map/ppermute | solution.py:253
  16.3 1.8 %probs.6 = (bf16[512,128]{1,0:T(8,128)(2,1)S(1)}, bf16[512,128]{1,0:T(8,128)(2,1)S(1)}, bf16[512,256]{1,0:T(8,128)(2,1)S(1)}, bf16[512,256]{1,0:T(8,128)(2,1)S(1...) custom-call(s32[384,1]{1,0:T(8,128)S(1)} %get-tuple-element.44.segment_ref, ...), custom_call_target="tpu_custom_call" | custom-call | flops 2000000000 | bytes 1310720 | tf_op jit(solution)/shard_map/probs/pallas_call | solution.py:109
  18.1 2.3 %collective-permute-done.8.refs_3_ = bf16[32,4608]{1,0:T(8,128)(2,1)S(1)} collective-permute-done((bf16[32,4608]{1,0:T(8,128)(2,1)S(1)}, bf16[32,4608]{1,0:T(8,128)(2,1)S(1)}, u32[]{:S(2)}, u32[]{:S(2)}) %collective-permute-start.8) | collective-permute-done | bytes 294944 | tf_op jit(solution)/shard_map/ppermute | solution.py:253
  20.5 1.9 %collective-permute-start.12 = (bf16[32,4608]{1,0:T(8,128)(2,1)S(1)}, bf16[32,4608]{1,0:T(8,128)(2,1)S(1)}, u32[]{:S(2)}, u32[]{:S(2)}) collective-permute-start(bf16[32,4608]{1,0:T(8,128)(2,1)S(1)} %collective-permute-done.11.refs_4_), channel_id=1, source_target_pairs={{4,0},{8,4},{12,8},{14,12},{10,14},{6,10},{2,6},{0,2},{5,1},{9,5},... | collective-permute-start | bytes 884744 | tf_op jit(solution)/shard_map/ppermute | solution.py:253
  22.5 1.8 %probs.5 = (bf16[512,128]{1,0:T(8,128)(2,1)S(1)}, bf16[512,128]{1,0:T(8,128)(2,1)S(1)}, bf16[512,256]{1,0:T(8,128)(2,1)S(1)}, bf16[512,256]{1,0:T(8,128)(2,1)S(1...) custom-call(s32[384,1]{1,0:T(8,128)S(1)} %get-tuple-element.44.segment_ref, ...), custom_call_target="tpu_custom_call" | custom-call | flops 2000000000 | bytes 1310720 | tf_op jit(solution)/shard_map/probs/pallas_call | solution.py:109
  24.7 2.0 %collective-permute-start.6 = (bf16[32,4608]{1,0:T(8,128)(2,1)S(1)}, bf16[32,4608]{1,0:T(8,128)(2,1)S(1)}, u32[]{:S(2)}, u32[]{:S(2)}) collective-permute-start(bf16[32,4608]{1,0:T(8,128)(2,1)S(1)} %collective-permute-done.5.refs_3_), channel_id=1, source_target_pairs={{4,0},{8,4},{12,8},{14,12},{10,14},{6,10},{2,6},{0,2},{5,1},{9,5},... | collective-permute-start | bytes 884744 | tf_op jit(solution)/shard_map/ppermute | solution.py:253
  26.8 1.8 %probs.4 = (bf16[512,128]{1,0:T(8,128)(2,1)S(1)}, bf16[512,128]{1,0:T(8,128)(2,1)S(1)}, bf16[512,256]{1,0:T(8,128)(2,1)S(1)}, bf16[512,256]{1,0:T(8,128)(2,1)S(1...) custom-call(s32[384,1]{1,0:T(8,128)S(1)} %get-tuple-element.44.segment_ref, ...), custom_call_target="tpu_custom_call" | custom-call | flops 2000000000 | bytes 1310720 | tf_op jit(solution)/shard_map/probs/pallas_call | solution.py:109
  28.6 4.5 %collective-permute-done.9.refs_6_.refs_1_ = bf16[32,4608]{1,0:T(8,128)(2,1)S(1)} collective-permute-done((bf16[32,4608]{1,0:T(8,128)(2,1)S(1)}, bf16[32,4608]{1,0:T(8,128)(2,1)S(1)}, u32[]{:S(2)}, u32[]{:S(2)}) %collective-permute-start.9) | collective-permute-done | bytes 294944 | tf_op jit(solution)/shard_map/ppermute | solution.py:253
  33.2 1.9 %collective-permute-start.13 = (bf16[32,4608]{1,0:T(8,128)(2,1)S(1)}, bf16[32,4608]{1,0:T(8,128)(2,1)S(1)}, u32[]{:S(2)}, u32[]{:S(2)}) collective-permute-start(bf16[32,4608]{1,0:T(8,128)(2,1)S(1)} %collective-permute-done.12.refs_7_.refs_2_), channel_id=1, source_target_pairs={{4,0},{8,4},{12,8},{14,12},{10,14},{6,10},{2,6},{0,2},{5,1},{9,5},... | collective-permute-start | bytes 884744 | tf_op jit(solution)/shard_map/ppermute | solution.py:253
  35.1 1.1 %lowrank.4 = (f32[384,64]{1,0:T(8,128)S(1)}, bf16[192,512]{1,0:T(8,128)(2,1)S(1)}) custom-call(s32[384,1]{1,0:T(8,128)S(1)} %get-tuple-element.40.place_ref, bf16[384,4096]{1,0:T(8,128)(2,1)S(1)} %copy-done.3, bf16[32,4608]{1,0:T(8,128)(2,1)S(1)} %get-tuple-element.76.refs_0_, bf16[32,4608]{1,0:T(8,128)(2,1)S(1)} %get-tuple-element.75.refs_1_, ...), custom_call_target="tpu_custom_call" | custom-call | flops 1700000000 | bytes 4915200 | tf_op jit(solution)/shard_map/lowrank/pallas_call | solution.py:147
  36.2 1.2 %collective-permute-done.6.refs_3_ = bf16[32,4608]{1,0:T(8,128)(2,1)S(1)} collective-permute-done((bf16[32,4608]{1,0:T(8,128)(2,1)S(1)}, bf16[32,4608]{1,0:T(8,128)(2,1)S(1)}, u32[]{:S(2)}, u32[]{:S(2)}) %collective-permute-start.6) | collective-permute-done | bytes 294944 | tf_op jit(solution)/shard_map/ppermute | solution.py:253
  37.4 2.0 %collective-permute-start.7 = (bf16[32,4608]{1,0:T(8,128)(2,1)S(1)}, bf16[32,4608]{1,0:T(8,128)(2,1)S(1)}, u32[]{:S(2)}, u32[]{:S(2)}) collective-permute-start(bf16[32,4608]{1,0:T(8,128)(2,1)S(1)} %collective-permute-done.6.refs_3_), channel_id=1, source_target_pairs={{4,0},{8,4},{12,8},{14,12},{10,14},{6,10},{2,6},{0,2},{5,1},{9,5},... | collective-permute-start | bytes 884744 | tf_op jit(solution)/shard_map/ppermute | solution.py:253
  39.5 1.1 %lowrank.5 = (f32[384,64]{1,0:T(8,128)S(1)}, bf16[128,512]{1,0:T(8,128)(2,1)S(1)}) custom-call(s32[384,1]{1,0:T(8,128)S(1)} %get-tuple-element.40.place_ref, bf16[384,4096]{1,0:T(8,128)(2,1)S(1)} %copy-done.3, bf16[32,4608]{1,0:T(8,128)(2,1)S(1)} %collective-permute-done.1.refs_0_, bf16[32,4608]{1,0:T(8,128)(2,1)S(1)} %collective-permute-done.9.refs_6_.refs_1_, ...), custom_call_target="tpu_custom_call" | custom-call | flops 1700000000 | bytes 4325376 | tf_op jit(solution)/shard_map/lowrank/pallas_call | solution.py:147
  40.6 5.2 %collective-permute-done.10.refs_1_ = bf16[32,4608]{1,0:T(8,128)(2,1)S(1)} collective-permute-done((bf16[32,4608]{1,0:T(8,128)(2,1)S(1)}, bf16[32,4608]{1,0:T(8,128)(2,1)S(1)}, u32[]{:S(2)}, u32[]{:S(2)}) %collective-permute-start.10) | collective-permute-done | bytes 294944 | tf_op jit(solution)/shard_map/ppermute | solution.py:253
  46.8 2.4 %collective-permute-done.7.refs_1_ = bf16[32,4608]{1,0:T(8,128)(2,1)S(1)} collective-permute-done((bf16[32,4608]{1,0:T(8,128)(2,1)S(1)}, bf16[32,4608]{1,0:T(8,128)(2,1)S(1)}, u32[]{:S(2)}, u32[]{:S(2)}) %collective-permute-start.7) | collective-permute-done | bytes 294944 | tf_op jit(solution)/shard_map/ppermute | solution.py:253
  49.2 1.4 %collective-permute-done.3.refs_0_ = bf16[32,4608]{1,0:T(8,128)(2,1)S(1)} collective-permute-done((bf16[32,4608]{1,0:T(8,128)(2,1)S(1)}, bf16[32,4608]{1,0:T(8,128)(2,1)S(1)}, u32[]{:S(2)}, u32[]{:S(2)}) %collective-permute-start.3) | collective-permute-done | bytes 294944 | tf_op jit(solution)/shard_map/ppermute | solution.py:253
  51.6 1.4 %collective-permute-done.14.theirs_ref = f32[384,64]{1,0:T(8,128)S(1)} collective-permute-done((f32[384,64]{1,0:T(8,128)S(1)}, f32[384,64]{1,0:T(8,128)S(1)}, u32[]{:S(2)}, u32[]{:S(2)}) %collective-permute-start.14) | collective-permute-done | bytes 98336 | tf_op jit(solution)/shard_map/ppermute | solution.py:279
  53.1 2.8 %attend.1 = bf16[384,4096]{1,0:T(8,128)(2,1)} custom-call(s32[384,1]{1,0:T(8,128)S(1)} %get-tuple-element.40.place_ref, f32[384,64]{1,0:T(8,128)S(1)} %get-tuple-element.50.mine_ref, f32[384,64]{1,0:T(8,128)S(1)} %collective-permute-done.14.theirs_ref, bf16[384,512]{1,0:T(8,128)(2,1)S(1)} %copy-done, bf16[192,512]{1,0:T(8,128)(2,1)S(1)} %get-tuple-element.51.refs_0_, ...), custom_call_target="tpu_custom_call" | custom-call | tf_op jit(solution)/shard_map/attend/pallas_call | solution.py:214
  (33 shorter events, 6.4 us)
Async XLA Ops:
  0.0 11.3 %copy-start.5 = (bf16[384,512]{1,0:T(8,128)(2,1)S(1)}, bf16[384,512]{1,0:T(8,128)(2,1)}, u32[]{:S(2)}) copy-start(bf16[384,512]{1,0:T(8,128)(2,1)} %k_ref.7) | copy-start | bytes 1179652
  1.2 13.1 %collective-permute-start.4 = (bf16[32,4608]{1,0:T(8,128)(2,1)S(1)}, bf16[32,4608]{1,0:T(8,128)(2,1)S(1)}, u32[]{:S(2)}, u32[]{:S(2)}) collective-permute-start(bf16[32,4608]{1,0:T(8,128)(2,1)S(1)} %get-tuple-element.75.refs_1_), channel_id=1, source_target_pairs={{4,0},{8,4},{12,8},{14,12},{10,14},{6,10},{2,6},{0,2},{5,1},{9,5},... | collective-permute-start | bytes 884744 | tf_op jit(solution)/shard_map/ppermute | solution.py:253
  4.2 12.0 %collective-permute-start = (bf16[32,4608]{1,0:T(8,128)(2,1)S(1)}, bf16[32,4608]{1,0:T(8,128)(2,1)S(1)}, u32[]{:S(2)}, u32[]{:S(2)}) collective-permute-start(bf16[32,4608]{1,0:T(8,128)(2,1)S(1)} %get-tuple-element.76.refs_0_), channel_id=1, source_target_pairs={{0,4},{4,8},{8,12},{12,14},{14,10},{10,6},{6,2},{2,0},{1,5},{5,9},... | collective-permute-start | bytes 884744 | tf_op jit(solution)/shard_map/ppermute | solution.py:253
  4.3 16.1 %collective-permute-start.8 = (bf16[32,4608]{1,0:T(8,128)(2,1)S(1)}, bf16[32,4608]{1,0:T(8,128)(2,1)S(1)}, u32[]{:S(2)}, u32[]{:S(2)}) collective-permute-start(bf16[32,4608]{1,0:T(8,128)(2,1)S(1)} %get-tuple-element.75.refs_1_), channel_id=1, source_target_pairs={{0,4},{4,8},{8,12},{12,14},{14,10},{10,6},{6,2},{2,0},{1,5},{5,9},... | collective-permute-start | bytes 884744 | tf_op jit(solution)/shard_map/ppermute | solution.py:253
  6.3 14.3 %collective-permute-start.11 = (bf16[32,4608]{1,0:T(8,128)(2,1)S(1)}, bf16[32,4608]{1,0:T(8,128)(2,1)S(1)}, u32[]{:S(2)}, u32[]{:S(2)}) collective-permute-start(bf16[32,4608]{1,0:T(8,128)(2,1)S(1)} %get-tuple-element.76.refs_0_), channel_id=1, source_target_pairs={{4,0},{8,4},{12,8},{14,12},{10,14},{6,10},{2,6},{0,2},{5,1},{9,5},... | collective-permute-start | bytes 884744 | tf_op jit(solution)/shard_map/ppermute | solution.py:253
  6.3 1.9 %copy-start.1 = (bf16[384,4096]{1,0:T(8,128)(2,1)S(1)}, bf16[384,4096]{1,0:T(8,128)(2,1)}, u32[]{:S(2)}) copy-start(bf16[384,4096]{1,0:T(8,128)(2,1)} %q_ref.7) | copy-start | bytes 9437188
  8.2 1.0 %copy-start.4 = (bf16[384,512]{1,0:T(8,128)(2,1)S(1)}, bf16[384,512]{1,0:T(8,128)(2,1)}, u32[]{:S(2)}) copy-start(bf16[384,512]{1,0:T(8,128)(2,1)} %k_ref.7) | copy-start | bytes 1179652
  9.2 0.7 %copy-start.6 = (s32[384,1]{0,1:T(1,128)S(1)}, s32[384,1]{0,1:T(1,128)}, u32[]{:S(2)}) copy-start(s32[384,1]{0,1:T(1,128)} %param.12) | copy-start | bytes 4612
  9.9 0.7 %copy-start.7 = (s32[1,4]{1,0:T(1,128)S(1)}, s32[1,4]{1,0:T(1,128)}, u32[]{:S(2)}) copy-start(s32[1,4]{1,0:T(1,128)} %lengths_ref.1) | copy-start | bytes 52
  10.6 1.9 %copy-start.2 = (bf16[384,4096]{1,0:T(8,128)(2,1)S(1)}, bf16[384,4096]{1,0:T(8,128)(2,1)}, u32[]{:S(2)}) copy-start(bf16[384,4096]{1,0:T(8,128)(2,1)} %q_ref.7) | copy-start | bytes 9437188
  14.2 10.5 %collective-permute-start.5 = (bf16[32,4608]{1,0:T(8,128)(2,1)S(1)}, bf16[32,4608]{1,0:T(8,128)(2,1)S(1)}, u32[]{:S(2)}, u32[]{:S(2)}) collective-permute-start(bf16[32,4608]{1,0:T(8,128)(2,1)S(1)} %collective-permute-done.4.refs_5_), channel_id=1, source_target_pairs={{4,0},{8,4},{12,8},{14,12},{10,14},{6,10},{2,6},{0,2},{5,1},{9,5},... | collective-permute-start | bytes 884744 | tf_op jit(solution)/shard_map/ppermute | solution.py:253
  16.2 10.6 %collective-permute-start.1 = (bf16[32,4608]{1,0:T(8,128)(2,1)S(1)}, bf16[32,4608]{1,0:T(8,128)(2,1)S(1)}, u32[]{:S(2)}, u32[]{:S(2)}) collective-permute-start(bf16[32,4608]{1,0:T(8,128)(2,1)S(1)} %collective-permute-done.refs_2_), channel_id=1, source_target_pairs={{0,4},{4,8},{8,12},{12,14},{14,10},{10,6},{6,2},{2,0},{1,5},{5,9},... | collective-permute-start | bytes 884744 | tf_op jit(solution)/shard_map/ppermute | solution.py:253
  20.4 12.6 %collective-permute-start.9 = (bf16[32,4608]{1,0:T(8,128)(2,1)S(1)}, bf16[32,4608]{1,0:T(8,128)(2,1)S(1)}, u32[]{:S(2)}, u32[]{:S(2)}) collective-permute-start(bf16[32,4608]{1,0:T(8,128)(2,1)S(1)} %collective-permute-done.8.refs_3_), channel_id=1, source_target_pairs={{0,4},{4,8},{8,12},{12,14},{14,10},{10,6},{6,2},{2,0},{1,5},{5,9},... | collective-permute-start | bytes 884744 | tf_op jit(solution)/shard_map/ppermute | solution.py:253
  20.5 12.6 %collective-permute-start.12 = (bf16[32,4608]{1,0:T(8,128)(2,1)S(1)}, bf16[32,4608]{1,0:T(8,128)(2,1)S(1)}, u32[]{:S(2)}, u32[]{:S(2)}) collective-permute-start(bf16[32,4608]{1,0:T(8,128)(2,1)S(1)} %collective-permute-done.11.refs_4_), channel_id=1, source_target_pairs={{4,0},{8,4},{12,8},{14,12},{10,14},{6,10},{2,6},{0,2},{5,1},{9,5},... | collective-permute-start | bytes 884744 | tf_op jit(solution)/shard_map/ppermute | solution.py:253
  24.2 10.9 %copy-start.3 = (bf16[384,4096]{1,0:T(8,128)(2,1)S(1)}, bf16[384,4096]{1,0:T(8,128)(2,1)}, u32[]{:S(2)}) copy-start(bf16[384,4096]{1,0:T(8,128)(2,1)} %x_ref.7) | copy-start | bytes 9437188
  24.7 12.6 %collective-permute-start.6 = (bf16[32,4608]{1,0:T(8,128)(2,1)S(1)}, bf16[32,4608]{1,0:T(8,128)(2,1)S(1)}, u32[]{:S(2)}, u32[]{:S(2)}) collective-permute-start(bf16[32,4608]{1,0:T(8,128)(2,1)S(1)} %collective-permute-done.5.refs_3_), channel_id=1, source_target_pairs={{4,0},{8,4},{12,8},{14,12},{10,14},{6,10},{2,6},{0,2},{5,1},{9,5},... | collective-permute-start | bytes 884744 | tf_op jit(solution)/shard_map/ppermute | solution.py:253
  26.8 12.6 %collective-permute-start.2 = (bf16[32,4608]{1,0:T(8,128)(2,1)S(1)}, bf16[32,4608]{1,0:T(8,128)(2,1)S(1)}, u32[]{:S(2)}, u32[]{:S(2)}) collective-permute-start(bf16[32,4608]{1,0:T(8,128)(2,1)S(1)} %collective-permute-done.1.refs_0_), channel_id=1, source_target_pairs={{0,4},{4,8},{8,12},{12,14},{14,10},{10,6},{6,2},{2,0},{1,5},{5,9},... | collective-permute-start | bytes 884744 | tf_op jit(solution)/shard_map/ppermute | solution.py:253
  33.1 12.6 %collective-permute-start.10 = (bf16[32,4608]{1,0:T(8,128)(2,1)S(1)}, bf16[32,4608]{1,0:T(8,128)(2,1)S(1)}, u32[]{:S(2)}, u32[]{:S(2)}) collective-permute-start(bf16[32,4608]{1,0:T(8,128)(2,1)S(1)} %collective-permute-done.9.refs_6_.refs_1_), channel_id=1, source_target_pairs={{0,4},{4,8},{8,12},{12,14},{14,10},{10,6},{6,2},{2,0},{1,5},{5,9},... | collective-permute-start | bytes 884744 | tf_op jit(solution)/shard_map/ppermute | solution.py:253
  33.2 12.6 %collective-permute-start.13 = (bf16[32,4608]{1,0:T(8,128)(2,1)S(1)}, bf16[32,4608]{1,0:T(8,128)(2,1)S(1)}, u32[]{:S(2)}, u32[]{:S(2)}) collective-permute-start(bf16[32,4608]{1,0:T(8,128)(2,1)S(1)} %collective-permute-done.12.refs_7_.refs_2_), channel_id=1, source_target_pairs={{4,0},{8,4},{12,8},{14,12},{10,14},{6,10},{2,6},{0,2},{5,1},{9,5},... | collective-permute-start | bytes 884744 | tf_op jit(solution)/shard_map/ppermute | solution.py:253
  37.4 11.8 %collective-permute-start.7 = (bf16[32,4608]{1,0:T(8,128)(2,1)S(1)}, bf16[32,4608]{1,0:T(8,128)(2,1)S(1)}, u32[]{:S(2)}, u32[]{:S(2)}) collective-permute-start(bf16[32,4608]{1,0:T(8,128)(2,1)S(1)} %collective-permute-done.6.refs_3_), channel_id=1, source_target_pairs={{4,0},{8,4},{12,8},{14,12},{10,14},{6,10},{2,6},{0,2},{5,1},{9,5},... | collective-permute-start | bytes 884744 | tf_op jit(solution)/shard_map/ppermute | solution.py:253
  39.4 11.2 %collective-permute-start.3 = (bf16[32,4608]{1,0:T(8,128)(2,1)S(1)}, bf16[32,4608]{1,0:T(8,128)(2,1)S(1)}, u32[]{:S(2)}, u32[]{:S(2)}) collective-permute-start(bf16[32,4608]{1,0:T(8,128)(2,1)S(1)} %collective-permute-done.2.refs_0_), channel_id=1, source_target_pairs={{0,4},{4,8},{8,12},{12,14},{14,10},{10,6},{6,2},{2,0},{1,5},{5,9},... | collective-permute-start | bytes 884744 | tf_op jit(solution)/shard_map/ppermute | solution.py:253
  50.6 2.5 %copy-start = (bf16[384,512]{1,0:T(8,128)(2,1)S(1)}, bf16[384,512]{1,0:T(8,128)(2,1)}, u32[]{:S(2)}) copy-start(bf16[384,512]{1,0:T(8,128)(2,1)} %base_ref.1) | copy-start | bytes 1179652
  51.5 1.5 %collective-permute-start.14 = (f32[384,64]{1,0:T(8,128)S(1)}, f32[384,64]{1,0:T(8,128)S(1)}, u32[]{:S(2)}, u32[]{:S(2)}) collective-permute-start(f32[384,64]{1,0:T(8,128)S(1)} %get-tuple-element.50.mine_ref), channel_id=1, source_target_pairs={{0,1},{1,0},{2,3},{3,2},{4,5},{5,4},{6,7},{7,6},{8,9},{9,8},{10,11... | collective-permute-start | bytes 294920 | tf_op jit(solution)/shard_map/ppermute | solution.py:279

commit v9 on v8

--- a/solution.py
+++ b/solution.py
@@ -50,7 +50,7 @@
 
 
 def masks_kernel(n, me_ref, lengths_ref, adapter_ref, near_q_ref, near_k_ref, *refs):
-    place_ref, segment_ref, across_ref = refs
+    place_ref, segment_ref, across_ref, slot_ref, slot_across_ref = refs
     distance = ring_place(me_ref[0], n) - ring_place(adapter_ref[...], n)
     distance = jnp.where(distance < 0, distance + n, distance)
     place = jnp.where(distance <= n // 2, jnp.maximum(2 * distance - 1, 0), 2 * (n - distance))
@@ -63,17 +63,25 @@
         segment = segment + (position >= end).astype(jnp.int32)
     across_ref[...] = segment
     segment_ref[...] = column(segment)
+    rows = place.shape[1]
+    last = place == n - 1
+    earlier = lax.broadcasted_iota(jnp.int32, (rows, rows), 0) < lax.broadcasted_iota(jnp.int32, (rows, rows), 1)
+    ones = jnp.where(jnp.broadcast_to(last, (8, rows)), 1.0, 0.0).astype(jnp.bfloat16)
+    count = jnp.dot(ones, jnp.where(earlier, 1.0, 0.0).astype(jnp.bfloat16), preferred_element_type=jnp.float32)
+    slot = jnp.where(last, count[:1, :].astype(jnp.int32), -1)
+    slot_across_ref[...] = slot
+    slot_ref[...] = column(slot)
 
 
 def masks(n, lengths, adapter_row, queries, keys):
     rows = keys.shape[0]
-    tall = jax.ShapeDtypeStruct((rows, 1), jnp.int32)
+    tall, flat = [jax.ShapeDtypeStruct(shape, jnp.int32) for shape in ((rows, 1), (1, rows))]
     me = jnp.reshape(lax.axis_index("rep"), (1,)).astype(jnp.int32)
     return pl.pallas_call(
         functools.partial(masks_kernel, n),
-        out_shape=[tall, tall, jax.ShapeDtypeStruct((1, rows), jnp.int32)],
+        out_shape=[tall, tall, flat, tall, flat],
         in_specs=[SMEM, SMEM, VMEM, VMEM, VMEM],
-        out_specs=[VMEM] * 3,
+        out_specs=[VMEM] * 5,
         cost_estimate=pl.CostEstimate(flops=1_000_000_000, bytes_accessed=16 * rows, transcendentals=0),
         compiler_params=pltpu.CompilerParams(vmem_limit_bytes=4 * 2**20),
         name="masks",
@@ -102,21 +110,21 @@
             p_ref[head * TILE : (head + 1) * TILE, :] = (weights * inverse).astype(jnp.bfloat16)
 
 
-def probs_of(segment, across, queries, keys, kv_head):
+def probs_of(segment, across, queries, keys, kv_head, after):
     rows = keys.shape[0]
     shapes = [(GROUP * TILE, width) for _, _, width in windows(rows)]
     elements = sum(a * b for a, b in shapes)
     return pl.pallas_call(
         functools.partial(probs_kernel, kv_head),
         out_shape=[jax.ShapeDtypeStruct(s, jnp.bfloat16) for s in shapes],
-        in_specs=[VMEM] * 4,
+        in_specs=[VMEM] * 4 + [pl.BlockSpec(memory_space=pl.ANY)] * len(after),
         out_specs=[VMEM] * len(shapes),
         cost_estimate=pl.CostEstimate(
             flops=2_000_000_000, bytes_accessed=2 * elements, transcendentals=elements
         ),
         compiler_params=pltpu.CompilerParams(vmem_limit_bytes=12 * 2**20),
         name="probs",
-    )(segment, across, queries, keys)
+    )(segment, across, queries, keys, *after)
 
 
 def lowrank_kernel(at, count, place_ref, x_ref, *refs):
@@ -160,30 +168,80 @@
     )(*operands)
 
 
-def attend_kernel(kv_heads, place_ref, mine_ref, theirs_ref, base_ref, *refs):
+def last_rows_kernel(slot_across_ref, x_ref, out_ref):
+    room, rows = out_ref.shape[0], x_ref.shape[0]
+    pick = lax.broadcasted_iota(jnp.int32, (room, rows), 0) == slot_across_ref[...]
+    pick = jnp.where(pick, 1.0, 0.0).astype(jnp.bfloat16)
+    step = 1024
+    for at in range(0, x_ref.shape[1], step):
+        picked = jnp.dot(pick, x_ref[:, at : at + step], preferred_element_type=jnp.float32)
+        out_ref[:, at : at + step] = picked.astype(jnp.bfloat16)
+
+
+def last_rows(slot_across, x, room):
+    return pl.pallas_call(
+        last_rows_kernel,
+        out_shape=jax.ShapeDtypeStruct((room, x.shape[1]), x.dtype),
+        in_specs=[VMEM, VMEM],
+        out_specs=VMEM,
+        cost_estimate=pl.CostEstimate(flops=1_500_000_000, bytes_accessed=2 * x.size, transcendentals=0),
+        compiler_params=pltpu.CompilerParams(vmem_limit_bytes=8 * 2**20),
+        name="last_rows",
+    )(slot_across, x)
+
+
+def last_probs_kernel(slot_ref, *refs):
+    tiles = windows(slot_ref.shape[0])
+    p_refs, out_refs = refs[: 2 * len(tiles)], refs[2 * len(tiles) :]
+    for i, (_, first, width) in enumerate(tiles):
+        pick = lax.broadcasted_iota(jnp.int32, (width, 128), 1) == slot_ref[first : first + width, :]
+        pick = jnp.where(pick, 1.0, 0.0).astype(jnp.bfloat16)
+        for side in range(2):
+            picked = jnp.dot(p_refs[side * len(tiles) + i][...], pick, preferred_element_type=jnp.float32)
+            out_refs[i][:, side * 128 : (side + 1) * 128] = picked.astype(jnp.bfloat16)
+
+
+def last_probs(slot, left, right):
+    pieces = left + right
+    return pl.pallas_call(
+        last_probs_kernel,
+        out_shape=[jax.ShapeDtypeStruct((p.shape[0], 256), p.dtype) for p in left],
+        in_specs=[VMEM] * (1 + len(pieces)),
+        out_specs=[VMEM] * len(left),
+        cost_estimate=pl.CostEstimate(
+            flops=1_500_000_000, bytes_accessed=2 * sum(p.size for p in pieces), transcendentals=0
+        ),
+        compiler_params=pltpu.CompilerParams(vmem_limit_bytes=6 * 2**20),
+        name="last_probs",
+    )(slot, *pieces)
+
+
+def early_kernel(kv_heads, place_ref, mine_ref, theirs_ref, base_ref, *refs):
     rows = base_ref.shape[0]
     tiles = windows(rows)
-    up_refs = refs[: -kv_heads * len(tiles) - 3]
-    p_refs = refs[len(up_refs) : -3]
-    out_ref, block, sems = refs[-3:]
+    up_refs = refs[: -kv_heads * len(tiles) - 1]
+    p_refs, out_ref = refs[len(up_refs) : -1], refs[-1]
     rank = mine_ref.shape[1]
-    n = sum(up_ref.shape[0] for up_ref in up_refs) // rank
+    held = sum(up_ref.shape[0] for up_ref in up_refs)
+    pairs = -(-held // (2 * rank))
     place = place_ref[...]
     lowrank = (mine_ref[...] + theirs_ref[...]).astype(jnp.bfloat16)
     twice = jnp.concatenate([lowrank, lowrank], axis=1)
     second = (lax.broadcasted_iota(jnp.int32, twice.shape, 1) >= rank).astype(jnp.int32)
     offset = place - second
     spread = jnp.concatenate(
-        [jnp.where(offset == i, twice, jnp.zeros_like(twice)) for i in range(0, n, 2)], axis=1
+        [jnp.where(offset == 2 * i, twice, jnp.zeros_like(twice)) for i in range(pairs)], axis=1
     )
-    up = jnp.concatenate([up_ref[...] for up_ref in up_refs], axis=0)
-    delta = jnp.dot(spread, up, preferred_element_type=jnp.float32).astype(jnp.bfloat16)
+    ups = [up_ref[...] for up_ref in up_refs]
+    if held < 2 * rank * pairs:
+        ups.append(jnp.zeros((2 * rank * pairs - held, base_ref.shape[1]), jnp.bfloat16))
+    delta = jnp.dot(
+        spread, jnp.concatenate(ups, axis=0), preferred_element_type=jnp.float32
+    ).astype(jnp.bfloat16)
     values = (
         base_ref[...].astype(jnp.float32) + adapter_scale * delta.astype(jnp.float32)
     ).astype(jnp.bfloat16)
-    copies = []
     wide = GROUP * HEAD_SIZE
-    done = 0
     for kv in range(kv_heads):
         columns = slice(kv * HEAD_SIZE, (kv + 1) * HEAD_SIZE)
         for i, (start, first, width) in enumerate(tiles):
@@ -191,35 +249,101 @@
                 p_refs[kv * len(tiles) + i][...],
                 values[first : first + width, columns],
                 preferred_element_type=jnp.float32,
-            ).astype(jnp.bfloat16)
+            )
             for head in range(GROUP):
                 at = kv * wide + head * HEAD_SIZE
-                block[start : start + TILE, at : at + HEAD_SIZE] = mixed[head * TILE : (head + 1) * TILE, :]
-            if 2 * (i + 1) in (len(tiles), 2 * len(tiles)):
-                part = slice(0, rows // 2) if 2 * (i + 1) == len(tiles) else slice(rows // 2, rows)
-                span = slice(kv * wide, (kv + 1) * wide)
-                copy = pltpu.make_async_copy(block.at[part, span], out_ref.at[part, span], sems.at[done])
+                out_ref[start : start + TILE, at : at + HEAD_SIZE] = mixed[head * TILE : (head + 1) * TILE, :]
+
+
+def early_product(place, mine, theirs, base, ups, probs):
+    rows, value_portion = base.shape
+    kv_heads = value_portion // HEAD_SIZE
+    flat = [p for per_head in probs for p in per_head]
+    return pl.pallas_call(
+        functools.partial(early_kernel, kv_heads),
+        out_shape=jax.ShapeDtypeStruct((rows, kv_heads * GROUP * HEAD_SIZE), jnp.float32),
+        in_specs=[VMEM] * (4 + len(ups) + len(flat)),
+        out_specs=VMEM,
+        cost_estimate=pl.CostEstimate(flops=50_000_000, bytes_accessed=4 * rows, transcendentals=0),
+        compiler_params=pltpu.CompilerParams(vmem_limit_bytes=8 * 2**20),
+        name="early_product",
+    )(place, mine, theirs, base, *ups, *flat)
+
+
+def last_lowrank_kernel(x_ref, low_ref, high_ref, *refs):
+    out_ref, up_ref = refs[-2:]
+    features = x_ref.shape[1]
+    stacked = jnp.concatenate([low_ref[:, :features], high_ref[:, :features]], axis=0)
+    out_ref[...] = lax.dot_general(x_ref[...], stacked, NT, preferred_element_type=jnp.float32)
+    up_ref[...] = jnp.concatenate([low_ref[:, features:], high_ref[:, features:]], axis=0)
+
+
+def last_lowrank(x, low, high, after):
+    rank, columns = 2 * low.shape[0], low.shape[1] - x.shape[1]
+    return pl.pallas_call(
+        last_lowrank_kernel,
+        out_shape=[
+            jax.ShapeDtypeStruct((x.shape[0], rank), jnp.float32),
+            jax.ShapeDtypeStruct((rank, columns), low.dtype),
+        ],
+        in_specs=[VMEM] * 3 + [pl.BlockSpec(memory_space=pl.ANY)] * len(after),
+        out_specs=[VMEM, VMEM],
+        cost_estimate=pl.CostEstimate(flops=600_000_000, bytes_accessed=2 * x.size, transcendentals=0),
+        compiler_params=pltpu.CompilerParams(vmem_limit_bytes=6 * 2**20),
+        name="last_lowrank",
+    )(x, low, high, *after)
+
+
+def finish_kernel(mine_ref, theirs_ref, up_ref, early_ref, *refs):
+    p_refs, (out_ref, block, sems) = refs[:-3], refs[-3:]
+    rows = early_ref.shape[0]
+    tiles = windows(rows)
+    wide = GROUP * HEAD_SIZE
+    lowrank = (mine_ref[...] + theirs_ref[...]).astype(jnp.bfloat16)
+    delta = jnp.dot(lowrank, up_ref[...], preferred_element_type=jnp.float32).astype(jnp.bfloat16)
+    change = (adapter_scale * delta.astype(jnp.float32)).astype(jnp.bfloat16)
+    room = change.shape[0]
+    if room < 128:
+        change = jnp.concatenate([change, jnp.zeros((128 - room, change.shape[1]), jnp.bfloat16)], axis=0)
+    none = jnp.zeros((128, HEAD_SIZE), jnp.bfloat16)
+    copies = []
+    for pair in range(len(p_refs) // len(tiles)):
+        at = 2 * pair * HEAD_SIZE
+        left, right = change[:, at : at + HEAD_SIZE], change[:, at + HEAD_SIZE : at + 2 * HEAD_SIZE]
+        both = jnp.concatenate(
+            [jnp.concatenate([left, none], axis=1), jnp.concatenate([none, right], axis=1)], axis=0
+        )
+        for i, (start, _, _) in enumerate(tiles):
+            added = jnp.dot(p_refs[pair * len(tiles) + i][...], both, preferred_element_type=jnp.float32)
+            for side in range(2):
+                for head in range(GROUP):
+                    at = (2 * pair + side) * wide + head * HEAD_SIZE
+                    part = added[head * TILE : (head + 1) * TILE, side * HEAD_SIZE : (side + 1) * HEAD_SIZE]
+                    whole = early_ref[start : start + TILE, at : at + HEAD_SIZE] + part
+                    block[start : start + TILE, at : at + HEAD_SIZE] = whole.astype(jnp.bfloat16)
+            if i % 2 == 1:
+                rows_done = slice(start - TILE, start + TILE)
+                span = slice(2 * pair * wide, 2 * (pair + 1) * wide)
+                copy = pltpu.make_async_copy(
+                    block.at[rows_done, span], out_ref.at[rows_done, span], sems.at[len(copies)]
+                )
                 copy.start()
                 copies.append(copy)
-                done += 1
     for copy in copies:
         copy.wait()
 
 
-def attend(place, mine, theirs, base, ups, probs):
-    rows, value_portion = base.shape
-    kv_heads = value_portion // HEAD_SIZE
-    wide = kv_heads * GROUP * HEAD_SIZE
-    flat = [p for per_head in probs for p in per_head]
-    return pl.pallas_call(
-        functools.partial(attend_kernel, kv_heads),
-        out_shape=jax.ShapeDtypeStruct((rows, wide), jnp.bfloat16),
-        in_specs=[VMEM] * (4 + len(ups) + len(flat)),
+def finish(mine, theirs, up, early, picked):
+    flat = [p for pair in picked for p in pair]
+    return pl.pallas_call(
+        finish_kernel,
+        out_shape=jax.ShapeDtypeStruct(early.shape, jnp.bfloat16),
+        in_specs=[VMEM] * (4 + len(flat)),
         out_specs=pl.BlockSpec(memory_space=pl.ANY),
-        scratch_shapes=[pltpu.VMEM((rows, wide), jnp.bfloat16), pltpu.SemaphoreType.DMA((2 * kv_heads,))],
-        compiler_params=pltpu.CompilerParams(vmem_limit_bytes=12 * 2**20),
-        name="attend",
-    )(place, mine, theirs, base, *ups, *flat)
+        scratch_shapes=[pltpu.VMEM(early.shape, jnp.bfloat16), pltpu.SemaphoreType.DMA((len(flat) // 2,))],
+        compiler_params=pltpu.CompilerParams(vmem_limit_bytes=10 * 2**20),
+        name="finish",
+    )(mine, theirs, up, early, *flat)
 
 
 def on_device(
@@ -242,7 +366,7 @@
     both = jnp.concatenate([down, adapter_up_weight[0]], axis=1)
     rank = both.shape[0]
     own_low, own_high = both[: rank // 2], both[rank // 2 :]
-    place, segment, across = masks(
+    place, segment, across, slot, slot_across = masks(
         n, sequence_lengths, adapter_of_row.reshape(1, -1), queries, stacked_key_rows
     )
     low, high = {0: own_low}, {0: own_high}
@@ -265,26 +389,24 @@
         for pair in ([low[step], high[-step]], [high[step], low[-step]])
     ]
     probs = [
-        probs_of(segment, across, queries, stacked_key_rows, kv) for kv in range(kv_heads)
+        probs_of(segment, across, queries, stacked_key_rows, kv, [low[1], high[-1]] if kv > 0 else [])
+        for kv in range(kv_heads)
     ]
 
+    picked = [last_probs(slot, probs[kv], probs[kv + 1]) for kv in range(0, kv_heads, 2)]
+    most = 2 * normed_token_rows.shape[0] // n
+    x_last = last_rows(slot_across, normed_token_rows, -(-most // 16) * 16)
+
     partial, ups = None, []
-    for lo, hi in [(0, 3)] + [(a, a + 2) for a in range(3, n - 1, 2)] + [(n - 1, n)]:
+    for lo, hi in [(0, 3)] + [(a, a + 2) for a in range(3, n - 1, 2)]:
         pieces = [piece for d in distances[lo:hi] for piece in (low[d], high[d])]
         after = arrivals[kv_heads - 1] if lo == 0 else []
-        if hi == n:
-            after = [p[0] for p in probs]
-        partial, up = lowrank_of(lo, place, normed_token_rows, partial, pieces, after)
+        partial, up = lowrank_of(lo, place, normed_token_rows, partial, pieces, after + ([x_last] + [p[0] for p in picked] if lo == n - 5 else []))
         ups.append(up)
-    other = lax.ppermute(partial, "tp", [(0, 1), (1, 0)])
-    return attend(
-        place,
-        partial,
-        other,
-        base_value_rows,
-        ups,
-        probs,
-    )
+    swap = [(0, 1), (1, 0)]
+    early = early_product(place, partial, lax.ppermute(partial, "tp", swap), base_value_rows, ups, probs)
+    last, last_up = last_lowrank(x_last, low[far], high[far], [early])
+    return finish(last, lax.ppermute(last, "tp", swap), last_up, early, picked)
 
 
 def solution(mesh):

time: 56.2 us -> 55.2 us (0.982)
  waiting for transfers between devices: 18.9 us -> 12.6 us
  Pallas kernels: 14.7 us -> 18.1 us
  starting transfers between devices: 15.5 us -> 17.1 us
    ppermute x14, waiting for transfers between devices: 17.5 us -> 10 us  [pass_round(): piece = lax.ppermute(piece, 'rep', pairs)]
    pallas_call x1 -> x6, Pallas kernels: 2.75 us -> 6.99 us  [the longest x1 2.22 us: finish(): pl.pallas_call(finish_kernel, out_shape=jax.ShapeDtypeStruct(early.shape,...]
    ppermute x14, starting transfers between devices: 15.5 us -> 16.8 us  [pass_round(): piece = lax.ppermute(piece, 'rep', pairs)]
    ppermute x1 -> x2, waiting for transfers between devices: 1.43 us -> 2.52 us  [the longest x1 1.43 us: on_device(): lax.ppermute(partial, 'tp', swap)]
    pallas_call x4 -> x3, Pallas kernels: 4.15 us -> 3.18 us  [lowrank_of(): pl.pallas_call(functools.partial(lowrank_kernel, at, len(pieces)), out_sh...]
  transfers between devices with their start and end apart: 15 -> 16, of which waited for: 8 -> 8; matrix products, arithmetic and copies ran while one was open for 0% -> 0% of each run, Pallas kernels for 20% -> 28%
where the time goes in v9:
time: 55.2 us; the launch traced here: 54.9 us
  Pallas kernels  18.1 us (33%)
  starting transfers between devices  17.1 us (31%)
  waiting for transfers between devices  12.6 us (23%)
  local copies, waits for them, and re-layouts  5.7 us (10%)
  other arithmetic  1.11 us (2%)
    ppermute x14, starting transfers between devices, pass_round(): piece = lax.ppermute(piece, 'rep', pairs)  16.8 us
    ppermute x14, waiting for transfers between devices, pass_round(): piece = lax.ppermute(piece, 'rep', pairs)  10 us
    pallas_call x4, Pallas kernels, probs_of(): pl.pallas_call(functools.partial(probs_kernel, kv_head), out_shape=[jax.S...  7.08 us
    unnamed x16, local copies, waits for them, and re-layouts  5.7 us
    pallas_call x3, Pallas kernels, lowrank_of(): pl.pallas_call(functools.partial(lowrank_kernel, at, len(pieces)), out_sh...  3.18 us
    pallas_call x1, Pallas kernels, finish(): pl.pallas_call(finish_kernel, out_shape=jax.ShapeDtypeStruct(early.shape,...  2.22 us
    pallas_call x1, Pallas kernels, early_product(): pl.pallas_call(functools.partial(early_kernel, kv_heads), out_shape=jax.S...  1.89 us
    pallas_call x2, Pallas kernels, last_probs(): pl.pallas_call(last_probs_kernel, out_shape=[jax.ShapeDtypeStruct((p.shap...  1.82 us
  transfers between devices with their start and end apart: 16, of which 8 were waited for; matrix products, arithmetic and copies ran while one was open for 0% of the time, Pallas kernels for 28%

profile of v9, /device:TPU:0, one launch (start us, length us, event | category | flops | bytes accessed | tf_op | source)
XLA Modules:
  0.0 54.9 jit_solution(16689521697914205994)
XLA Ops:
  0.0 1.1 %pad_maximum_fusion = (bf16[32,4608]{1,0:T(8,128)(2,1)S(1)}, bf16[32,4608]{1,0:T(8,128)(2,1)S(1)}) fusion(bf16[64,512]{1,0:T(8,128)(2,1)} %bitcast.8, bf16[64,4096]{1,0:T(8,128)(2,1)} %bitcast.7), kind=kLoop, calls=%fused_computation.3 | loop fusion | flops 1179648 | bytes 1179648 | tf_op jit(solution)/shard_map/concatenate | solution.py:366
  1.1 3.1 %collective-permute-start.8 = (bf16[32,4608]{1,0:T(8,128)(2,1)S(1)}, bf16[32,4608]{1,0:T(8,128)(2,1)S(1)}, u32[]{:S(2)}, u32[]{:S(2)}) collective-permute-start(bf16[32,4608]{1,0:T(8,128)(2,1)S(1)} %get-tuple-element.103.refs_1_), channel_id=1, source_target_pairs={{0,4},{4,8},{8,12},{12,14},{14,10},{10,6},{6,2},{2,0},{1,5},{5,9},... | collective-permute-start | bytes 884744 | tf_op jit(solution)/shard_map/ppermute | solution.py:377
  4.2 2.0 %collective-permute-start.11 = (bf16[32,4608]{1,0:T(8,128)(2,1)S(1)}, bf16[32,4608]{1,0:T(8,128)(2,1)S(1)}, u32[]{:S(2)}, u32[]{:S(2)}) collective-permute-start(bf16[32,4608]{1,0:T(8,128)(2,1)S(1)} %get-tuple-element.104.refs_0_), channel_id=1, source_target_pairs={{4,0},{8,4},{12,8},{14,12},{10,14},{6,10},{2,6},{0,2},{5,1},{9,5},... | collective-permute-start | bytes 884744 | tf_op jit(solution)/shard_map/ppermute | solution.py:377
  6.3 1.9 %copy-done.1 = bf16[384,4096]{1,0:T(8,128)(2,1)S(1)} copy-done((bf16[384,4096]{1,0:T(8,128)(2,1)S(1)}, bf16[384,4096]{1,0:T(8,128)(2,1)}, u32[]{:S(2)}) %copy-start.1) | copy-done | bytes 3145752
  13.5 1.8 %probs.4 = (bf16[512,128]{1,0:T(8,128)(2,1)S(1)}, bf16[512,128]{1,0:T(8,128)(2,1)S(1)}, bf16[512,256]{1,0:T(8,128)(2,1)S(1)}, bf16[512,256]{1,0:T(8,128)(2,1)S(1...) custom-call(s32[384,1]{1,0:T(8,128)S(1)} %get-tuple-element.58.segment_ref, ...), custom_call_target="tpu_custom_call" | custom-call | flops 2000000000 | bytes 1310720 | tf_op jit(solution)/shard_map/probs/pallas_call | solution.py:117
  15.3 2.0 %collective-permute-start.9 = (bf16[32,4608]{1,0:T(8,128)(2,1)S(1)}, bf16[32,4608]{1,0:T(8,128)(2,1)S(1)}, u32[]{:S(2)}, u32[]{:S(2)}) collective-permute-start(bf16[32,4608]{1,0:T(8,128)(2,1)S(1)} %collective-permute-done.8.refs_3_), channel_id=1, source_target_pairs={{0,4},{4,8},{8,12},{12,14},{14,10},{10,6},{6,2},{2,0},{1,5},{5,9},... | collective-permute-start | bytes 884744 | tf_op jit(solution)/shard_map/ppermute | solution.py:377
  17.9 1.9 %collective-permute-start.1 = (bf16[32,4608]{1,0:T(8,128)(2,1)S(1)}, bf16[32,4608]{1,0:T(8,128)(2,1)S(1)}, u32[]{:S(2)}, u32[]{:S(2)}) collective-permute-start(bf16[32,4608]{1,0:T(8,128)(2,1)S(1)} %collective-permute-done.refs_2_.refs_0_), channel_id=1, source_target_pairs={{0,4},{4,8},{8,12},{12,14},{14,10},{10,6},{6,2},{2,0},{1,5},{5,9},... | collective-permute-start | bytes 884744 | tf_op jit(solution)/shard_map/ppermute | solution.py:377
  19.8 1.8 %probs.7 = (bf16[512,128]{1,0:T(8,128)(2,1)S(1)}, bf16[512,128]{1,0:T(8,128)(2,1)S(1)}, bf16[512,256]{1,0:T(8,128)(2,1)S(1)}, bf16[512,256]{1,0:T(8,128)(2,1)S(1...) custom-call(s32[384,1]{1,0:T(8,128)S(1)} %get-tuple-element.58.segment_ref, ...), custom_call_target="tpu_custom_call" | custom-call | flops 2000000000 | bytes 1310720 | tf_op jit(solution)/shard_map/probs/pallas_call | solution.py:117
  21.5 1.8 %probs.6 = (bf16[512,128]{1,0:T(8,128)(2,1)S(1)}, bf16[512,128]{1,0:T(8,128)(2,1)S(1)}, bf16[512,256]{1,0:T(8,128)(2,1)S(1)}, bf16[512,256]{1,0:T(8,128)(2,1)S(1...) custom-call(s32[384,1]{1,0:T(8,128)S(1)} %get-tuple-element.58.segment_ref, ...), custom_call_target="tpu_custom_call" | custom-call | flops 2000000000 | bytes 1310720 | tf_op jit(solution)/shard_map/probs/pallas_call | solution.py:117
  23.5 1.8 %probs.5 = (bf16[512,128]{1,0:T(8,128)(2,1)S(1)}, bf16[512,128]{1,0:T(8,128)(2,1)S(1)}, bf16[512,256]{1,0:T(8,128)(2,1)S(1)}, bf16[512,256]{1,0:T(8,128)(2,1)S(1...) custom-call(s32[384,1]{1,0:T(8,128)S(1)} %get-tuple-element.58.segment_ref, ...), custom_call_target="tpu_custom_call" | custom-call | flops 2000000000 | bytes 1310720 | tf_op jit(solution)/shard_map/probs/pallas_call | solution.py:117
  26.4 1.7 %collective-permute-start.6 = (bf16[32,4608]{1,0:T(8,128)(2,1)S(1)}, bf16[32,4608]{1,0:T(8,128)(2,1)S(1)}, u32[]{:S(2)}, u32[]{:S(2)}) collective-permute-start(bf16[32,4608]{1,0:T(8,128)(2,1)S(1)} %collective-permute-done.5.refs_3_), channel_id=1, source_target_pairs={{4,0},{8,4},{12,8},{14,12},{10,14},{6,10},{2,6},{0,2},{5,1},{9,5},... | collective-permute-start | bytes 884744 | tf_op jit(solution)/shard_map/ppermute | solution.py:377
  28.1 2.0 %collective-permute-done.1.refs_0_ = bf16[32,4608]{1,0:T(8,128)(2,1)S(1)} collective-permute-done((bf16[32,4608]{1,0:T(8,128)(2,1)S(1)}, bf16[32,4608]{1,0:T(8,128)(2,1)S(1)}, u32[]{:S(2)}, u32[]{:S(2)}) %collective-permute-start.1) | collective-permute-done | bytes 294944 | tf_op jit(solution)/shard_map/ppermute | solution.py:377
  30.1 1.8 %collective-permute-start.2 = (bf16[32,4608]{1,0:T(8,128)(2,1)S(1)}, bf16[32,4608]{1,0:T(8,128)(2,1)S(1)}, u32[]{:S(2)}, u32[]{:S(2)}) collective-permute-start(bf16[32,4608]{1,0:T(8,128)(2,1)S(1)} %collective-permute-done.1.refs_0_), channel_id=1, source_target_pairs={{0,4},{4,8},{8,12},{12,14},{14,10},{10,6},{6,2},{2,0},{1,5},{5,9},... | collective-permute-start | bytes 884744 | tf_op jit(solution)/shard_map/ppermute | solution.py:377
  32.8 1.6 %collective-permute-start.10 = (bf16[32,4608]{1,0:T(8,128)(2,1)S(1)}, bf16[32,4608]{1,0:T(8,128)(2,1)S(1)}, u32[]{:S(2)}, u32[]{:S(2)}) collective-permute-start(bf16[32,4608]{1,0:T(8,128)(2,1)S(1)} %collective-permute-done.9.refs_6_.refs_1_), channel_id=1, source_target_pairs={{0,4},{4,8},{8,12},{12,14},{14,10},{10,6},{6,2},{2,0},{1,5},{5,9},... | collective-permute-start | bytes 884744 | tf_op jit(solution)/shard_map/ppermute | solution.py:377
  34.9 1.1 %lowrank.3 = (f32[384,64]{1,0:T(8,128)S(1)}, bf16[192,512]{1,0:T(8,128)(2,1)S(1)}) custom-call(s32[384,1]{1,0:T(8,128)S(1)} %get-tuple-element.55.place_ref, bf16[384,4096]{1,0:T(8,128)(2,1)S(1)} %copy-done.3, bf16[32,4608]{1,0:T(8,128)(2,1)S(1)} %get-tuple-element.104.refs_0_, bf16[32,4608]{1,0:T(8,128)(2,1)S(1)} %get-tuple-element.103.refs_1_, ...), custom_call_target="tpu_custom_call" | custom-call | flops 1700000000 | bytes 4915200 | tf_op jit(solution)/shard_map/lowrank/pallas_call | solution.py:155
  36.0 3.7 %collective-permute-done.6.refs_3_ = bf16[32,4608]{1,0:T(8,128)(2,1)S(1)} collective-permute-done((bf16[32,4608]{1,0:T(8,128)(2,1)S(1)}, bf16[32,4608]{1,0:T(8,128)(2,1)S(1)}, u32[]{:S(2)}, u32[]{:S(2)}) %collective-permute-start.6) | collective-permute-done | bytes 294944 | tf_op jit(solution)/shard_map/ppermute | solution.py:377
  40.0 1.8 %collective-permute-start.3 = (bf16[32,4608]{1,0:T(8,128)(2,1)S(1)}, bf16[32,4608]{1,0:T(8,128)(2,1)S(1)}, u32[]{:S(2)}, u32[]{:S(2)}) collective-permute-start(bf16[32,4608]{1,0:T(8,128)(2,1)S(1)} %collective-permute-done.2.refs_0_), channel_id=1, source_target_pairs={{0,4},{4,8},{8,12},{12,14},{14,10},{10,6},{6,2},{2,0},{1,5},{5,9},... | collective-permute-start | bytes 884744 | tf_op jit(solution)/shard_map/ppermute | solution.py:377
  41.8 1.1 %lowrank.4 = (f32[384,64]{1,0:T(8,128)S(1)}, bf16[128,512]{1,0:T(8,128)(2,1)S(1)}) custom-call(s32[384,1]{1,0:T(8,128)S(1)} %get-tuple-element.55.place_ref, bf16[384,4096]{1,0:T(8,128)(2,1)S(1)} %copy-done.3, bf16[32,4608]{1,0:T(8,128)(2,1)S(1)} %collective-permute-done.1.refs_0_, bf16[32,4608]{1,0:T(8,128)(2,1)S(1)} %collective-permute-done.9.refs_6_.refs_1_, ...), custom_call_target="tpu_custom_call" | custom-call | flops 1700000000 | bytes 4325376 | tf_op jit(solution)/shard_map/lowrank/pallas_call | solution.py:155
  42.9 3.5 %collective-permute-done.10.refs_1_ = bf16[32,4608]{1,0:T(8,128)(2,1)S(1)} collective-permute-done((bf16[32,4608]{1,0:T(8,128)(2,1)S(1)}, bf16[32,4608]{1,0:T(8,128)(2,1)S(1)}, u32[]{:S(2)}, u32[]{:S(2)}) %collective-permute-start.10) | collective-permute-done | bytes 294944 | tf_op jit(solution)/shard_map/ppermute | solution.py:377
  46.4 1.1 %lowrank.5 = (f32[384,64]{1,0:T(8,128)S(1)}, bf16[128,512]{1,0:T(8,128)(2,1)S(1)}) custom-call(s32[384,1]{1,0:T(8,128)S(1)} %get-tuple-element.55.place_ref, bf16[384,4096]{1,0:T(8,128)(2,1)S(1)} %copy-done.3, bf16[32,4608]{1,0:T(8,128)(2,1)S(1)} %collective-permute-done.2.refs_0_, bf16[32,4608]{1,0:T(8,128)(2,1)S(1)} %collective-permute-done.10.refs_1_, ...), custom_call_target="tpu_custom_call" | custom-call | flops 1700000000 | bytes 4325376 | tf_op jit(solution)/shard_map/lowrank/pallas_call | solution.py:155
  47.5 1.4 %collective-permute-done.14.theirs_ref = f32[384,64]{1,0:T(8,128)S(1)} collective-permute-done((f32[384,64]{1,0:T(8,128)S(1)}, f32[384,64]{1,0:T(8,128)S(1)}, u32[]{:S(2)}, u32[]{:S(2)}) %collective-permute-start.14) | collective-permute-done | bytes 98336 | tf_op jit(solution)/shard_map/ppermute | solution.py:407
  49.0 1.9 %early_product.1.refs_0_.early_ref = f32[384,4096]{1,0:T(8,128)S(1)} custom-call(s32[384,1]{1,0:T(8,128)S(1)} %get-tuple-element.55.place_ref, f32[384,64]{1,0:T(8,128)S(1)} %get-tuple-element.87.mine_ref, f32[384,64]{1,0:T(8,128)S(1)} %collective-permute-done.14.theirs_ref, bf16[384,512]{1,0:T(8,128)(2,1)S(1)} %copy-done, ...), custom_call_target="tpu_custom_call" | custom-call | flops 50000000 | bytes 1536 | tf_op jit(solution)/shard_map/early_product/pallas_call | solution.py:262
  51.4 1.1 %collective-permute-done.15.theirs_ref = f32[96,64]{1,0:T(8,128)S(1)} collective-permute-done((f32[96,64]{1,0:T(8,128)S(1)}, f32[96,64]{1,0:T(8,128)S(1)}, u32[]{:S(2)}, u32[]{:S(2)}) %collective-permute-start.15) | collective-permute-done | bytes 24608 | tf_op jit(solution)/shard_map/ppermute | solution.py:409
  52.5 2.2 %finish.1 = bf16[384,4096]{1,0:T(8,128)(2,1)} custom-call(f32[96,64]{1,0:T(8,128)S(1)} %get-tuple-element.91.mine_ref, f32[96,64]{1,0:T(8,128)S(1)} %collective-permute-done.15.theirs_ref, bf16[64,512]{1,0:T(8,128)(2,1)S(1)} %get-tuple-element.92.up_ref, f32[384,4096]{1,0:T(8,128)S(1)} %early_product.1.refs_0_.early_ref, ...), custom_call_target="tpu_custom_call" | custom-call | tf_op jit(solution)/shard_map/finish/pallas_call | solution.py:338
  (39 shorter events, 9.6 us)
Async XLA Ops:
  1.1 14.2 %collective-permute-start.8 = (bf16[32,4608]{1,0:T(8,128)(2,1)S(1)}, bf16[32,4608]{1,0:T(8,128)(2,1)S(1)}, u32[]{:S(2)}, u32[]{:S(2)}) collective-permute-start(bf16[32,4608]{1,0:T(8,128)(2,1)S(1)} %get-tuple-element.103.refs_1_), channel_id=1, source_target_pairs={{0,4},{4,8},{8,12},{12,14},{14,10},{10,6},{6,2},{2,0},{1,5},{5,9},... | collective-permute-start | bytes 884744 | tf_op jit(solution)/shard_map/ppermute | solution.py:377
  4.2 13.2 %collective-permute-start.4 = (bf16[32,4608]{1,0:T(8,128)(2,1)S(1)}, bf16[32,4608]{1,0:T(8,128)(2,1)S(1)}, u32[]{:S(2)}, u32[]{:S(2)}) collective-permute-start(bf16[32,4608]{1,0:T(8,128)(2,1)S(1)} %get-tuple-element.103.refs_1_), channel_id=1, source_target_pairs={{4,0},{8,4},{12,8},{14,12},{10,14},{6,10},{2,6},{0,2},{5,1},{9,5},... | collective-permute-start | bytes 884744 | tf_op jit(solution)/shard_map/ppermute | solution.py:377
  4.2 19.1 %collective-permute-start.11 = (bf16[32,4608]{1,0:T(8,128)(2,1)S(1)}, bf16[32,4608]{1,0:T(8,128)(2,1)S(1)}, u32[]{:S(2)}, u32[]{:S(2)}) collective-permute-start(bf16[32,4608]{1,0:T(8,128)(2,1)S(1)} %get-tuple-element.104.refs_0_), channel_id=1, source_target_pairs={{4,0},{8,4},{12,8},{14,12},{10,14},{6,10},{2,6},{0,2},{5,1},{9,5},... | collective-permute-start | bytes 884744 | tf_op jit(solution)/shard_map/ppermute | solution.py:377
  6.2 11.7 %collective-permute-start = (bf16[32,4608]{1,0:T(8,128)(2,1)S(1)}, bf16[32,4608]{1,0:T(8,128)(2,1)S(1)}, u32[]{:S(2)}, u32[]{:S(2)}) collective-permute-start(bf16[32,4608]{1,0:T(8,128)(2,1)S(1)} %get-tuple-element.104.refs_0_), channel_id=1, source_target_pairs={{0,4},{4,8},{8,12},{12,14},{14,10},{10,6},{6,2},{2,0},{1,5},{5,9},... | collective-permute-start | bytes 884744 | tf_op jit(solution)/shard_map/ppermute | solution.py:377
  6.2 1.9 %copy-start.1 = (bf16[384,4096]{1,0:T(8,128)(2,1)S(1)}, bf16[384,4096]{1,0:T(8,128)(2,1)}, u32[]{:S(2)}) copy-start(bf16[384,4096]{1,0:T(8,128)(2,1)} %q_ref.7) | copy-start | bytes 9437188
  8.1 1.0 %copy-start.4 = (bf16[384,512]{1,0:T(8,128)(2,1)S(1)}, bf16[384,512]{1,0:T(8,128)(2,1)}, u32[]{:S(2)}) copy-start(bf16[384,512]{1,0:T(8,128)(2,1)} %k_ref.7) | copy-start | bytes 1179652
  9.1 0.7 %copy-start.6 = (s32[384,1]{0,1:T(1,128)S(1)}, s32[384,1]{0,1:T(1,128)}, u32[]{:S(2)}) copy-start(s32[384,1]{0,1:T(1,128)} %param.12) | copy-start | bytes 4612
  9.8 0.7 %copy-start.7 = (s32[1,4]{1,0:T(1,128)S(1)}, s32[1,4]{1,0:T(1,128)}, u32[]{:S(2)}) copy-start(s32[1,4]{1,0:T(1,128)} %lengths_ref.1) | copy-start | bytes 52
  10.5 1.9 %copy-start.3 = (bf16[384,4096]{1,0:T(8,128)(2,1)S(1)}, bf16[384,4096]{1,0:T(8,128)(2,1)}, u32[]{:S(2)}) copy-start(bf16[384,4096]{1,0:T(8,128)(2,1)} %x_ref.7) | copy-start | bytes 9437188
  11.3 2.2 %copy-start.2 = (bf16[384,4096]{1,0:T(8,128)(2,1)S(1)}, bf16[384,4096]{1,0:T(8,128)(2,1)}, u32[]{:S(2)}) copy-start(bf16[384,4096]{1,0:T(8,128)(2,1)} %q_ref.7) | copy-start | bytes 9437188
  11.3 2.2 %copy-start.5 = (bf16[384,512]{1,0:T(8,128)(2,1)S(1)}, bf16[384,512]{1,0:T(8,128)(2,1)}, u32[]{:S(2)}) copy-start(bf16[384,512]{1,0:T(8,128)(2,1)} %k_ref.7) | copy-start | bytes 1179652
  15.3 17.5 %collective-permute-start.9 = (bf16[32,4608]{1,0:T(8,128)(2,1)S(1)}, bf16[32,4608]{1,0:T(8,128)(2,1)S(1)}, u32[]{:S(2)}, u32[]{:S(2)}) collective-permute-start(bf16[32,4608]{1,0:T(8,128)(2,1)S(1)} %collective-permute-done.8.refs_3_), channel_id=1, source_target_pairs={{0,4},{4,8},{8,12},{12,14},{14,10},{10,6},{6,2},{2,0},{1,5},{5,9},... | collective-permute-start | bytes 884744 | tf_op jit(solution)/shard_map/ppermute | solution.py:377
  17.4 9.0 %collective-permute-start.5 = (bf16[32,4608]{1,0:T(8,128)(2,1)S(1)}, bf16[32,4608]{1,0:T(8,128)(2,1)S(1)}, u32[]{:S(2)}, u32[]{:S(2)}) collective-permute-start(bf16[32,4608]{1,0:T(8,128)(2,1)S(1)} %collective-permute-done.4.refs_5_.refs_1_), channel_id=1, source_target_pairs={{4,0},{8,4},{12,8},{14,12},{10,14},{6,10},{2,6},{0,2},{5,1},{9,5},... | collective-permute-start | bytes 884744 | tf_op jit(solution)/shard_map/ppermute | solution.py:377
  17.9 12.2 %collective-permute-start.1 = (bf16[32,4608]{1,0:T(8,128)(2,1)S(1)}, bf16[32,4608]{1,0:T(8,128)(2,1)S(1)}, u32[]{:S(2)}, u32[]{:S(2)}) collective-permute-start(bf16[32,4608]{1,0:T(8,128)(2,1)S(1)} %collective-permute-done.refs_2_.refs_0_), channel_id=1, source_target_pairs={{0,4},{4,8},{8,12},{12,14},{14,10},{10,6},{6,2},{2,0},{1,5},{5,9},... | collective-permute-start | bytes 884744 | tf_op jit(solution)/shard_map/ppermute | solution.py:377
  23.3 11.1 %collective-permute-start.12 = (bf16[32,4608]{1,0:T(8,128)(2,1)S(1)}, bf16[32,4608]{1,0:T(8,128)(2,1)S(1)}, u32[]{:S(2)}, u32[]{:S(2)}) collective-permute-start(bf16[32,4608]{1,0:T(8,128)(2,1)S(1)} %collective-permute-done.11.refs_4_), channel_id=1, source_target_pairs={{4,0},{8,4},{12,8},{14,12},{10,14},{6,10},{2,6},{0,2},{5,1},{9,5},... | collective-permute-start | bytes 884744 | tf_op jit(solution)/shard_map/ppermute | solution.py:377
  26.4 13.3 %collective-permute-start.6 = (bf16[32,4608]{1,0:T(8,128)(2,1)S(1)}, bf16[32,4608]{1,0:T(8,128)(2,1)S(1)}, u32[]{:S(2)}, u32[]{:S(2)}) collective-permute-start(bf16[32,4608]{1,0:T(8,128)(2,1)S(1)} %collective-permute-done.5.refs_3_), channel_id=1, source_target_pairs={{4,0},{8,4},{12,8},{14,12},{10,14},{6,10},{2,6},{0,2},{5,1},{9,5},... | collective-permute-start | bytes 884744 | tf_op jit(solution)/shard_map/ppermute | solution.py:377
  30.1 9.9 %collective-permute-start.2 = (bf16[32,4608]{1,0:T(8,128)(2,1)S(1)}, bf16[32,4608]{1,0:T(8,128)(2,1)S(1)}, u32[]{:S(2)}, u32[]{:S(2)}) collective-permute-start(bf16[32,4608]{1,0:T(8,128)(2,1)S(1)} %collective-permute-done.1.refs_0_), channel_id=1, source_target_pairs={{0,4},{4,8},{8,12},{12,14},{14,10},{10,6},{6,2},{2,0},{1,5},{5,9},... | collective-permute-start | bytes 884744 | tf_op jit(solution)/shard_map/ppermute | solution.py:377
  32.8 13.5 %collective-permute-start.10 = (bf16[32,4608]{1,0:T(8,128)(2,1)S(1)}, bf16[32,4608]{1,0:T(8,128)(2,1)S(1)}, u32[]{:S(2)}, u32[]{:S(2)}) collective-permute-start(bf16[32,4608]{1,0:T(8,128)(2,1)S(1)} %collective-permute-done.9.refs_6_.refs_1_), channel_id=1, source_target_pairs={{0,4},{4,8},{8,12},{12,14},{14,10},{10,6},{6,2},{2,0},{1,5},{5,9},... | collective-permute-start | bytes 884744 | tf_op jit(solution)/shard_map/ppermute | solution.py:377
  34.4 11.9 %collective-permute-start.13 = (bf16[32,4608]{1,0:T(8,128)(2,1)S(1)}, bf16[32,4608]{1,0:T(8,128)(2,1)S(1)}, u32[]{:S(2)}, u32[]{:S(2)}) collective-permute-start(bf16[32,4608]{1,0:T(8,128)(2,1)S(1)} %collective-permute-done.12.refs_7_.refs_2_), channel_id=1, source_target_pairs={{4,0},{8,4},{12,8},{14,12},{10,14},{6,10},{2,6},{0,2},{5,1},{9,5},... | collective-permute-start | bytes 884744 | tf_op jit(solution)/shard_map/ppermute | solution.py:377
  39.6 11.2 %collective-permute-start.7 = (bf16[32,4608]{1,0:T(8,128)(2,1)S(1)}, bf16[32,4608]{1,0:T(8,128)(2,1)S(1)}, u32[]{:S(2)}, u32[]{:S(2)}) collective-permute-start(bf16[32,4608]{1,0:T(8,128)(2,1)S(1)} %collective-permute-done.6.refs_3_), channel_id=1, source_target_pairs={{4,0},{8,4},{12,8},{14,12},{10,14},{6,10},{2,6},{0,2},{5,1},{9,5},... | collective-permute-start | bytes 884744 | tf_op jit(solution)/shard_map/ppermute | solution.py:377
  40.0 10.8 %collective-permute-start.3 = (bf16[32,4608]{1,0:T(8,128)(2,1)S(1)}, bf16[32,4608]{1,0:T(8,128)(2,1)S(1)}, u32[]{:S(2)}, u32[]{:S(2)}) collective-permute-start(bf16[32,4608]{1,0:T(8,128)(2,1)S(1)} %collective-permute-done.2.refs_0_), channel_id=1, source_target_pairs={{0,4},{4,8},{8,12},{12,14},{14,10},{10,6},{6,2},{2,0},{1,5},{5,9},... | collective-permute-start | bytes 884744 | tf_op jit(solution)/shard_map/ppermute | solution.py:377
  46.4 2.6 %copy-start = (bf16[384,512]{1,0:T(8,128)(2,1)S(1)}, bf16[384,512]{1,0:T(8,128)(2,1)}, u32[]{:S(2)}) copy-start(bf16[384,512]{1,0:T(8,128)(2,1)} %base_ref.1) | copy-start | bytes 1179652
  47.4 1.5 %collective-permute-start.14 = (f32[384,64]{1,0:T(8,128)S(1)}, f32[384,64]{1,0:T(8,128)S(1)}, u32[]{:S(2)}, u32[]{:S(2)}) collective-permute-start(f32[384,64]{1,0:T(8,128)S(1)} %get-tuple-element.87.mine_ref), channel_id=1, source_target_pairs={{0,1},{1,0},{2,3},{3,2},{4,5},{5,4},{6,7},{7,6},{8,9},{9,8},{10,11... | collective-permute-start | bytes 294920 | tf_op jit(solution)/shard_map/ppermute | solution.py:407
  51.2 1.3 %collective-permute-start.15 = (f32[96,64]{1,0:T(8,128)S(1)}, f32[96,64]{1,0:T(8,128)S(1)}, u32[]{:S(2)}, u32[]{:S(2)}) collective-permute-start(f32[96,64]{1,0:T(8,128)S(1)} %get-tuple-element.91.mine_ref), channel_id=1, source_target_pairs={{0,1},{1,0},{2,3},{3,2},{4,5},{5,4},{6,7},{7,6},{8,9},{9,8},{10,11... | collective-permute-start | bytes 73736 | tf_op jit(solution)/shard_map/ppermute | solution.py:409

commit v10 on v9

--- a/solution.py
+++ b/solution.py
@@ -110,21 +110,21 @@
             p_ref[head * TILE : (head + 1) * TILE, :] = (weights * inverse).astype(jnp.bfloat16)
 
 
-def probs_of(segment, across, queries, keys, kv_head, after):
+def probs_of(segment, across, queries, keys, kv_head):
     rows = keys.shape[0]
     shapes = [(GROUP * TILE, width) for _, _, width in windows(rows)]
     elements = sum(a * b for a, b in shapes)
     return pl.pallas_call(
         functools.partial(probs_kernel, kv_head),
         out_shape=[jax.ShapeDtypeStruct(s, jnp.bfloat16) for s in shapes],
-        in_specs=[VMEM] * 4 + [pl.BlockSpec(memory_space=pl.ANY)] * len(after),
+        in_specs=[VMEM] * 4,
         out_specs=[VMEM] * len(shapes),
         cost_estimate=pl.CostEstimate(
             flops=2_000_000_000, bytes_accessed=2 * elements, transcendentals=elements
         ),
         compiler_params=pltpu.CompilerParams(vmem_limit_bytes=12 * 2**20),
         name="probs",
-    )(segment, across, queries, keys, *after)
+    )(segment, across, queries, keys)
 
 
 def lowrank_kernel(at, count, place_ref, x_ref, *refs):
@@ -184,7 +184,7 @@
         out_shape=jax.ShapeDtypeStruct((room, x.shape[1]), x.dtype),
         in_specs=[VMEM, VMEM],
         out_specs=VMEM,
-        cost_estimate=pl.CostEstimate(flops=1_500_000_000, bytes_accessed=2 * x.size, transcendentals=0),
+        cost_estimate=pl.CostEstimate(flops=100_000_000, bytes_accessed=2 * x.shape[0], transcendentals=0),
         compiler_params=pltpu.CompilerParams(vmem_limit_bytes=8 * 2**20),
         name="last_rows",
     )(slot_across, x)
@@ -209,7 +209,7 @@
         in_specs=[VMEM] * (1 + len(pieces)),
         out_specs=[VMEM] * len(left),
         cost_estimate=pl.CostEstimate(
-            flops=1_500_000_000, bytes_accessed=2 * sum(p.size for p in pieces), transcendentals=0
+            flops=100_000_000, bytes_accessed=2 * slot.size, transcendentals=0
         ),
         compiler_params=pltpu.CompilerParams(vmem_limit_bytes=6 * 2**20),
         name="last_probs",
@@ -389,8 +389,7 @@
         for pair in ([low[step], high[-step]], [high[step], low[-step]])
     ]
     probs = [
-        probs_of(segment, across, queries, stacked_key_rows, kv, [low[1], high[-1]] if kv > 0 else [])
-        for kv in range(kv_heads)
+        probs_of(segment, across, queries, stacked_key_rows, kv) for kv in range(kv_heads)
     ]
 
     picked = [last_probs(slot, probs[kv], probs[kv + 1]) for kv in range(0, kv_heads, 2)]

time: 55.2 us -> 54.9 us (level)
  waiting for transfers between devices: 12.6 us -> 14.2 us
  starting transfers between devices: 17.1 us -> 15.6 us
    ppermute x14, waiting for transfers between devices: 10 us -> 11.5 us  [pass_round(): piece = lax.ppermute(piece, 'rep', pairs)]
    ppermute x14, starting transfers between devices: 16.8 us -> 15.5 us  [pass_round(): piece = lax.ppermute(piece, 'rep', pairs)]
  transfers between devices with their start and end apart: 16 -> 16, of which waited for: 8 -> 7; matrix products, arithmetic and copies ran while one was open for 0% -> 0% of each run, Pallas kernels for 28% -> 28%
where the time goes in v10:
time: 54.9 us; the launch traced here: 54.6 us
  Pallas kernels  18.1 us (33%)
  starting transfers between devices  15.6 us (28%)
  waiting for transfers between devices  14.2 us (26%)
  local copies, waits for them, and re-layouts  5.27 us (10%)
  other arithmetic  1.16 us (2%)
    ppermute x14, starting transfers between devices, pass_round(): piece = lax.ppermute(piece, 'rep', pairs)  15.5 us
    ppermute x14, waiting for transfers between devices, pass_round(): piece = lax.ppermute(piece, 'rep', pairs)  11.5 us
    pallas_call x4, Pallas kernels, probs_of(): pl.pallas_call(functools.partial(probs_kernel, kv_head), out_shape=[jax.S...  7.06 us
    unnamed x16, local copies, waits for them, and re-layouts  5.27 us
    pallas_call x3, Pallas kernels, lowrank_of(): pl.pallas_call(functools.partial(lowrank_kernel, at, len(pieces)), out_sh...  3.15 us
    pallas_call x1, Pallas kernels, finish(): pl.pallas_call(finish_kernel, out_shape=jax.ShapeDtypeStruct(early.shape,...  2.22 us
    pallas_call x1, Pallas kernels, early_product(): pl.pallas_call(functools.partial(early_kernel, kv_heads), out_shape=jax.S...  1.9 us
    pallas_call x2, Pallas kernels, last_probs(): pl.pallas_call(last_probs_kernel, out_shape=[jax.ShapeDtypeStruct((p.shap...  1.82 us
  transfers between devices with their start and end apart: 16, of which 7 were waited for; matrix products, arithmetic and copies ran while one was open for 0% of the time, Pallas kernels for 28%

profile of v10, /device:TPU:0, one launch (start us, length us, event | category | flops | bytes accessed | tf_op | source)
XLA Modules:
  0.0 54.6 jit_solution(835149543578457868)
XLA Ops:
  0.0 1.2 %pad_maximum_fusion = (bf16[32,4608]{1,0:T(8,128)(2,1)S(1)}, bf16[32,4608]{1,0:T(8,128)(2,1)S(1)}) fusion(bf16[64,512]{1,0:T(8,128)(2,1)} %bitcast.8, bf16[64,4096]{1,0:T(8,128)(2,1)} %bitcast.7), kind=kLoop, calls=%fused_computation.3 | loop fusion | flops 1179648 | bytes 1179648 | tf_op jit(solution)/shard_map/concatenate | solution.py:366
  1.2 3.0 %collective-permute-start.4 = (bf16[32,4608]{1,0:T(8,128)(2,1)S(1)}, bf16[32,4608]{1,0:T(8,128)(2,1)S(1)}, u32[]{:S(2)}, u32[]{:S(2)}) collective-permute-start(bf16[32,4608]{1,0:T(8,128)(2,1)S(1)} %get-tuple-element.103.refs_1_), channel_id=1, source_target_pairs={{4,0},{8,4},{12,8},{14,12},{10,14},{6,10},{2,6},{0,2},{5,1},{9,5},... | collective-permute-start | bytes 884744 | tf_op jit(solution)/shard_map/ppermute | solution.py:377
  4.3 2.0 %collective-permute-start.8 = (bf16[32,4608]{1,0:T(8,128)(2,1)S(1)}, bf16[32,4608]{1,0:T(8,128)(2,1)S(1)}, u32[]{:S(2)}, u32[]{:S(2)}) collective-permute-start(bf16[32,4608]{1,0:T(8,128)(2,1)S(1)} %get-tuple-element.103.refs_1_), channel_id=1, source_target_pairs={{0,4},{4,8},{8,12},{12,14},{14,10},{10,6},{6,2},{2,0},{1,5},{5,9},... | collective-permute-start | bytes 884744 | tf_op jit(solution)/shard_map/ppermute | solution.py:377
  6.3 1.9 %copy-done.2 = bf16[384,4096]{1,0:T(8,128)(2,1)S(1)} copy-done((bf16[384,4096]{1,0:T(8,128)(2,1)S(1)}, bf16[384,4096]{1,0:T(8,128)(2,1)}, u32[]{:S(2)}) %copy-start.2) | copy-done | bytes 3145752
  12.4 1.8 %probs.7 = (bf16[512,128]{1,0:T(8,128)(2,1)S(1)}, bf16[512,128]{1,0:T(8,128)(2,1)S(1)}, bf16[512,256]{1,0:T(8,128)(2,1)S(1)}, bf16[512,256]{1,0:T(8,128)(2,1)S(1...) custom-call(s32[384,1]{1,0:T(8,128)S(1)} %get-tuple-element.58.segment_ref, ...), custom_call_target="tpu_custom_call" | custom-call | flops 2000000000 | bytes 1310720 | tf_op jit(solution)/shard_map/probs/pallas_call | solution.py:117
  14.2 2.0 %collective-permute-start.5 = (bf16[32,4608]{1,0:T(8,128)(2,1)S(1)}, bf16[32,4608]{1,0:T(8,128)(2,1)S(1)}, u32[]{:S(2)}, u32[]{:S(2)}) collective-permute-start(bf16[32,4608]{1,0:T(8,128)(2,1)S(1)} %collective-permute-done.4.refs_5_), channel_id=1, source_target_pairs={{4,0},{8,4},{12,8},{14,12},{10,14},{6,10},{2,6},{0,2},{5,1},{9,5},... | collective-permute-start | bytes 884744 | tf_op jit(solution)/shard_map/ppermute | solution.py:377
  16.3 1.8 %probs.5 = (bf16[512,128]{1,0:T(8,128)(2,1)S(1)}, bf16[512,128]{1,0:T(8,128)(2,1)S(1)}, bf16[512,256]{1,0:T(8,128)(2,1)S(1)}, bf16[512,256]{1,0:T(8,128)(2,1)S(1...) custom-call(s32[384,1]{1,0:T(8,128)S(1)} %get-tuple-element.58.segment_ref, ...), custom_call_target="tpu_custom_call" | custom-call | flops 2000000000 | bytes 1310720 | tf_op jit(solution)/shard_map/probs/pallas_call | solution.py:117
  18.1 2.3 %collective-permute-done.8.refs_3_ = bf16[32,4608]{1,0:T(8,128)(2,1)S(1)} collective-permute-done((bf16[32,4608]{1,0:T(8,128)(2,1)S(1)}, bf16[32,4608]{1,0:T(8,128)(2,1)S(1)}, u32[]{:S(2)}, u32[]{:S(2)}) %collective-permute-start.8) | collective-permute-done | bytes 294944 | tf_op jit(solution)/shard_map/ppermute | solution.py:377
  20.5 1.9 %collective-permute-start.12 = (bf16[32,4608]{1,0:T(8,128)(2,1)S(1)}, bf16[32,4608]{1,0:T(8,128)(2,1)S(1)}, u32[]{:S(2)}, u32[]{:S(2)}) collective-permute-start(bf16[32,4608]{1,0:T(8,128)(2,1)S(1)} %collective-permute-done.11.refs_4_), channel_id=1, source_target_pairs={{4,0},{8,4},{12,8},{14,12},{10,14},{6,10},{2,6},{0,2},{5,1},{9,5},... | collective-permute-start | bytes 884744 | tf_op jit(solution)/shard_map/ppermute | solution.py:377
  22.5 1.8 %probs.4 = (bf16[512,128]{1,0:T(8,128)(2,1)S(1)}, bf16[512,128]{1,0:T(8,128)(2,1)S(1)}, bf16[512,256]{1,0:T(8,128)(2,1)S(1)}, bf16[512,256]{1,0:T(8,128)(2,1)S(1...) custom-call(s32[384,1]{1,0:T(8,128)S(1)} %get-tuple-element.58.segment_ref, ...), custom_call_target="tpu_custom_call" | custom-call | flops 2000000000 | bytes 1310720 | tf_op jit(solution)/shard_map/probs/pallas_call | solution.py:117
  25.9 1.6 %collective-permute-start.6 = (bf16[32,4608]{1,0:T(8,128)(2,1)S(1)}, bf16[32,4608]{1,0:T(8,128)(2,1)S(1)}, u32[]{:S(2)}, u32[]{:S(2)}) collective-permute-start(bf16[32,4608]{1,0:T(8,128)(2,1)S(1)} %collective-permute-done.5.refs_3_), channel_id=1, source_target_pairs={{4,0},{8,4},{12,8},{14,12},{10,14},{6,10},{2,6},{0,2},{5,1},{9,5},... | collective-permute-start | bytes 884744 | tf_op jit(solution)/shard_map/ppermute | solution.py:377
  28.0 1.8 %probs.6 = (bf16[512,128]{1,0:T(8,128)(2,1)S(1)}, bf16[512,128]{1,0:T(8,128)(2,1)S(1)}, bf16[512,256]{1,0:T(8,128)(2,1)S(1)}, bf16[512,256]{1,0:T(8,128)(2,1)S(1...) custom-call(s32[384,1]{1,0:T(8,128)S(1)} %get-tuple-element.58.segment_ref, ...), custom_call_target="tpu_custom_call" | custom-call | flops 2000000000 | bytes 1310720 | tf_op jit(solution)/shard_map/probs/pallas_call | solution.py:117
  30.7 2.4 %collective-permute-done.9.refs_6_.refs_1_ = bf16[32,4608]{1,0:T(8,128)(2,1)S(1)} collective-permute-done((bf16[32,4608]{1,0:T(8,128)(2,1)S(1)}, bf16[32,4608]{1,0:T(8,128)(2,1)S(1)}, u32[]{:S(2)}, u32[]{:S(2)}) %collective-permute-start.9) | collective-permute-done | bytes 294944 | tf_op jit(solution)/shard_map/ppermute | solution.py:377
  33.2 1.9 %collective-permute-start.13 = (bf16[32,4608]{1,0:T(8,128)(2,1)S(1)}, bf16[32,4608]{1,0:T(8,128)(2,1)S(1)}, u32[]{:S(2)}, u32[]{:S(2)}) collective-permute-start(bf16[32,4608]{1,0:T(8,128)(2,1)S(1)} %collective-permute-done.12.refs_7_.refs_2_), channel_id=1, source_target_pairs={{4,0},{8,4},{12,8},{14,12},{10,14},{6,10},{2,6},{0,2},{5,1},{9,5},... | collective-permute-start | bytes 884744 | tf_op jit(solution)/shard_map/ppermute | solution.py:377
  35.1 1.1 %lowrank.3 = (f32[384,64]{1,0:T(8,128)S(1)}, bf16[192,512]{1,0:T(8,128)(2,1)S(1)}) custom-call(s32[384,1]{1,0:T(8,128)S(1)} %get-tuple-element.55.place_ref, bf16[384,4096]{1,0:T(8,128)(2,1)S(1)} %copy-done, bf16[32,4608]{1,0:T(8,128)(2,1)S(1)} %get-tuple-element.104.refs_0_, bf16[32,4608]{1,0:T(8,128)(2,1)S(1)} %get-tuple-element.103.refs_1_, ...), custom_call_target="tpu_custom_call" | custom-call | flops 1700000000 | bytes 4915200 | tf_op jit(solution)/shard_map/lowrank/pallas_call | solution.py:155
  36.2 1.2 %collective-permute-done.6.refs_3_ = bf16[32,4608]{1,0:T(8,128)(2,1)S(1)} collective-permute-done((bf16[32,4608]{1,0:T(8,128)(2,1)S(1)}, bf16[32,4608]{1,0:T(8,128)(2,1)S(1)}, u32[]{:S(2)}, u32[]{:S(2)}) %collective-permute-start.6) | collective-permute-done | bytes 294944 | tf_op jit(solution)/shard_map/ppermute | solution.py:377
  37.4 2.0 %collective-permute-start.7 = (bf16[32,4608]{1,0:T(8,128)(2,1)S(1)}, bf16[32,4608]{1,0:T(8,128)(2,1)S(1)}, u32[]{:S(2)}, u32[]{:S(2)}) collective-permute-start(bf16[32,4608]{1,0:T(8,128)(2,1)S(1)} %collective-permute-done.6.refs_3_), channel_id=1, source_target_pairs={{4,0},{8,4},{12,8},{14,12},{10,14},{6,10},{2,6},{0,2},{5,1},{9,5},... | collective-permute-start | bytes 884744 | tf_op jit(solution)/shard_map/ppermute | solution.py:377
  39.5 1.0 %lowrank.4 = (f32[384,64]{1,0:T(8,128)S(1)}, bf16[128,512]{1,0:T(8,128)(2,1)S(1)}) custom-call(s32[384,1]{1,0:T(8,128)S(1)} %get-tuple-element.55.place_ref, bf16[384,4096]{1,0:T(8,128)(2,1)S(1)} %copy-done, bf16[32,4608]{1,0:T(8,128)(2,1)S(1)} %collective-permute-done.1.refs_0_, bf16[32,4608]{1,0:T(8,128)(2,1)S(1)} %collective-permute-done.9.refs_6_.refs_1_, ...), custom_call_target="tpu_custom_call" | custom-call | flops 1700000000 | bytes 4325376 | tf_op jit(solution)/shard_map/lowrank/pallas_call | solution.py:155
  40.5 5.2 %collective-permute-done.10.refs_1_ = bf16[32,4608]{1,0:T(8,128)(2,1)S(1)} collective-permute-done((bf16[32,4608]{1,0:T(8,128)(2,1)S(1)}, bf16[32,4608]{1,0:T(8,128)(2,1)S(1)}, u32[]{:S(2)}, u32[]{:S(2)}) %collective-permute-start.10) | collective-permute-done | bytes 294944 | tf_op jit(solution)/shard_map/ppermute | solution.py:377
  45.7 1.0 %lowrank.5 = (f32[384,64]{1,0:T(8,128)S(1)}, bf16[128,512]{1,0:T(8,128)(2,1)S(1)}) custom-call(s32[384,1]{1,0:T(8,128)S(1)} %get-tuple-element.55.place_ref, bf16[384,4096]{1,0:T(8,128)(2,1)S(1)} %copy-done, bf16[32,4608]{1,0:T(8,128)(2,1)S(1)} %collective-permute-done.2.refs_0_, bf16[32,4608]{1,0:T(8,128)(2,1)S(1)} %collective-permute-done.10.refs_1_, ...), custom_call_target="tpu_custom_call" | custom-call | flops 1700000000 | bytes 4325376 | tf_op jit(solution)/shard_map/lowrank/pallas_call | solution.py:155
  46.9 1.4 %collective-permute-done.14.theirs_ref = f32[384,64]{1,0:T(8,128)S(1)} collective-permute-done((f32[384,64]{1,0:T(8,128)S(1)}, f32[384,64]{1,0:T(8,128)S(1)}, u32[]{:S(2)}, u32[]{:S(2)}) %collective-permute-start.14) | collective-permute-done | bytes 98336 | tf_op jit(solution)/shard_map/ppermute | solution.py:406
  48.3 1.9 %early_product.1.refs_0_.early_ref = f32[384,4096]{1,0:T(8,128)S(1)} custom-call(s32[384,1]{1,0:T(8,128)S(1)} %get-tuple-element.55.place_ref, f32[384,64]{1,0:T(8,128)S(1)} %get-tuple-element.87.mine_ref, f32[384,64]{1,0:T(8,128)S(1)} %collective-permute-done.14.theirs_ref, bf16[384,512]{1,0:T(8,128)(2,1)S(1)} %copy-done.1, ...), custom_call_target="tpu_custom_call" | custom-call | flops 50000000 | bytes 1536 | tf_op jit(solution)/shard_map/early_product/pallas_call | solution.py:262
  51.0 1.2 %collective-permute-done.15.theirs_ref = f32[96,64]{1,0:T(8,128)S(1)} collective-permute-done((f32[96,64]{1,0:T(8,128)S(1)}, f32[96,64]{1,0:T(8,128)S(1)}, u32[]{:S(2)}, u32[]{:S(2)}) %collective-permute-start.15) | collective-permute-done | bytes 24608 | tf_op jit(solution)/shard_map/ppermute | solution.py:408
  52.2 2.2 %finish.1 = bf16[384,4096]{1,0:T(8,128)(2,1)} custom-call(f32[96,64]{1,0:T(8,128)S(1)} %get-tuple-element.91.mine_ref, f32[96,64]{1,0:T(8,128)S(1)} %collective-permute-done.15.theirs_ref, bf16[64,512]{1,0:T(8,128)(2,1)S(1)} %get-tuple-element.92.up_ref, f32[384,4096]{1,0:T(8,128)S(1)} %early_product.1.refs_0_.early_ref, ...), custom_call_target="tpu_custom_call" | custom-call | tf_op jit(solution)/shard_map/finish/pallas_call | solution.py:338
  (39 shorter events, 8.7 us)
Async XLA Ops:
  0.0 11.4 %copy-start.5 = (bf16[384,512]{1,0:T(8,128)(2,1)S(1)}, bf16[384,512]{1,0:T(8,128)(2,1)}, u32[]{:S(2)}) copy-start(bf16[384,512]{1,0:T(8,128)(2,1)} %k_ref.7) | copy-start | bytes 1179652
  1.2 13.1 %collective-permute-start.4 = (bf16[32,4608]{1,0:T(8,128)(2,1)S(1)}, bf16[32,4608]{1,0:T(8,128)(2,1)S(1)}, u32[]{:S(2)}, u32[]{:S(2)}) collective-permute-start(bf16[32,4608]{1,0:T(8,128)(2,1)S(1)} %get-tuple-element.103.refs_1_), channel_id=1, source_target_pairs={{4,0},{8,4},{12,8},{14,12},{10,14},{6,10},{2,6},{0,2},{5,1},{9,5},... | collective-permute-start | bytes 884744 | tf_op jit(solution)/shard_map/ppermute | solution.py:377
  4.2 12.0 %collective-permute-start = (bf16[32,4608]{1,0:T(8,128)(2,1)S(1)}, bf16[32,4608]{1,0:T(8,128)(2,1)S(1)}, u32[]{:S(2)}, u32[]{:S(2)}) collective-permute-start(bf16[32,4608]{1,0:T(8,128)(2,1)S(1)} %get-tuple-element.104.refs_0_), channel_id=1, source_target_pairs={{0,4},{4,8},{8,12},{12,14},{14,10},{10,6},{6,2},{2,0},{1,5},{5,9},... | collective-permute-start | bytes 884744 | tf_op jit(solution)/shard_map/ppermute | solution.py:377
  4.3 16.1 %collective-permute-start.8 = (bf16[32,4608]{1,0:T(8,128)(2,1)S(1)}, bf16[32,4608]{1,0:T(8,128)(2,1)S(1)}, u32[]{:S(2)}, u32[]{:S(2)}) collective-permute-start(bf16[32,4608]{1,0:T(8,128)(2,1)S(1)} %get-tuple-element.103.refs_1_), channel_id=1, source_target_pairs={{0,4},{4,8},{8,12},{12,14},{14,10},{10,6},{6,2},{2,0},{1,5},{5,9},... | collective-permute-start | bytes 884744 | tf_op jit(solution)/shard_map/ppermute | solution.py:377
  6.3 14.3 %collective-permute-start.11 = (bf16[32,4608]{1,0:T(8,128)(2,1)S(1)}, bf16[32,4608]{1,0:T(8,128)(2,1)S(1)}, u32[]{:S(2)}, u32[]{:S(2)}) collective-permute-start(bf16[32,4608]{1,0:T(8,128)(2,1)S(1)} %get-tuple-element.104.refs_0_), channel_id=1, source_target_pairs={{4,0},{8,4},{12,8},{14,12},{10,14},{6,10},{2,6},{0,2},{5,1},{9,5},... | collective-permute-start | bytes 884744 | tf_op jit(solution)/shard_map/ppermute | solution.py:377
  6.3 1.9 %copy-start.2 = (bf16[384,4096]{1,0:T(8,128)(2,1)S(1)}, bf16[384,4096]{1,0:T(8,128)(2,1)}, u32[]{:S(2)}) copy-start(bf16[384,4096]{1,0:T(8,128)(2,1)} %q_ref.7) | copy-start | bytes 9437188
  8.2 1.0 %copy-start.4 = (bf16[384,512]{1,0:T(8,128)(2,1)S(1)}, bf16[384,512]{1,0:T(8,128)(2,1)}, u32[]{:S(2)}) copy-start(bf16[384,512]{1,0:T(8,128)(2,1)} %k_ref.7) | copy-start | bytes 1179652
  9.2 0.7 %copy-start.6 = (s32[384,1]{0,1:T(1,128)S(1)}, s32[384,1]{0,1:T(1,128)}, u32[]{:S(2)}) copy-start(s32[384,1]{0,1:T(1,128)} %param.12) | copy-start | bytes 4612
  9.9 0.7 %copy-start.7 = (s32[1,4]{1,0:T(1,128)S(1)}, s32[1,4]{1,0:T(1,128)}, u32[]{:S(2)}) copy-start(s32[1,4]{1,0:T(1,128)} %lengths_ref.1) | copy-start | bytes 52
  10.6 1.9 %copy-start.3 = (bf16[384,4096]{1,0:T(8,128)(2,1)S(1)}, bf16[384,4096]{1,0:T(8,128)(2,1)}, u32[]{:S(2)}) copy-start(bf16[384,4096]{1,0:T(8,128)(2,1)} %q_ref.7) | copy-start | bytes 9437188
  14.2 11.7 %collective-permute-start.5 = (bf16[32,4608]{1,0:T(8,128)(2,1)S(1)}, bf16[32,4608]{1,0:T(8,128)(2,1)S(1)}, u32[]{:S(2)}, u32[]{:S(2)}) collective-permute-start(bf16[32,4608]{1,0:T(8,128)(2,1)S(1)} %collective-permute-done.4.refs_5_), channel_id=1, source_target_pairs={{4,0},{8,4},{12,8},{14,12},{10,14},{6,10},{2,6},{0,2},{5,1},{9,5},... | collective-permute-start | bytes 884744 | tf_op jit(solution)/shard_map/ppermute | solution.py:377
  16.2 11.4 %collective-permute-start.1 = (bf16[32,4608]{1,0:T(8,128)(2,1)S(1)}, bf16[32,4608]{1,0:T(8,128)(2,1)S(1)}, u32[]{:S(2)}, u32[]{:S(2)}) collective-permute-start(bf16[32,4608]{1,0:T(8,128)(2,1)S(1)} %collective-permute-done.refs_2_), channel_id=1, source_target_pairs={{0,4},{4,8},{8,12},{12,14},{14,10},{10,6},{6,2},{2,0},{1,5},{5,9},... | collective-permute-start | bytes 884744 | tf_op jit(solution)/shard_map/ppermute | solution.py:377
  18.1 6.2 %copy-start = (bf16[384,4096]{1,0:T(8,128)(2,1)S(1)}, bf16[384,4096]{1,0:T(8,128)(2,1)}, u32[]{:S(2)}) copy-start(bf16[384,4096]{1,0:T(8,128)(2,1)} %x_ref.7) | copy-start | bytes 9437188
  20.4 12.6 %collective-permute-start.9 = (bf16[32,4608]{1,0:T(8,128)(2,1)S(1)}, bf16[32,4608]{1,0:T(8,128)(2,1)S(1)}, u32[]{:S(2)}, u32[]{:S(2)}) collective-permute-start(bf16[32,4608]{1,0:T(8,128)(2,1)S(1)} %collective-permute-done.8.refs_3_), channel_id=1, source_target_pairs={{0,4},{4,8},{8,12},{12,14},{14,10},{10,6},{6,2},{2,0},{1,5},{5,9},... | collective-permute-start | bytes 884744 | tf_op jit(solution)/shard_map/ppermute | solution.py:377
  20.5 12.6 %collective-permute-start.12 = (bf16[32,4608]{1,0:T(8,128)(2,1)S(1)}, bf16[32,4608]{1,0:T(8,128)(2,1)S(1)}, u32[]{:S(2)}, u32[]{:S(2)}) collective-permute-start(bf16[32,4608]{1,0:T(8,128)(2,1)S(1)} %collective-permute-done.11.refs_4_), channel_id=1, source_target_pairs={{4,0},{8,4},{12,8},{14,12},{10,14},{6,10},{2,6},{0,2},{5,1},{9,5},... | collective-permute-start | bytes 884744 | tf_op jit(solution)/shard_map/ppermute | solution.py:377
  25.9 11.5 %collective-permute-start.6 = (bf16[32,4608]{1,0:T(8,128)(2,1)S(1)}, bf16[32,4608]{1,0:T(8,128)(2,1)S(1)}, u32[]{:S(2)}, u32[]{:S(2)}) collective-permute-start(bf16[32,4608]{1,0:T(8,128)(2,1)S(1)} %collective-permute-done.5.refs_3_), channel_id=1, source_target_pairs={{4,0},{8,4},{12,8},{14,12},{10,14},{6,10},{2,6},{0,2},{5,1},{9,5},... | collective-permute-start | bytes 884744 | tf_op jit(solution)/shard_map/ppermute | solution.py:377
  27.5 11.9 %collective-permute-start.2 = (bf16[32,4608]{1,0:T(8,128)(2,1)S(1)}, bf16[32,4608]{1,0:T(8,128)(2,1)S(1)}, u32[]{:S(2)}, u32[]{:S(2)}) collective-permute-start(bf16[32,4608]{1,0:T(8,128)(2,1)S(1)} %collective-permute-done.1.refs_0_), channel_id=1, source_target_pairs={{0,4},{4,8},{8,12},{12,14},{14,10},{10,6},{6,2},{2,0},{1,5},{5,9},... | collective-permute-start | bytes 884744 | tf_op jit(solution)/shard_map/ppermute | solution.py:377
  33.1 12.6 %collective-permute-start.10 = (bf16[32,4608]{1,0:T(8,128)(2,1)S(1)}, bf16[32,4608]{1,0:T(8,128)(2,1)S(1)}, u32[]{:S(2)}, u32[]{:S(2)}) collective-permute-start(bf16[32,4608]{1,0:T(8,128)(2,1)S(1)} %collective-permute-done.9.refs_6_.refs_1_), channel_id=1, source_target_pairs={{0,4},{4,8},{8,12},{12,14},{14,10},{10,6},{6,2},{2,0},{1,5},{5,9},... | collective-permute-start | bytes 884744 | tf_op jit(solution)/shard_map/ppermute | solution.py:377
  33.2 12.6 %collective-permute-start.13 = (bf16[32,4608]{1,0:T(8,128)(2,1)S(1)}, bf16[32,4608]{1,0:T(8,128)(2,1)S(1)}, u32[]{:S(2)}, u32[]{:S(2)}) collective-permute-start(bf16[32,4608]{1,0:T(8,128)(2,1)S(1)} %collective-permute-done.12.refs_7_.refs_2_), channel_id=1, source_target_pairs={{4,0},{8,4},{12,8},{14,12},{10,14},{6,10},{2,6},{0,2},{5,1},{9,5},... | collective-permute-start | bytes 884744 | tf_op jit(solution)/shard_map/ppermute | solution.py:377
  37.4 12.8 %collective-permute-start.7 = (bf16[32,4608]{1,0:T(8,128)(2,1)S(1)}, bf16[32,4608]{1,0:T(8,128)(2,1)S(1)}, u32[]{:S(2)}, u32[]{:S(2)}) collective-permute-start(bf16[32,4608]{1,0:T(8,128)(2,1)S(1)} %collective-permute-done.6.refs_3_), channel_id=1, source_target_pairs={{4,0},{8,4},{12,8},{14,12},{10,14},{6,10},{2,6},{0,2},{5,1},{9,5},... | collective-permute-start | bytes 884744 | tf_op jit(solution)/shard_map/ppermute | solution.py:377
  39.4 11.2 %collective-permute-start.3 = (bf16[32,4608]{1,0:T(8,128)(2,1)S(1)}, bf16[32,4608]{1,0:T(8,128)(2,1)S(1)}, u32[]{:S(2)}, u32[]{:S(2)}) collective-permute-start(bf16[32,4608]{1,0:T(8,128)(2,1)S(1)} %collective-permute-done.2.refs_0_), channel_id=1, source_target_pairs={{0,4},{4,8},{8,12},{12,14},{14,10},{10,6},{6,2},{2,0},{1,5},{5,9},... | collective-permute-start | bytes 884744 | tf_op jit(solution)/shard_map/ppermute | solution.py:377
  45.7 2.6 %copy-start.1 = (bf16[384,512]{1,0:T(8,128)(2,1)S(1)}, bf16[384,512]{1,0:T(8,128)(2,1)}, u32[]{:S(2)}) copy-start(bf16[384,512]{1,0:T(8,128)(2,1)} %base_ref.1) | copy-start | bytes 1179652
  46.8 1.5 %collective-permute-start.14 = (f32[384,64]{1,0:T(8,128)S(1)}, f32[384,64]{1,0:T(8,128)S(1)}, u32[]{:S(2)}, u32[]{:S(2)}) collective-permute-start(f32[384,64]{1,0:T(8,128)S(1)} %get-tuple-element.87.mine_ref), channel_id=1, source_target_pairs={{0,1},{1,0},{2,3},{3,2},{4,5},{5,4},{6,7},{7,6},{8,9},{9,8},{10,11... | collective-permute-start | bytes 294920 | tf_op jit(solution)/shard_map/ppermute | solution.py:406
  50.9 1.3 %collective-permute-start.15 = (f32[96,64]{1,0:T(8,128)S(1)}, f32[96,64]{1,0:T(8,128)S(1)}, u32[]{:S(2)}, u32[]{:S(2)}) collective-permute-start(f32[96,64]{1,0:T(8,128)S(1)} %get-tuple-element.91.mine_ref), channel_id=1, source_target_pairs={{0,1},{1,0},{2,3},{3,2},{4,5},{5,4},{6,7},{7,6},{8,9},{9,8},{10,11... | collective-permute-start | bytes 73736 | tf_op jit(solution)/shard_map/ppermute | solution.py:408

commit v11 on v10

--- a/solution.py
+++ b/solution.py
@@ -314,21 +314,24 @@
             [jnp.concatenate([left, none], axis=1), jnp.concatenate([none, right], axis=1)], axis=0
         )
         for i, (start, _, _) in enumerate(tiles):
-            added = jnp.dot(p_refs[pair * len(tiles) + i][...], both, preferred_element_type=jnp.float32)
-            for side in range(2):
-                for head in range(GROUP):
-                    at = (2 * pair + side) * wide + head * HEAD_SIZE
-                    part = added[head * TILE : (head + 1) * TILE, side * HEAD_SIZE : (side + 1) * HEAD_SIZE]
-                    whole = early_ref[start : start + TILE, at : at + HEAD_SIZE] + part
-                    block[start : start + TILE, at : at + HEAD_SIZE] = whole.astype(jnp.bfloat16)
-            if i % 2 == 1:
-                rows_done = slice(start - TILE, start + TILE)
-                span = slice(2 * pair * wide, 2 * (pair + 1) * wide)
-                copy = pltpu.make_async_copy(
-                    block.at[rows_done, span], out_ref.at[rows_done, span], sems.at[len(copies)]
-                )
-                copy.start()
-                copies.append(copy)
+            p_ref = p_refs[pair * len(tiles) + i]
+            for half in range(2):
+                heads = range(half * GROUP // 2, (half + 1) * GROUP // 2)
+                near = slice(heads[0] * TILE, (heads[-1] + 1) * TILE)
+                added = jnp.dot(p_ref[near, :], both, preferred_element_type=jnp.float32)
+                for side in range(2):
+                    for k, head in enumerate(heads):
+                        at = (2 * pair + side) * wide + head * HEAD_SIZE
+                        part = added[k * TILE : (k + 1) * TILE, side * HEAD_SIZE : (side + 1) * HEAD_SIZE]
+                        whole = early_ref[start : start + TILE, at : at + HEAD_SIZE] + part
+                        block[start : start + TILE, at : at + HEAD_SIZE] = whole.astype(jnp.bfloat16)
+            rows_done = slice(start, start + TILE)
+            span = slice(2 * pair * wide, 2 * (pair + 1) * wide)
+            copy = pltpu.make_async_copy(
+                block.at[rows_done, span], out_ref.at[rows_done, span], sems.at[len(copies)]
+            )
+            copy.start()
+            copies.append(copy)
     for copy in copies:
         copy.wait()
 
@@ -340,7 +343,7 @@
         out_shape=jax.ShapeDtypeStruct(early.shape, jnp.bfloat16),
         in_specs=[VMEM] * (4 + len(flat)),
         out_specs=pl.BlockSpec(memory_space=pl.ANY),
-        scratch_shapes=[pltpu.VMEM(early.shape, jnp.bfloat16), pltpu.SemaphoreType.DMA((len(flat) // 2,))],
+        scratch_shapes=[pltpu.VMEM(early.shape, jnp.bfloat16), pltpu.SemaphoreType.DMA((len(flat),))],
         compiler_params=pltpu.CompilerParams(vmem_limit_bytes=10 * 2**20),
         name="finish",
     )(mine, theirs, up, early, *flat)

time: 54.9 us -> 54.8 us (level)
  no operation moved by 1% of the time
where the time goes in v11:
time: 54.8 us; the launch traced here: 54.5 us
  Pallas kernels  18 us (33%)
  starting transfers between devices  15.6 us (28%)
  waiting for transfers between devices  14.2 us (26%)
  local copies, waits for them, and re-layouts  5.27 us (10%)
  other arithmetic  1.16 us (2%)
    ppermute x14, starting transfers between devices, pass_round(): piece = lax.ppermute(piece, 'rep', pairs)  15.5 us
    ppermute x14, waiting for transfers between devices, pass_round(): piece = lax.ppermute(piece, 'rep', pairs)  11.5 us
    pallas_call x4, Pallas kernels, probs_of(): pl.pallas_call(functools.partial(probs_kernel, kv_head), out_shape=[jax.S...  7.06 us
    unnamed x16, local copies, waits for them, and re-layouts  5.27 us
    pallas_call x3, Pallas kernels, lowrank_of(): pl.pallas_call(functools.partial(lowrank_kernel, at, len(pieces)), out_sh...  3.15 us
    pallas_call x1, Pallas kernels, finish(): pl.pallas_call(finish_kernel, out_shape=jax.ShapeDtypeStruct(early.shape,...  2.13 us
    pallas_call x1, Pallas kernels, early_product(): pl.pallas_call(functools.partial(early_kernel, kv_heads), out_shape=jax.S...  1.9 us
    pallas_call x2, Pallas kernels, last_probs(): pl.pallas_call(last_probs_kernel, out_shape=[jax.ShapeDtypeStruct((p.shap...  1.82 us
  transfers between devices with their start and end apart: 16, of which 7 were waited for; matrix products, arithmetic and copies ran while one was open for 0% of the time, Pallas kernels for 28%

profile of v11, /device:TPU:0, one launch (start us, length us, event | category | flops | bytes accessed | tf_op | source)
XLA Modules:
  0.0 54.5 jit_solution(246184942246701867)
XLA Ops:
  0.0 1.2 %pad_maximum_fusion = (bf16[32,4608]{1,0:T(8,128)(2,1)S(1)}, bf16[32,4608]{1,0:T(8,128)(2,1)S(1)}) fusion(bf16[64,512]{1,0:T(8,128)(2,1)} %bitcast.8, bf16[64,4096]{1,0:T(8,128)(2,1)} %bitcast.7), kind=kLoop, calls=%fused_computation.3 | loop fusion | flops 1179648 | bytes 1179648 | tf_op jit(solution)/shard_map/concatenate | solution.py:369
  1.2 3.0 %collective-permute-start.4 = (bf16[32,4608]{1,0:T(8,128)(2,1)S(1)}, bf16[32,4608]{1,0:T(8,128)(2,1)S(1)}, u32[]{:S(2)}, u32[]{:S(2)}) collective-permute-start(bf16[32,4608]{1,0:T(8,128)(2,1)S(1)} %get-tuple-element.103.refs_1_), channel_id=1, source_target_pairs={{4,0},{8,4},{12,8},{14,12},{10,14},{6,10},{2,6},{0,2},{5,1},{9,5},... | collective-permute-start | bytes 884744 | tf_op jit(solution)/shard_map/ppermute | solution.py:380
  4.3 2.0 %collective-permute-start.8 = (bf16[32,4608]{1,0:T(8,128)(2,1)S(1)}, bf16[32,4608]{1,0:T(8,128)(2,1)S(1)}, u32[]{:S(2)}, u32[]{:S(2)}) collective-permute-start(bf16[32,4608]{1,0:T(8,128)(2,1)S(1)} %get-tuple-element.103.refs_1_), channel_id=1, source_target_pairs={{0,4},{4,8},{8,12},{12,14},{14,10},{10,6},{6,2},{2,0},{1,5},{5,9},... | collective-permute-start | bytes 884744 | tf_op jit(solution)/shard_map/ppermute | solution.py:380
  6.3 1.9 %copy-done.2 = bf16[384,4096]{1,0:T(8,128)(2,1)S(1)} copy-done((bf16[384,4096]{1,0:T(8,128)(2,1)S(1)}, bf16[384,4096]{1,0:T(8,128)(2,1)}, u32[]{:S(2)}) %copy-start.2) | copy-done | bytes 3145752
  12.4 1.8 %probs.7 = (bf16[512,128]{1,0:T(8,128)(2,1)S(1)}, bf16[512,128]{1,0:T(8,128)(2,1)S(1)}, bf16[512,256]{1,0:T(8,128)(2,1)S(1)}, bf16[512,256]{1,0:T(8,128)(2,1)S(1...) custom-call(s32[384,1]{1,0:T(8,128)S(1)} %get-tuple-element.58.segment_ref, ...), custom_call_target="tpu_custom_call" | custom-call | flops 2000000000 | bytes 1310720 | tf_op jit(solution)/shard_map/probs/pallas_call | solution.py:117
  14.2 2.0 %collective-permute-start.5 = (bf16[32,4608]{1,0:T(8,128)(2,1)S(1)}, bf16[32,4608]{1,0:T(8,128)(2,1)S(1)}, u32[]{:S(2)}, u32[]{:S(2)}) collective-permute-start(bf16[32,4608]{1,0:T(8,128)(2,1)S(1)} %collective-permute-done.4.refs_5_), channel_id=1, source_target_pairs={{4,0},{8,4},{12,8},{14,12},{10,14},{6,10},{2,6},{0,2},{5,1},{9,5},... | collective-permute-start | bytes 884744 | tf_op jit(solution)/shard_map/ppermute | solution.py:380
  16.3 1.8 %probs.5 = (bf16[512,128]{1,0:T(8,128)(2,1)S(1)}, bf16[512,128]{1,0:T(8,128)(2,1)S(1)}, bf16[512,256]{1,0:T(8,128)(2,1)S(1)}, bf16[512,256]{1,0:T(8,128)(2,1)S(1...) custom-call(s32[384,1]{1,0:T(8,128)S(1)} %get-tuple-element.58.segment_ref, ...), custom_call_target="tpu_custom_call" | custom-call | flops 2000000000 | bytes 1310720 | tf_op jit(solution)/shard_map/probs/pallas_call | solution.py:117
  18.1 2.3 %collective-permute-done.8.refs_3_ = bf16[32,4608]{1,0:T(8,128)(2,1)S(1)} collective-permute-done((bf16[32,4608]{1,0:T(8,128)(2,1)S(1)}, bf16[32,4608]{1,0:T(8,128)(2,1)S(1)}, u32[]{:S(2)}, u32[]{:S(2)}) %collective-permute-start.8) | collective-permute-done | bytes 294944 | tf_op jit(solution)/shard_map/ppermute | solution.py:380
  20.5 1.9 %collective-permute-start.12 = (bf16[32,4608]{1,0:T(8,128)(2,1)S(1)}, bf16[32,4608]{1,0:T(8,128)(2,1)S(1)}, u32[]{:S(2)}, u32[]{:S(2)}) collective-permute-start(bf16[32,4608]{1,0:T(8,128)(2,1)S(1)} %collective-permute-done.11.refs_4_), channel_id=1, source_target_pairs={{4,0},{8,4},{12,8},{14,12},{10,14},{6,10},{2,6},{0,2},{5,1},{9,5},... | collective-permute-start | bytes 884744 | tf_op jit(solution)/shard_map/ppermute | solution.py:380
  22.5 1.8 %probs.4 = (bf16[512,128]{1,0:T(8,128)(2,1)S(1)}, bf16[512,128]{1,0:T(8,128)(2,1)S(1)}, bf16[512,256]{1,0:T(8,128)(2,1)S(1)}, bf16[512,256]{1,0:T(8,128)(2,1)S(1...) custom-call(s32[384,1]{1,0:T(8,128)S(1)} %get-tuple-element.58.segment_ref, ...), custom_call_target="tpu_custom_call" | custom-call | flops 2000000000 | bytes 1310720 | tf_op jit(solution)/shard_map/probs/pallas_call | solution.py:117
  25.9 1.6 %collective-permute-start.6 = (bf16[32,4608]{1,0:T(8,128)(2,1)S(1)}, bf16[32,4608]{1,0:T(8,128)(2,1)S(1)}, u32[]{:S(2)}, u32[]{:S(2)}) collective-permute-start(bf16[32,4608]{1,0:T(8,128)(2,1)S(1)} %collective-permute-done.5.refs_3_), channel_id=1, source_target_pairs={{4,0},{8,4},{12,8},{14,12},{10,14},{6,10},{2,6},{0,2},{5,1},{9,5},... | collective-permute-start | bytes 884744 | tf_op jit(solution)/shard_map/ppermute | solution.py:380
  28.0 1.8 %probs.6 = (bf16[512,128]{1,0:T(8,128)(2,1)S(1)}, bf16[512,128]{1,0:T(8,128)(2,1)S(1)}, bf16[512,256]{1,0:T(8,128)(2,1)S(1)}, bf16[512,256]{1,0:T(8,128)(2,1)S(1...) custom-call(s32[384,1]{1,0:T(8,128)S(1)} %get-tuple-element.58.segment_ref, ...), custom_call_target="tpu_custom_call" | custom-call | flops 2000000000 | bytes 1310720 | tf_op jit(solution)/shard_map/probs/pallas_call | solution.py:117
  30.7 2.4 %collective-permute-done.9.refs_6_.refs_1_ = bf16[32,4608]{1,0:T(8,128)(2,1)S(1)} collective-permute-done((bf16[32,4608]{1,0:T(8,128)(2,1)S(1)}, bf16[32,4608]{1,0:T(8,128)(2,1)S(1)}, u32[]{:S(2)}, u32[]{:S(2)}) %collective-permute-start.9) | collective-permute-done | bytes 294944 | tf_op jit(solution)/shard_map/ppermute | solution.py:380
  33.2 1.9 %collective-permute-start.13 = (bf16[32,4608]{1,0:T(8,128)(2,1)S(1)}, bf16[32,4608]{1,0:T(8,128)(2,1)S(1)}, u32[]{:S(2)}, u32[]{:S(2)}) collective-permute-start(bf16[32,4608]{1,0:T(8,128)(2,1)S(1)} %collective-permute-done.12.refs_7_.refs_2_), channel_id=1, source_target_pairs={{4,0},{8,4},{12,8},{14,12},{10,14},{6,10},{2,6},{0,2},{5,1},{9,5},... | collective-permute-start | bytes 884744 | tf_op jit(solution)/shard_map/ppermute | solution.py:380
  35.1 1.1 %lowrank.3 = (f32[384,64]{1,0:T(8,128)S(1)}, bf16[192,512]{1,0:T(8,128)(2,1)S(1)}) custom-call(s32[384,1]{1,0:T(8,128)S(1)} %get-tuple-element.55.place_ref, bf16[384,4096]{1,0:T(8,128)(2,1)S(1)} %copy-done, bf16[32,4608]{1,0:T(8,128)(2,1)S(1)} %get-tuple-element.104.refs_0_, bf16[32,4608]{1,0:T(8,128)(2,1)S(1)} %get-tuple-element.103.refs_1_, ...), custom_call_target="tpu_custom_call" | custom-call | flops 1700000000 | bytes 4915200 | tf_op jit(solution)/shard_map/lowrank/pallas_call | solution.py:155
  36.2 1.2 %collective-permute-done.6.refs_3_ = bf16[32,4608]{1,0:T(8,128)(2,1)S(1)} collective-permute-done((bf16[32,4608]{1,0:T(8,128)(2,1)S(1)}, bf16[32,4608]{1,0:T(8,128)(2,1)S(1)}, u32[]{:S(2)}, u32[]{:S(2)}) %collective-permute-start.6) | collective-permute-done | bytes 294944 | tf_op jit(solution)/shard_map/ppermute | solution.py:380
  37.4 2.0 %collective-permute-start.7 = (bf16[32,4608]{1,0:T(8,128)(2,1)S(1)}, bf16[32,4608]{1,0:T(8,128)(2,1)S(1)}, u32[]{:S(2)}, u32[]{:S(2)}) collective-permute-start(bf16[32,4608]{1,0:T(8,128)(2,1)S(1)} %collective-permute-done.6.refs_3_), channel_id=1, source_target_pairs={{4,0},{8,4},{12,8},{14,12},{10,14},{6,10},{2,6},{0,2},{5,1},{9,5},... | collective-permute-start | bytes 884744 | tf_op jit(solution)/shard_map/ppermute | solution.py:380
  39.5 1.0 %lowrank.4 = (f32[384,64]{1,0:T(8,128)S(1)}, bf16[128,512]{1,0:T(8,128)(2,1)S(1)}) custom-call(s32[384,1]{1,0:T(8,128)S(1)} %get-tuple-element.55.place_ref, bf16[384,4096]{1,0:T(8,128)(2,1)S(1)} %copy-done, bf16[32,4608]{1,0:T(8,128)(2,1)S(1)} %collective-permute-done.1.refs_0_, bf16[32,4608]{1,0:T(8,128)(2,1)S(1)} %collective-permute-done.9.refs_6_.refs_1_, ...), custom_call_target="tpu_custom_call" | custom-call | flops 1700000000 | bytes 4325376 | tf_op jit(solution)/shard_map/lowrank/pallas_call | solution.py:155
  40.5 5.2 %collective-permute-done.10.refs_1_ = bf16[32,4608]{1,0:T(8,128)(2,1)S(1)} collective-permute-done((bf16[32,4608]{1,0:T(8,128)(2,1)S(1)}, bf16[32,4608]{1,0:T(8,128)(2,1)S(1)}, u32[]{:S(2)}, u32[]{:S(2)}) %collective-permute-start.10) | collective-permute-done | bytes 294944 | tf_op jit(solution)/shard_map/ppermute | solution.py:380
  45.7 1.0 %lowrank.5 = (f32[384,64]{1,0:T(8,128)S(1)}, bf16[128,512]{1,0:T(8,128)(2,1)S(1)}) custom-call(s32[384,1]{1,0:T(8,128)S(1)} %get-tuple-element.55.place_ref, bf16[384,4096]{1,0:T(8,128)(2,1)S(1)} %copy-done, bf16[32,4608]{1,0:T(8,128)(2,1)S(1)} %collective-permute-done.2.refs_0_, bf16[32,4608]{1,0:T(8,128)(2,1)S(1)} %collective-permute-done.10.refs_1_, ...), custom_call_target="tpu_custom_call" | custom-call | flops 1700000000 | bytes 4325376 | tf_op jit(solution)/shard_map/lowrank/pallas_call | solution.py:155
  46.9 1.4 %collective-permute-done.14.theirs_ref = f32[384,64]{1,0:T(8,128)S(1)} collective-permute-done((f32[384,64]{1,0:T(8,128)S(1)}, f32[384,64]{1,0:T(8,128)S(1)}, u32[]{:S(2)}, u32[]{:S(2)}) %collective-permute-start.14) | collective-permute-done | bytes 98336 | tf_op jit(solution)/shard_map/ppermute | solution.py:409
  48.3 1.9 %early_product.1.refs_0_.early_ref = f32[384,4096]{1,0:T(8,128)S(1)} custom-call(s32[384,1]{1,0:T(8,128)S(1)} %get-tuple-element.55.place_ref, f32[384,64]{1,0:T(8,128)S(1)} %get-tuple-element.87.mine_ref, f32[384,64]{1,0:T(8,128)S(1)} %collective-permute-done.14.theirs_ref, bf16[384,512]{1,0:T(8,128)(2,1)S(1)} %copy-done.1, ...), custom_call_target="tpu_custom_call" | custom-call | flops 50000000 | bytes 1536 | tf_op jit(solution)/shard_map/early_product/pallas_call | solution.py:262
  51.0 1.2 %collective-permute-done.15.theirs_ref = f32[96,64]{1,0:T(8,128)S(1)} collective-permute-done((f32[96,64]{1,0:T(8,128)S(1)}, f32[96,64]{1,0:T(8,128)S(1)}, u32[]{:S(2)}, u32[]{:S(2)}) %collective-permute-start.15) | collective-permute-done | bytes 24608 | tf_op jit(solution)/shard_map/ppermute | solution.py:411
  52.2 2.1 %finish.1 = bf16[384,4096]{1,0:T(8,128)(2,1)} custom-call(f32[96,64]{1,0:T(8,128)S(1)} %get-tuple-element.91.mine_ref, f32[96,64]{1,0:T(8,128)S(1)} %collective-permute-done.15.theirs_ref, bf16[64,512]{1,0:T(8,128)(2,1)S(1)} %get-tuple-element.92.up_ref, f32[384,4096]{1,0:T(8,128)S(1)} %early_product.1.refs_0_.early_ref, ...), custom_call_target="tpu_custom_call" | custom-call | tf_op jit(solution)/shard_map/finish/pallas_call | solution.py:341
  (39 shorter events, 8.7 us)
Async XLA Ops:
  0.0 11.4 %copy-start.5 = (bf16[384,512]{1,0:T(8,128)(2,1)S(1)}, bf16[384,512]{1,0:T(8,128)(2,1)}, u32[]{:S(2)}) copy-start(bf16[384,512]{1,0:T(8,128)(2,1)} %k_ref.7) | copy-start | bytes 1179652
  1.2 13.1 %collective-permute-start.4 = (bf16[32,4608]{1,0:T(8,128)(2,1)S(1)}, bf16[32,4608]{1,0:T(8,128)(2,1)S(1)}, u32[]{:S(2)}, u32[]{:S(2)}) collective-permute-start(bf16[32,4608]{1,0:T(8,128)(2,1)S(1)} %get-tuple-element.103.refs_1_), channel_id=1, source_target_pairs={{4,0},{8,4},{12,8},{14,12},{10,14},{6,10},{2,6},{0,2},{5,1},{9,5},... | collective-permute-start | bytes 884744 | tf_op jit(solution)/shard_map/ppermute | solution.py:380
  4.2 12.0 %collective-permute-start = (bf16[32,4608]{1,0:T(8,128)(2,1)S(1)}, bf16[32,4608]{1,0:T(8,128)(2,1)S(1)}, u32[]{:S(2)}, u32[]{:S(2)}) collective-permute-start(bf16[32,4608]{1,0:T(8,128)(2,1)S(1)} %get-tuple-element.104.refs_0_), channel_id=1, source_target_pairs={{0,4},{4,8},{8,12},{12,14},{14,10},{10,6},{6,2},{2,0},{1,5},{5,9},... | collective-permute-start | bytes 884744 | tf_op jit(solution)/shard_map/ppermute | solution.py:380
  4.3 16.1 %collective-permute-start.8 = (bf16[32,4608]{1,0:T(8,128)(2,1)S(1)}, bf16[32,4608]{1,0:T(8,128)(2,1)S(1)}, u32[]{:S(2)}, u32[]{:S(2)}) collective-permute-start(bf16[32,4608]{1,0:T(8,128)(2,1)S(1)} %get-tuple-element.103.refs_1_), channel_id=1, source_target_pairs={{0,4},{4,8},{8,12},{12,14},{14,10},{10,6},{6,2},{2,0},{1,5},{5,9},... | collective-permute-start | bytes 884744 | tf_op jit(solution)/shard_map/ppermute | solution.py:380
  6.3 14.3 %collective-permute-start.11 = (bf16[32,4608]{1,0:T(8,128)(2,1)S(1)}, bf16[32,4608]{1,0:T(8,128)(2,1)S(1)}, u32[]{:S(2)}, u32[]{:S(2)}) collective-permute-start(bf16[32,4608]{1,0:T(8,128)(2,1)S(1)} %get-tuple-element.104.refs_0_), channel_id=1, source_target_pairs={{4,0},{8,4},{12,8},{14,12},{10,14},{6,10},{2,6},{0,2},{5,1},{9,5},... | collective-permute-start | bytes 884744 | tf_op jit(solution)/shard_map/ppermute | solution.py:380
  6.3 1.9 %copy-start.2 = (bf16[384,4096]{1,0:T(8,128)(2,1)S(1)}, bf16[384,4096]{1,0:T(8,128)(2,1)}, u32[]{:S(2)}) copy-start(bf16[384,4096]{1,0:T(8,128)(2,1)} %q_ref.7) | copy-start | bytes 9437188
  8.2 1.0 %copy-start.4 = (bf16[384,512]{1,0:T(8,128)(2,1)S(1)}, bf16[384,512]{1,0:T(8,128)(2,1)}, u32[]{:S(2)}) copy-start(bf16[384,512]{1,0:T(8,128)(2,1)} %k_ref.7) | copy-start | bytes 1179652
  9.2 0.7 %copy-start.6 = (s32[384,1]{0,1:T(1,128)S(1)}, s32[384,1]{0,1:T(1,128)}, u32[]{:S(2)}) copy-start(s32[384,1]{0,1:T(1,128)} %param.12) | copy-start | bytes 4612
  9.9 0.7 %copy-start.7 = (s32[1,4]{1,0:T(1,128)S(1)}, s32[1,4]{1,0:T(1,128)}, u32[]{:S(2)}) copy-start(s32[1,4]{1,0:T(1,128)} %lengths_ref.1) | copy-start | bytes 52
  10.6 1.9 %copy-start.3 = (bf16[384,4096]{1,0:T(8,128)(2,1)S(1)}, bf16[384,4096]{1,0:T(8,128)(2,1)}, u32[]{:S(2)}) copy-start(bf16[384,4096]{1,0:T(8,128)(2,1)} %q_ref.7) | copy-start | bytes 9437188
  14.2 11.7 %collective-permute-start.5 = (bf16[32,4608]{1,0:T(8,128)(2,1)S(1)}, bf16[32,4608]{1,0:T(8,128)(2,1)S(1)}, u32[]{:S(2)}, u32[]{:S(2)}) collective-permute-start(bf16[32,4608]{1,0:T(8,128)(2,1)S(1)} %collective-permute-done.4.refs_5_), channel_id=1, source_target_pairs={{4,0},{8,4},{12,8},{14,12},{10,14},{6,10},{2,6},{0,2},{5,1},{9,5},... | collective-permute-start | bytes 884744 | tf_op jit(solution)/shard_map/ppermute | solution.py:380
  16.2 11.4 %collective-permute-start.1 = (bf16[32,4608]{1,0:T(8,128)(2,1)S(1)}, bf16[32,4608]{1,0:T(8,128)(2,1)S(1)}, u32[]{:S(2)}, u32[]{:S(2)}) collective-permute-start(bf16[32,4608]{1,0:T(8,128)(2,1)S(1)} %collective-permute-done.refs_2_), channel_id=1, source_target_pairs={{0,4},{4,8},{8,12},{12,14},{14,10},{10,6},{6,2},{2,0},{1,5},{5,9},... | collective-permute-start | bytes 884744 | tf_op jit(solution)/shard_map/ppermute | solution.py:380
  18.1 6.2 %copy-start = (bf16[384,4096]{1,0:T(8,128)(2,1)S(1)}, bf16[384,4096]{1,0:T(8,128)(2,1)}, u32[]{:S(2)}) copy-start(bf16[384,4096]{1,0:T(8,128)(2,1)} %x_ref.7) | copy-start | bytes 9437188
  20.4 12.6 %collective-permute-start.9 = (bf16[32,4608]{1,0:T(8,128)(2,1)S(1)}, bf16[32,4608]{1,0:T(8,128)(2,1)S(1)}, u32[]{:S(2)}, u32[]{:S(2)}) collective-permute-start(bf16[32,4608]{1,0:T(8,128)(2,1)S(1)} %collective-permute-done.8.refs_3_), channel_id=1, source_target_pairs={{0,4},{4,8},{8,12},{12,14},{14,10},{10,6},{6,2},{2,0},{1,5},{5,9},... | collective-permute-start | bytes 884744 | tf_op jit(solution)/shard_map/ppermute | solution.py:380
  20.5 12.6 %collective-permute-start.12 = (bf16[32,4608]{1,0:T(8,128)(2,1)S(1)}, bf16[32,4608]{1,0:T(8,128)(2,1)S(1)}, u32[]{:S(2)}, u32[]{:S(2)}) collective-permute-start(bf16[32,4608]{1,0:T(8,128)(2,1)S(1)} %collective-permute-done.11.refs_4_), channel_id=1, source_target_pairs={{4,0},{8,4},{12,8},{14,12},{10,14},{6,10},{2,6},{0,2},{5,1},{9,5},... | collective-permute-start | bytes 884744 | tf_op jit(solution)/shard_map/ppermute | solution.py:380
  25.9 11.5 %collective-permute-start.6 = (bf16[32,4608]{1,0:T(8,128)(2,1)S(1)}, bf16[32,4608]{1,0:T(8,128)(2,1)S(1)}, u32[]{:S(2)}, u32[]{:S(2)}) collective-permute-start(bf16[32,4608]{1,0:T(8,128)(2,1)S(1)} %collective-permute-done.5.refs_3_), channel_id=1, source_target_pairs={{4,0},{8,4},{12,8},{14,12},{10,14},{6,10},{2,6},{0,2},{5,1},{9,5},... | collective-permute-start | bytes 884744 | tf_op jit(solution)/shard_map/ppermute | solution.py:380
  27.5 11.9 %collective-permute-start.2 = (bf16[32,4608]{1,0:T(8,128)(2,1)S(1)}, bf16[32,4608]{1,0:T(8,128)(2,1)S(1)}, u32[]{:S(2)}, u32[]{:S(2)}) collective-permute-start(bf16[32,4608]{1,0:T(8,128)(2,1)S(1)} %collective-permute-done.1.refs_0_), channel_id=1, source_target_pairs={{0,4},{4,8},{8,12},{12,14},{14,10},{10,6},{6,2},{2,0},{1,5},{5,9},... | collective-permute-start | bytes 884744 | tf_op jit(solution)/shard_map/ppermute | solution.py:380
  33.1 12.6 %collective-permute-start.10 = (bf16[32,4608]{1,0:T(8,128)(2,1)S(1)}, bf16[32,4608]{1,0:T(8,128)(2,1)S(1)}, u32[]{:S(2)}, u32[]{:S(2)}) collective-permute-start(bf16[32,4608]{1,0:T(8,128)(2,1)S(1)} %collective-permute-done.9.refs_6_.refs_1_), channel_id=1, source_target_pairs={{0,4},{4,8},{8,12},{12,14},{14,10},{10,6},{6,2},{2,0},{1,5},{5,9},... | collective-permute-start | bytes 884744 | tf_op jit(solution)/shard_map/ppermute | solution.py:380
  33.2 12.6 %collective-permute-start.13 = (bf16[32,4608]{1,0:T(8,128)(2,1)S(1)}, bf16[32,4608]{1,0:T(8,128)(2,1)S(1)}, u32[]{:S(2)}, u32[]{:S(2)}) collective-permute-start(bf16[32,4608]{1,0:T(8,128)(2,1)S(1)} %collective-permute-done.12.refs_7_.refs_2_), channel_id=1, source_target_pairs={{4,0},{8,4},{12,8},{14,12},{10,14},{6,10},{2,6},{0,2},{5,1},{9,5},... | collective-permute-start | bytes 884744 | tf_op jit(solution)/shard_map/ppermute | solution.py:380
  37.4 12.8 %collective-permute-start.7 = (bf16[32,4608]{1,0:T(8,128)(2,1)S(1)}, bf16[32,4608]{1,0:T(8,128)(2,1)S(1)}, u32[]{:S(2)}, u32[]{:S(2)}) collective-permute-start(bf16[32,4608]{1,0:T(8,128)(2,1)S(1)} %collective-permute-done.6.refs_3_), channel_id=1, source_target_pairs={{4,0},{8,4},{12,8},{14,12},{10,14},{6,10},{2,6},{0,2},{5,1},{9,5},... | collective-permute-start | bytes 884744 | tf_op jit(solution)/shard_map/ppermute | solution.py:380
  39.4 11.2 %collective-permute-start.3 = (bf16[32,4608]{1,0:T(8,128)(2,1)S(1)}, bf16[32,4608]{1,0:T(8,128)(2,1)S(1)}, u32[]{:S(2)}, u32[]{:S(2)}) collective-permute-start(bf16[32,4608]{1,0:T(8,128)(2,1)S(1)} %collective-permute-done.2.refs_0_), channel_id=1, source_target_pairs={{0,4},{4,8},{8,12},{12,14},{14,10},{10,6},{6,2},{2,0},{1,5},{5,9},... | collective-permute-start | bytes 884744 | tf_op jit(solution)/shard_map/ppermute | solution.py:380
  45.7 2.6 %copy-start.1 = (bf16[384,512]{1,0:T(8,128)(2,1)S(1)}, bf16[384,512]{1,0:T(8,128)(2,1)}, u32[]{:S(2)}) copy-start(bf16[384,512]{1,0:T(8,128)(2,1)} %base_ref.1) | copy-start | bytes 1179652
  46.8 1.5 %collective-permute-start.14 = (f32[384,64]{1,0:T(8,128)S(1)}, f32[384,64]{1,0:T(8,128)S(1)}, u32[]{:S(2)}, u32[]{:S(2)}) collective-permute-start(f32[384,64]{1,0:T(8,128)S(1)} %get-tuple-element.87.mine_ref), channel_id=1, source_target_pairs={{0,1},{1,0},{2,3},{3,2},{4,5},{5,4},{6,7},{7,6},{8,9},{9,8},{10,11... | collective-permute-start | bytes 294920 | tf_op jit(solution)/shard_map/ppermute | solution.py:409
  50.9 1.3 %collective-permute-start.15 = (f32[96,64]{1,0:T(8,128)S(1)}, f32[96,64]{1,0:T(8,128)S(1)}, u32[]{:S(2)}, u32[]{:S(2)}) collective-permute-start(f32[96,64]{1,0:T(8,128)S(1)} %get-tuple-element.91.mine_ref), channel_id=1, source_target_pairs={{0,1},{1,0},{2,3},{3,2},{4,5},{5,4},{6,7},{7,6},{8,9},{9,8},{10,11... | collective-permute-start | bytes 73736 | tf_op jit(solution)/shard_map/ppermute | solution.py:411

commit v12 on v11

--- a/solution.py
+++ b/solution.py
@@ -42,6 +42,35 @@
     if n == 8:
         return jnp.where(replica & 1 == 0, replica >> 1, n - 1 - (replica >> 1))
     return replica
+
+
+def pack_kernel(down_ref, up_ref, low_ref, high_ref, sems):
+    half, features = low_ref.shape[0], down_ref.shape[1]
+    copies = []
+    for i, piece_ref in enumerate((low_ref, high_ref)):
+        ranks = slice(i * half, (i + 1) * half)
+        for part_ref, columns in ((down_ref, slice(0, features)), (up_ref, slice(features, piece_ref.shape[1]))):
+            copies.append(
+                pltpu.make_async_copy(part_ref.at[ranks, :], piece_ref.at[:, columns], sems.at[len(copies)])
+            )
+    for copy in copies:
+        copy.start()
+    for copy in copies:
+        copy.wait()
+
+
+def pack(down, up):
+    piece = jax.ShapeDtypeStruct((down.shape[0] // 2, down.shape[1] + up.shape[1]), down.dtype)
+    return pl.pallas_call(
+        pack_kernel,
+        out_shape=[piece, piece],
+        in_specs=[pl.BlockSpec(memory_space=pl.ANY)] * 2,
+        out_specs=[pl.BlockSpec(memory_space=pl.ANY)] * 2,
+        scratch_shapes=[pltpu.SemaphoreType.DMA((4,))],
+        cost_estimate=pl.CostEstimate(flops=0, bytes_accessed=4 * piece.size, transcendentals=0),
+        compiler_params=pltpu.CompilerParams(vmem_limit_bytes=60 * 2**20),
+        name="pack",
+    )(down, up)
 
 
 def column(row):
@@ -366,9 +395,7 @@
     far = n // 2
     distances = [0] + [d for step in range(1, far) for d in (step, -step)] + [far]
     down = jnp.swapaxes(adapter_down_weight[0], 0, 1)
-    both = jnp.concatenate([down, adapter_up_weight[0]], axis=1)
-    rank = both.shape[0]
-    own_low, own_high = both[: rank // 2], both[rank // 2 :]
+    own_low, own_high = pack(down, adapter_up_weight[0])
     place, segment, across, slot, slot_across = masks(
         n, sequence_lengths, adapter_of_row.reshape(1, -1), queries, stacked_key_rows
     )

time: 54.8 us -> 72.9 us (1.33)
  Pallas kernels: 18 us -> 37 us
  other arithmetic: 1.16 us -> 0 us
    pallas_call x0 -> x1, Pallas kernels: none -> 19 us  [pack(): pl.pallas_call(pack_kernel, out_shape=[piece, piece], in_specs=[pl.BlockS...]
    concatenate x1 -> x0, other arithmetic: 1.16 us -> none  [on_device(): both = jnp.concatenate([down, adapter_up_weight[0]], axis=1)]
    unnamed x16 -> x20, local copies, waits for them, and re-layouts: 5.27 us -> 5.28 us
  transfers between devices with their start and end apart: 16 -> 16, of which waited for: 7 -> 7; matrix products, arithmetic and copies ran while one was open for 0% -> 0% of each run, Pallas kernels for 28% -> 21%
where the time goes in v12:
time: 72.9 us; the launch traced here: 72.6 us
  Pallas kernels  37 us (51%)
  starting transfers between devices  15.6 us (21%)
  waiting for transfers between devices  14.4 us (20%)
  local copies, waits for them, and re-layouts  5.28 us (7%)
    pallas_call x1, Pallas kernels, pack(): pl.pallas_call(pack_kernel, out_shape=[piece, piece], in_specs=[pl.BlockS...  19 us
    ppermute x14, starting transfers between devices, pass_round(): piece = lax.ppermute(piece, 'rep', pairs)  15.5 us
    ppermute x14, waiting for transfers between devices, pass_round(): piece = lax.ppermute(piece, 'rep', pairs)  11.8 us
    pallas_call x4, Pallas kernels, probs_of(): pl.pallas_call(functools.partial(probs_kernel, kv_head), out_shape=[jax.S...  7.07 us
    unnamed x20, local copies, waits for them, and re-layouts  5.28 us
    pallas_call x3, Pallas kernels, lowrank_of(): pl.pallas_call(functools.partial(lowrank_kernel, at, len(pieces)), out_sh...  3.15 us
    pallas_call x1, Pallas kernels, finish(): pl.pallas_call(finish_kernel, out_shape=jax.ShapeDtypeStruct(early.shape,...  2.13 us
    pallas_call x1, Pallas kernels, early_product(): pl.pallas_call(functools.partial(early_kernel, kv_heads), out_shape=jax.S...  1.89 us
  transfers between devices with their start and end apart: 16, of which 7 were waited for; matrix products, arithmetic and copies ran while one was open for 0% of the time, Pallas kernels for 21%

profile of v12, /device:TPU:0, one launch (start us, length us, event | category | flops | bytes accessed | tf_op | source)
XLA Modules:
  0.0 72.6 jit_solution(11557902416491751717)
XLA Ops:
  0.0 19.0 %pack.1 = (bf16[32,4608]{1,0:T(8,128)(2,1)}, bf16[32,4608]{1,0:T(8,128)(2,1)}) custom-call(bf16[64,4096]{1,0:T(8,128)(2,1)} %bitcast.7, bf16[64,512]{1,0:T(8,128)(2,1)} %bitcast.8), custom_call_target="tpu_custom_call" | custom-call | bytes 589824 | tf_op jit(solution)/shard_map/pack/pallas_call | solution.py:64
  19.0 3.1 %collective-permute-start = (bf16[32,4608]{1,0:T(8,128)(2,1)}, bf16[32,4608]{1,0:T(8,128)(2,1)S(1)}, u32[]{:S(2)}, u32[]{:S(2)}) collective-permute-start(bf16[32,4608]{1,0:T(8,128)(2,1)} %get-tuple-element.57.refs_0_), channel_id=1, source_target_pairs={{0,4},{4,8},{8,12},{12,14},{14,10},{10,6},{6,2},{2,0},{1,5},{5,9},... | collective-permute-start | bytes 884744 | tf_op jit(solution)/shard_map/ppermute | solution.py:407
  22.1 2.0 %collective-permute-start.11 = (bf16[32,4608]{1,0:T(8,128)(2,1)}, bf16[32,4608]{1,0:T(8,128)(2,1)S(1)}, u32[]{:S(2)}, u32[]{:S(2)}) collective-permute-start(bf16[32,4608]{1,0:T(8,128)(2,1)} %get-tuple-element.57.refs_0_), channel_id=1, source_target_pairs={{4,0},{8,4},{12,8},{14,12},{10,14},{6,10},{2,6},{0,2},{5,1},{9,5},... | collective-permute-start | bytes 884744 | tf_op jit(solution)/shard_map/ppermute | solution.py:407
  24.2 1.9 %copy-done.2 = bf16[384,4096]{1,0:T(8,128)(2,1)S(1)} copy-done((bf16[384,4096]{1,0:T(8,128)(2,1)S(1)}, bf16[384,4096]{1,0:T(8,128)(2,1)}, u32[]{:S(2)}) %copy-start.2) | copy-done | bytes 3145752
  30.3 1.8 %probs.7 = (bf16[512,128]{1,0:T(8,128)(2,1)S(1)}, bf16[512,128]{1,0:T(8,128)(2,1)S(1)}, bf16[512,256]{1,0:T(8,128)(2,1)S(1)}, bf16[512,256]{1,0:T(8,128)(2,1)S(1...) custom-call(s32[384,1]{1,0:T(8,128)S(1)} %get-tuple-element.62.segment_ref, ...), custom_call_target="tpu_custom_call" | custom-call | flops 2000000000 | bytes 1310720 | tf_op jit(solution)/shard_map/probs/pallas_call | solution.py:146
  32.0 2.0 %collective-permute-start.1 = (bf16[32,4608]{1,0:T(8,128)(2,1)S(1)}, bf16[32,4608]{1,0:T(8,128)(2,1)S(1)}, u32[]{:S(2)}, u32[]{:S(2)}) collective-permute-start(bf16[32,4608]{1,0:T(8,128)(2,1)S(1)} %collective-permute-done.refs_2_), channel_id=1, source_target_pairs={{0,4},{4,8},{8,12},{12,14},{14,10},{10,6},{6,2},{2,0},{1,5},{5,9},... | collective-permute-start | bytes 884744 | tf_op jit(solution)/shard_map/ppermute | solution.py:407
  34.1 1.8 %probs.5 = (bf16[512,128]{1,0:T(8,128)(2,1)S(1)}, bf16[512,128]{1,0:T(8,128)(2,1)S(1)}, bf16[512,256]{1,0:T(8,128)(2,1)S(1)}, bf16[512,256]{1,0:T(8,128)(2,1)S(1...) custom-call(s32[384,1]{1,0:T(8,128)S(1)} %get-tuple-element.62.segment_ref, ...), custom_call_target="tpu_custom_call" | custom-call | flops 2000000000 | bytes 1310720 | tf_op jit(solution)/shard_map/probs/pallas_call | solution.py:146
  35.9 2.6 %collective-permute-done.11.refs_4_ = bf16[32,4608]{1,0:T(8,128)(2,1)S(1)} collective-permute-done((bf16[32,4608]{1,0:T(8,128)(2,1)}, bf16[32,4608]{1,0:T(8,128)(2,1)S(1)}, u32[]{:S(2)}, u32[]{:S(2)}) %collective-permute-start.11) | collective-permute-done | bytes 294944 | tf_op jit(solution)/shard_map/ppermute | solution.py:407
  38.6 2.0 %collective-permute-start.9 = (bf16[32,4608]{1,0:T(8,128)(2,1)S(1)}, bf16[32,4608]{1,0:T(8,128)(2,1)S(1)}, u32[]{:S(2)}, u32[]{:S(2)}) collective-permute-start(bf16[32,4608]{1,0:T(8,128)(2,1)S(1)} %collective-permute-done.8.refs_3_), channel_id=1, source_target_pairs={{0,4},{4,8},{8,12},{12,14},{14,10},{10,6},{6,2},{2,0},{1,5},{5,9},... | collective-permute-start | bytes 884744 | tf_op jit(solution)/shard_map/ppermute | solution.py:407
  40.6 1.8 %probs.4 = (bf16[512,128]{1,0:T(8,128)(2,1)S(1)}, bf16[512,128]{1,0:T(8,128)(2,1)S(1)}, bf16[512,256]{1,0:T(8,128)(2,1)S(1)}, bf16[512,256]{1,0:T(8,128)(2,1)S(1...) custom-call(s32[384,1]{1,0:T(8,128)S(1)} %get-tuple-element.62.segment_ref, ...), custom_call_target="tpu_custom_call" | custom-call | flops 2000000000 | bytes 1310720 | tf_op jit(solution)/shard_map/probs/pallas_call | solution.py:146
  44.0 1.6 %collective-permute-start.2 = (bf16[32,4608]{1,0:T(8,128)(2,1)S(1)}, bf16[32,4608]{1,0:T(8,128)(2,1)S(1)}, u32[]{:S(2)}, u32[]{:S(2)}) collective-permute-start(bf16[32,4608]{1,0:T(8,128)(2,1)S(1)} %collective-permute-done.1.refs_0_), channel_id=1, source_target_pairs={{0,4},{4,8},{8,12},{12,14},{14,10},{10,6},{6,2},{2,0},{1,5},{5,9},... | collective-permute-start | bytes 884744 | tf_op jit(solution)/shard_map/ppermute | solution.py:407
  46.1 1.8 %probs.6 = (bf16[512,128]{1,0:T(8,128)(2,1)S(1)}, bf16[512,128]{1,0:T(8,128)(2,1)S(1)}, bf16[512,256]{1,0:T(8,128)(2,1)S(1)}, bf16[512,256]{1,0:T(8,128)(2,1)S(1...) custom-call(s32[384,1]{1,0:T(8,128)S(1)} %get-tuple-element.62.segment_ref, ...), custom_call_target="tpu_custom_call" | custom-call | flops 2000000000 | bytes 1310720 | tf_op jit(solution)/shard_map/probs/pallas_call | solution.py:146
  48.8 2.4 %collective-permute-done.12.refs_7_.refs_2_ = bf16[32,4608]{1,0:T(8,128)(2,1)S(1)} collective-permute-done((bf16[32,4608]{1,0:T(8,128)(2,1)S(1)}, bf16[32,4608]{1,0:T(8,128)(2,1)S(1)}, u32[]{:S(2)}, u32[]{:S(2)}) %collective-permute-start.12) | collective-permute-done | bytes 294944 | tf_op jit(solution)/shard_map/ppermute | solution.py:407
  51.2 2.0 %collective-permute-start.10 = (bf16[32,4608]{1,0:T(8,128)(2,1)S(1)}, bf16[32,4608]{1,0:T(8,128)(2,1)S(1)}, u32[]{:S(2)}, u32[]{:S(2)}) collective-permute-start(bf16[32,4608]{1,0:T(8,128)(2,1)S(1)} %collective-permute-done.9.refs_6_.refs_1_), channel_id=1, source_target_pairs={{0,4},{4,8},{8,12},{12,14},{14,10},{10,6},{6,2},{2,0},{1,5},{5,9},... | collective-permute-start | bytes 884744 | tf_op jit(solution)/shard_map/ppermute | solution.py:407
  53.2 1.1 %lowrank.3 = (f32[384,64]{1,0:T(8,128)S(1)}, bf16[192,512]{1,0:T(8,128)(2,1)S(1)}) custom-call(s32[384,1]{1,0:T(8,128)S(1)} %get-tuple-element.59.place_ref, bf16[384,4096]{1,0:T(8,128)(2,1)S(1)} %copy-done, bf16[32,4608]{1,0:T(8,128)(2,1)S(1)} %copy-done.6, bf16[32,4608]{1,0:T(8,128)(2,1)S(1)} %copy-done.7, ...), custom_call_target="tpu_custom_call" | custom-call | flops 1700000000 | bytes 4915200 | tf_op jit(solution)/shard_map/lowrank/pallas_call | solution.py:184
  54.3 1.1 %collective-permute-done.2.refs_0_ = bf16[32,4608]{1,0:T(8,128)(2,1)S(1)} collective-permute-done((bf16[32,4608]{1,0:T(8,128)(2,1)S(1)}, bf16[32,4608]{1,0:T(8,128)(2,1)S(1)}, u32[]{:S(2)}, u32[]{:S(2)}) %collective-permute-start.2) | collective-permute-done | bytes 294944 | tf_op jit(solution)/shard_map/ppermute | solution.py:407
  55.4 2.1 %collective-permute-start.3 = (bf16[32,4608]{1,0:T(8,128)(2,1)S(1)}, bf16[32,4608]{1,0:T(8,128)(2,1)S(1)}, u32[]{:S(2)}, u32[]{:S(2)}) collective-permute-start(bf16[32,4608]{1,0:T(8,128)(2,1)S(1)} %collective-permute-done.2.refs_0_), channel_id=1, source_target_pairs={{0,4},{4,8},{8,12},{12,14},{14,10},{10,6},{6,2},{2,0},{1,5},{5,9},... | collective-permute-start | bytes 884744 | tf_op jit(solution)/shard_map/ppermute | solution.py:407
  57.5 1.0 %lowrank.4 = (f32[384,64]{1,0:T(8,128)S(1)}, bf16[128,512]{1,0:T(8,128)(2,1)S(1)}) custom-call(s32[384,1]{1,0:T(8,128)S(1)} %get-tuple-element.59.place_ref, bf16[384,4096]{1,0:T(8,128)(2,1)S(1)} %copy-done, bf16[32,4608]{1,0:T(8,128)(2,1)S(1)} %collective-permute-done.1.refs_0_, bf16[32,4608]{1,0:T(8,128)(2,1)S(1)} %collective-permute-done.9.refs_6_.refs_1_, ...), custom_call_target="tpu_custom_call" | custom-call | flops 1700000000 | bytes 4325376 | tf_op jit(solution)/shard_map/lowrank/pallas_call | solution.py:184
  58.6 5.3 %collective-permute-done.13.refs_2_ = bf16[32,4608]{1,0:T(8,128)(2,1)S(1)} collective-permute-done((bf16[32,4608]{1,0:T(8,128)(2,1)S(1)}, bf16[32,4608]{1,0:T(8,128)(2,1)S(1)}, u32[]{:S(2)}, u32[]{:S(2)}) %collective-permute-start.13) | collective-permute-done | bytes 294944 | tf_op jit(solution)/shard_map/ppermute | solution.py:407
  63.8 1.0 %lowrank.5 = (f32[384,64]{1,0:T(8,128)S(1)}, bf16[128,512]{1,0:T(8,128)(2,1)S(1)}) custom-call(s32[384,1]{1,0:T(8,128)S(1)} %get-tuple-element.59.place_ref, bf16[384,4096]{1,0:T(8,128)(2,1)S(1)} %copy-done, bf16[32,4608]{1,0:T(8,128)(2,1)S(1)} %collective-permute-done.2.refs_0_, bf16[32,4608]{1,0:T(8,128)(2,1)S(1)} %collective-permute-done.10.refs_1_, ...), custom_call_target="tpu_custom_call" | custom-call | flops 1700000000 | bytes 4325376 | tf_op jit(solution)/shard_map/lowrank/pallas_call | solution.py:184
  65.0 1.4 %collective-permute-done.14.theirs_ref = f32[384,64]{1,0:T(8,128)S(1)} collective-permute-done((f32[384,64]{1,0:T(8,128)S(1)}, f32[384,64]{1,0:T(8,128)S(1)}, u32[]{:S(2)}, u32[]{:S(2)}) %collective-permute-start.14) | collective-permute-done | bytes 98336 | tf_op jit(solution)/shard_map/ppermute | solution.py:436
  66.4 1.9 %early_product.1.refs_0_.early_ref = f32[384,4096]{1,0:T(8,128)S(1)} custom-call(s32[384,1]{1,0:T(8,128)S(1)} %get-tuple-element.59.place_ref, f32[384,64]{1,0:T(8,128)S(1)} %get-tuple-element.91.mine_ref, f32[384,64]{1,0:T(8,128)S(1)} %collective-permute-done.14.theirs_ref, bf16[384,512]{1,0:T(8,128)(2,1)S(1)} %copy-done.1, ...), custom_call_target="tpu_custom_call" | custom-call | flops 50000000 | bytes 1536 | tf_op jit(solution)/shard_map/early_product/pallas_call | solution.py:291
  69.1 1.2 %collective-permute-done.15.theirs_ref = f32[96,64]{1,0:T(8,128)S(1)} collective-permute-done((f32[96,64]{1,0:T(8,128)S(1)}, f32[96,64]{1,0:T(8,128)S(1)}, u32[]{:S(2)}, u32[]{:S(2)}) %collective-permute-start.15) | collective-permute-done | bytes 24608 | tf_op jit(solution)/shard_map/ppermute | solution.py:438
  70.3 2.1 %finish.1 = bf16[384,4096]{1,0:T(8,128)(2,1)} custom-call(f32[96,64]{1,0:T(8,128)S(1)} %get-tuple-element.95.mine_ref, f32[96,64]{1,0:T(8,128)S(1)} %collective-permute-done.15.theirs_ref, bf16[64,512]{1,0:T(8,128)(2,1)S(1)} %get-tuple-element.96.up_ref, f32[384,4096]{1,0:T(8,128)S(1)} %early_product.1.refs_0_.early_ref, ...), custom_call_target="tpu_custom_call" | custom-call | tf_op jit(solution)/shard_map/finish/pallas_call | solution.py:370
  (43 shorter events, 8.3 us)
Async XLA Ops:
  0.0 29.2 %copy-start.5 = (bf16[384,512]{1,0:T(8,128)(2,1)S(1)}, bf16[384,512]{1,0:T(8,128)(2,1)}, u32[]{:S(2)}) copy-start(bf16[384,512]{1,0:T(8,128)(2,1)} %k_ref.7) | copy-start | bytes 1179652
  19.0 13.0 %collective-permute-start = (bf16[32,4608]{1,0:T(8,128)(2,1)}, bf16[32,4608]{1,0:T(8,128)(2,1)S(1)}, u32[]{:S(2)}, u32[]{:S(2)}) collective-permute-start(bf16[32,4608]{1,0:T(8,128)(2,1)} %get-tuple-element.57.refs_0_), channel_id=1, source_target_pairs={{0,4},{4,8},{8,12},{12,14},{14,10},{10,6},{6,2},{2,0},{1,5},{5,9},... | collective-permute-start | bytes 884744 | tf_op jit(solution)/shard_map/ppermute | solution.py:407
  22.1 12.0 %collective-permute-start.4 = (bf16[32,4608]{1,0:T(8,128)(2,1)}, bf16[32,4608]{1,0:T(8,128)(2,1)S(1)}, u32[]{:S(2)}, u32[]{:S(2)}) collective-permute-start(bf16[32,4608]{1,0:T(8,128)(2,1)} %get-tuple-element.58.refs_1_), channel_id=1, source_target_pairs={{4,0},{8,4},{12,8},{14,12},{10,14},{6,10},{2,6},{0,2},{5,1},{9,5},... | collective-permute-start | bytes 884744 | tf_op jit(solution)/shard_map/ppermute | solution.py:407
  22.1 16.5 %collective-permute-start.11 = (bf16[32,4608]{1,0:T(8,128)(2,1)}, bf16[32,4608]{1,0:T(8,128)(2,1)S(1)}, u32[]{:S(2)}, u32[]{:S(2)}) collective-permute-start(bf16[32,4608]{1,0:T(8,128)(2,1)} %get-tuple-element.57.refs_0_), channel_id=1, source_target_pairs={{4,0},{8,4},{12,8},{14,12},{10,14},{6,10},{2,6},{0,2},{5,1},{9,5},... | collective-permute-start | bytes 884744 | tf_op jit(solution)/shard_map/ppermute | solution.py:407
  24.1 14.5 %collective-permute-start.8 = (bf16[32,4608]{1,0:T(8,128)(2,1)}, bf16[32,4608]{1,0:T(8,128)(2,1)S(1)}, u32[]{:S(2)}, u32[]{:S(2)}) collective-permute-start(bf16[32,4608]{1,0:T(8,128)(2,1)} %get-tuple-element.58.refs_1_), channel_id=1, source_target_pairs={{0,4},{4,8},{8,12},{12,14},{14,10},{10,6},{6,2},{2,0},{1,5},{5,9},... | collective-permute-start | bytes 884744 | tf_op jit(solution)/shard_map/ppermute | solution.py:407
  24.1 1.9 %copy-start.2 = (bf16[384,4096]{1,0:T(8,128)(2,1)S(1)}, bf16[384,4096]{1,0:T(8,128)(2,1)}, u32[]{:S(2)}) copy-start(bf16[384,4096]{1,0:T(8,128)(2,1)} %q_ref.7) | copy-start | bytes 9437188
  26.0 1.0 %copy-start.4 = (bf16[384,512]{1,0:T(8,128)(2,1)S(1)}, bf16[384,512]{1,0:T(8,128)(2,1)}, u32[]{:S(2)}) copy-start(bf16[384,512]{1,0:T(8,128)(2,1)} %k_ref.7) | copy-start | bytes 1179652
  28.4 1.9 %copy-start.3 = (bf16[384,4096]{1,0:T(8,128)(2,1)S(1)}, bf16[384,4096]{1,0:T(8,128)(2,1)}, u32[]{:S(2)}) copy-start(bf16[384,4096]{1,0:T(8,128)(2,1)} %q_ref.7) | copy-start | bytes 9437188
  32.0 12.0 %collective-permute-start.1 = (bf16[32,4608]{1,0:T(8,128)(2,1)S(1)}, bf16[32,4608]{1,0:T(8,128)(2,1)S(1)}, u32[]{:S(2)}, u32[]{:S(2)}) collective-permute-start(bf16[32,4608]{1,0:T(8,128)(2,1)S(1)} %collective-permute-done.refs_2_), channel_id=1, source_target_pairs={{0,4},{4,8},{8,12},{12,14},{14,10},{10,6},{6,2},{2,0},{1,5},{5,9},... | collective-permute-start | bytes 884744 | tf_op jit(solution)/shard_map/ppermute | solution.py:407
  34.1 11.6 %collective-permute-start.5 = (bf16[32,4608]{1,0:T(8,128)(2,1)S(1)}, bf16[32,4608]{1,0:T(8,128)(2,1)S(1)}, u32[]{:S(2)}, u32[]{:S(2)}) collective-permute-start(bf16[32,4608]{1,0:T(8,128)(2,1)S(1)} %collective-permute-done.4.refs_5_), channel_id=1, source_target_pairs={{4,0},{8,4},{12,8},{14,12},{10,14},{6,10},{2,6},{0,2},{5,1},{9,5},... | collective-permute-start | bytes 884744 | tf_op jit(solution)/shard_map/ppermute | solution.py:407
  35.9 6.5 %copy-start = (bf16[384,4096]{1,0:T(8,128)(2,1)S(1)}, bf16[384,4096]{1,0:T(8,128)(2,1)}, u32[]{:S(2)}) copy-start(bf16[384,4096]{1,0:T(8,128)(2,1)} %x_ref.7) | copy-start | bytes 9437188
  38.6 12.6 %collective-permute-start.12 = (bf16[32,4608]{1,0:T(8,128)(2,1)S(1)}, bf16[32,4608]{1,0:T(8,128)(2,1)S(1)}, u32[]{:S(2)}, u32[]{:S(2)}) collective-permute-start(bf16[32,4608]{1,0:T(8,128)(2,1)S(1)} %collective-permute-done.11.refs_4_), channel_id=1, source_target_pairs={{4,0},{8,4},{12,8},{14,12},{10,14},{6,10},{2,6},{0,2},{5,1},{9,5},... | collective-permute-start | bytes 884744 | tf_op jit(solution)/shard_map/ppermute | solution.py:407
  38.6 12.6 %collective-permute-start.9 = (bf16[32,4608]{1,0:T(8,128)(2,1)S(1)}, bf16[32,4608]{1,0:T(8,128)(2,1)S(1)}, u32[]{:S(2)}, u32[]{:S(2)}) collective-permute-start(bf16[32,4608]{1,0:T(8,128)(2,1)S(1)} %collective-permute-done.8.refs_3_), channel_id=1, source_target_pairs={{0,4},{4,8},{8,12},{12,14},{14,10},{10,6},{6,2},{2,0},{1,5},{5,9},... | collective-permute-start | bytes 884744 | tf_op jit(solution)/shard_map/ppermute | solution.py:407
  44.0 9.2 %copy-start.6 = (bf16[32,4608]{1,0:T(8,128)(2,1)S(1)}, bf16[32,4608]{1,0:T(8,128)(2,1)}, u32[]{:S(2)}) copy-start(bf16[32,4608]{1,0:T(8,128)(2,1)} %get-tuple-element.57.refs_0_) | copy-start | bytes 884740
  44.0 9.2 %copy-start.7 = (bf16[32,4608]{1,0:T(8,128)(2,1)S(1)}, bf16[32,4608]{1,0:T(8,128)(2,1)}, u32[]{:S(2)}) copy-start(bf16[32,4608]{1,0:T(8,128)(2,1)} %get-tuple-element.58.refs_1_) | copy-start | bytes 884740
  44.0 11.3 %collective-permute-start.2 = (bf16[32,4608]{1,0:T(8,128)(2,1)S(1)}, bf16[32,4608]{1,0:T(8,128)(2,1)S(1)}, u32[]{:S(2)}, u32[]{:S(2)}) collective-permute-start(bf16[32,4608]{1,0:T(8,128)(2,1)S(1)} %collective-permute-done.1.refs_0_), channel_id=1, source_target_pairs={{0,4},{4,8},{8,12},{12,14},{14,10},{10,6},{6,2},{2,0},{1,5},{5,9},... | collective-permute-start | bytes 884744 | tf_op jit(solution)/shard_map/ppermute | solution.py:407
  45.7 11.8 %collective-permute-start.6 = (bf16[32,4608]{1,0:T(8,128)(2,1)S(1)}, bf16[32,4608]{1,0:T(8,128)(2,1)S(1)}, u32[]{:S(2)}, u32[]{:S(2)}) collective-permute-start(bf16[32,4608]{1,0:T(8,128)(2,1)S(1)} %collective-permute-done.5.refs_3_), channel_id=1, source_target_pairs={{4,0},{8,4},{12,8},{14,12},{10,14},{6,10},{2,6},{0,2},{5,1},{9,5},... | collective-permute-start | bytes 884744 | tf_op jit(solution)/shard_map/ppermute | solution.py:407
  51.2 12.6 %collective-permute-start.13 = (bf16[32,4608]{1,0:T(8,128)(2,1)S(1)}, bf16[32,4608]{1,0:T(8,128)(2,1)S(1)}, u32[]{:S(2)}, u32[]{:S(2)}) collective-permute-start(bf16[32,4608]{1,0:T(8,128)(2,1)S(1)} %collective-permute-done.12.refs_7_.refs_2_), channel_id=1, source_target_pairs={{4,0},{8,4},{12,8},{14,12},{10,14},{6,10},{2,6},{0,2},{5,1},{9,5},... | collective-permute-start | bytes 884744 | tf_op jit(solution)/shard_map/ppermute | solution.py:407
  51.2 12.6 %collective-permute-start.10 = (bf16[32,4608]{1,0:T(8,128)(2,1)S(1)}, bf16[32,4608]{1,0:T(8,128)(2,1)S(1)}, u32[]{:S(2)}, u32[]{:S(2)}) collective-permute-start(bf16[32,4608]{1,0:T(8,128)(2,1)S(1)} %collective-permute-done.9.refs_6_.refs_1_), channel_id=1, source_target_pairs={{0,4},{4,8},{8,12},{12,14},{14,10},{10,6},{6,2},{2,0},{1,5},{5,9},... | collective-permute-start | bytes 884744 | tf_op jit(solution)/shard_map/ppermute | solution.py:407
  55.4 12.9 %collective-permute-start.3 = (bf16[32,4608]{1,0:T(8,128)(2,1)S(1)}, bf16[32,4608]{1,0:T(8,128)(2,1)S(1)}, u32[]{:S(2)}, u32[]{:S(2)}) collective-permute-start(bf16[32,4608]{1,0:T(8,128)(2,1)S(1)} %collective-permute-done.2.refs_0_), channel_id=1, source_target_pairs={{0,4},{4,8},{8,12},{12,14},{14,10},{10,6},{6,2},{2,0},{1,5},{5,9},... | collective-permute-start | bytes 884744 | tf_op jit(solution)/shard_map/ppermute | solution.py:407
  57.5 11.2 %collective-permute-start.7 = (bf16[32,4608]{1,0:T(8,128)(2,1)S(1)}, bf16[32,4608]{1,0:T(8,128)(2,1)S(1)}, u32[]{:S(2)}, u32[]{:S(2)}) collective-permute-start(bf16[32,4608]{1,0:T(8,128)(2,1)S(1)} %collective-permute-done.6.refs_3_), channel_id=1, source_target_pairs={{4,0},{8,4},{12,8},{14,12},{10,14},{6,10},{2,6},{0,2},{5,1},{9,5},... | collective-permute-start | bytes 884744 | tf_op jit(solution)/shard_map/ppermute | solution.py:407
  63.8 2.6 %copy-start.1 = (bf16[384,512]{1,0:T(8,128)(2,1)S(1)}, bf16[384,512]{1,0:T(8,128)(2,1)}, u32[]{:S(2)}) copy-start(bf16[384,512]{1,0:T(8,128)(2,1)} %base_ref.1) | copy-start | bytes 1179652
  64.9 1.5 %collective-permute-start.14 = (f32[384,64]{1,0:T(8,128)S(1)}, f32[384,64]{1,0:T(8,128)S(1)}, u32[]{:S(2)}, u32[]{:S(2)}) collective-permute-start(f32[384,64]{1,0:T(8,128)S(1)} %get-tuple-element.91.mine_ref), channel_id=1, source_target_pairs={{0,1},{1,0},{2,3},{3,2},{4,5},{5,4},{6,7},{7,6},{8,9},{9,8},{10,11... | collective-permute-start | bytes 294920 | tf_op jit(solution)/shard_map/ppermute | solution.py:436
  69.0 1.3 %collective-permute-start.15 = (f32[96,64]{1,0:T(8,128)S(1)}, f32[96,64]{1,0:T(8,128)S(1)}, u32[]{:S(2)}, u32[]{:S(2)}) collective-permute-start(f32[96,64]{1,0:T(8,128)S(1)} %get-tuple-element.95.mine_ref), channel_id=1, source_target_pairs={{0,1},{1,0},{2,3},{3,2},{4,5},{5,4},{6,7},{7,6},{8,9},{9,8},{10,11... | collective-permute-start | bytes 73736 | tf_op jit(solution)/shard_map/ppermute | solution.py:438
  (2 other events, 1.3 us)

commit v13 on v11

--- a/solution.py
+++ b/solution.py
@@ -161,7 +161,7 @@
         in_specs=[VMEM] * used + [pl.BlockSpec(memory_space=pl.ANY)] * len(after),
         out_specs=[VMEM, VMEM],
         cost_estimate=pl.CostEstimate(
-            flops=1_700_000_000, bytes_accessed=2 * rows * features + size, transcendentals=0
+            flops=1_000_000_000, bytes_accessed=2 * rows + size // features, transcendentals=0
         ),
         compiler_params=pltpu.CompilerParams(vmem_limit_bytes=8 * 2**20 + 2 * x.size + 2 * size),
         name="lowrank",

time: 54.8 us -> 54.8 us (level)
  local copies, waits for them, and re-layouts: 5.27 us -> 4.24 us
  waiting for transfers between devices: 14.2 us -> 15.2 us
    ppermute x14, waiting for transfers between devices: 11.5 us -> 12.6 us  [pass_round(): piece = lax.ppermute(piece, 'rep', pairs)]
    unnamed x16, local copies, waits for them, and re-layouts: 5.27 us -> 4.24 us
  transfers between devices with their start and end apart: 16 -> 16, of which waited for: 7 -> 8; matrix products, arithmetic and copies ran while one was open for 0% -> 0% of each run, Pallas kernels for 28% -> 28%
where the time goes in v13:
time: 54.8 us; the launch traced here: 54.5 us
  Pallas kernels  18 us (33%)
  starting transfers between devices  15.6 us (28%)
  waiting for transfers between devices  15.2 us (28%)
  local copies, waits for them, and re-layouts  4.24 us (8%)
  other arithmetic  1.16 us (2%)
    ppermute x14, starting transfers between devices, pass_round(): piece = lax.ppermute(piece, 'rep', pairs)  15.5 us
    ppermute x14, waiting for transfers between devices, pass_round(): piece = lax.ppermute(piece, 'rep', pairs)  12.6 us
    pallas_call x4, Pallas kernels, probs_of(): pl.pallas_call(functools.partial(probs_kernel, kv_head), out_shape=[jax.S...  7.01 us
    unnamed x16, local copies, waits for them, and re-layouts  4.24 us
    pallas_call x3, Pallas kernels, lowrank_of(): pl.pallas_call(functools.partial(lowrank_kernel, at, len(pieces)), out_sh...  3.18 us
    pallas_call x1, Pallas kernels, finish(): pl.pallas_call(finish_kernel, out_shape=jax.ShapeDtypeStruct(early.shape,...  2.13 us
    pallas_call x1, Pallas kernels, early_product(): pl.pallas_call(functools.partial(early_kernel, kv_heads), out_shape=jax.S...  1.9 us
    pallas_call x2, Pallas kernels, last_probs(): pl.pallas_call(last_probs_kernel, out_shape=[jax.ShapeDtypeStruct((p.shap...  1.84 us
  transfers between devices with their start and end apart: 16, of which 8 were waited for; matrix products, arithmetic and copies ran while one was open for 0% of the time, Pallas kernels for 28%

profile of v13, /device:TPU:0, one launch (start us, length us, event | category | flops | bytes accessed | tf_op | source)
XLA Modules:
  0.0 54.5 jit_solution(7787047442581713714)
XLA Ops:
  0.0 1.2 %pad_maximum_fusion = (bf16[32,4608]{1,0:T(8,128)(2,1)S(1)}, bf16[32,4608]{1,0:T(8,128)(2,1)S(1)}) fusion(bf16[64,512]{1,0:T(8,128)(2,1)} %bitcast.8, bf16[64,4096]{1,0:T(8,128)(2,1)} %bitcast.7), kind=kLoop, calls=%fused_computation.3 | loop fusion | flops 1179648 | bytes 1179648 | tf_op jit(solution)/shard_map/concatenate | solution.py:369
  1.2 3.0 %collective-permute-start.4 = (bf16[32,4608]{1,0:T(8,128)(2,1)S(1)}, bf16[32,4608]{1,0:T(8,128)(2,1)S(1)}, u32[]{:S(2)}, u32[]{:S(2)}) collective-permute-start(bf16[32,4608]{1,0:T(8,128)(2,1)S(1)} %get-tuple-element.103.refs_1_), channel_id=1, source_target_pairs={{4,0},{8,4},{12,8},{14,12},{10,14},{6,10},{2,6},{0,2},{5,1},{9,5},... | collective-permute-start | bytes 884744 | tf_op jit(solution)/shard_map/ppermute | solution.py:380
  4.3 2.0 %collective-permute-start.8 = (bf16[32,4608]{1,0:T(8,128)(2,1)S(1)}, bf16[32,4608]{1,0:T(8,128)(2,1)S(1)}, u32[]{:S(2)}, u32[]{:S(2)}) collective-permute-start(bf16[32,4608]{1,0:T(8,128)(2,1)S(1)} %get-tuple-element.103.refs_1_), channel_id=1, source_target_pairs={{0,4},{4,8},{8,12},{12,14},{14,10},{10,6},{6,2},{2,0},{1,5},{5,9},... | collective-permute-start | bytes 884744 | tf_op jit(solution)/shard_map/ppermute | solution.py:380
  6.3 1.9 %copy-done.2 = bf16[384,4096]{1,0:T(8,128)(2,1)S(1)} copy-done((bf16[384,4096]{1,0:T(8,128)(2,1)S(1)}, bf16[384,4096]{1,0:T(8,128)(2,1)}, u32[]{:S(2)}) %copy-start.2) | copy-done | bytes 3145752
  8.2 1.0 %copy-done.4 = bf16[384,512]{1,0:T(8,128)(2,1)S(1)} copy-done((bf16[384,512]{1,0:T(8,128)(2,1)S(1)}, bf16[384,512]{1,0:T(8,128)(2,1)}, u32[]{:S(2)}) %copy-start.4) | copy-done | bytes 393240
  12.1 2.0 %collective-permute-start.5 = (bf16[32,4608]{1,0:T(8,128)(2,1)S(1)}, bf16[32,4608]{1,0:T(8,128)(2,1)S(1)}, u32[]{:S(2)}, u32[]{:S(2)}) collective-permute-start(bf16[32,4608]{1,0:T(8,128)(2,1)S(1)} %collective-permute-done.4.refs_5_), channel_id=1, source_target_pairs={{4,0},{8,4},{12,8},{14,12},{10,14},{6,10},{2,6},{0,2},{5,1},{9,5},... | collective-permute-start | bytes 884744 | tf_op jit(solution)/shard_map/ppermute | solution.py:380
  14.2 1.8 %probs.7 = (bf16[512,128]{1,0:T(8,128)(2,1)S(1)}, bf16[512,128]{1,0:T(8,128)(2,1)S(1)}, bf16[512,256]{1,0:T(8,128)(2,1)S(1)}, bf16[512,256]{1,0:T(8,128)(2,1)S(1...) custom-call(s32[384,1]{1,0:T(8,128)S(1)} %get-tuple-element.58.segment_ref, ...), custom_call_target="tpu_custom_call" | custom-call | flops 2000000000 | bytes 1310720 | tf_op jit(solution)/shard_map/probs/pallas_call | solution.py:117
  16.0 4.5 %collective-permute-done.8.refs_3_ = bf16[32,4608]{1,0:T(8,128)(2,1)S(1)} collective-permute-done((bf16[32,4608]{1,0:T(8,128)(2,1)S(1)}, bf16[32,4608]{1,0:T(8,128)(2,1)S(1)}, u32[]{:S(2)}, u32[]{:S(2)}) %collective-permute-start.8) | collective-permute-done | bytes 294944 | tf_op jit(solution)/shard_map/ppermute | solution.py:380
  20.5 1.9 %collective-permute-start.12 = (bf16[32,4608]{1,0:T(8,128)(2,1)S(1)}, bf16[32,4608]{1,0:T(8,128)(2,1)S(1)}, u32[]{:S(2)}, u32[]{:S(2)}) collective-permute-start(bf16[32,4608]{1,0:T(8,128)(2,1)S(1)} %collective-permute-done.11.refs_4_), channel_id=1, source_target_pairs={{4,0},{8,4},{12,8},{14,12},{10,14},{6,10},{2,6},{0,2},{5,1},{9,5},... | collective-permute-start | bytes 884744 | tf_op jit(solution)/shard_map/ppermute | solution.py:380
  22.5 1.8 %probs.6 = (bf16[512,128]{1,0:T(8,128)(2,1)S(1)}, bf16[512,128]{1,0:T(8,128)(2,1)S(1)}, bf16[512,256]{1,0:T(8,128)(2,1)S(1)}, bf16[512,256]{1,0:T(8,128)(2,1)S(1...) custom-call(s32[384,1]{1,0:T(8,128)S(1)} %get-tuple-element.58.segment_ref, ...), custom_call_target="tpu_custom_call" | custom-call | flops 2000000000 | bytes 1310720 | tf_op jit(solution)/shard_map/probs/pallas_call | solution.py:117
  24.7 2.0 %collective-permute-start.6 = (bf16[32,4608]{1,0:T(8,128)(2,1)S(1)}, bf16[32,4608]{1,0:T(8,128)(2,1)S(1)}, u32[]{:S(2)}, u32[]{:S(2)}) collective-permute-start(bf16[32,4608]{1,0:T(8,128)(2,1)S(1)} %collective-permute-done.5.refs_3_), channel_id=1, source_target_pairs={{4,0},{8,4},{12,8},{14,12},{10,14},{6,10},{2,6},{0,2},{5,1},{9,5},... | collective-permute-start | bytes 884744 | tf_op jit(solution)/shard_map/ppermute | solution.py:380
  26.8 1.8 %probs.5 = (bf16[512,128]{1,0:T(8,128)(2,1)S(1)}, bf16[512,128]{1,0:T(8,128)(2,1)S(1)}, bf16[512,256]{1,0:T(8,128)(2,1)S(1)}, bf16[512,256]{1,0:T(8,128)(2,1)S(1...) custom-call(s32[384,1]{1,0:T(8,128)S(1)} %get-tuple-element.58.segment_ref, ...), custom_call_target="tpu_custom_call" | custom-call | flops 2000000000 | bytes 1310720 | tf_op jit(solution)/shard_map/probs/pallas_call | solution.py:117
  28.6 4.5 %collective-permute-done.9.refs_6_.refs_1_ = bf16[32,4608]{1,0:T(8,128)(2,1)S(1)} collective-permute-done((bf16[32,4608]{1,0:T(8,128)(2,1)S(1)}, bf16[32,4608]{1,0:T(8,128)(2,1)S(1)}, u32[]{:S(2)}, u32[]{:S(2)}) %collective-permute-start.9) | collective-permute-done | bytes 294944 | tf_op jit(solution)/shard_map/ppermute | solution.py:380
  33.2 1.9 %collective-permute-start.13 = (bf16[32,4608]{1,0:T(8,128)(2,1)S(1)}, bf16[32,4608]{1,0:T(8,128)(2,1)S(1)}, u32[]{:S(2)}, u32[]{:S(2)}) collective-permute-start(bf16[32,4608]{1,0:T(8,128)(2,1)S(1)} %collective-permute-done.12.refs_7_.refs_2_), channel_id=1, source_target_pairs={{4,0},{8,4},{12,8},{14,12},{10,14},{6,10},{2,6},{0,2},{5,1},{9,5},... | collective-permute-start | bytes 884744 | tf_op jit(solution)/shard_map/ppermute | solution.py:380
  35.1 1.8 %probs.4 = (bf16[512,128]{1,0:T(8,128)(2,1)S(1)}, bf16[512,128]{1,0:T(8,128)(2,1)S(1)}, bf16[512,256]{1,0:T(8,128)(2,1)S(1)}, bf16[512,256]{1,0:T(8,128)(2,1)S(1...) custom-call(s32[384,1]{1,0:T(8,128)S(1)} %get-tuple-element.58.segment_ref, ...), custom_call_target="tpu_custom_call" | custom-call | flops 2000000000 | bytes 1310720 | tf_op jit(solution)/shard_map/probs/pallas_call | solution.py:117
  39.5 1.6 %collective-permute-start.7 = (bf16[32,4608]{1,0:T(8,128)(2,1)S(1)}, bf16[32,4608]{1,0:T(8,128)(2,1)S(1)}, u32[]{:S(2)}, u32[]{:S(2)}) collective-permute-start(bf16[32,4608]{1,0:T(8,128)(2,1)S(1)} %collective-permute-done.6.refs_3_), channel_id=1, source_target_pairs={{4,0},{8,4},{12,8},{14,12},{10,14},{6,10},{2,6},{0,2},{5,1},{9,5},... | collective-permute-start | bytes 884744 | tf_op jit(solution)/shard_map/ppermute | solution.py:380
  41.5 1.1 %lowrank.3 = (f32[384,64]{1,0:T(8,128)S(1)}, bf16[192,512]{1,0:T(8,128)(2,1)S(1)}) custom-call(s32[384,1]{1,0:T(8,128)S(1)} %get-tuple-element.55.place_ref, bf16[384,4096]{1,0:T(8,128)(2,1)S(1)} %copy-done, bf16[32,4608]{1,0:T(8,128)(2,1)S(1)} %get-tuple-element.104.refs_0_, bf16[32,4608]{1,0:T(8,128)(2,1)S(1)} %get-tuple-element.103.refs_1_, ...), custom_call_target="tpu_custom_call" | custom-call | flops 1000000000 | bytes 1200 | tf_op jit(solution)/shard_map/lowrank/pallas_call | solution.py:155
  42.6 1.1 %lowrank.4 = (f32[384,64]{1,0:T(8,128)S(1)}, bf16[128,512]{1,0:T(8,128)(2,1)S(1)}) custom-call(s32[384,1]{1,0:T(8,128)S(1)} %get-tuple-element.55.place_ref, bf16[384,4096]{1,0:T(8,128)(2,1)S(1)} %copy-done, bf16[32,4608]{1,0:T(8,128)(2,1)S(1)} %collective-permute-done.1.refs_0_, bf16[32,4608]{1,0:T(8,128)(2,1)S(1)} %collective-permute-done.9.refs_6_.refs_1_, ...), custom_call_target="tpu_custom_call" | custom-call | flops 1000000000 | bytes 1056 | tf_op jit(solution)/shard_map/lowrank/pallas_call | solution.py:155
  43.7 2.0 %collective-permute-done.10.refs_1_ = bf16[32,4608]{1,0:T(8,128)(2,1)S(1)} collective-permute-done((bf16[32,4608]{1,0:T(8,128)(2,1)S(1)}, bf16[32,4608]{1,0:T(8,128)(2,1)S(1)}, u32[]{:S(2)}, u32[]{:S(2)}) %collective-permute-start.10) | collective-permute-done | bytes 294944 | tf_op jit(solution)/shard_map/ppermute | solution.py:380
  45.7 1.0 %lowrank.5 = (f32[384,64]{1,0:T(8,128)S(1)}, bf16[128,512]{1,0:T(8,128)(2,1)S(1)}) custom-call(s32[384,1]{1,0:T(8,128)S(1)} %get-tuple-element.55.place_ref, bf16[384,4096]{1,0:T(8,128)(2,1)S(1)} %copy-done, bf16[32,4608]{1,0:T(8,128)(2,1)S(1)} %collective-permute-done.2.refs_0_, bf16[32,4608]{1,0:T(8,128)(2,1)S(1)} %collective-permute-done.10.refs_1_, ...), custom_call_target="tpu_custom_call" | custom-call | flops 1000000000 | bytes 1056 | tf_op jit(solution)/shard_map/lowrank/pallas_call | solution.py:155
  46.8 1.4 %collective-permute-done.14.theirs_ref = f32[384,64]{1,0:T(8,128)S(1)} collective-permute-done((f32[384,64]{1,0:T(8,128)S(1)}, f32[384,64]{1,0:T(8,128)S(1)}, u32[]{:S(2)}, u32[]{:S(2)}) %collective-permute-start.14) | collective-permute-done | bytes 98336 | tf_op jit(solution)/shard_map/ppermute | solution.py:409
  48.3 1.9 %early_product.1.refs_0_.early_ref = f32[384,4096]{1,0:T(8,128)S(1)} custom-call(s32[384,1]{1,0:T(8,128)S(1)} %get-tuple-element.55.place_ref, f32[384,64]{1,0:T(8,128)S(1)} %get-tuple-element.87.mine_ref, f32[384,64]{1,0:T(8,128)S(1)} %collective-permute-done.14.theirs_ref, bf16[384,512]{1,0:T(8,128)(2,1)S(1)} %copy-done.1, ...), custom_call_target="tpu_custom_call" | custom-call | flops 50000000 | bytes 1536 | tf_op jit(solution)/shard_map/early_product/pallas_call | solution.py:262
  51.0 1.2 %collective-permute-done.15.theirs_ref = f32[96,64]{1,0:T(8,128)S(1)} collective-permute-done((f32[96,64]{1,0:T(8,128)S(1)}, f32[96,64]{1,0:T(8,128)S(1)}, u32[]{:S(2)}, u32[]{:S(2)}) %collective-permute-start.15) | collective-permute-done | bytes 24608 | tf_op jit(solution)/shard_map/ppermute | solution.py:411
  52.2 2.1 %finish.1 = bf16[384,4096]{1,0:T(8,128)(2,1)} custom-call(f32[96,64]{1,0:T(8,128)S(1)} %get-tuple-element.91.mine_ref, f32[96,64]{1,0:T(8,128)S(1)} %collective-permute-done.15.theirs_ref, bf16[64,512]{1,0:T(8,128)(2,1)S(1)} %get-tuple-element.92.up_ref, f32[384,4096]{1,0:T(8,128)S(1)} %early_product.1.refs_0_.early_ref, ...), custom_call_target="tpu_custom_call" | custom-call | tf_op jit(solution)/shard_map/finish/pallas_call | solution.py:341
  (39 shorter events, 7.9 us)
Async XLA Ops:
  0.0 14.2 %copy-start.5 = (bf16[384,512]{1,0:T(8,128)(2,1)S(1)}, bf16[384,512]{1,0:T(8,128)(2,1)}, u32[]{:S(2)}) copy-start(bf16[384,512]{1,0:T(8,128)(2,1)} %k_ref.7) | copy-start | bytes 1179652
  1.2 10.9 %collective-permute-start.4 = (bf16[32,4608]{1,0:T(8,128)(2,1)S(1)}, bf16[32,4608]{1,0:T(8,128)(2,1)S(1)}, u32[]{:S(2)}, u32[]{:S(2)}) collective-permute-start(bf16[32,4608]{1,0:T(8,128)(2,1)S(1)} %get-tuple-element.103.refs_1_), channel_id=1, source_target_pairs={{4,0},{8,4},{12,8},{14,12},{10,14},{6,10},{2,6},{0,2},{5,1},{9,5},... | collective-permute-start | bytes 884744 | tf_op jit(solution)/shard_map/ppermute | solution.py:380
  4.2 9.9 %collective-permute-start = (bf16[32,4608]{1,0:T(8,128)(2,1)S(1)}, bf16[32,4608]{1,0:T(8,128)(2,1)S(1)}, u32[]{:S(2)}, u32[]{:S(2)}) collective-permute-start(bf16[32,4608]{1,0:T(8,128)(2,1)S(1)} %get-tuple-element.104.refs_0_), channel_id=1, source_target_pairs={{0,4},{4,8},{8,12},{12,14},{14,10},{10,6},{6,2},{2,0},{1,5},{5,9},... | collective-permute-start | bytes 884744 | tf_op jit(solution)/shard_map/ppermute | solution.py:380
  4.3 16.1 %collective-permute-start.8 = (bf16[32,4608]{1,0:T(8,128)(2,1)S(1)}, bf16[32,4608]{1,0:T(8,128)(2,1)S(1)}, u32[]{:S(2)}, u32[]{:S(2)}) collective-permute-start(bf16[32,4608]{1,0:T(8,128)(2,1)S(1)} %get-tuple-element.103.refs_1_), channel_id=1, source_target_pairs={{0,4},{4,8},{8,12},{12,14},{14,10},{10,6},{6,2},{2,0},{1,5},{5,9},... | collective-permute-start | bytes 884744 | tf_op jit(solution)/shard_map/ppermute | solution.py:380
  6.3 14.3 %collective-permute-start.11 = (bf16[32,4608]{1,0:T(8,128)(2,1)S(1)}, bf16[32,4608]{1,0:T(8,128)(2,1)S(1)}, u32[]{:S(2)}, u32[]{:S(2)}) collective-permute-start(bf16[32,4608]{1,0:T(8,128)(2,1)S(1)} %get-tuple-element.104.refs_0_), channel_id=1, source_target_pairs={{4,0},{8,4},{12,8},{14,12},{10,14},{6,10},{2,6},{0,2},{5,1},{9,5},... | collective-permute-start | bytes 884744 | tf_op jit(solution)/shard_map/ppermute | solution.py:380
  6.3 1.9 %copy-start.2 = (bf16[384,4096]{1,0:T(8,128)(2,1)S(1)}, bf16[384,4096]{1,0:T(8,128)(2,1)}, u32[]{:S(2)}) copy-start(bf16[384,4096]{1,0:T(8,128)(2,1)} %q_ref.7) | copy-start | bytes 9437188
  8.2 1.0 %copy-start.4 = (bf16[384,512]{1,0:T(8,128)(2,1)S(1)}, bf16[384,512]{1,0:T(8,128)(2,1)}, u32[]{:S(2)}) copy-start(bf16[384,512]{1,0:T(8,128)(2,1)} %k_ref.7) | copy-start | bytes 1179652
  9.2 0.7 %copy-start.6 = (s32[384,1]{0,1:T(1,128)S(1)}, s32[384,1]{0,1:T(1,128)}, u32[]{:S(2)}) copy-start(s32[384,1]{0,1:T(1,128)} %param.12) | copy-start | bytes 4612
  9.9 0.7 %copy-start.7 = (s32[1,4]{1,0:T(1,128)S(1)}, s32[1,4]{1,0:T(1,128)}, u32[]{:S(2)}) copy-start(s32[1,4]{1,0:T(1,128)} %lengths_ref.1) | copy-start | bytes 52
  10.6 3.6 %copy-start.3 = (bf16[384,4096]{1,0:T(8,128)(2,1)S(1)}, bf16[384,4096]{1,0:T(8,128)(2,1)}, u32[]{:S(2)}) copy-start(bf16[384,4096]{1,0:T(8,128)(2,1)} %q_ref.7) | copy-start | bytes 9437188
  12.1 12.6 %collective-permute-start.5 = (bf16[32,4608]{1,0:T(8,128)(2,1)S(1)}, bf16[32,4608]{1,0:T(8,128)(2,1)S(1)}, u32[]{:S(2)}, u32[]{:S(2)}) collective-permute-start(bf16[32,4608]{1,0:T(8,128)(2,1)S(1)} %collective-permute-done.4.refs_5_), channel_id=1, source_target_pairs={{4,0},{8,4},{12,8},{14,12},{10,14},{6,10},{2,6},{0,2},{5,1},{9,5},... | collective-permute-start | bytes 884744 | tf_op jit(solution)/shard_map/ppermute | solution.py:380
  14.1 12.6 %collective-permute-start.1 = (bf16[32,4608]{1,0:T(8,128)(2,1)S(1)}, bf16[32,4608]{1,0:T(8,128)(2,1)S(1)}, u32[]{:S(2)}, u32[]{:S(2)}) collective-permute-start(bf16[32,4608]{1,0:T(8,128)(2,1)S(1)} %collective-permute-done.refs_2_), channel_id=1, source_target_pairs={{0,4},{4,8},{8,12},{12,14},{14,10},{10,6},{6,2},{2,0},{1,5},{5,9},... | collective-permute-start | bytes 884744 | tf_op jit(solution)/shard_map/ppermute | solution.py:380
  20.4 12.6 %collective-permute-start.9 = (bf16[32,4608]{1,0:T(8,128)(2,1)S(1)}, bf16[32,4608]{1,0:T(8,128)(2,1)S(1)}, u32[]{:S(2)}, u32[]{:S(2)}) collective-permute-start(bf16[32,4608]{1,0:T(8,128)(2,1)S(1)} %collective-permute-done.8.refs_3_), channel_id=1, source_target_pairs={{0,4},{4,8},{8,12},{12,14},{14,10},{10,6},{6,2},{2,0},{1,5},{5,9},... | collective-permute-start | bytes 884744 | tf_op jit(solution)/shard_map/ppermute | solution.py:380
  20.5 12.6 %collective-permute-start.12 = (bf16[32,4608]{1,0:T(8,128)(2,1)S(1)}, bf16[32,4608]{1,0:T(8,128)(2,1)S(1)}, u32[]{:S(2)}, u32[]{:S(2)}) collective-permute-start(bf16[32,4608]{1,0:T(8,128)(2,1)S(1)} %collective-permute-done.11.refs_4_), channel_id=1, source_target_pairs={{4,0},{8,4},{12,8},{14,12},{10,14},{6,10},{2,6},{0,2},{5,1},{9,5},... | collective-permute-start | bytes 884744 | tf_op jit(solution)/shard_map/ppermute | solution.py:380
  24.7 14.7 %collective-permute-start.6 = (bf16[32,4608]{1,0:T(8,128)(2,1)S(1)}, bf16[32,4608]{1,0:T(8,128)(2,1)S(1)}, u32[]{:S(2)}, u32[]{:S(2)}) collective-permute-start(bf16[32,4608]{1,0:T(8,128)(2,1)S(1)} %collective-permute-done.5.refs_3_), channel_id=1, source_target_pairs={{4,0},{8,4},{12,8},{14,12},{10,14},{6,10},{2,6},{0,2},{5,1},{9,5},... | collective-permute-start | bytes 884744 | tf_op jit(solution)/shard_map/ppermute | solution.py:380
  26.8 14.3 %collective-permute-start.2 = (bf16[32,4608]{1,0:T(8,128)(2,1)S(1)}, bf16[32,4608]{1,0:T(8,128)(2,1)S(1)}, u32[]{:S(2)}, u32[]{:S(2)}) collective-permute-start(bf16[32,4608]{1,0:T(8,128)(2,1)S(1)} %collective-permute-done.1.refs_0_), channel_id=1, source_target_pairs={{0,4},{4,8},{8,12},{12,14},{14,10},{10,6},{6,2},{2,0},{1,5},{5,9},... | collective-permute-start | bytes 884744 | tf_op jit(solution)/shard_map/ppermute | solution.py:380
  28.6 8.3 %copy-start = (bf16[384,4096]{1,0:T(8,128)(2,1)S(1)}, bf16[384,4096]{1,0:T(8,128)(2,1)}, u32[]{:S(2)}) copy-start(bf16[384,4096]{1,0:T(8,128)(2,1)} %x_ref.7) | copy-start | bytes 9437188
  33.1 12.6 %collective-permute-start.10 = (bf16[32,4608]{1,0:T(8,128)(2,1)S(1)}, bf16[32,4608]{1,0:T(8,128)(2,1)S(1)}, u32[]{:S(2)}, u32[]{:S(2)}) collective-permute-start(bf16[32,4608]{1,0:T(8,128)(2,1)S(1)} %collective-permute-done.9.refs_6_.refs_1_), channel_id=1, source_target_pairs={{0,4},{4,8},{8,12},{12,14},{14,10},{10,6},{6,2},{2,0},{1,5},{5,9},... | collective-permute-start | bytes 884744 | tf_op jit(solution)/shard_map/ppermute | solution.py:380
  33.2 12.6 %collective-permute-start.13 = (bf16[32,4608]{1,0:T(8,128)(2,1)S(1)}, bf16[32,4608]{1,0:T(8,128)(2,1)S(1)}, u32[]{:S(2)}, u32[]{:S(2)}) collective-permute-start(bf16[32,4608]{1,0:T(8,128)(2,1)S(1)} %collective-permute-done.12.refs_7_.refs_2_), channel_id=1, source_target_pairs={{4,0},{8,4},{12,8},{14,12},{10,14},{6,10},{2,6},{0,2},{5,1},{9,5},... | collective-permute-start | bytes 884744 | tf_op jit(solution)/shard_map/ppermute | solution.py:380
  39.5 10.7 %collective-permute-start.7 = (bf16[32,4608]{1,0:T(8,128)(2,1)S(1)}, bf16[32,4608]{1,0:T(8,128)(2,1)S(1)}, u32[]{:S(2)}, u32[]{:S(2)}) collective-permute-start(bf16[32,4608]{1,0:T(8,128)(2,1)S(1)} %collective-permute-done.6.refs_3_), channel_id=1, source_target_pairs={{4,0},{8,4},{12,8},{14,12},{10,14},{6,10},{2,6},{0,2},{5,1},{9,5},... | collective-permute-start | bytes 884744 | tf_op jit(solution)/shard_map/ppermute | solution.py:380
  41.1 9.5 %collective-permute-start.3 = (bf16[32,4608]{1,0:T(8,128)(2,1)S(1)}, bf16[32,4608]{1,0:T(8,128)(2,1)S(1)}, u32[]{:S(2)}, u32[]{:S(2)}) collective-permute-start(bf16[32,4608]{1,0:T(8,128)(2,1)S(1)} %collective-permute-done.2.refs_0_), channel_id=1, source_target_pairs={{0,4},{4,8},{8,12},{12,14},{14,10},{10,6},{6,2},{2,0},{1,5},{5,9},... | collective-permute-start | bytes 884744 | tf_op jit(solution)/shard_map/ppermute | solution.py:380
  43.7 4.6 %copy-start.1 = (bf16[384,512]{1,0:T(8,128)(2,1)S(1)}, bf16[384,512]{1,0:T(8,128)(2,1)}, u32[]{:S(2)}) copy-start(bf16[384,512]{1,0:T(8,128)(2,1)} %base_ref.1) | copy-start | bytes 1179652
  46.8 1.5 %collective-permute-start.14 = (f32[384,64]{1,0:T(8,128)S(1)}, f32[384,64]{1,0:T(8,128)S(1)}, u32[]{:S(2)}, u32[]{:S(2)}) collective-permute-start(f32[384,64]{1,0:T(8,128)S(1)} %get-tuple-element.87.mine_ref), channel_id=1, source_target_pairs={{0,1},{1,0},{2,3},{3,2},{4,5},{5,4},{6,7},{7,6},{8,9},{9,8},{10,11... | collective-permute-start | bytes 294920 | tf_op jit(solution)/shard_map/ppermute | solution.py:409
  50.9 1.3 %collective-permute-start.15 = (f32[96,64]{1,0:T(8,128)S(1)}, f32[96,64]{1,0:T(8,128)S(1)}, u32[]{:S(2)}, u32[]{:S(2)}) collective-permute-start(f32[96,64]{1,0:T(8,128)S(1)} %get-tuple-element.91.mine_ref), channel_id=1, source_target_pairs={{0,1},{1,0},{2,3},{3,2},{4,5},{5,4},{6,7},{7,6},{8,9},{9,8},{10,11... | collective-permute-start | bytes 73736 | tf_op jit(solution)/shard_map/ppermute | solution.py:411
